TPU v7x, 32 devices: a whole 2x2x4 slice. The times are simulated.
32 devices in a mesh: sec: 4 (over y, x), lat: 8 (over z, core).
Axes of the slice: x: 2, y: 2, z: 4, core: 2. Of those that a mesh axis runs over, the one named last changes fastest.
Arguments:
- spectra: float32 [32, 96, 768], P('lat', 'sec'), may hold values from 0.2 to 2
- turning: float32 [32, 96], P('lat', 'sec'), may hold values from -0.45 to 0.45
- currents: float32 [32, 96, 64], P('lat', 'sec'), may hold values from -3 to 3
- drag_rates: float32 [32], replicated, may hold values from 0.02 to 0.3
- land_mask: int32 [32, 96], P('lat', 'sec'), may hold values 0 or 1
- ocean_target: int32 [32, 96], P('lat', 'sec'), may hold values from 0 to 3, as said below
Outputs:
- spectra_out: float32 [32, 96, 768], P('lat', 'sec')
- currents_out: float32 [32, 96, 64], P('lat', 'sec')
Inputs may be any that keep to these rules, and one draw needn't show every extreme that they name: `ocean_target`: in each device's block of 4 x 24 columns every target value appears on exactly 24 columns.
All inputs are finite; a program needn't handle non-finite values. No bound on the sum of `land_mask` on one device may be relied on, other than what follows from the above.
Results may differ from a plain program's by a relative error of at most 0.0003.
Values sent between devices are 32-bit elements; how exact they have to be, the bound alone decides.
No kernel may reach another device: no remote copies, remote signals or barrier semaphores. Data moves between devices by JAX's collectives and lax.ppermute only.
A program may use at most 64 MiB of HBM per device.

v0:
```python
import math

import jax
import jax.numpy as jnp
from jax import lax
from jax.sharding import PartitionSpec as P

NFREQ = 24
NDIR = 32
STEPS = 3


stokes_scale = 0.1
ocean_dt = 0.3
current_gain = 0.2


def with_halo(cells, sides, width):
    for axis, dim in sides:
        count = lax.axis_size(axis)
        ends = count - 1
        head = lax.slice_in_dim(cells, 0, width, axis=dim)
        tail = lax.slice_in_dim(cells, cells.shape[dim] - width, cells.shape[dim], axis=dim)
        cells = jnp.concatenate(
            [
                lax.ppermute(tail, axis, [(i, (i + 1) % count) for i in range(ends)]),
                cells,
                lax.ppermute(head, axis, [((i + 1) % count, i) for i in range(ends)]),
            ],
            axis=dim,
        )
    return cells


def build_tables(nfreq, ndir, ndepth):
    fraction = jnp.arange(nfreq, dtype=jnp.float32) / (nfreq - 1)
    angles = (jnp.arange(ndir, dtype=jnp.float32) + 0.5) * (2.0 * math.pi / ndir)
    east_part = jnp.cos(angles)
    north_part = jnp.sin(angles)
    courant = 0.1 + 0.3 * fraction
    levels = jnp.arange(ndepth, dtype=jnp.float32)
    depth_level = 0.5 + (ndepth - 2) * (1.0 - fraction)
    weights = jnp.maximum(1.0 - jnp.abs(levels[None, :] - depth_level[:, None]), 0.0)
    mean_weights = weights / jnp.sum(weights, axis=1, keepdims=True)
    x_rate = (courant[:, None] * east_part[None, :]).reshape(-1)
    y_rate = (courant[:, None] * north_part[None, :]).reshape(-1)
    compass = jnp.stack([east_part, north_part])
    eye_freq = jnp.eye(nfreq, dtype=jnp.float32)
    eye_two = jnp.eye(2, dtype=jnp.float32)
    stokes_matrix = (
        stokes_scale * weights[:, None, None, :] * compass.T[None, :, :, None]
    ).reshape(nfreq * ndir, 2 * ndepth)
    moment_matrix = (eye_freq[:, None, None, :] * compass.T[None, :, :, None]).reshape(
        nfreq * ndir, 2 * nfreq
    )
    profile_matrix = (stokes_scale * eye_two[:, None, :, None] * weights[None, :, None, :]).reshape(
        2 * nfreq, 2 * ndepth
    )
    average_matrix = (eye_two[:, None, :, None] * mean_weights.T[None, :, None, :]).reshape(
        2 * ndepth, 2 * nfreq
    )
    turn_gain = 1.0 - 0.5 * fraction
    growth = current_gain * (1.0 + fraction)
    return (
        east_part,
        north_part,
        x_rate,
        y_rate,
        stokes_matrix,
        moment_matrix,
        profile_matrix,
        average_matrix,
        turn_gain,
        growth,
    )


def upwind(center, west, east, south, north, x_rate, y_rate):
    along_x = jnp.maximum(x_rate, 0.0) * (center - west) + jnp.minimum(x_rate, 0.0) * (
        east - center
    )
    along_y = jnp.maximum(y_rate, 0.0) * (center - south) + jnp.minimum(y_rate, 0.0) * (
        north - center
    )
    return center - along_x - along_y


def turn_grow(
    advected, turning, current_eff, east_part, north_part, turn_gain, growth, nfreq, ndir
):
    layout = advected.shape
    spread = advected.reshape(layout[:-1] + (nfreq, ndir))
    turn_rate = turning[..., None, None] * turn_gain[:, None]
    behind = jnp.roll(spread, 1, axis=-1)
    forward = jnp.roll(spread, -1, axis=-1)
    turned = (
        spread
        - jnp.maximum(turn_rate, 0.0) * (spread - behind)
        - jnp.minimum(turn_rate, 0.0) * (forward - spread)
    )
    zonal = current_eff[..., :nfreq]
    meridional = current_eff[..., nfreq:]
    aligned = zonal[..., None] * east_part + meridional[..., None] * north_part
    grown = turned * (1.0 + growth[:, None] * aligned)
    return grown.reshape(layout)


def ocean_step(currents, padded, stokes, coriolis, keep, ndepth):
    zonal = currents[..., :ndepth]
    meridional = currents[..., ndepth:]
    shear = 0.5 * (padded[1:-1, 2:, ndepth:] - padded[1:-1, :-2, ndepth:]) - 0.5 * (
        padded[2:, 1:-1, :ndepth] - padded[:-2, 1:-1, :ndepth]
    )
    spin = coriolis[:, None, None] + shear
    new_zonal = keep * (zonal + ocean_dt * spin * (meridional + stokes[..., ndepth:]))
    new_merid = keep * (meridional - ocean_dt * spin * (zonal + stokes[..., :ndepth]))
    return jnp.concatenate([new_zonal, new_merid], axis=-1)


def couple(outgoing, homeward):
    return (
        lax.all_to_all(outgoing, "sec", split_axis=0, concat_axis=0, tiled=True),
        lax.all_to_all(homeward, "sec", split_axis=0, concat_axis=0, tiled=True),
    )


def neighbours(spectra):
    padded = with_halo(spectra, (("lat", 0), ("sec", 1)), 1)
    return (padded[1:-1, :-2], padded[1:-1, 2:], padded[:-2, 1:-1], padded[2:, 1:-1])


def per_device(spectra, turning, currents, drag_rates, land_mask, ocean_target):
    lat_rows, lon_cols, spectral = spectra.shape
    depth_count = drag_rates.shape[0]
    sections = lax.axis_size("sec")
    column_count = lat_rows * lon_cols
    (
        east_part,
        north_part,
        x_rate,
        y_rate,
        stokes_matrix,
        moment_matrix,
        profile_matrix,
        average_matrix,
        turn_gain,
        growth,
    ) = build_tables(NFREQ, NDIR, depth_count)
    order = jnp.argsort(ocean_target.reshape(-1), stable=True)
    inverse = jnp.argsort(order, stable=True)
    sea = land_mask.astype(jnp.float32)[..., None]
    keep = 1.0 - drag_rates
    global_rows = (lax.axis_index("lat") * lat_rows + jnp.arange(lat_rows, dtype=jnp.int32)).astype(
        jnp.float32
    )
    coriolis = 0.2 + 0.6 * global_rows / (lat_rows * lax.axis_size("lat"))
    highest = lax.Precision.HIGHEST
    for iteration in range(STEPS):
        flat_waves = spectra.reshape(column_count, spectral)
        flat_ocean = currents.reshape(column_count, 2 * depth_count)
        outgoing = jnp.dot(flat_waves, stokes_matrix, precision=highest)[order]
        arrived, returned = couple(outgoing.reshape(sections, -1), flat_ocean.reshape(sections, -1))
        arrived = arrived.reshape(column_count, -1)
        returned = returned.reshape(column_count, -1)[inverse]
        current_eff = jnp.dot(returned, average_matrix, precision=highest)
        west, east, south, north = neighbours(spectra)
        ocean_padded = with_halo(currents, (("lat", 0), ("sec", 1)), 1)
        advected = upwind(spectra, west, east, south, north, x_rate, y_rate)
        new_spectra = (
            turn_grow(
                advected,
                turning,
                current_eff.reshape(lat_rows, lon_cols, -1),
                east_part,
                north_part,
                turn_gain,
                growth,
                NFREQ,
                NDIR,
            )
            * sea
        )
        currents = (
            ocean_step(
                currents,
                ocean_padded,
                arrived.reshape(lat_rows, lon_cols, -1),
                coriolis,
                keep,
                depth_count,
            )
            * sea
        )
        spectra = new_spectra
    return (spectra, currents)


def solution(mesh):
    return jax.shard_map(
        per_device,
        mesh=mesh,
        in_specs=(
            P("lat", "sec", None),
            P("lat", "sec"),
            P("lat", "sec", None),
            P(),
            P("lat", "sec"),
            P("lat", "sec"),
        ),
        out_specs=(P("lat", "sec", None), P("lat", "sec", None)),
        check_vma=False,
    )
```

profile of v0, /device:TPU:1, one launch (start us, length us, event | category | flops | bytes accessed | tf_op | source)
XLA Modules:
  0.0 165.2 jit_solution(5355007670806132623)
XLA Ops:
  1.6 4.7 %collective-permute-start = (f32[1,24,768]{2,1,0:T(8,128)S(1)}, f32[1,24,768]{2,1,0:T(8,128)S(1)}, u32[]{:S(2)}, u32[]{:S(2)}) collective-permute-start(f32[1,24,768]{2,1,0:T(8,128)S(1)} %get-tuple-element.30), channel_id=1, source_target_pairs={{0,1},{1,2},{2,3},{3,4},{4,5},{5,6},{6,7},{8,9},{9,10},{10,11},{11... | collective-permute-start | bytes 221192 | tf_op jit(solution)/shard_map/ppermute | solution.py:26
  6.3 1.9 %collective-permute-start.1 = (f32[1,24,768]{2,1,0:T(8,128)S(1)}, f32[1,24,768]{2,1,0:T(8,128)S(1)}, u32[]{:S(2)}, u32[]{:S(2)}) collective-permute-start(f32[1,24,768]{2,1,0:T(8,128)S(1)} %get-tuple-element.31), channel_id=1, source_target_pairs={{1,0},{2,1},{3,2},{4,3},{5,4},{6,5},{7,6},{9,8},{10,9},{11,10},{12... | collective-permute-start | bytes 221192 | tf_op jit(solution)/shard_map/ppermute | solution.py:28
  8.3 1.5 all_to_all.32
  9.8 3.4 %all-to-all-start = ((f32[4,1,1536]{2,1,0:T(1,128)}), f32[4,1,1536]{2,1,0:T(1,128)S(1)}, u32[]{:S(2)}, u32[]{:S(2)}) async-start(f32[4,1,1536]{2,1,0:T(1,128)} %all_to_all.32), calls=%async_computation | async-start | bytes 49152 | tf_op jit(solution)/shard_map/all_to_all | solution.py:123
  13.9 3.9 %collective-permute-start.8 = (f32[1,24,64]{2,1,0:T(8,128)S(1)}, f32[1,24,64]{2,1,0:T(8,128)S(1)}, u32[]{:S(2)}, u32[]{:S(2)}) collective-permute-start(f32[1,24,64]{2,1,0:T(8,128)S(1)} %get-tuple-element.47), channel_id=1, source_target_pairs={{0,1},{1,2},{2,3},{3,4},{4,5},{5,6},{6,7},{8,9},{9,10},{10,11},{11... | collective-permute-start | bytes 18440 | tf_op jit(solution)/shard_map/ppermute | solution.py:26
  17.9 1.9 %collective-permute-start.9 = (f32[1,24,64]{2,1,0:T(8,128)S(1)}, f32[1,24,64]{2,1,0:T(8,128)S(1)}, u32[]{:S(2)}, u32[]{:S(2)}) collective-permute-start(f32[1,24,64]{2,1,0:T(8,128)S(1)} %get-tuple-element.46), channel_id=1, source_target_pairs={{1,0},{2,1},{3,2},{4,3},{5,4},{6,5},{7,6},{9,8},{10,9},{11,10},{12... | collective-permute-start | bytes 18440 | tf_op jit(solution)/shard_map/ppermute | solution.py:28
  21.2 2.5 %sort.31 = (s32[96]{0:T(128)}, s32[96]{0:T(128)S(1)}) sort(s32[96]{0:T(128)S(1)} %reshape.366, s32[96]{0:T(128)S(1)} %iota.138), dimensions={0}, to_apply=%region_0.0 | sort | flops 672 | bytes 1536 | tf_op jit(solution)/shard_map/jit(argsort)/sort | solution.py:149
  23.7 2.5 %sort.32 = (s32[96]{0:T(128)}, s32[96]{0:T(128)S(1)}) sort(s32[96]{0:T(128)S(1)} %get-tuple-element.4, s32[96]{0:T(128)S(1)} %iota.139), dimensions={0}, to_apply=%region_1.0 | sort | flops 672 | bytes 1536 | tf_op jit(solution)/shard_map/jit(argsort)/sort | solution.py:150
  30.2 4.3 %collective-permute-start.11 = (f32[6,1,64]{2,1,0:T(1,128)S(1)}, f32[6,1,64]{2,1,0:T(1,128)S(1)}, u32[]{:S(2)}, u32[]{:S(2)}) collective-permute-start(f32[6,1,64]{2,1,0:T(1,128)S(1)} %get-tuple-element.37), channel_id=1, source_target_pairs={{0,8},{8,16},{16,24},{1,9},{9,17},{17,25},{2,10},{10,18},{18,26},{... | collective-permute-start | bytes 4616 | tf_op jit(solution)/shard_map/ppermute | solution.py:26
  34.5 3.6 %all-to-all-start.1 = ((f32[4,1,1536]{2,1,0:T(1,128)}), f32[4,1,1536]{2,1,0:T(1,128)S(1)}, u32[]{:S(2)}, u32[]{:S(2)}) async-start(f32[4,1,1536]{2,1,0:T(1,128)} %all_to_all.42), calls=%async_computation.1 | async-start | bytes 49152 | tf_op jit(solution)/shard_map/all_to_all | solution.py:122
  42.3 5.6 %collective-permute-start.16 = (f32[1,24,64]{2,1,0:T(8,128)S(1)}, f32[1,24,64]{2,1,0:T(8,128)S(1)}, u32[]{:S(2)}, u32[]{:S(2)}) collective-permute-start(f32[1,24,64]{2,1,0:T(8,128)S(1)} %get-tuple-element.45), channel_id=1, source_target_pairs={{0,1},{1,2},{2,3},{3,4},{4,5},{5,6},{6,7},{8,9},{9,10},{10,11},{11... | collective-permute-start | bytes 18440 | tf_op jit(solution)/shard_map/ppermute | solution.py:26
  47.9 1.9 %collective-permute-start.17 = (f32[1,24,64]{2,1,0:T(8,128)S(1)}, f32[1,24,64]{2,1,0:T(8,128)S(1)}, u32[]{:S(2)}, u32[]{:S(2)}) collective-permute-start(f32[1,24,64]{2,1,0:T(8,128)S(1)} %get-tuple-element.44), channel_id=1, source_target_pairs={{1,0},{2,1},{3,2},{4,3},{5,4},{6,5},{7,6},{9,8},{10,9},{11,10},{12... | collective-permute-start | bytes 18440 | tf_op jit(solution)/shard_map/ppermute | solution.py:28
  54.3 3.3 %all-to-all-start.2 = ((f32[4,1,1536]{2,1,0:T(1,128)}), f32[4,1,1536]{2,1,0:T(1,128)S(1)}, u32[]{:S(2)}, u32[]{:S(2)}) async-start(f32[4,1,1536]{2,1,0:T(1,128)} %mul.933), calls=%async_computation.2 | async-start | bytes 49152 | tf_op jit(solution)/shard_map/all_to_all | solution.py:123
  59.5 4.6 %collective-permute-start.19 = (f32[6,1,64]{2,1,0:T(1,128)}, f32[6,1,64]{2,1,0:T(1,128)}, u32[]{:S(2)}, u32[]{:S(2)}) collective-permute-start(f32[6,1,64]{2,1,0:T(1,128)} %get-tuple-element.35), channel_id=1, source_target_pairs={{0,8},{8,16},{16,24},{1,9},{9,17},{17,25},{2,10},{10,18},{18,26},{... | collective-permute-start | bytes 4616 | tf_op jit(solution)/shard_map/ppermute | solution.py:26
  64.9 3.6 %collective-permute-start.2 = (f32[6,1,768]{2,1,0:T(1,128)S(1)}, f32[6,1,768]{2,1,0:T(1,128)S(1)}, u32[]{:S(2)}, u32[]{:S(2)}) collective-permute-start(f32[6,1,768]{2,1,0:T(1,128)S(1)} %get-tuple-element.24), channel_id=1, source_target_pairs={{0,8},{8,16},{16,24},{1,9},{9,17},{17,25},{2,10},{10,18},{18,26},{... | collective-permute-start | bytes 55304 | tf_op jit(solution)/shard_map/ppermute | solution.py:26
  70.1 3.0 %collective-permute-done.3 = f32[6,1,768]{2,1,0:T(1,128)S(1)} collective-permute-done((f32[6,1,768]{2,1,0:T(1,128)S(1)}, f32[6,1,768]{2,1,0:T(1,128)S(1)}, u32[]{:S(2)}, u32[]{:S(2)}) %collective-permute-start.3) | collective-permute-done | bytes 18464 | tf_op jit(solution)/shard_map/ppermute | solution.py:28
  80.0 3.3 %all-to-all-start.3 = ((f32[4,1,1536]{2,1,0:T(1,128)}), f32[4,1,1536]{2,1,0:T(1,128)S(1)}, u32[]{:S(2)}, u32[]{:S(2)}) async-start(f32[4,1,1536]{2,1,0:T(1,128)} %all_to_all.43), calls=%async_computation.3 | async-start | bytes 49152 | tf_op jit(solution)/shard_map/all_to_all | solution.py:122
  88.7 7.1 %collective-permute-start.20 = (f32[1,24,64]{2,1,0:T(8,128)S(1)}, f32[1,24,64]{2,1,0:T(8,128)S(1)}, u32[]{:S(2)}, u32[]{:S(2)}) collective-permute-start(f32[1,24,64]{2,1,0:T(8,128)S(1)} %get-tuple-element.39), channel_id=1, source_target_pairs={{0,1},{1,2},{2,3},{3,4},{4,5},{5,6},{6,7},{8,9},{9,10},{10,11},{11... | collective-permute-start | bytes 18440 | tf_op jit(solution)/shard_map/ppermute | solution.py:26
  95.9 1.9 %collective-permute-start.21 = (f32[1,24,64]{2,1,0:T(8,128)S(1)}, f32[1,24,64]{2,1,0:T(8,128)S(1)}, u32[]{:S(2)}, u32[]{:S(2)}) collective-permute-start(f32[1,24,64]{2,1,0:T(8,128)S(1)} %get-tuple-element.38), channel_id=1, source_target_pairs={{1,0},{2,1},{3,2},{4,3},{5,4},{6,5},{7,6},{9,8},{10,9},{11,10},{12... | collective-permute-start | bytes 18440 | tf_op jit(solution)/shard_map/ppermute | solution.py:28
  97.8 3.6 %collective-permute-start.4 = (f32[1,24,768]{2,1,0:T(8,128)S(1)}, f32[1,24,768]{2,1,0:T(8,128)S(1)}, u32[]{:S(2)}, u32[]{:S(2)}) collective-permute-start(f32[1,24,768]{2,1,0:T(8,128)S(1)} %get-tuple-element.28), channel_id=1, source_target_pairs={{0,1},{1,2},{2,3},{3,4},{4,5},{5,6},{6,7},{8,9},{9,10},{10,11},{11... | collective-permute-start | bytes 221192 | tf_op jit(solution)/shard_map/ppermute | solution.py:26
  101.5 1.9 %collective-permute-start.5 = (f32[1,24,768]{2,1,0:T(8,128)S(1)}, f32[1,24,768]{2,1,0:T(8,128)S(1)}, u32[]{:S(2)}, u32[]{:S(2)}) collective-permute-start(f32[1,24,768]{2,1,0:T(8,128)S(1)} %get-tuple-element.29), channel_id=1, source_target_pairs={{1,0},{2,1},{3,2},{4,3},{5,4},{6,5},{7,6},{9,8},{10,9},{11,10},{12... | collective-permute-start | bytes 221192 | tf_op jit(solution)/shard_map/ppermute | solution.py:28
  104.1 3.3 %all-to-all-start.4 = ((f32[4,1,1536]{2,1,0:T(1,128)}), f32[4,1,1536]{2,1,0:T(1,128)S(1)}, u32[]{:S(2)}, u32[]{:S(2)}) async-start(f32[4,1,1536]{2,1,0:T(1,128)} %mul.957), calls=%async_computation.4 | async-start | bytes 49152 | tf_op jit(solution)/shard_map/all_to_all | solution.py:123
  109.3 4.6 %collective-permute-start.23 = (f32[6,1,64]{2,1,0:T(1,128)}, f32[6,1,64]{2,1,0:T(1,128)}, u32[]{:S(2)}, u32[]{:S(2)}) collective-permute-start(f32[6,1,64]{2,1,0:T(1,128)} %get-tuple-element.33), channel_id=1, source_target_pairs={{0,8},{8,16},{16,24},{1,9},{9,17},{17,25},{2,10},{10,18},{18,26},{... | collective-permute-start | bytes 4616 | tf_op jit(solution)/shard_map/ppermute | solution.py:26
  115.0 3.8 %collective-permute-start.6 = (f32[6,1,768]{2,1,0:T(1,128)S(1)}, f32[6,1,768]{2,1,0:T(1,128)S(1)}, u32[]{:S(2)}, u32[]{:S(2)}) collective-permute-start(f32[6,1,768]{2,1,0:T(1,128)S(1)} %get-tuple-element.22), channel_id=1, source_target_pairs={{0,8},{8,16},{16,24},{1,9},{9,17},{17,25},{2,10},{10,18},{18,26},{... | collective-permute-start | bytes 55304 | tf_op jit(solution)/shard_map/ppermute | solution.py:26
  128.0 1.6 pad_maximum_fusion.3
  134.0 3.9 %all-to-all-start.5 = ((f32[4,1,1536]{2,1,0:T(1,128)}), f32[4,1,1536]{2,1,0:T(1,128)S(1)}, u32[]{:S(2)}, u32[]{:S(2)}) async-start(f32[4,1,1536]{2,1,0:T(1,128)} %all_to_all.44), calls=%async_computation.5 | async-start | bytes 49152 | tf_op jit(solution)/shard_map/all_to_all | solution.py:122
  137.9 5.3 %collective-permute-start.12 = (f32[1,24,768]{2,1,0:T(8,128)S(1)}, f32[1,24,768]{2,1,0:T(8,128)S(1)}, u32[]{:S(2)}, u32[]{:S(2)}) collective-permute-start(f32[1,24,768]{2,1,0:T(8,128)S(1)} %get-tuple-element.26), channel_id=1, source_target_pairs={{0,1},{1,2},{2,3},{3,4},{4,5},{5,6},{6,7},{8,9},{9,10},{10,11},{11... | collective-permute-start | bytes 221192 | tf_op jit(solution)/shard_map/ppermute | solution.py:26
  143.2 1.9 %collective-permute-start.13 = (f32[1,24,768]{2,1,0:T(8,128)S(1)}, f32[1,24,768]{2,1,0:T(8,128)S(1)}, u32[]{:S(2)}, u32[]{:S(2)}) collective-permute-start(f32[1,24,768]{2,1,0:T(8,128)S(1)} %get-tuple-element.27), channel_id=1, source_target_pairs={{1,0},{2,1},{3,2},{4,3},{5,4},{6,5},{7,6},{9,8},{10,9},{11,10},{12... | collective-permute-start | bytes 221192 | tf_op jit(solution)/shard_map/ppermute | solution.py:28
  147.0 1.9 %collective-permute-done.13 = f32[1,24,768]{2,1,0:T(8,128)S(1)} collective-permute-done((f32[1,24,768]{2,1,0:T(8,128)S(1)}, f32[1,24,768]{2,1,0:T(8,128)S(1)}, u32[]{:S(2)}, u32[]{:S(2)}) %collective-permute-start.13) | collective-permute-done | bytes 73760 | tf_op jit(solution)/shard_map/ppermute | solution.py:28
  148.9 3.6 %collective-permute-start.14 = (f32[6,1,768]{2,1,0:T(1,128)S(1)}, f32[6,1,768]{2,1,0:T(1,128)S(1)}, u32[]{:S(2)}, u32[]{:S(2)}) collective-permute-start(f32[6,1,768]{2,1,0:T(1,128)S(1)} %get-tuple-element.20), channel_id=1, source_target_pairs={{0,8},{8,16},{16,24},{1,9},{9,17},{17,25},{2,10},{10,18},{18,26},{... | collective-permute-start | bytes 55304 | tf_op jit(solution)/shard_map/ppermute | solution.py:26
  154.6 2.5 %collective-permute-done.15 = f32[6,1,768]{2,1,0:T(1,128)S(1)} collective-permute-done((f32[6,1,768]{2,1,0:T(1,128)S(1)}, f32[6,1,768]{2,1,0:T(1,128)S(1)}, u32[]{:S(2)}, u32[]{:S(2)}) %collective-permute-start.15) | collective-permute-done | bytes 18464 | tf_op jit(solution)/shard_map/ppermute | solution.py:28
  161.3 1.6 pad_maximum_fusion.5
  (266 shorter events, 58.9 us)
Async XLA Ops:
  1.6 63.2 %collective-permute-start = (f32[1,24,768]{2,1,0:T(8,128)S(1)}, f32[1,24,768]{2,1,0:T(8,128)S(1)}, u32[]{:S(2)}, u32[]{:S(2)}) collective-permute-start(f32[1,24,768]{2,1,0:T(8,128)S(1)} %get-tuple-element.30), channel_id=1, source_target_pairs={{0,1},{1,2},{2,3},{3,4},{4,5},{5,6},{6,7},{8,9},{9,10},{10,11},{11... | collective-permute-start | bytes 221192 | tf_op jit(solution)/shard_map/ppermute | solution.py:26
  6.3 58.5 %collective-permute-start.1 = (f32[1,24,768]{2,1,0:T(8,128)S(1)}, f32[1,24,768]{2,1,0:T(8,128)S(1)}, u32[]{:S(2)}, u32[]{:S(2)}) collective-permute-start(f32[1,24,768]{2,1,0:T(8,128)S(1)} %get-tuple-element.31), channel_id=1, source_target_pairs={{1,0},{2,1},{3,2},{4,3},{5,4},{6,5},{7,6},{9,8},{10,9},{11,10},{12... | collective-permute-start | bytes 221192 | tf_op jit(solution)/shard_map/ppermute | solution.py:28
  9.8 24.8 %all-to-all-start = ((f32[4,1,1536]{2,1,0:T(1,128)}), f32[4,1,1536]{2,1,0:T(1,128)S(1)}, u32[]{:S(2)}, u32[]{:S(2)}) async-start(f32[4,1,1536]{2,1,0:T(1,128)} %all_to_all.32), calls=%async_computation | async-start | bytes 49152 | tf_op jit(solution)/shard_map/all_to_all | solution.py:123
  13.9 14.9 %collective-permute-start.8 = (f32[1,24,64]{2,1,0:T(8,128)S(1)}, f32[1,24,64]{2,1,0:T(8,128)S(1)}, u32[]{:S(2)}, u32[]{:S(2)}) collective-permute-start(f32[1,24,64]{2,1,0:T(8,128)S(1)} %get-tuple-element.47), channel_id=1, source_target_pairs={{0,1},{1,2},{2,3},{3,4},{4,5},{5,6},{6,7},{8,9},{9,10},{10,11},{11... | collective-permute-start | bytes 18440 | tf_op jit(solution)/shard_map/ppermute | solution.py:26
  17.9 11.1 %collective-permute-start.9 = (f32[1,24,64]{2,1,0:T(8,128)S(1)}, f32[1,24,64]{2,1,0:T(8,128)S(1)}, u32[]{:S(2)}, u32[]{:S(2)}) collective-permute-start(f32[1,24,64]{2,1,0:T(8,128)S(1)} %get-tuple-element.46), channel_id=1, source_target_pairs={{1,0},{2,1},{3,2},{4,3},{5,4},{6,5},{7,6},{9,8},{10,9},{11,10},{12... | collective-permute-start | bytes 18440 | tf_op jit(solution)/shard_map/ppermute | solution.py:28
  26.3 37.9 %copy-start.45 = (s32[1024]{0:T(1024)}, s32[1024]{0:T(1024)S(1)}, u32[]{:S(2)}) copy-start(s32[1024]{0:T(1024)S(1)} %pad_clamp_fusion.1) | copy-start | bytes 12292
  28.9 13.0 %collective-permute-start.10 = (f32[6,1,64]{2,1,0:T(1,128)S(1)}, f32[6,1,64]{2,1,0:T(1,128)S(1)}, u32[]{:S(2)}, u32[]{:S(2)}) collective-permute-start(f32[6,1,64]{2,1,0:T(1,128)S(1)} %get-tuple-element.36), channel_id=1, source_target_pairs={{8,0},{16,8},{24,16},{9,1},{17,9},{25,17},{10,2},{18,10},{26,18},{... | collective-permute-start | bytes 4616 | tf_op jit(solution)/shard_map/ppermute | solution.py:28
  30.2 11.7 %collective-permute-start.11 = (f32[6,1,64]{2,1,0:T(1,128)S(1)}, f32[6,1,64]{2,1,0:T(1,128)S(1)}, u32[]{:S(2)}, u32[]{:S(2)}) collective-permute-start(f32[6,1,64]{2,1,0:T(1,128)S(1)} %get-tuple-element.37), channel_id=1, source_target_pairs={{0,8},{8,16},{16,24},{1,9},{9,17},{17,25},{2,10},{10,18},{18,26},{... | collective-permute-start | bytes 4616 | tf_op jit(solution)/shard_map/ppermute | solution.py:26
  34.5 7.2 %all-to-all-start.1 = ((f32[4,1,1536]{2,1,0:T(1,128)}), f32[4,1,1536]{2,1,0:T(1,128)S(1)}, u32[]{:S(2)}, u32[]{:S(2)}) async-start(f32[4,1,1536]{2,1,0:T(1,128)} %all_to_all.42), calls=%async_computation.1 | async-start | bytes 49152 | tf_op jit(solution)/shard_map/all_to_all | solution.py:122
  38.3 31.6 %copy-start.17 = (f32[64,48,1]{0,1,2:T(8,128)}, f32[64,48,1]{0,1,2:T(8,128)S(1)}, u32[]{:S(2)}) copy-start(f32[64,48,1]{0,1,2:T(8,128)S(1)} %reshape.428) | copy-start | bytes 36868
  42.3 15.3 %collective-permute-start.16 = (f32[1,24,64]{2,1,0:T(8,128)S(1)}, f32[1,24,64]{2,1,0:T(8,128)S(1)}, u32[]{:S(2)}, u32[]{:S(2)}) collective-permute-start(f32[1,24,64]{2,1,0:T(8,128)S(1)} %get-tuple-element.45), channel_id=1, source_target_pairs={{0,1},{1,2},{2,3},{3,4},{4,5},{5,6},{6,7},{8,9},{9,10},{10,11},{11... | collective-permute-start | bytes 18440 | tf_op jit(solution)/shard_map/ppermute | solution.py:26
  47.9 9.6 %collective-permute-start.17 = (f32[1,24,64]{2,1,0:T(8,128)S(1)}, f32[1,24,64]{2,1,0:T(8,128)S(1)}, u32[]{:S(2)}, u32[]{:S(2)}) collective-permute-start(f32[1,24,64]{2,1,0:T(8,128)S(1)} %get-tuple-element.44), channel_id=1, source_target_pairs={{1,0},{2,1},{3,2},{4,3},{5,4},{6,5},{7,6},{9,8},{10,9},{11,10},{12... | collective-permute-start | bytes 18440 | tf_op jit(solution)/shard_map/ppermute | solution.py:28
  54.3 9.8 %all-to-all-start.2 = ((f32[4,1,1536]{2,1,0:T(1,128)}), f32[4,1,1536]{2,1,0:T(1,128)S(1)}, u32[]{:S(2)}, u32[]{:S(2)}) async-start(f32[4,1,1536]{2,1,0:T(1,128)} %mul.933), calls=%async_computation.2 | async-start | bytes 49152 | tf_op jit(solution)/shard_map/all_to_all | solution.py:123
  58.2 28.7 %collective-permute-start.18 = (f32[6,1,64]{2,1,0:T(1,128)}, f32[6,1,64]{2,1,0:T(1,128)}, u32[]{:S(2)}, u32[]{:S(2)}) collective-permute-start(f32[6,1,64]{2,1,0:T(1,128)} %get-tuple-element.34), channel_id=1, source_target_pairs={{8,0},{16,8},{24,16},{9,1},{17,9},{25,17},{10,2},{18,10},{26,18},{... | collective-permute-start | bytes 4616 | tf_op jit(solution)/shard_map/ppermute | solution.py:28
  59.5 27.5 %collective-permute-start.19 = (f32[6,1,64]{2,1,0:T(1,128)}, f32[6,1,64]{2,1,0:T(1,128)}, u32[]{:S(2)}, u32[]{:S(2)}) collective-permute-start(f32[6,1,64]{2,1,0:T(1,128)} %get-tuple-element.35), channel_id=1, source_target_pairs={{0,8},{8,16},{16,24},{1,9},{9,17},{17,25},{2,10},{10,18},{18,26},{... | collective-permute-start | bytes 4616 | tf_op jit(solution)/shard_map/ppermute | solution.py:26
  64.9 5.2 %collective-permute-start.2 = (f32[6,1,768]{2,1,0:T(1,128)S(1)}, f32[6,1,768]{2,1,0:T(1,128)S(1)}, u32[]{:S(2)}, u32[]{:S(2)}) collective-permute-start(f32[6,1,768]{2,1,0:T(1,128)S(1)} %get-tuple-element.24), channel_id=1, source_target_pairs={{0,8},{8,16},{16,24},{1,9},{9,17},{17,25},{2,10},{10,18},{18,26},{... | collective-permute-start | bytes 55304 | tf_op jit(solution)/shard_map/ppermute | solution.py:26
  68.6 4.5 %collective-permute-start.3 = (f32[6,1,768]{2,1,0:T(1,128)S(1)}, f32[6,1,768]{2,1,0:T(1,128)S(1)}, u32[]{:S(2)}, u32[]{:S(2)}) collective-permute-start(f32[6,1,768]{2,1,0:T(1,128)S(1)} %get-tuple-element.25), channel_id=1, source_target_pairs={{8,0},{16,8},{24,16},{9,1},{17,9},{25,17},{10,2},{18,10},{26,18},{... | collective-permute-start | bytes 55304 | tf_op jit(solution)/shard_map/ppermute | solution.py:28
  80.0 6.8 %all-to-all-start.3 = ((f32[4,1,1536]{2,1,0:T(1,128)}), f32[4,1,1536]{2,1,0:T(1,128)S(1)}, u32[]{:S(2)}, u32[]{:S(2)}) async-start(f32[4,1,1536]{2,1,0:T(1,128)} %all_to_all.43), calls=%async_computation.3 | async-start | bytes 49152 | tf_op jit(solution)/shard_map/all_to_all | solution.py:122
  88.7 18.6 %collective-permute-start.20 = (f32[1,24,64]{2,1,0:T(8,128)S(1)}, f32[1,24,64]{2,1,0:T(8,128)S(1)}, u32[]{:S(2)}, u32[]{:S(2)}) collective-permute-start(f32[1,24,64]{2,1,0:T(8,128)S(1)} %get-tuple-element.39), channel_id=1, source_target_pairs={{0,1},{1,2},{2,3},{3,4},{4,5},{5,6},{6,7},{8,9},{9,10},{10,11},{11... | collective-permute-start | bytes 18440 | tf_op jit(solution)/shard_map/ppermute | solution.py:26
  95.9 11.5 %collective-permute-start.21 = (f32[1,24,64]{2,1,0:T(8,128)S(1)}, f32[1,24,64]{2,1,0:T(8,128)S(1)}, u32[]{:S(2)}, u32[]{:S(2)}) collective-permute-start(f32[1,24,64]{2,1,0:T(8,128)S(1)} %get-tuple-element.38), channel_id=1, source_target_pairs={{1,0},{2,1},{3,2},{4,3},{5,4},{6,5},{7,6},{9,8},{10,9},{11,10},{12... | collective-permute-start | bytes 18440 | tf_op jit(solution)/shard_map/ppermute | solution.py:28
  97.8 17.1 %collective-permute-start.4 = (f32[1,24,768]{2,1,0:T(8,128)S(1)}, f32[1,24,768]{2,1,0:T(8,128)S(1)}, u32[]{:S(2)}, u32[]{:S(2)}) collective-permute-start(f32[1,24,768]{2,1,0:T(8,128)S(1)} %get-tuple-element.28), channel_id=1, source_target_pairs={{0,1},{1,2},{2,3},{3,4},{4,5},{5,6},{6,7},{8,9},{9,10},{10,11},{11... | collective-permute-start | bytes 221192 | tf_op jit(solution)/shard_map/ppermute | solution.py:26
  101.5 13.5 %collective-permute-start.5 = (f32[1,24,768]{2,1,0:T(8,128)S(1)}, f32[1,24,768]{2,1,0:T(8,128)S(1)}, u32[]{:S(2)}, u32[]{:S(2)}) collective-permute-start(f32[1,24,768]{2,1,0:T(8,128)S(1)} %get-tuple-element.29), channel_id=1, source_target_pairs={{1,0},{2,1},{3,2},{4,3},{5,4},{6,5},{7,6},{9,8},{10,9},{11,10},{12... | collective-permute-start | bytes 221192 | tf_op jit(solution)/shard_map/ppermute | solution.py:28
  104.1 9.8 %all-to-all-start.4 = ((f32[4,1,1536]{2,1,0:T(1,128)}), f32[4,1,1536]{2,1,0:T(1,128)S(1)}, u32[]{:S(2)}, u32[]{:S(2)}) async-start(f32[4,1,1536]{2,1,0:T(1,128)} %mul.957), calls=%async_computation.4 | async-start | bytes 49152 | tf_op jit(solution)/shard_map/all_to_all | solution.py:123
  108.0 37.4 %collective-permute-start.22 = (f32[6,1,64]{2,1,0:T(1,128)}, f32[6,1,64]{2,1,0:T(1,128)}, u32[]{:S(2)}, u32[]{:S(2)}) collective-permute-start(f32[6,1,64]{2,1,0:T(1,128)} %get-tuple-element.32), channel_id=1, source_target_pairs={{8,0},{16,8},{24,16},{9,1},{17,9},{25,17},{10,2},{18,10},{26,18},{... | collective-permute-start | bytes 4616 | tf_op jit(solution)/shard_map/ppermute | solution.py:28
  109.3 36.1 %collective-permute-start.23 = (f32[6,1,64]{2,1,0:T(1,128)}, f32[6,1,64]{2,1,0:T(1,128)}, u32[]{:S(2)}, u32[]{:S(2)}) collective-permute-start(f32[6,1,64]{2,1,0:T(1,128)} %get-tuple-element.33), channel_id=1, source_target_pairs={{0,8},{8,16},{16,24},{1,9},{9,17},{17,25},{2,10},{10,18},{18,26},{... | collective-permute-start | bytes 4616 | tf_op jit(solution)/shard_map/ppermute | solution.py:26
  115.0 8.0 %collective-permute-start.6 = (f32[6,1,768]{2,1,0:T(1,128)S(1)}, f32[6,1,768]{2,1,0:T(1,128)S(1)}, u32[]{:S(2)}, u32[]{:S(2)}) collective-permute-start(f32[6,1,768]{2,1,0:T(1,128)S(1)} %get-tuple-element.22), channel_id=1, source_target_pairs={{0,8},{8,16},{16,24},{1,9},{9,17},{17,25},{2,10},{10,18},{18,26},{... | collective-permute-start | bytes 55304 | tf_op jit(solution)/shard_map/ppermute | solution.py:26
  118.8 4.5 %collective-permute-start.7 = (f32[6,1,768]{2,1,0:T(1,128)S(1)}, f32[6,1,768]{2,1,0:T(1,128)S(1)}, u32[]{:S(2)}, u32[]{:S(2)}) collective-permute-start(f32[6,1,768]{2,1,0:T(1,128)S(1)} %get-tuple-element.23), channel_id=1, source_target_pairs={{8,0},{16,8},{24,16},{9,1},{17,9},{25,17},{10,2},{18,10},{26,18},{... | collective-permute-start | bytes 55304 | tf_op jit(solution)/shard_map/ppermute | solution.py:28
  134.0 11.2 %all-to-all-start.5 = ((f32[4,1,1536]{2,1,0:T(1,128)}), f32[4,1,1536]{2,1,0:T(1,128)S(1)}, u32[]{:S(2)}, u32[]{:S(2)}) async-start(f32[4,1,1536]{2,1,0:T(1,128)} %all_to_all.44), calls=%async_computation.5 | async-start | bytes 49152 | tf_op jit(solution)/shard_map/all_to_all | solution.py:122
  137.9 9.1 %collective-permute-start.12 = (f32[1,24,768]{2,1,0:T(8,128)S(1)}, f32[1,24,768]{2,1,0:T(8,128)S(1)}, u32[]{:S(2)}, u32[]{:S(2)}) collective-permute-start(f32[1,24,768]{2,1,0:T(8,128)S(1)} %get-tuple-element.26), channel_id=1, source_target_pairs={{0,1},{1,2},{2,3},{3,4},{4,5},{5,6},{6,7},{8,9},{9,10},{10,11},{11... | collective-permute-start | bytes 221192 | tf_op jit(solution)/shard_map/ppermute | solution.py:26
  143.2 5.7 %collective-permute-start.13 = (f32[1,24,768]{2,1,0:T(8,128)S(1)}, f32[1,24,768]{2,1,0:T(8,128)S(1)}, u32[]{:S(2)}, u32[]{:S(2)}) collective-permute-start(f32[1,24,768]{2,1,0:T(8,128)S(1)} %get-tuple-element.27), channel_id=1, source_target_pairs={{1,0},{2,1},{3,2},{4,3},{5,4},{6,5},{7,6},{9,8},{10,9},{11,10},{12... | collective-permute-start | bytes 221192 | tf_op jit(solution)/shard_map/ppermute | solution.py:28
  148.9 5.7 %collective-permute-start.14 = (f32[6,1,768]{2,1,0:T(1,128)S(1)}, f32[6,1,768]{2,1,0:T(1,128)S(1)}, u32[]{:S(2)}, u32[]{:S(2)}) collective-permute-start(f32[6,1,768]{2,1,0:T(1,128)S(1)} %get-tuple-element.20), channel_id=1, source_target_pairs={{0,8},{8,16},{16,24},{1,9},{9,17},{17,25},{2,10},{10,18},{18,26},{... | collective-permute-start | bytes 55304 | tf_op jit(solution)/shard_map/ppermute | solution.py:26
  152.6 4.5 %collective-permute-start.15 = (f32[6,1,768]{2,1,0:T(1,128)S(1)}, f32[6,1,768]{2,1,0:T(1,128)S(1)}, u32[]{:S(2)}, u32[]{:S(2)}) collective-permute-start(f32[6,1,768]{2,1,0:T(1,128)S(1)} %get-tuple-element.21), channel_id=1, source_target_pairs={{8,0},{16,8},{24,16},{9,1},{17,9},{25,17},{10,2},{18,10},{26,18},{... | collective-permute-start | bytes 55304 | tf_op jit(solution)/shard_map/ppermute | solution.py:28
  (47 other events, 269.0 us)
where the time goes:
time: 167 us; the launch traced here: 165 us
  starting transfers between devices  94.9 us (57%)
  local copies, waits for them, and re-layouts  36.9 us (22%)
  other arithmetic  20.2 us (12%)
  waiting for transfers between devices  9.55 us (6%)
  between operations  1.82 us (1%)
  matrix products  1.76 us (1%)
    ppermute x12, starting transfers between devices, with_halo(): lax.ppermute(tail, axis, [(i, (i + 1) % count) for i in range(ends)])  54.9 us
    ppermute x12, starting transfers between devices, with_halo(): lax.ppermute(head, axis, [((i + 1) % count, i) for i in range(ends)])  19.3 us
    all_to_all x3, starting transfers between devices, couple(): lax.all_to_all(outgoing, 'sec', split_axis=0, concat_axis=0, tiled=True)  10.8 us
    all_to_all x3, starting transfers between devices, couple(): lax.all_to_all(homeward, 'sec', split_axis=0, concat_axis=0, tiled=True)  9.95 us
    mul x12, local copies, waits for them, and re-layouts, turn_grow(): aligned = zonal[..., None] * east_part + meridional[..., None] * north_part  8.46 us
    ppermute x12, waiting for transfers between devices, with_halo(): lax.ppermute(head, axis, [((i + 1) % count, i) for i in range(ends)])  7.72 us
    slice x6, local copies, waits for them, and re-layouts, turn_grow(): behind = jnp.roll(spread, 1, axis=-1)  4.32 us
  transfers between devices with their start and end apart: 30, of which 6 were waited for; matrix products, arithmetic and copies ran while one was open for 26% of the time, Pallas kernels for 0%

commit v1 on v0

v1 whole, which is shorter than its diff:
```python
import functools
import math

import jax
import jax.numpy as jnp
import ml_dtypes
import numpy as np
from jax import lax
from jax.experimental import pallas as pl
from jax.experimental.pallas import tpu as pltpu
from jax.sharding import PartitionSpec as P

NFREQ = 24
NDIR = 32
STEPS = 3

stokes_scale = 0.1
ocean_dt = 0.3
current_gain = 0.2

LANES = 128
VMEM = pl.BlockSpec(memory_space=pltpu.VMEM)
F32 = jnp.float32
BF16 = jnp.bfloat16


def split_halves(table):
    high = table.astype(ml_dtypes.bfloat16)
    low = (table - high.astype(np.float64)).astype(ml_dtypes.bfloat16)
    return high, low


def build_tables(nfreq, ndir, ndepth):
    fraction = np.arange(nfreq) / (nfreq - 1)
    angles = (np.arange(ndir) + 0.5) * (2.0 * math.pi / ndir)
    east_part, north_part = np.cos(angles), np.sin(angles)
    courant = 0.1 + 0.3 * fraction
    depth_level = 0.5 + (ndepth - 2) * (1.0 - fraction)
    weights = np.maximum(1.0 - np.abs(np.arange(ndepth)[None, :] - depth_level[:, None]), 0.0)
    mean_weights = weights / weights.sum(axis=1, keepdims=True)
    x_rate = np.abs(courant[:, None] * east_part[None, :]).reshape(-1)
    y_rate = np.abs(courant[:, None] * north_part[None, :]).reshape(-1)
    turn_gain = np.repeat(1.0 - 0.5 * fraction, ndir)
    rates = np.stack([1.0 - x_rate - y_rate, x_rate, y_rate, turn_gain] * 2).astype(np.float32)
    compass = np.stack([east_part, north_part])
    stokes = (stokes_scale * weights[:, None, None, :] * compass.T[None, :, :, None]).reshape(
        nfreq * ndir, 2 * ndepth
    )
    growth = current_gain * (1.0 + fraction)
    grow = (
        growth[None, None, :, None] * mean_weights.T[None, :, :, None] * compass[:, None, None, :]
    ).reshape(2 * ndepth, nfreq * ndir)
    stokes_high, stokes_low = split_halves(stokes)
    grow_high, grow_low = split_halves(grow)
    return (
        rates,
        np.concatenate([stokes_high, stokes_low], axis=1),
        np.concatenate([grow_high, grow_high, grow_low, grow_low], axis=0),
    )


def sec_exchanges(count):
    if count % 4 == 0:
        far = count // 4
        return [
            [((i // 4 + hop) % far) * 4 + ((i % 4) ^ flip) for i in range(count)]
            for hop in range(far)
            for flip in range(4)
            if hop or flip
        ]
    return [[(i + hop) % count for i in range(count)] for hop in range(1, count)]


class Plan:
    def __init__(self, sections, bands, rows, cols, spectral, depth):
        self.sections, self.bands = sections, bands
        self.rows, self.cols, self.spectral, self.depth = rows, cols, spectral, depth
        self.columns = rows * cols
        self.chunk = self.columns // sections
        self.tiles = spectral // LANES
        self.exchanges = sec_exchanges(sections)
        self.edges = [
            any(abs(target - i) == 1 for i, target in enumerate(table)) for table in self.exchanges
        ]
        self.sec_rows = [
            self.chunk + (self.tiles * rows + 8 if edge else 0) for edge in self.edges
        ]

    def partner(self, section, number):
        if self.sections % 4 == 0:
            far = self.sections // 4
            hop, flip = divmod(number + 1, 4)
            high, low = lax.div(section, 4), lax.rem(section, 4)
            flipped = low
            if flip & 1:
                flipped = flipped + 1 - 2 * lax.rem(flipped, 2)
            if flip & 2:
                flipped = flipped + 2 - 4 * lax.div(flipped, 2)
            return (
                lax.rem(high + hop, far) * 4 + flipped,
                lax.rem(high + far - hop, far) * 4 + flipped,
            )
        hop = number + 1
        return (
            lax.rem(section + hop, self.sections),
            lax.rem(section + self.sections - hop, self.sections),
        )


def lane_of(shape):
    return lax.broadcasted_iota(jnp.int32, shape, len(shape) - 1)


def dot(a, b):
    return jnp.dot(a, b, preferred_element_type=F32)


def send_parts(plan, section, even, waves, ocean, permute_t, coupling, sec_out, lat_out):
    chunk, tiles, rows, cols = plan.chunk, plan.tiles, plan.rows, plan.cols
    shape = (plan.columns, LANES)
    lane = lane_of(shape)
    total = None
    for start in range(0, plan.spectral, 256):
        part = waves[:, :, start : start + 256].reshape(plan.columns, 256)
        high = part.astype(BF16)
        low = (part - high.astype(F32)).astype(BF16)
        product = dot(jnp.concatenate([high, low], axis=0), coupling["stokes"][start : start + 256, :])
        total = product if total is None else total + product
    moments = total[: plan.columns] + total[plan.columns :]
    moments = moments + pltpu.roll(moments, LANES // 2, 1)
    high = moments.astype(BF16).astype(F32)
    halves = jnp.where(lane < LANES // 2, high, moments - high).astype(BF16)
    ordered = dot(permute_t, halves)
    ordered = ordered + pltpu.roll(ordered, LANES // 2, 1)
    packed = jnp.where(lane < LANES // 2, ocean, ordered)
    coupling["packed"][...] = packed
    ocean = ocean.reshape(rows, cols, LANES)
    for number, out in enumerate(sec_out):
        target, _ = plan.partner(section, number)
        out[0:chunk, :] = coupling["packed"][pl.ds(pl.multiple_of(target * chunk, 8), chunk), :]
        if not plan.edges[number]:
            continue
        eastward = target == section + 1
        for row in range(rows):
            edge = jnp.where(
                eastward, waves[row, cols - 1 : cols, :], waves[row, 0:1, :]
            )
            for tile in range(tiles):
                place = chunk + tile * rows + row
                out[place : place + 1, :] = edge[:, tile * LANES : (tile + 1) * LANES]
            place = chunk + tiles * rows + row
            out[place : place + 1, :] = jnp.where(
                eastward, ocean[row, cols - 1 : cols, :], ocean[row, 0:1, :]
            )
    near, far = lat_out
    for out, northward in ((near, even), (far, jnp.logical_not(even))):
        out[:, 0 : plan.spectral] = jnp.where(northward, waves[rows - 1], waves[0])
        out[:, plan.spectral :] = jnp.where(northward, ocean[rows - 1], ocean[0])


def first_kernel(plan, axes, *refs):
    waves, turning, currents, drag, mask, target, stokes_table = refs[:7]
    refs = refs[7:]
    permute_out, permute_t_out, turn_out, sea_out, keep_out, ocean_out, packed_out = refs[:7]
    refs = refs[7:]
    sec_out, lat_out = refs[: len(plan.exchanges)], refs[len(plan.exchanges) :]
    section, band = lax.axis_index(axes[1]), lax.axis_index(axes[0])
    even = lax.rem(band, 2) == 0
    columns, rows = plan.columns, plan.rows

    across = lane_of((columns, columns))
    down = lax.broadcasted_iota(jnp.int32, (columns, columns), 0)
    here = across == down

    def row_of(ref):
        return jnp.concatenate([ref[row : row + 1, :] for row in range(rows)], axis=1)

    def column_of(row):
        spread = jnp.broadcast_to(row, (columns, columns))
        return jnp.sum(jnp.where(here, spread, jnp.zeros_like(spread)), axis=1, keepdims=True)

    target_row = row_of(target).astype(F32)
    target_col = column_of(target_row)
    same = target_col == target_row
    rank_col = jnp.sum(jnp.where(same & (across < down), 1.0, 0.0), axis=1, keepdims=True)
    rank_row = jnp.sum(jnp.where(same & (down < across), 1.0, 0.0), axis=0, keepdims=True)
    slot_col = target_col * float(plan.chunk) + rank_col
    slot_row = target_row * float(plan.chunk) + rank_row
    permute = jnp.where(slot_col == across.astype(F32), 1.0, 0.0)
    permute_t = jnp.where(slot_row == down.astype(F32), 1.0, 0.0)
    permute_out[...] = permute.astype(BF16)
    permute_t = permute_t.astype(BF16)
    permute_t_out[...] = permute_t
    turn_out[...] = jnp.broadcast_to(column_of(row_of(turning)), (columns, LANES))
    sea_out[...] = jnp.broadcast_to(column_of(row_of(mask).astype(F32)), (columns, LANES))
    keep = 1.0 - drag[...].reshape(1, plan.depth)
    blank = jnp.zeros((1, LANES - 2 * plan.depth), F32)
    keep_out[...] = jnp.broadcast_to(jnp.concatenate([keep, keep, blank], axis=1), (8, LANES))
    flat = currents[...].reshape(columns, 2 * plan.depth)
    ocean = jnp.concatenate([flat, jnp.zeros((columns, LANES - 2 * plan.depth), F32)], axis=1)
    ocean_out[...] = ocean
    coupling = {"stokes": stokes_table, "packed": packed_out}
    send_parts(plan, section, even, waves, ocean, permute_t, coupling, sec_out, lat_out)


def step_kernel(plan, axes, last, *refs):
    waves, ocean_in, packed_in, permute, permute_t, turn, sea, keep, rates, stokes, grow = refs[:11]
    refs = refs[11:]
    count = len(plan.exchanges)
    sec_in, lat_in = refs[:count], refs[count : count + 2]
    refs = refs[count + 2 :]
    waves_out, ocean_out = refs[:2]
    refs = refs[2:]
    if not last:
        packed_out, sec_out, lat_out = refs[0], refs[1 : count + 1], refs[count + 1 : count + 3]
        refs = refs[count + 3 :]
    coupled, factor, west_edge, east_edge = refs
    section, band = lax.axis_index(axes[1]), lax.axis_index(axes[0])
    even = lax.rem(band, 2) == 0
    rows, cols, tiles, chunk = plan.rows, plan.cols, plan.tiles, plan.chunk
    columns = plan.columns

    own = pl.ds(pl.multiple_of(section * chunk, 8), chunk)
    coupled[own, :] = packed_in[own, :]
    west_edge[...] = jnp.zeros_like(west_edge)
    east_edge[...] = jnp.zeros_like(east_edge)
    for number, message in enumerate(sec_in):
        _, source = plan.partner(section, number)
        coupled[pl.ds(pl.multiple_of(source * chunk, 8), chunk), :] = message[0:chunk, :]
        if plan.edges[number]:

            @pl.when(source == section + 1)
            def _():
                east_edge[...] = message[chunk:, :]

            @pl.when(source == section - 1)
            def _():
                west_edge[...] = message[chunk:, :]

    arrived = coupled[...]
    lane = lane_of((columns, LANES))
    high = arrived.astype(BF16).astype(F32)
    halves = jnp.where(lane < LANES // 2, high, pltpu.roll(arrived - high, LANES // 2, 1))
    at_waves = dot(permute[...], halves.astype(BF16)).astype(BF16)
    factor[...] = dot(jnp.concatenate([at_waves, at_waves], axis=1), grow[...])

    near, far = lat_in
    block = (cols, LANES)
    direction = lax.rem(lane_of(block), NDIR)
    eastward = (direction < NDIR // 4) | (direction >= 3 * NDIR // 4)
    northward = direction < NDIR // 2
    first, final = direction == 0, direction == NDIR - 1
    place = lax.broadcasted_iota(jnp.int32, block, 0)
    at_west, at_east = place == 0, place == cols - 1
    for tile in range(tiles):
        lanes = slice(tile * LANES, (tile + 1) * LANES)
        stay, along_x, along_y, gain = (rates[k : k + 1, lanes] for k in range(4))
        south_edge = jnp.where(even, far[:, lanes], near[:, lanes])
        north_edge = jnp.where(even, near[:, lanes], far[:, lanes])
        for row in range(rows):
            flat = slice(row * cols, (row + 1) * cols)
            edge = slice(tile * rows + row, tile * rows + row + 1)
            center = waves[row, :, lanes]
            west = jnp.where(at_west, west_edge[edge, :], pltpu.roll(center, 1, 0))
            east = jnp.where(at_east, east_edge[edge, :], pltpu.roll(center, cols - 1, 0))
            south = waves[row - 1, :, lanes] if row else south_edge
            north = waves[row + 1, :, lanes] if row < rows - 1 else north_edge
            moved = (
                stay * center
                + along_x * jnp.where(eastward, west, east)
                + along_y * jnp.where(northward, south, north)
            )
            behind = jnp.where(
                first, pltpu.roll(moved, LANES - (NDIR - 1), 1), pltpu.roll(moved, 1, 1)
            )
            forward = jnp.where(
                final, pltpu.roll(moved, NDIR - 1, 1), pltpu.roll(moved, LANES - 1, 1)
            )
            rate = turn[flat, :]
            turned = moved - jnp.abs(rate) * gain * (moved - jnp.where(rate > 0.0, behind, forward))
            waves_out[row, :, lanes] = turned * (1.0 + factor[flat, lanes]) * sea[flat, :]

    half = plan.depth
    span = 2 * half
    side = lane_of(block)
    zonal = side < half

    def swapped(value):
        return jnp.where(zonal, pltpu.roll(value, LANES - half, 1), pltpu.roll(value, half, 1))

    wave_lanes = slice(plan.spectral, plan.spectral + LANES)
    south_edge = jnp.where(even, far[:, wave_lanes], near[:, wave_lanes])
    north_edge = jnp.where(even, near[:, wave_lanes], far[:, wave_lanes])
    new_ocean = []
    for row in range(rows):
        flat = slice(row * cols, (row + 1) * cols)
        edge = slice(tiles * rows + row, tiles * rows + row + 1)
        center = ocean_in[flat, :]
        west = jnp.where(at_west, west_edge[edge, :], pltpu.roll(center, 1, 0))
        east = jnp.where(at_east, east_edge[edge, :], pltpu.roll(center, cols - 1, 0))
        south = ocean_in[(row - 1) * cols : row * cols, :] if row else south_edge
        north = (
            ocean_in[(row + 1) * cols : (row + 2) * cols, :] if row < rows - 1 else north_edge
        )
        shear = 0.5 * jnp.where(zonal, south - north, east - west)
        shear = shear + swapped(shear)
        y = (band * rows + row).astype(F32)
        spin = 0.2 + 0.6 * y / float(plan.bands * rows) + shear
        pushed = swapped(center + pltpu.roll(coupled[flat, :], LANES // 2, 1))
        turn_by = ocean_dt * spin * pushed
        new = keep[0:1, :] * (center + jnp.where(zonal, turn_by, -turn_by)) * sea[flat, :]
        if last:
            ocean_out[row] = new[:, :span]
        else:
            ocean_out[flat, :] = new
            new_ocean.append(new)
    if not last:
        coupling = {"stokes": stokes, "packed": packed_out}
        send_parts(
            plan,
            section,
            even,
            waves_out,
            jnp.concatenate(new_ocean, axis=0),
            permute_t[...],
            coupling,
            sec_out,
            lat_out,
        )


def per_device(plan, axes, spectra, turning, currents, drag_rates, land_mask, ocean_target):
    rates, stokes, grow = (
        jnp.asarray(table) for table in build_tables(NFREQ, NDIR, drag_rates.shape[0])
    )
    columns = plan.columns
    shape = jax.ShapeDtypeStruct
    params = pltpu.CompilerParams(vmem_limit_bytes=32 * 1024 * 1024)
    messages = [shape((rows, LANES), F32) for rows in plan.sec_rows] + [
        shape((plan.cols, plan.spectral + LANES), F32)
    ] * 2
    state = shape((columns, LANES), F32)

    def call(kernel, outs, scratch, *args):
        return pl.pallas_call(
            kernel,
            out_shape=outs,
            in_specs=[VMEM] * len(args),
            out_specs=[VMEM] * len(outs),
            scratch_shapes=scratch,
            compiler_params=params,
        )(*args)

    def exchange(sent):
        count = plan.sections
        near = [(i, i ^ 1) for i in range(plan.bands) if i ^ 1 < plan.bands]
        far = [(i, ((i + 1) ^ 1) - 1) for i in range(1, plan.bands) if ((i + 1) ^ 1) - 1 < plan.bands]
        got = [
            lax.ppermute(message, axes[1], [(i, table[i]) for i in range(count)])
            for message, table in zip(sent, plan.exchanges)
        ]
        got.append(lax.ppermute(sent[-2], axes[0], near))
        got.append(lax.ppermute(sent[-1], axes[0], far))
        return got

    square = shape((columns, columns), BF16)
    permute, permute_t, turn, sea, keep, ocean, packed, *sent = call(
        functools.partial(first_kernel, plan, axes),
        [square, square, state, state, shape((8, LANES), F32), state, state] + messages,
        [],
        spectra,
        turning,
        currents,
        drag_rates,
        land_mask,
        ocean_target,
        stokes,
    )
    waves = spectra
    edge = pltpu.VMEM((plan.tiles * plan.rows + 8, LANES), F32)
    scratch = [pltpu.VMEM((columns, LANES), F32), pltpu.VMEM((columns, plan.spectral), F32), edge, edge]
    for step in range(STEPS):
        last = step == STEPS - 1
        got = exchange(sent)
        outs = [
            shape(spectra.shape, F32),
            shape(currents.shape, F32) if last else state,
        ] + ([] if last else [state] + messages)
        result = call(
            functools.partial(step_kernel, plan, axes, last),
            outs,
            scratch,
            waves,
            ocean,
            packed,
            permute,
            permute_t,
            turn,
            sea,
            keep,
            rates,
            stokes,
            grow,
            *got,
        )
        waves, ocean = result[:2]
        if not last:
            packed, *sent = result[2:]
    return waves, ocean


def solution(mesh):
    sections, bands = mesh.shape["sec"], mesh.shape["lat"]

    def local(spectra, turning, currents, drag_rates, land_mask, ocean_target):
        rows, cols, spectral = spectra.shape
        plan = Plan(sections, bands, rows, cols, spectral, drag_rates.shape[0])
        return per_device(
            plan, ("lat", "sec"), spectra, turning, currents, drag_rates, land_mask, ocean_target
        )

    return jax.shard_map(
        local,
        mesh=mesh,
        in_specs=(
            P("lat", "sec", None),
            P("lat", "sec"),
            P("lat", "sec", None),
            P(),
            P("lat", "sec"),
            P("lat", "sec"),
        ),
        out_specs=(P("lat", "sec", None), P("lat", "sec", None)),
        check_vma=False,
    )
```

time: 167 us -> 38.4 us (0.23)
  starting transfers between devices: 94.9 us -> 20.8 us
  local copies, waits for them, and re-layouts: 36.9 us -> 6.37 us
  other arithmetic: 20.2 us -> 0 us
  Pallas kernels: 0 us -> 3.67 us
  waiting for transfers between devices: 9.55 us -> 6.41 us
  matrix products: 1.76 us -> 0 us
    ppermute x24 -> x15, starting transfers between devices: 74.1 us -> 20.8 us  [the longest x3 12.4 us: exchange(): got.append(lax.ppermute(sent[-1], axes[0], far))]
    all_to_all x6 -> x0, starting transfers between devices: 20.8 us -> none  [the longest x3 10.8 us: couple(): lax.all_to_all(outgoing, 'sec', split_axis=0, concat_axis=0, tiled=True)]
    mul x28 -> x0, local copies, waits for them, and re-layouts: 12.6 us -> none  [the longest x12 8.46 us: turn_grow(): aligned = zonal[..., None] * east_part + meridional[..., None] * north_part]
    mul x16 -> x0, other arithmetic: 7.89 us -> none  [the longest x3 3.22 us: per_device(): turn_grow(advected, turning, current_eff.reshape(lat_rows, lon_cols, -1),...]
    slice x17 -> x0, local copies, waits for them, and re-layouts: 6.29 us -> none  [the longest x6 4.32 us: turn_grow(): behind = jnp.roll(spread, 1, axis=-1)]
    sort x2 -> x0, other arithmetic: 5.08 us -> none  [the longest x1 2.54 us: per_device(): order = jnp.argsort(ocean_target.reshape(-1), stable=True)]
    concatenate x8 -> x0, local copies, waits for them, and re-layouts: 4.8 us -> none  [the longest x3 3.11 us: turn_grow(): behind = jnp.roll(spread, 1, axis=-1)]
    concatenate x5 -> x0, other arithmetic: 4.7 us -> none  [the longest x2 3.28 us: turn_grow(): forward = jnp.roll(spread, -1, axis=-1)]
  transfers between devices with their start and end apart: 30 -> 15, of which waited for: 6 -> 3; matrix products, arithmetic and copies ran while one was open for 26% -> 0% of each run, Pallas kernels for 0% -> 0%
where the time goes in v1:
time: 38.4 us; the launch traced here: 38 us
  starting transfers between devices  20.8 us (54%)
  waiting for transfers between devices  6.41 us (17%)
  local copies, waits for them, and re-layouts  6.37 us (17%)
  Pallas kernels  3.67 us (10%)
  between operations  0.78 us (2%)
    ppermute x3, starting transfers between devices, exchange(): got.append(lax.ppermute(sent[-1], axes[0], far))  12.4 us
    ppermute x9, starting transfers between devices, exchange(): lax.ppermute(message, axes[1], [(i, table[i]) for i in range(count)])  8.14 us
    ppermute x9, waiting for transfers between devices, exchange(): lax.ppermute(message, axes[1], [(i, table[i]) for i in range(count)])  6.39 us
    unnamed x22, local copies, waits for them, and re-layouts  6.37 us
    pallas_call x4, Pallas kernels, call(): pl.pallas_call(kernel, out_shape=outs, in_specs=[VMEM] * len(args), out_s...  3.67 us
  transfers between devices with their start and end apart: 15, of which 3 were waited for; matrix products, arithmetic and copies ran while one was open for 0% of the time, Pallas kernels for 0%

profile of v1, /device:TPU:1, one launch (start us, length us, event | category | flops | bytes accessed | tf_op | source)
XLA Modules:
  0.0 38.0 jit_solution(18054950446116420550)
XLA Ops:
  0.6 0.0 copy-start
  0.6 0.0 copy-start.1
  0.7 1.0 %copy-done.1 = bf16[768,128]{1,0:T(8,128)(2,1)S(1)} copy-done((bf16[768,128]{1,0:T(8,128)(2,1)S(1)}, bf16[768,128]{1,0:T(8,128)(2,1)}, u32[]{:S(2)}) %copy-start.1) | copy-done | bytes 196632
  1.6 1.0 %copy-done.4 = f32[4,24,768]{2,1,0:T(8,128)S(1)} copy-done((f32[4,24,768]{2,1,0:T(8,128)S(1)}, f32[4,24,768]{2,1,0:T(8,128)}, u32[]{:S(2)}) %copy-start.4) | copy-done | bytes 294936
  2.6 0.8 %copy-done.6 = f32[4,24,64]{2,1,0:T(8,128)S(1)} copy-done((f32[4,24,64]{2,1,0:T(8,128)S(1)}, f32[4,24,64]{2,1,0:T(8,128)}, u32[]{:S(2)}) %copy-start.6) | copy-done | bytes 24600
  3.4 0.7 %copy-done.7 = f32[4,24]{1,0:T(4,128)S(1)} copy-done((f32[4,24]{1,0:T(4,128)S(1)}, f32[4,24]{1,0:T(4,128)}, u32[]{:S(2)}) %copy-start.7) | copy-done | bytes 408
  4.1 0.7 %copy-done.8 = s32[4,24]{1,0:T(4,128)S(1)} copy-done((s32[4,24]{1,0:T(4,128)S(1)}, s32[4,24]{1,0:T(4,128)}, u32[]{:S(2)}) %copy-start.8) | copy-done | bytes 408
  4.8 0.7 %copy-done.9 = s32[4,24]{1,0:T(4,128)S(1)} copy-done((s32[4,24]{1,0:T(4,128)S(1)}, s32[4,24]{1,0:T(4,128)}, u32[]{:S(2)}) %copy-start.9) | copy-done | bytes 408
  5.4 0.7 %copy-done.10 = f32[32]{0:T(128)S(1)} copy-done((f32[32]{0:T(128)S(1)}, f32[32]{0:T(128)}, u32[]{:S(2)}) %copy-start.10) | copy-done | bytes 152
  6.1 0.5 %shard_map.104 = (bf16[96,96]{1,0:T(8,128)(2,1)S(1)}, bf16[96,96]{1,0:T(8,128)(2,1)S(1)}, f32[96,128]{1,0:T(8,128)S(1)}, f32[96,128]{1,0:T(8,128)S(1)}, f32[8,12...) custom-call(f32[4,24,768]{2,1,0:T(8,128)S(1)} %copy-done.4, ...), custom_call_target="tpu_custom_call" | custom-call | tf_op jit(solution)/shard_map/pallas_call | solution.py:345
  6.6 0.1 collective-permute-start.3
  6.7 4.6 %collective-permute-start.4 = (f32[24,896]{1,0:T(8,128)S(1)}, f32[24,896]{1,0:T(8,128)S(1)}, u32[]{:S(2)}, u32[]{:S(2)}) collective-permute-start(f32[24,896]{1,0:T(8,128)S(1)} %get-tuple-element.41), channel_id=1, source_target_pairs={{1,2},{2,1},{3,4},{4,3},{5,6},{6,5},{9,10},{10,9},{11,12},{12,11},... | collective-permute-start | bytes 258056 | tf_op jit(solution)/shard_map/ppermute | solution.py:363
  11.3 1.3 %collective-permute-start = (f32[56,128]{1,0:T(8,128)S(1)}, f32[56,128]{1,0:T(8,128)S(1)}, u32[]{:S(2)}, u32[]{:S(2)}) collective-permute-start(f32[56,128]{1,0:T(8,128)S(1)} %get-tuple-element.37), channel_id=1, source_target_pairs={{0,8},{8,0},{16,24},{24,16},{1,9},{9,1},{17,25},{25,17},{2,10},{10... | collective-permute-start | bytes 86024 | tf_op jit(solution)/shard_map/ppermute | solution.py:359
  12.6 1.2 %collective-permute-start.2 = (f32[56,128]{1,0:T(8,128)S(1)}, f32[56,128]{1,0:T(8,128)S(1)}, u32[]{:S(2)}, u32[]{:S(2)}) collective-permute-start(f32[56,128]{1,0:T(8,128)S(1)} %get-tuple-element.39), channel_id=1, source_target_pairs={{0,24},{8,16},{16,8},{24,0},{1,25},{9,17},{17,9},{25,1},{2,26},{10... | collective-permute-start | bytes 86024 | tf_op jit(solution)/shard_map/ppermute | solution.py:359
  13.8 0.2 collective-permute-start.1
  14.0 2.3 %collective-permute-done.1.refs_12_ = f32[24,128]{1,0:T(8,128)S(1)} collective-permute-done((f32[24,128]{1,0:T(8,128)S(1)}, f32[24,128]{1,0:T(8,128)S(1)}, u32[]{:S(2)}, u32[]{:S(2)}) %collective-permute-start.1) | collective-permute-done | bytes 12320 | tf_op jit(solution)/shard_map/ppermute | solution.py:359
  16.4 0.9 %copy-done.2 = bf16[768,128]{1,0:T(8,128)(2,1)S(1)} copy-done((bf16[768,128]{1,0:T(8,128)(2,1)S(1)}, bf16[768,128]{1,0:T(8,128)(2,1)}, u32[]{:S(2)}) %copy-start.2) | copy-done | bytes 196632
  17.3 0.9 %shard_map.105 = (f32[4,24,768]{2,1,0:T(8,128)S(1)}, f32[96,128]{1,0:T(8,128)S(1)}, f32[96,128]{1,0:T(8,128)S(1)}, f32[56,128]{1,0:T(8,128)S(1)}, f32[24,128]{1,...) custom-call(f32[4,24,768]{2,1,0:T(8,128)S(1)} %copy-done.4, ...), custom_call_target="tpu_custom_call" | custom-call | tf_op jit(solution)/shard_map/pallas_call | solution.py:345
  18.2 0.1 collective-permute-start.8
  18.3 4.2 %collective-permute-start.9 = (f32[24,896]{1,0:T(8,128)S(1)}, f32[24,896]{1,0:T(8,128)S(1)}, u32[]{:S(2)}, u32[]{:S(2)}) collective-permute-start(f32[24,896]{1,0:T(8,128)S(1)} %get-tuple-element.49), channel_id=1, source_target_pairs={{1,2},{2,1},{3,4},{4,3},{5,6},{6,5},{9,10},{10,9},{11,12},{12,11},... | collective-permute-start | bytes 258056 | tf_op jit(solution)/shard_map/ppermute | solution.py:363
  22.6 1.2 %collective-permute-start.5 = (f32[56,128]{1,0:T(8,128)S(1)}, f32[56,128]{1,0:T(8,128)S(1)}, u32[]{:S(2)}, u32[]{:S(2)}) collective-permute-start(f32[56,128]{1,0:T(8,128)S(1)} %get-tuple-element.45), channel_id=1, source_target_pairs={{0,8},{8,0},{16,24},{24,16},{1,9},{9,1},{17,25},{25,17},{2,10},{10... | collective-permute-start | bytes 86024 | tf_op jit(solution)/shard_map/ppermute | solution.py:359
  23.8 1.0 %collective-permute-start.7 = (f32[56,128]{1,0:T(8,128)S(1)}, f32[56,128]{1,0:T(8,128)S(1)}, u32[]{:S(2)}, u32[]{:S(2)}) collective-permute-start(f32[56,128]{1,0:T(8,128)S(1)} %get-tuple-element.47), channel_id=1, source_target_pairs={{0,24},{8,16},{16,8},{24,0},{1,25},{9,17},{17,9},{25,1},{2,26},{10... | collective-permute-start | bytes 86024 | tf_op jit(solution)/shard_map/ppermute | solution.py:359
  24.7 0.5 %collective-permute-start.6 = (f32[24,128]{1,0:T(8,128)S(1)}, f32[24,128]{1,0:T(8,128)S(1)}, u32[]{:S(2)}, u32[]{:S(2)}) collective-permute-start(f32[24,128]{1,0:T(8,128)S(1)} %get-tuple-element.46), channel_id=1, source_target_pairs={{0,16},{8,24},{16,0},{24,8},{1,17},{9,25},{17,1},{25,9},{2,18},{10... | collective-permute-start | bytes 36872 | tf_op jit(solution)/shard_map/ppermute | solution.py:359
  25.3 2.2 %collective-permute-done.6.refs_12_ = f32[24,128]{1,0:T(8,128)S(1)} collective-permute-done((f32[24,128]{1,0:T(8,128)S(1)}, f32[24,128]{1,0:T(8,128)S(1)}, u32[]{:S(2)}, u32[]{:S(2)}) %collective-permute-start.6) | collective-permute-done | bytes 12320 | tf_op jit(solution)/shard_map/ppermute | solution.py:359
  27.5 1.0 %shard_map.106 = (f32[4,24,768]{2,1,0:T(8,128)S(1)}, f32[96,128]{1,0:T(8,128)S(1)}, f32[96,128]{1,0:T(8,128)S(1)}, f32[56,128]{1,0:T(8,128)S(1)}, f32[24,128]{1,...) custom-call(f32[4,24,768]{2,1,0:T(8,128)S(1)} %get-tuple-element.42.refs_0_, ...), custom_call_target="tpu_custom_call" | custom-call | tf_op jit(solution)/shard_map/pallas_call | solution.py:345
  28.5 0.1 collective-permute-start.13
  28.6 3.6 %collective-permute-start.14 = (f32[24,896]{1,0:T(8,128)S(1)}, f32[24,896]{1,0:T(8,128)S(1)}, u32[]{:S(2)}, u32[]{:S(2)}) collective-permute-start(f32[24,896]{1,0:T(8,128)S(1)} %get-tuple-element.57), channel_id=1, source_target_pairs={{1,2},{2,1},{3,4},{4,3},{5,6},{6,5},{9,10},{10,9},{11,12},{12,11},... | collective-permute-start | bytes 258056 | tf_op jit(solution)/shard_map/ppermute | solution.py:363
  32.3 0.7 %collective-permute-start.10 = (f32[56,128]{1,0:T(8,128)S(1)}, f32[56,128]{1,0:T(8,128)S(1)}, u32[]{:S(2)}, u32[]{:S(2)}) collective-permute-start(f32[56,128]{1,0:T(8,128)S(1)} %get-tuple-element.53), channel_id=1, source_target_pairs={{0,8},{8,0},{16,24},{24,16},{1,9},{9,1},{17,25},{25,17},{2,10},{10... | collective-permute-start | bytes 86024 | tf_op jit(solution)/shard_map/ppermute | solution.py:359
  33.0 1.3 %collective-permute-start.12 = (f32[56,128]{1,0:T(8,128)S(1)}, f32[56,128]{1,0:T(8,128)S(1)}, u32[]{:S(2)}, u32[]{:S(2)}) collective-permute-start(f32[56,128]{1,0:T(8,128)S(1)} %get-tuple-element.55), channel_id=1, source_target_pairs={{0,24},{8,16},{16,8},{24,0},{1,25},{9,17},{17,9},{25,1},{2,26},{10... | collective-permute-start | bytes 86024 | tf_op jit(solution)/shard_map/ppermute | solution.py:359
  34.2 0.7 %collective-permute-start.11 = (f32[24,128]{1,0:T(8,128)S(1)}, f32[24,128]{1,0:T(8,128)S(1)}, u32[]{:S(2)}, u32[]{:S(2)}) collective-permute-start(f32[24,128]{1,0:T(8,128)S(1)} %get-tuple-element.54), channel_id=1, source_target_pairs={{0,16},{8,24},{16,0},{24,8},{1,17},{9,25},{17,1},{25,9},{2,18},{10... | collective-permute-start | bytes 36872 | tf_op jit(solution)/shard_map/ppermute | solution.py:359
  35.0 1.8 %collective-permute-done.11.refs_12_ = f32[24,128]{1,0:T(8,128)S(1)} collective-permute-done((f32[24,128]{1,0:T(8,128)S(1)}, f32[24,128]{1,0:T(8,128)S(1)}, u32[]{:S(2)}, u32[]{:S(2)}) %collective-permute-start.11) | collective-permute-done | bytes 12320 | tf_op jit(solution)/shard_map/ppermute | solution.py:359
  36.8 1.2 %shard_map.107 = (f32[4,24,768]{2,1,0:T(8,128)}, f32[4,24,64]{2,1,0:T(8,128)}) custom-call(f32[4,24,768]{2,1,0:T(8,128)S(1)} %get-tuple-element.50.refs_0_, f32[96,128]{1,0:T(8,128)S(1)} %get-tuple-element.51.refs_1_, f32[96,128]{1,0:T(8,128)S(1)} %get-tuple-element.52.refs_2_, bf16[96,96]{1,0:T(8,128)(2,1)S(1)} %get-tuple-element.32.refs_3_, ...), custom_call_target="tpu_custom_call" | custom-call | tf_op jit(solution)/shard_map/pallas_call | solution.py:345
  (24 shorter events, 0.1 us)
Async XLA Ops:
  0.6 15.7 %copy-start = (bf16[256,768]{1,0:T(8,128)(2,1)S(1)}, bf16[256,768]{1,0:T(8,128)(2,1)}, u32[]{:S(2)}) copy-start(bf16[256,768]{1,0:T(8,128)(2,1)} %constant.8.clone.refs_10_) | copy-start | bytes 1179652
  0.6 1.0 %copy-start.1 = (bf16[768,128]{1,0:T(8,128)(2,1)S(1)}, bf16[768,128]{1,0:T(8,128)(2,1)}, u32[]{:S(2)}) copy-start(bf16[768,128]{1,0:T(8,128)(2,1)} %constant.7.clone.refs_6_.refs_9_) | copy-start | bytes 589828
  1.6 1.0 %copy-start.4 = (f32[4,24,768]{2,1,0:T(8,128)S(1)}, f32[4,24,768]{2,1,0:T(8,128)}, u32[]{:S(2)}) copy-start(f32[4,24,768]{2,1,0:T(8,128)} %refs_0_.3) | copy-start | bytes 884740
  2.6 0.8 %copy-start.6 = (f32[4,24,64]{2,1,0:T(8,128)S(1)}, f32[4,24,64]{2,1,0:T(8,128)}, u32[]{:S(2)}) copy-start(f32[4,24,64]{2,1,0:T(8,128)} %refs_2_.1) | copy-start | bytes 73732
  3.4 0.7 %copy-start.7 = (f32[4,24]{1,0:T(4,128)S(1)}, f32[4,24]{1,0:T(4,128)}, u32[]{:S(2)}) copy-start(f32[4,24]{1,0:T(4,128)} %refs_1_.1) | copy-start | bytes 1156
  4.1 0.7 %copy-start.8 = (s32[4,24]{1,0:T(4,128)S(1)}, s32[4,24]{1,0:T(4,128)}, u32[]{:S(2)}) copy-start(s32[4,24]{1,0:T(4,128)} %refs_4_.1) | copy-start | bytes 1156
  4.7 0.7 %copy-start.9 = (s32[4,24]{1,0:T(4,128)S(1)}, s32[4,24]{1,0:T(4,128)}, u32[]{:S(2)}) copy-start(s32[4,24]{1,0:T(4,128)} %refs_5_.1) | copy-start | bytes 1156
  5.4 0.7 %copy-start.10 = (f32[32]{0:T(128)S(1)}, f32[32]{0:T(128)}, u32[]{:S(2)}) copy-start(f32[32]{0:T(128)} %refs_3_.1) | copy-start | bytes 388
  6.1 10.3 %copy-start.5 = (f32[8,768]{1,0:T(8,128)S(1)}, f32[8,768]{1,0:T(8,128)}, u32[]{:S(2)}) copy-start(f32[8,768]{1,0:T(8,128)} %constant.6.clone.refs_8_) | copy-start | bytes 73732
  6.6 9.7 %collective-permute-start.3 = (f32[24,896]{1,0:T(8,128)S(1)}, f32[24,896]{1,0:T(8,128)S(1)}, u32[]{:S(2)}, u32[]{:S(2)}) collective-permute-start(f32[24,896]{1,0:T(8,128)S(1)} %get-tuple-element.40), channel_id=1, source_target_pairs={{0,1},{1,0},{2,3},{3,2},{4,5},{5,4},{6,7},{7,6},{8,9},{9,8},{10,11... | collective-permute-start | bytes 258056 | tf_op jit(solution)/shard_map/ppermute | solution.py:362
  6.7 9.6 %collective-permute-start.4 = (f32[24,896]{1,0:T(8,128)S(1)}, f32[24,896]{1,0:T(8,128)S(1)}, u32[]{:S(2)}, u32[]{:S(2)}) collective-permute-start(f32[24,896]{1,0:T(8,128)S(1)} %get-tuple-element.41), channel_id=1, source_target_pairs={{1,2},{2,1},{3,4},{4,3},{5,6},{6,5},{9,10},{10,9},{11,12},{12,11},... | collective-permute-start | bytes 258056 | tf_op jit(solution)/shard_map/ppermute | solution.py:363
  11.3 5.0 %collective-permute-start = (f32[56,128]{1,0:T(8,128)S(1)}, f32[56,128]{1,0:T(8,128)S(1)}, u32[]{:S(2)}, u32[]{:S(2)}) collective-permute-start(f32[56,128]{1,0:T(8,128)S(1)} %get-tuple-element.37), channel_id=1, source_target_pairs={{0,8},{8,0},{16,24},{24,16},{1,9},{9,1},{17,25},{25,17},{2,10},{10... | collective-permute-start | bytes 86024 | tf_op jit(solution)/shard_map/ppermute | solution.py:359
  12.6 3.8 %collective-permute-start.2 = (f32[56,128]{1,0:T(8,128)S(1)}, f32[56,128]{1,0:T(8,128)S(1)}, u32[]{:S(2)}, u32[]{:S(2)}) collective-permute-start(f32[56,128]{1,0:T(8,128)S(1)} %get-tuple-element.39), channel_id=1, source_target_pairs={{0,24},{8,16},{16,8},{24,0},{1,25},{9,17},{17,9},{25,1},{2,26},{10... | collective-permute-start | bytes 86024 | tf_op jit(solution)/shard_map/ppermute | solution.py:359
  13.8 2.5 %collective-permute-start.1 = (f32[24,128]{1,0:T(8,128)S(1)}, f32[24,128]{1,0:T(8,128)S(1)}, u32[]{:S(2)}, u32[]{:S(2)}) collective-permute-start(f32[24,128]{1,0:T(8,128)S(1)} %get-tuple-element.38), channel_id=1, source_target_pairs={{0,16},{8,24},{16,0},{24,8},{1,17},{9,25},{17,1},{25,9},{2,18},{10... | collective-permute-start | bytes 36872 | tf_op jit(solution)/shard_map/ppermute | solution.py:359
  16.4 0.9 %copy-start.2 = (bf16[768,128]{1,0:T(8,128)(2,1)S(1)}, bf16[768,128]{1,0:T(8,128)(2,1)}, u32[]{:S(2)}) copy-start(bf16[768,128]{1,0:T(8,128)(2,1)} %constant.7.clone.refs_6_.refs_9_) | copy-start | bytes 589828
  17.3 10.2 %copy-start.3 = (bf16[768,128]{1,0:T(8,128)(2,1)S(1)}, bf16[768,128]{1,0:T(8,128)(2,1)}, u32[]{:S(2)}) copy-start(bf16[768,128]{1,0:T(8,128)(2,1)} %constant.7.clone.refs_6_.refs_9_) | copy-start | bytes 589828
  18.2 9.3 %collective-permute-start.8 = (f32[24,896]{1,0:T(8,128)S(1)}, f32[24,896]{1,0:T(8,128)S(1)}, u32[]{:S(2)}, u32[]{:S(2)}) collective-permute-start(f32[24,896]{1,0:T(8,128)S(1)} %get-tuple-element.48), channel_id=1, source_target_pairs={{0,1},{1,0},{2,3},{3,2},{4,5},{5,4},{6,7},{7,6},{8,9},{9,8},{10,11... | collective-permute-start | bytes 258056 | tf_op jit(solution)/shard_map/ppermute | solution.py:362
  18.3 9.2 %collective-permute-start.9 = (f32[24,896]{1,0:T(8,128)S(1)}, f32[24,896]{1,0:T(8,128)S(1)}, u32[]{:S(2)}, u32[]{:S(2)}) collective-permute-start(f32[24,896]{1,0:T(8,128)S(1)} %get-tuple-element.49), channel_id=1, source_target_pairs={{1,2},{2,1},{3,4},{4,3},{5,6},{6,5},{9,10},{10,9},{11,12},{12,11},... | collective-permute-start | bytes 258056 | tf_op jit(solution)/shard_map/ppermute | solution.py:363
  22.6 5.0 %collective-permute-start.5 = (f32[56,128]{1,0:T(8,128)S(1)}, f32[56,128]{1,0:T(8,128)S(1)}, u32[]{:S(2)}, u32[]{:S(2)}) collective-permute-start(f32[56,128]{1,0:T(8,128)S(1)} %get-tuple-element.45), channel_id=1, source_target_pairs={{0,8},{8,0},{16,24},{24,16},{1,9},{9,1},{17,25},{25,17},{2,10},{10... | collective-permute-start | bytes 86024 | tf_op jit(solution)/shard_map/ppermute | solution.py:359
  23.8 3.8 %collective-permute-start.7 = (f32[56,128]{1,0:T(8,128)S(1)}, f32[56,128]{1,0:T(8,128)S(1)}, u32[]{:S(2)}, u32[]{:S(2)}) collective-permute-start(f32[56,128]{1,0:T(8,128)S(1)} %get-tuple-element.47), channel_id=1, source_target_pairs={{0,24},{8,16},{16,8},{24,0},{1,25},{9,17},{17,9},{25,1},{2,26},{10... | collective-permute-start | bytes 86024 | tf_op jit(solution)/shard_map/ppermute | solution.py:359
  24.7 2.8 %collective-permute-start.6 = (f32[24,128]{1,0:T(8,128)S(1)}, f32[24,128]{1,0:T(8,128)S(1)}, u32[]{:S(2)}, u32[]{:S(2)}) collective-permute-start(f32[24,128]{1,0:T(8,128)S(1)} %get-tuple-element.46), channel_id=1, source_target_pairs={{0,16},{8,24},{16,0},{24,8},{1,17},{9,25},{17,1},{25,9},{2,18},{10... | collective-permute-start | bytes 36872 | tf_op jit(solution)/shard_map/ppermute | solution.py:359
  28.5 8.3 %collective-permute-start.13 = (f32[24,896]{1,0:T(8,128)S(1)}, f32[24,896]{1,0:T(8,128)S(1)}, u32[]{:S(2)}, u32[]{:S(2)}) collective-permute-start(f32[24,896]{1,0:T(8,128)S(1)} %get-tuple-element.56), channel_id=1, source_target_pairs={{0,1},{1,0},{2,3},{3,2},{4,5},{5,4},{6,7},{7,6},{8,9},{9,8},{10,11... | collective-permute-start | bytes 258056 | tf_op jit(solution)/shard_map/ppermute | solution.py:362
  28.6 8.2 %collective-permute-start.14 = (f32[24,896]{1,0:T(8,128)S(1)}, f32[24,896]{1,0:T(8,128)S(1)}, u32[]{:S(2)}, u32[]{:S(2)}) collective-permute-start(f32[24,896]{1,0:T(8,128)S(1)} %get-tuple-element.57), channel_id=1, source_target_pairs={{1,2},{2,1},{3,4},{4,3},{5,6},{6,5},{9,10},{10,9},{11,12},{12,11},... | collective-permute-start | bytes 258056 | tf_op jit(solution)/shard_map/ppermute | solution.py:363
  32.3 4.5 %collective-permute-start.10 = (f32[56,128]{1,0:T(8,128)S(1)}, f32[56,128]{1,0:T(8,128)S(1)}, u32[]{:S(2)}, u32[]{:S(2)}) collective-permute-start(f32[56,128]{1,0:T(8,128)S(1)} %get-tuple-element.53), channel_id=1, source_target_pairs={{0,8},{8,0},{16,24},{24,16},{1,9},{9,1},{17,25},{25,17},{2,10},{10... | collective-permute-start | bytes 86024 | tf_op jit(solution)/shard_map/ppermute | solution.py:359
  33.0 3.8 %collective-permute-start.12 = (f32[56,128]{1,0:T(8,128)S(1)}, f32[56,128]{1,0:T(8,128)S(1)}, u32[]{:S(2)}, u32[]{:S(2)}) collective-permute-start(f32[56,128]{1,0:T(8,128)S(1)} %get-tuple-element.55), channel_id=1, source_target_pairs={{0,24},{8,16},{16,8},{24,0},{1,25},{9,17},{17,9},{25,1},{2,26},{10... | collective-permute-start | bytes 86024 | tf_op jit(solution)/shard_map/ppermute | solution.py:359
  34.2 2.5 %collective-permute-start.11 = (f32[24,128]{1,0:T(8,128)S(1)}, f32[24,128]{1,0:T(8,128)S(1)}, u32[]{:S(2)}, u32[]{:S(2)}) collective-permute-start(f32[24,128]{1,0:T(8,128)S(1)} %get-tuple-element.54), channel_id=1, source_target_pairs={{0,16},{8,24},{16,0},{24,8},{1,17},{9,25},{17,1},{25,9},{2,18},{10... | collective-permute-start | bytes 36872 | tf_op jit(solution)/shard_map/ppermute | solution.py:359

commit v2 on v1

v2 whole, which is shorter than its diff:
```python
import functools
import math

import jax
import jax.numpy as jnp
import ml_dtypes
import numpy as np
from jax import lax
from jax.experimental import pallas as pl
from jax.experimental.pallas import tpu as pltpu
from jax.sharding import PartitionSpec as P

NFREQ = 24
NDIR = 32
STEPS = 3

stokes_scale = 0.1
ocean_dt = 0.3
current_gain = 0.2

LANES = 128
F32 = jnp.float32
BF16 = jnp.bfloat16


def split_halves(table):
    high = table.astype(ml_dtypes.bfloat16)
    low = (table - high.astype(np.float64)).astype(ml_dtypes.bfloat16)
    return high, low


def build_tables(nfreq, ndir, ndepth):
    fraction = np.arange(nfreq) / (nfreq - 1)
    angles = (np.arange(ndir) + 0.5) * (2.0 * math.pi / ndir)
    east_part, north_part = np.cos(angles), np.sin(angles)
    courant = 0.1 + 0.3 * fraction
    depth_level = 0.5 + (ndepth - 2) * (1.0 - fraction)
    weights = np.maximum(1.0 - np.abs(np.arange(ndepth)[None, :] - depth_level[:, None]), 0.0)
    mean_weights = weights / weights.sum(axis=1, keepdims=True)
    x_rate = np.abs(courant[:, None] * east_part[None, :]).reshape(-1)
    y_rate = np.abs(courant[:, None] * north_part[None, :]).reshape(-1)
    turn_gain = np.repeat(1.0 - 0.5 * fraction, ndir)
    rates = np.stack([1.0 - x_rate - y_rate, x_rate, y_rate, turn_gain] * 2).astype(np.float32)
    compass = np.stack([east_part, north_part])
    stokes = (stokes_scale * weights[:, None, None, :] * compass.T[None, :, :, None]).reshape(
        nfreq * ndir, 2 * ndepth
    )
    growth = current_gain * (1.0 + fraction)
    grow = (
        growth[None, None, :, None] * mean_weights.T[None, :, :, None] * compass[:, None, None, :]
    ).reshape(2 * ndepth, nfreq * ndir)
    stokes_high, stokes_low = split_halves(stokes)
    grow_high, grow_low = split_halves(grow)
    return (
        np.concatenate([stokes_high, stokes_low], axis=1),
        rates,
        np.concatenate([grow_high, grow_high, grow_low, grow_low], axis=0)
        .reshape(8 * ndepth, -1, LANES)
        .transpose(1, 0, 2)
        .reshape(-1, LANES),
    )


def sec_exchanges(count):
    if count % 4 == 0:
        far = count // 4
        return [
            [((i // 4 + hop) % far) * 4 + ((i % 4) ^ flip) for i in range(count)]
            for hop in range(far)
            for flip in range(4)
            if hop or flip
        ]
    return [[(i + hop) % count for i in range(count)] for hop in range(1, count)]


class Plan:
    def __init__(self, sections, bands, rows, cols, spectral, depth):
        self.sections, self.bands = sections, bands
        self.rows, self.cols, self.spectral, self.depth = rows, cols, spectral, depth
        self.columns = rows * cols
        self.chunk = self.columns // sections
        self.tiles = spectral // LANES
        self.exchanges = sec_exchanges(sections)
        self.edges = [
            any(abs(target - i) == 1 for i, target in enumerate(table)) for table in self.exchanges
        ]
        self.sec_rows = [
            self.chunk + (self.tiles * rows + 8 if edge else 0) for edge in self.edges
        ]

    def partner(self, section, number):
        if self.sections % 4 == 0:
            far = self.sections // 4
            hop, flip = divmod(number + 1, 4)
            high, low = lax.div(section, 4), lax.rem(section, 4)
            flipped = low
            if flip & 1:
                flipped = flipped + 1 - 2 * lax.rem(flipped, 2)
            if flip & 2:
                flipped = flipped + 2 - 4 * lax.div(flipped, 2)
            return (
                lax.rem(high + hop, far) * 4 + flipped,
                lax.rem(high + far - hop, far) * 4 + flipped,
            )
        hop = number + 1
        return (
            lax.rem(section + hop, self.sections),
            lax.rem(section + self.sections - hop, self.sections),
        )


def lane_of(shape):
    return lax.broadcasted_iota(jnp.int32, shape, len(shape) - 1)


def dot(a, b):
    return jnp.dot(a, b, preferred_element_type=F32)


def split_value(value):
    high = value.astype(BF16).astype(F32)
    return jnp.where(lane_of(value.shape) < LANES // 2, high, value - high).astype(BF16)


def stokes_product(part, table):
    high = part.astype(BF16)
    low = (part - high.astype(F32)).astype(BF16)
    return dot(jnp.concatenate([high, low], axis=0), table)


def send_parts(plan, section, even, waves, ocean, total, permute_t, packed_out, sec_out, lat_out):
    chunk, tiles, rows, cols = plan.chunk, plan.tiles, plan.rows, plan.cols
    lane = lane_of((plan.columns, LANES))
    near, far = lat_out
    sea_rows = ocean.reshape(rows, cols, LANES)
    low_half = lax.rem(lane_of((cols, LANES)), NDIR) < NDIR // 2
    for out, northward in ((far, jnp.logical_not(even)), (near, even)):
        edge = jnp.where(northward, waves[rows - 1], waves[0])
        for tile in range(tiles // 2):
            first = edge[:, tile * LANES : (tile + 1) * LANES]
            second = edge[:, (tile + tiles // 2) * LANES : (tile + tiles // 2 + 1) * LANES]
            up = jnp.where(low_half, first, pltpu.roll(second, NDIR // 2, 1))
            down = jnp.where(low_half, pltpu.roll(second, LANES - NDIR // 2, 1), first)
            out[:, tile * LANES : (tile + 1) * LANES] = jnp.where(northward, up, down)
        out[:, plan.spectral // 2 :] = jnp.where(northward, sea_rows[rows - 1], sea_rows[0])
    moments = total[: plan.columns] + total[plan.columns :]
    moments = moments + pltpu.roll(moments, LANES // 2, 1)
    ordered = dot(permute_t, split_value(moments))
    ordered = ordered + pltpu.roll(ordered, LANES // 2, 1)
    packed_out[...] = jnp.where(lane < LANES // 2, ocean, ordered)
    for number, out in enumerate(sec_out):
        target, _ = plan.partner(section, number)
        out[0:chunk, :] = packed_out[pl.ds(pl.multiple_of(target * chunk, 8), chunk), :]
        if not plan.edges[number]:
            continue
        eastward = target == section + 1
        for row in range(rows):
            edge = jnp.where(eastward, waves[row, cols - 1 : cols, :], waves[row, 0:1, :])
            for tile in range(tiles):
                place = chunk + tile * rows + row
                out[place : place + 1, :] = edge[:, tile * LANES : (tile + 1) * LANES]
            place = chunk + tiles * rows + row
            out[place : place + 1, :] = jnp.where(
                eastward, sea_rows[row, cols - 1 : cols, :], sea_rows[row, 0:1, :]
            )


def first_kernel(plan, axes, *refs):
    waves_in, turning_in, currents_in, drag_in, mask_in, target_in = refs[:6]
    tables_in, refs = refs[6:9], refs[9:]
    waves, ocean_out, permute_out, permute_t_out, turn_out, sea_out, keep_out = refs[:7]
    tables_out, packed_out, refs = refs[7:10], refs[10], refs[11:]
    count = len(plan.exchanges)
    sec_out, lat_out, refs = refs[:count], refs[count : count + 2], refs[count + 2 :]
    turning, currents, drag, mask, target, done = refs
    pairs = [
        (target_in, target),
        (turning_in, turning),
        (mask_in, mask),
        (drag_in, drag),
        (waves_in, waves),
        (tables_in[0], tables_out[0]),
        (currents_in, currents),
        (tables_in[1], tables_out[1]),
        (tables_in[2], tables_out[2]),
    ]
    copies = [pltpu.make_async_copy(a, b, done.at[k]) for k, (a, b) in enumerate(pairs)]
    for copy in copies:
        copy.start()
    section, band = lax.axis_index(axes[1]), lax.axis_index(axes[0])
    even = lax.rem(band, 2) == 0
    columns, rows = plan.columns, plan.rows
    across = lane_of((columns, columns))
    down = lax.broadcasted_iota(jnp.int32, (columns, columns), 0)
    here = across == down

    def row_of(ref):
        return jnp.concatenate([ref[row : row + 1, :] for row in range(rows)], axis=1)

    def column_of(row):
        spread = jnp.broadcast_to(row, (columns, columns))
        return jnp.sum(jnp.where(here, spread, jnp.zeros_like(spread)), axis=1, keepdims=True)

    for copy in copies[:4]:
        copy.wait()
    sea = column_of(row_of(mask).astype(F32))
    target_row = row_of(target).astype(F32)
    target_col = column_of(target_row)
    same = target_col == target_row
    rank_col = jnp.sum(jnp.where(same & (across < down), 1.0, 0.0), axis=1, keepdims=True)
    rank_row = jnp.sum(jnp.where(same & (down < across), 1.0, 0.0), axis=0, keepdims=True)
    slot_col = target_col * float(plan.chunk) + rank_col
    slot_row = target_row * float(plan.chunk) + rank_row
    permute_out[...] = jnp.where(slot_col == across.astype(F32), sea, 0.0).astype(BF16)
    permute_t = jnp.where(slot_row == down.astype(F32), 1.0, 0.0).astype(BF16)
    permute_t_out[...] = permute_t
    turn_out[...] = jnp.broadcast_to(column_of(row_of(turning)), (columns, LANES))
    sea_out[...] = jnp.broadcast_to(sea, (columns, LANES))
    keep = 1.0 - drag[...].reshape(1, plan.depth)
    blank = jnp.zeros((1, LANES - 2 * plan.depth), F32)
    keep_out[...] = jnp.broadcast_to(jnp.concatenate([keep, keep, blank], axis=1), (8, LANES))
    for copy in copies[4:7]:
        copy.wait()
    flat = currents[...].reshape(columns, 2 * plan.depth)
    ocean = jnp.concatenate([flat, jnp.zeros((columns, LANES - 2 * plan.depth), F32)], axis=1)
    ocean_out[...] = ocean
    total = None
    for start in range(0, plan.spectral, 256):
        part = waves[:, :, start : start + 256].reshape(columns, 256)
        product = stokes_product(part, tables_out[0][start : start + 256, :])
        total = product if total is None else total + product
    send_parts(
        plan, section, even, waves, ocean, total, permute_t, packed_out, sec_out, lat_out
    )
    for copy in copies[7:]:
        copy.wait()


def move_kernel(plan, axes, *refs):
    waves, ocean, turn, rates = refs[:4]
    edge_numbers = [number for number, edge in enumerate(plan.edges) if edge]
    sec_in, refs = refs[4 : 4 + len(edge_numbers)], refs[4 + len(edge_numbers) :]
    near, far, turned_out, spin_out, west_edge, east_edge = refs
    section, band = lax.axis_index(axes[1]), lax.axis_index(axes[0])
    even = lax.rem(band, 2) == 0
    rows, cols, tiles, chunk = plan.rows, plan.cols, plan.tiles, plan.chunk

    west_edge[...] = jnp.zeros_like(west_edge)
    east_edge[...] = jnp.zeros_like(east_edge)
    for number, message in zip(edge_numbers, sec_in):
        _, source = plan.partner(section, number)

        @pl.when(source == section + 1)
        def _():
            east_edge[...] = message[chunk:, :]

        @pl.when(source == section - 1)
        def _():
            west_edge[...] = message[chunk:, :]

    block = (cols, LANES)
    direction = lax.rem(lane_of(block), NDIR)
    eastward = (direction < NDIR // 4) | (direction >= 3 * NDIR // 4)
    northward = direction < NDIR // 2
    first, final = direction == 0, direction == NDIR - 1
    place = lax.broadcasted_iota(jnp.int32, block, 0)
    at_west, at_east = place == 0, place == cols - 1
    for tile in range(tiles):
        lanes = slice(tile * LANES, (tile + 1) * LANES)
        stay, along_x, along_y, gain = (rates[k : k + 1, lanes] for k in range(4))
        half = tile % (tiles // 2)
        half = slice(half * LANES, (half + 1) * LANES)
        south_edge = jnp.where(even, far[:, half], near[:, half])
        north_edge = jnp.where(even, near[:, half], far[:, half])
        if tile >= tiles // 2:
            south_edge = pltpu.roll(south_edge, LANES - NDIR // 2, 1)
            north_edge = pltpu.roll(north_edge, NDIR // 2, 1)
        for row in range(rows):
            edge = slice(tile * rows + row, tile * rows + row + 1)
            center = waves[row, :, lanes]
            west = jnp.where(at_west, west_edge[edge, :], pltpu.roll(center, 1, 0))
            east = jnp.where(at_east, east_edge[edge, :], pltpu.roll(center, cols - 1, 0))
            south = waves[row - 1, :, lanes] if row else south_edge
            north = waves[row + 1, :, lanes] if row < rows - 1 else north_edge
            moved = (
                stay * center
                + along_x * jnp.where(eastward, west, east)
                + along_y * jnp.where(northward, south, north)
            )
            behind = jnp.where(
                first, pltpu.roll(moved, LANES - (NDIR - 1), 1), pltpu.roll(moved, 1, 1)
            )
            forward = jnp.where(
                final, pltpu.roll(moved, NDIR - 1, 1), pltpu.roll(moved, LANES - 1, 1)
            )
            rate = turn[row * cols : (row + 1) * cols, :]
            turned_out[row, :, lanes] = moved - jnp.abs(rate) * gain * (
                moved - jnp.where(rate > 0.0, behind, forward)
            )

    zonal = lane_of(block) < plan.depth
    half = slice(plan.spectral // 2, plan.spectral // 2 + LANES)
    south_edge = jnp.where(even, far[:, half], near[:, half])
    north_edge = jnp.where(even, near[:, half], far[:, half])
    for row in range(rows):
        flat = slice(row * cols, (row + 1) * cols)
        edge = slice(tiles * rows + row, tiles * rows + row + 1)
        center = ocean[flat, :]
        west = jnp.where(at_west, west_edge[edge, :], pltpu.roll(center, 1, 0))
        east = jnp.where(at_east, east_edge[edge, :], pltpu.roll(center, cols - 1, 0))
        south = ocean[(row - 1) * cols : row * cols, :] if row else south_edge
        north = ocean[(row + 1) * cols : (row + 2) * cols, :] if row < rows - 1 else north_edge
        shear = 0.5 * jnp.where(zonal, south - north, east - west)
        shear = shear + swapped(plan, shear)
        y = (band * rows + row).astype(F32)
        spin_out[flat, :] = 0.2 + 0.6 * y / float(plan.bands * rows) + shear


def swapped(plan, value):
    half = plan.depth
    zonal = lane_of(value.shape) < half
    return jnp.where(zonal, pltpu.roll(value, LANES - half, 1), pltpu.roll(value, half, 1))


def couple_kernel(plan, axes, last, *refs):
    turned, spin, ocean_in, packed_in, permute, permute_t, sea, keep, stokes, grow = refs[:10]
    refs = refs[10:]
    count = len(plan.exchanges)
    sec_in, refs = refs[:count], refs[count:]
    if last:
        waves_far, ocean_far, coupled, waves_out, ocean_out, done = refs
    else:
        waves_out, ocean_out, packed_out = refs[:3]
        sec_out, lat_out, coupled = refs[3 : count + 3], refs[count + 3 : count + 5], refs[-1]
    section, band = lax.axis_index(axes[1]), lax.axis_index(axes[0])
    even = lax.rem(band, 2) == 0
    rows, cols, chunk, columns = plan.rows, plan.cols, plan.chunk, plan.columns

    own = pl.ds(pl.multiple_of(section * chunk, 8), chunk)
    coupled[own, :] = packed_in[own, :]
    for number, message in enumerate(sec_in):
        _, source = plan.partner(section, number)
        coupled[pl.ds(pl.multiple_of(source * chunk, 8), chunk), :] = message[0:chunk, :]
    arrived = coupled[...]
    other = pltpu.roll(arrived, LANES // 2, 1)
    lane = lane_of((columns, LANES))
    both = jnp.where(lane < LANES // 2, arrived, other)
    at_waves = dot(permute[...], split_value(both)).astype(BF16)
    at_waves = jnp.concatenate([at_waves, at_waves], axis=1)

    pushed = swapped(plan, ocean_in[...] + other)
    turn_by = ocean_dt * spin[...] * pushed
    new = keep[0:1, :] * (ocean_in[...] + jnp.where(lane < plan.depth, turn_by, -turn_by)) * sea[...]
    if last:
        ocean_out[...] = new[:, : 2 * plan.depth].reshape(rows, cols, 2 * plan.depth)
        copies = [pltpu.make_async_copy(ocean_out, ocean_far, done.at[0])]
        copies[0].start()
    else:
        ocean_out[...] = new

    total = None
    wet = jnp.concatenate([sea[...], sea[...]], axis=1)
    for number, start in enumerate(range(0, plan.spectral, 256)):
        lanes = slice(start, start + 256)
        table = jnp.concatenate(
            [grow[(2 * number + k) * 256 : (2 * number + k + 1) * 256, :] for k in range(2)], axis=1
        )
        grown = turned[:, :, lanes].reshape(columns, 256) * (wet + dot(at_waves, table))
        waves_out[:, :, lanes] = grown.reshape(rows, cols, 256)
        if last:
            copy = pltpu.make_async_copy(
                waves_out.at[:, :, lanes], waves_far.at[:, :, lanes], done.at[number + 1]
            )
            copy.start()
            copies.append(copy)
        else:
            product = stokes_product(grown, stokes[lanes, :])
            total = product if total is None else total + product
    if last:
        for copy in copies:
            copy.wait()
        return
    send_parts(
        plan, section, even, waves_out, new, total, permute_t[...], packed_out, sec_out, lat_out
    )


def per_device(plan, axes, spectra, turning, currents, drag_rates, land_mask, ocean_target):
    tables = [jnp.asarray(table) for table in build_tables(NFREQ, NDIR, drag_rates.shape[0])]
    columns, rows, cols, spectral = plan.columns, plan.rows, plan.cols, plan.spectral
    shape = jax.ShapeDtypeStruct
    params = pltpu.CompilerParams(vmem_limit_bytes=32 * 1024 * 1024)
    messages = [shape((size, LANES), F32) for size in plan.sec_rows] + [
        shape((cols, spectral // 2 + LANES), F32)
    ] * 2
    state = shape((columns, LANES), F32)
    field = shape(spectra.shape, F32)
    square = shape((columns, columns), BF16)
    edge = pltpu.VMEM((plan.tiles * rows + 8, LANES), F32)
    coupled = pltpu.VMEM((columns, LANES), F32)
    spans = spectral // 256

    def call(kernel, outs, scratch, *args, space_in=pltpu.VMEM, space_out=pltpu.VMEM):
        return pl.pallas_call(
            kernel,
            out_shape=outs,
            in_specs=[pl.BlockSpec(memory_space=space_in)] * len(args),
            out_specs=[pl.BlockSpec(memory_space=space_out)] * len(outs),
            scratch_shapes=scratch,
            compiler_params=params,
        )(*args)

    def exchange(sent):
        near = [(i, i ^ 1) for i in range(plan.bands) if i ^ 1 < plan.bands]
        far = [(i, ((i + 1) ^ 1) - 1) for i in range(1, plan.bands) if ((i + 1) ^ 1) - 1 < plan.bands]
        got = [
            lax.ppermute(message, axes[1], list(enumerate(table)))
            for message, table in zip(sent, plan.exchanges)
        ]
        return got, lax.ppermute(sent[-2], axes[0], near), lax.ppermute(sent[-1], axes[0], far)

    waves, ocean, permute, permute_t, turn, sea, keep, stokes, rates, grow, packed, *sent = call(
        functools.partial(first_kernel, plan, axes),
        [field, state, square, square, state, state, shape((8, LANES), F32)]
        + [shape(table.shape, table.dtype) for table in tables]
        + [state]
        + messages,
        [
            pltpu.VMEM(turning.shape, F32),
            pltpu.VMEM(currents.shape, F32),
            pltpu.VMEM(drag_rates.shape, F32),
            pltpu.VMEM(land_mask.shape, jnp.int32),
            pltpu.VMEM(ocean_target.shape, jnp.int32),
            pltpu.SemaphoreType.DMA((9,)),
        ],
        spectra,
        turning,
        currents,
        drag_rates,
        land_mask,
        ocean_target,
        *tables,
        space_in=pltpu.HBM,
    )
    for step in range(STEPS):
        last = step == STEPS - 1
        got, near, far = exchange(sent)
        turned, spin = call(
            functools.partial(move_kernel, plan, axes),
            [field, state],
            [edge, edge],
            waves,
            ocean,
            turn,
            rates,
            *[message for message, edged in zip(got, plan.edges) if edged],
            near,
            far,
        )
        result = call(
            functools.partial(couple_kernel, plan, axes, last),
            [field, shape(currents.shape, F32)] if last else [field, state, state] + messages,
            [
                coupled,
                pltpu.VMEM(spectra.shape, F32),
                pltpu.VMEM(currents.shape, F32),
                pltpu.SemaphoreType.DMA((1 + spans,)),
            ]
            if last
            else [coupled],
            turned,
            spin,
            ocean,
            packed,
            permute,
            permute_t,
            sea,
            keep,
            stokes,
            grow,
            *got,
            space_out=pltpu.HBM if last else pltpu.VMEM,
        )
        waves, ocean = result[:2]
        if not last:
            packed, *sent = result[2:]
    return waves, ocean


def solution(mesh):
    sections, bands = mesh.shape["sec"], mesh.shape["lat"]

    def local(spectra, turning, currents, drag_rates, land_mask, ocean_target):
        rows, cols, spectral = spectra.shape
        plan = Plan(sections, bands, rows, cols, spectral, drag_rates.shape[0])
        return per_device(
            plan, ("lat", "sec"), spectra, turning, currents, drag_rates, land_mask, ocean_target
        )

    return jax.shard_map(
        local,
        mesh=mesh,
        in_specs=(
            P("lat", "sec", None),
            P("lat", "sec"),
            P("lat", "sec", None),
            P(),
            P("lat", "sec"),
            P("lat", "sec"),
        ),
        out_specs=(P("lat", "sec", None), P("lat", "sec", None)),
        check_vma=False,
    )
```

time: 38.4 us -> 41.3 us (1.076)
  Pallas kernels: 3.67 us -> 6.73 us
  waiting for transfers between devices: 6.41 us -> 5.55 us
  local copies, waits for them, and re-layouts: 6.37 us -> 7.11 us
    pallas_call x4 -> x7, Pallas kernels: 3.67 us -> 6.73 us  [call(): pl.pallas_call(kernel, out_shape=outs, in_specs=[pl.BlockSpec(memory_spac...]
    ppermute x15, waiting for transfers between devices: 6.41 us -> 5.55 us  [the longest x9 5.53 us: exchange(): lax.ppermute(message, axes[1], list(enumerate(table)))]
    unnamed x22 -> x18, local copies, waits for them, and re-layouts: 6.37 us -> 7.11 us
  transfers between devices with their start and end apart: 15 -> 15, of which waited for: 3 -> 6; matrix products, arithmetic and copies ran while one was open for 0% -> 0% of each run, Pallas kernels for 0% -> 5%
where the time goes in v2:
time: 41.3 us; the launch traced here: 40.9 us
  starting transfers between devices  20.7 us (50%)
  local copies, waits for them, and re-layouts  7.11 us (17%)
  Pallas kernels  6.73 us (16%)
  waiting for transfers between devices  5.55 us (13%)
  between operations  0.77 us (2%)
    ppermute x3, starting transfers between devices, exchange(): lax.ppermute(sent[-1], axes[0], far)  12.3 us
    ppermute x9, starting transfers between devices, exchange(): lax.ppermute(message, axes[1], list(enumerate(table)))  8.14 us
    unnamed x18, local copies, waits for them, and re-layouts  7.11 us
    pallas_call x7, Pallas kernels, call(): pl.pallas_call(kernel, out_shape=outs, in_specs=[pl.BlockSpec(memory_spac...  6.73 us
    ppermute x9, waiting for transfers between devices, exchange(): lax.ppermute(message, axes[1], list(enumerate(table)))  5.53 us
  transfers between devices with their start and end apart: 15, of which 6 were waited for; matrix products, arithmetic and copies ran while one was open for 0% of the time, Pallas kernels for 5%

profile of v2, /device:TPU:1, one launch (start us, length us, event | category | flops | bytes accessed | tf_op | source)
XLA Modules:
  0.0 40.9 jit_solution(3244340398747915046)
XLA Ops:
  0.6 1.0 %copy-done = bf16[1536,128]{1,0:T(8,128)(2,1)S(1)} copy-done((bf16[1536,128]{1,0:T(8,128)(2,1)S(1)}, bf16[1536,128]{1,0:T(8,128)(2,1)}, u32[]{:S(2)}) %copy-start) | copy-done | bytes 393240
  1.6 1.0 %copy-done.1 = f32[4,24,768]{2,1,0:T(8,128)S(1)} copy-done((f32[4,24,768]{2,1,0:T(8,128)S(1)}, f32[4,24,768]{2,1,0:T(8,128)}, u32[]{:S(2)}) %copy-start.1) | copy-done | bytes 294936
  2.6 0.9 %copy-done.2 = bf16[768,128]{1,0:T(8,128)(2,1)S(1)} copy-done((bf16[768,128]{1,0:T(8,128)(2,1)S(1)}, bf16[768,128]{1,0:T(8,128)(2,1)}, u32[]{:S(2)}) %copy-start.2) | copy-done | bytes 196632
  3.5 0.8 %copy-done.3 = f32[4,24,64]{2,1,0:T(8,128)S(1)} copy-done((f32[4,24,64]{2,1,0:T(8,128)S(1)}, f32[4,24,64]{2,1,0:T(8,128)}, u32[]{:S(2)}) %copy-start.3) | copy-done | bytes 24600
  4.3 0.7 %copy-done.4 = f32[8,768]{1,0:T(8,128)S(1)} copy-done((f32[8,768]{1,0:T(8,128)S(1)}, f32[8,768]{1,0:T(8,128)}, u32[]{:S(2)}) %copy-start.4) | copy-done | bytes 24600
  5.1 0.7 %copy-done.5 = f32[4,24]{1,0:T(4,128)S(1)} copy-done((f32[4,24]{1,0:T(4,128)S(1)}, f32[4,24]{1,0:T(4,128)}, u32[]{:S(2)}) %copy-start.5) | copy-done | bytes 408
  5.7 0.7 %copy-done.6 = s32[4,24]{1,0:T(4,128)S(1)} copy-done((s32[4,24]{1,0:T(4,128)S(1)}, s32[4,24]{1,0:T(4,128)}, u32[]{:S(2)}) %copy-start.6) | copy-done | bytes 408
  6.4 0.7 %copy-done.7 = s32[4,24]{1,0:T(4,128)S(1)} copy-done((s32[4,24]{1,0:T(4,128)S(1)}, s32[4,24]{1,0:T(4,128)}, u32[]{:S(2)}) %copy-start.7) | copy-done | bytes 408
  7.1 0.7 %copy-done.8 = f32[32]{0:T(128)S(1)} copy-done((f32[32]{0:T(128)S(1)}, f32[32]{0:T(128)}, u32[]{:S(2)}) %copy-start.8) | copy-done | bytes 152
  7.8 1.6 %shard_map.104 = (f32[4,24,768]{2,1,0:T(8,128)S(1)}, f32[96,128]{1,0:T(8,128)S(1)}, bf16[96,96]{1,0:T(8,128)(2,1)S(1)}, bf16[96,96]{1,0:T(8,128)(2,1)S(1)}, f32[...) custom-call(f32[4,24,768]{2,1,0:T(8,128)S(1)} %copy-done.1, ...), custom_call_target="tpu_custom_call" | custom-call | tf_op jit(solution)/shard_map/pallas_call | solution.py:404
  9.5 4.6 %collective-permute-start.3 = (f32[24,512]{1,0:T(8,128)S(1)}, f32[24,512]{1,0:T(8,128)S(1)}, u32[]{:S(2)}, u32[]{:S(2)}) collective-permute-start(f32[24,512]{1,0:T(8,128)S(1)} %get-tuple-element.47), channel_id=1, source_target_pairs={{1,2},{2,1},{3,4},{4,3},{5,6},{6,5},{9,10},{10,9},{11,12},{12,11},... | collective-permute-start | bytes 147464 | tf_op jit(solution)/shard_map/ppermute | solution.py:420
  14.1 1.3 %collective-permute-start = (f32[56,128]{1,0:T(8,128)S(1)}, f32[56,128]{1,0:T(8,128)S(1)}, u32[]{:S(2)}, u32[]{:S(2)}) collective-permute-start(f32[56,128]{1,0:T(8,128)S(1)} %get-tuple-element.44), channel_id=1, source_target_pairs={{0,8},{8,0},{16,24},{24,16},{1,9},{9,1},{17,25},{25,17},{2,10},{10... | collective-permute-start | bytes 86024 | tf_op jit(solution)/shard_map/ppermute | solution.py:417
  15.4 1.2 %collective-permute-start.1 = (f32[56,128]{1,0:T(8,128)S(1)}, f32[56,128]{1,0:T(8,128)S(1)}, u32[]{:S(2)}, u32[]{:S(2)}) collective-permute-start(f32[56,128]{1,0:T(8,128)S(1)} %get-tuple-element.45), channel_id=1, source_target_pairs={{0,24},{8,16},{16,8},{24,0},{1,25},{9,17},{17,9},{25,1},{2,26},{10... | collective-permute-start | bytes 86024 | tf_op jit(solution)/shard_map/ppermute | solution.py:417
  16.8 0.4 collective-permute-done.refs_4_.refs_10_
  17.2 1.8 %collective-permute-done.1.refs_5_.refs_12_ = f32[56,128]{1,0:T(8,128)S(1)} collective-permute-done((f32[56,128]{1,0:T(8,128)S(1)}, f32[56,128]{1,0:T(8,128)S(1)}, u32[]{:S(2)}, u32[]{:S(2)}) %collective-permute-start.1) | collective-permute-done | bytes 28704 | tf_op jit(solution)/shard_map/ppermute | solution.py:417
  19.0 0.7 %shard_map.105 = (f32[4,24,768]{2,1,0:T(8,128)S(1)}, f32[96,128]{1,0:T(8,128)S(1)}) custom-call(f32[4,24,768]{2,1,0:T(8,128)S(1)} %get-tuple-element.40.refs_0_, f32[96,128]{1,0:T(8,128)S(1)} %get-tuple-element.41.refs_1_.refs_2_, f32[96,128]{1,0:T(8,128)S(1)} %get-tuple-element.42.refs_2_, f32[8,768]{1,0:T(8,128)S(1)} %get-tuple-element.43.refs_3_, ...), custom_call_target="tpu_custom_call" | custom-call | tf_op jit(solution)/shard_map/pallas_call | solution.py:404
  19.6 1.0 %shard_map.106 = (f32[4,24,768]{2,1,0:T(8,128)S(1)}, f32[96,128]{1,0:T(8,128)S(1)}, f32[96,128]{1,0:T(8,128)S(1)}, f32[56,128]{1,0:T(8,128)S(1)}, f32[24,128]{1,...) custom-call(f32[4,24,768]{2,1,0:T(8,128)S(1)} %get-tuple-element.48.refs_0_, ...), custom_call_target="tpu_custom_call" | custom-call | tf_op jit(solution)/shard_map/pallas_call | solution.py:404
  20.8 4.1 %collective-permute-start.8 = (f32[24,512]{1,0:T(8,128)S(1)}, f32[24,512]{1,0:T(8,128)S(1)}, u32[]{:S(2)}, u32[]{:S(2)}) collective-permute-start(f32[24,512]{1,0:T(8,128)S(1)} %get-tuple-element.63), channel_id=1, source_target_pairs={{1,2},{2,1},{3,4},{4,3},{5,6},{6,5},{9,10},{10,9},{11,12},{12,11},... | collective-permute-start | bytes 147464 | tf_op jit(solution)/shard_map/ppermute | solution.py:420
  24.9 0.8 %collective-permute-start.5 = (f32[56,128]{1,0:T(8,128)S(1)}, f32[56,128]{1,0:T(8,128)S(1)}, u32[]{:S(2)}, u32[]{:S(2)}) collective-permute-start(f32[56,128]{1,0:T(8,128)S(1)} %get-tuple-element.60), channel_id=1, source_target_pairs={{0,8},{8,0},{16,24},{24,16},{1,9},{9,1},{17,25},{25,17},{2,10},{10... | collective-permute-start | bytes 86024 | tf_op jit(solution)/shard_map/ppermute | solution.py:417
  25.6 1.7 %collective-permute-start.6 = (f32[56,128]{1,0:T(8,128)S(1)}, f32[56,128]{1,0:T(8,128)S(1)}, u32[]{:S(2)}, u32[]{:S(2)}) collective-permute-start(f32[56,128]{1,0:T(8,128)S(1)} %get-tuple-element.61), channel_id=1, source_target_pairs={{0,24},{8,16},{16,8},{24,0},{1,25},{9,17},{17,9},{25,1},{2,26},{10... | collective-permute-start | bytes 86024 | tf_op jit(solution)/shard_map/ppermute | solution.py:417
  27.3 0.3 collective-permute-start.9
  27.7 1.6 %collective-permute-done.6.refs_5_.refs_12_ = f32[56,128]{1,0:T(8,128)S(1)} collective-permute-done((f32[56,128]{1,0:T(8,128)S(1)}, f32[56,128]{1,0:T(8,128)S(1)}, u32[]{:S(2)}, u32[]{:S(2)}) %collective-permute-start.6) | collective-permute-done | bytes 28704 | tf_op jit(solution)/shard_map/ppermute | solution.py:417
  29.3 0.6 %shard_map.107 = (f32[4,24,768]{2,1,0:T(8,128)S(1)}, f32[96,128]{1,0:T(8,128)S(1)}) custom-call(f32[4,24,768]{2,1,0:T(8,128)S(1)} %get-tuple-element.58.refs_0_, f32[96,128]{1,0:T(8,128)S(1)} %get-tuple-element.59.refs_1_.refs_2_, f32[96,128]{1,0:T(8,128)S(1)} %get-tuple-element.42.refs_2_, f32[8,768]{1,0:T(8,128)S(1)} %get-tuple-element.43.refs_3_, ...), custom_call_target="tpu_custom_call" | custom-call | tf_op jit(solution)/shard_map/pallas_call | solution.py:404
  29.9 1.0 %shard_map.108 = (f32[4,24,768]{2,1,0:T(8,128)S(1)}, f32[96,128]{1,0:T(8,128)S(1)}, f32[96,128]{1,0:T(8,128)S(1)}, f32[56,128]{1,0:T(8,128)S(1)}, f32[24,128]{1,...) custom-call(f32[4,24,768]{2,1,0:T(8,128)S(1)} %get-tuple-element.64.refs_0_, ...), custom_call_target="tpu_custom_call" | custom-call | tf_op jit(solution)/shard_map/pallas_call | solution.py:404
  31.0 3.7 %collective-permute-start.13 = (f32[24,512]{1,0:T(8,128)S(1)}, f32[24,512]{1,0:T(8,128)S(1)}, u32[]{:S(2)}, u32[]{:S(2)}) collective-permute-start(f32[24,512]{1,0:T(8,128)S(1)} %get-tuple-element.73), channel_id=1, source_target_pairs={{1,2},{2,1},{3,4},{4,3},{5,6},{6,5},{9,10},{10,9},{11,12},{12,11},... | collective-permute-start | bytes 147464 | tf_op jit(solution)/shard_map/ppermute | solution.py:420
  34.7 0.8 %collective-permute-start.10 = (f32[56,128]{1,0:T(8,128)S(1)}, f32[56,128]{1,0:T(8,128)S(1)}, u32[]{:S(2)}, u32[]{:S(2)}) collective-permute-start(f32[56,128]{1,0:T(8,128)S(1)} %get-tuple-element.70), channel_id=1, source_target_pairs={{0,8},{8,0},{16,24},{24,16},{1,9},{9,1},{17,25},{25,17},{2,10},{10... | collective-permute-start | bytes 86024 | tf_op jit(solution)/shard_map/ppermute | solution.py:417
  35.5 1.2 %collective-permute-start.11 = (f32[56,128]{1,0:T(8,128)S(1)}, f32[56,128]{1,0:T(8,128)S(1)}, u32[]{:S(2)}, u32[]{:S(2)}) collective-permute-start(f32[56,128]{1,0:T(8,128)S(1)} %get-tuple-element.71), channel_id=1, source_target_pairs={{0,24},{8,16},{16,8},{24,0},{1,25},{9,17},{17,9},{25,1},{2,26},{10... | collective-permute-start | bytes 86024 | tf_op jit(solution)/shard_map/ppermute | solution.py:417
  36.7 0.7 %collective-permute-start.14 = (f32[24,128]{1,0:T(8,128)S(1)}, f32[24,128]{1,0:T(8,128)S(1)}, u32[]{:S(2)}, u32[]{:S(2)}) collective-permute-start(f32[24,128]{1,0:T(8,128)S(1)} %get-tuple-element.77), channel_id=1, source_target_pairs={{0,16},{8,24},{16,0},{24,8},{1,17},{9,25},{17,1},{25,9},{2,18},{10... | collective-permute-start | bytes 36872 | tf_op jit(solution)/shard_map/ppermute | solution.py:417
  37.4 0.6 %collective-permute-done.10.refs_4_.refs_10_ = f32[56,128]{1,0:T(8,128)S(1)} collective-permute-done((f32[56,128]{1,0:T(8,128)S(1)}, f32[56,128]{1,0:T(8,128)S(1)}, u32[]{:S(2)}, u32[]{:S(2)}) %collective-permute-start.10) | collective-permute-done | bytes 28704 | tf_op jit(solution)/shard_map/ppermute | solution.py:417
  38.0 1.1 %collective-permute-done.11.refs_5_.refs_12_ = f32[56,128]{1,0:T(8,128)S(1)} collective-permute-done((f32[56,128]{1,0:T(8,128)S(1)}, f32[56,128]{1,0:T(8,128)S(1)}, u32[]{:S(2)}, u32[]{:S(2)}) %collective-permute-start.11) | collective-permute-done | bytes 28704 | tf_op jit(solution)/shard_map/ppermute | solution.py:417
  39.1 0.7 %shard_map.109 = (f32[4,24,768]{2,1,0:T(8,128)S(1)}, f32[96,128]{1,0:T(8,128)S(1)}) custom-call(f32[4,24,768]{2,1,0:T(8,128)S(1)} %get-tuple-element.68.refs_0_, f32[96,128]{1,0:T(8,128)S(1)} %get-tuple-element.69.refs_1_.refs_2_, f32[96,128]{1,0:T(8,128)S(1)} %get-tuple-element.42.refs_2_, f32[8,768]{1,0:T(8,128)S(1)} %get-tuple-element.43.refs_3_, ...), custom_call_target="tpu_custom_call" | custom-call | tf_op jit(solution)/shard_map/pallas_call | solution.py:404
  39.8 1.1 %shard_map.110 = (f32[4,24,768]{2,1,0:T(8,128)}, f32[4,24,64]{2,1,0:T(8,128)}) custom-call(f32[4,24,768]{2,1,0:T(8,128)S(1)} %get-tuple-element.74.refs_0_, f32[96,128]{1,0:T(8,128)S(1)} %get-tuple-element.75.refs_1_, f32[96,128]{1,0:T(8,128)S(1)} %get-tuple-element.69.refs_1_.refs_2_, f32[96,128]{1,0:T(8,128)S(1)} %get-tuple-element.76.refs_3_, ...), custom_call_target="tpu_custom_call" | custom-call | tf_op jit(solution)/shard_map/pallas_call | solution.py:404
  (23 shorter events, 0.6 us)
Async XLA Ops:
  0.6 1.0 %copy-start = (bf16[1536,128]{1,0:T(8,128)(2,1)S(1)}, bf16[1536,128]{1,0:T(8,128)(2,1)}, u32[]{:S(2)}) copy-start(bf16[1536,128]{1,0:T(8,128)(2,1)} %constant.8.clone.refs_8_) | copy-start | bytes 1179652
  1.6 1.0 %copy-start.1 = (f32[4,24,768]{2,1,0:T(8,128)S(1)}, f32[4,24,768]{2,1,0:T(8,128)}, u32[]{:S(2)}) copy-start(f32[4,24,768]{2,1,0:T(8,128)} %refs_0_.1) | copy-start | bytes 884740
  2.6 0.9 %copy-start.2 = (bf16[768,128]{1,0:T(8,128)(2,1)S(1)}, bf16[768,128]{1,0:T(8,128)(2,1)}, u32[]{:S(2)}) copy-start(bf16[768,128]{1,0:T(8,128)(2,1)} %constant.6.clone.refs_6_) | copy-start | bytes 589828
  3.5 0.8 %copy-start.3 = (f32[4,24,64]{2,1,0:T(8,128)S(1)}, f32[4,24,64]{2,1,0:T(8,128)}, u32[]{:S(2)}) copy-start(f32[4,24,64]{2,1,0:T(8,128)} %refs_2_.1) | copy-start | bytes 73732
  4.3 0.7 %copy-start.4 = (f32[8,768]{1,0:T(8,128)S(1)}, f32[8,768]{1,0:T(8,128)}, u32[]{:S(2)}) copy-start(f32[8,768]{1,0:T(8,128)} %constant.7.clone.refs_7_) | copy-start | bytes 73732
  5.1 0.7 %copy-start.5 = (f32[4,24]{1,0:T(4,128)S(1)}, f32[4,24]{1,0:T(4,128)}, u32[]{:S(2)}) copy-start(f32[4,24]{1,0:T(4,128)} %refs_1_.1) | copy-start | bytes 1156
  5.7 0.7 %copy-start.6 = (s32[4,24]{1,0:T(4,128)S(1)}, s32[4,24]{1,0:T(4,128)}, u32[]{:S(2)}) copy-start(s32[4,24]{1,0:T(4,128)} %refs_4_.1) | copy-start | bytes 1156
  6.4 0.7 %copy-start.7 = (s32[4,24]{1,0:T(4,128)S(1)}, s32[4,24]{1,0:T(4,128)}, u32[]{:S(2)}) copy-start(s32[4,24]{1,0:T(4,128)} %refs_5_.1) | copy-start | bytes 1156
  7.1 0.7 %copy-start.8 = (f32[32]{0:T(128)S(1)}, f32[32]{0:T(128)}, u32[]{:S(2)}) copy-start(f32[32]{0:T(128)} %refs_3_.1) | copy-start | bytes 388
  9.4 9.6 %collective-permute-start.2 = (f32[24,512]{1,0:T(8,128)S(1)}, f32[24,512]{1,0:T(8,128)S(1)}, u32[]{:S(2)}, u32[]{:S(2)}) collective-permute-start(f32[24,512]{1,0:T(8,128)S(1)} %get-tuple-element.46), channel_id=1, source_target_pairs={{0,1},{1,0},{2,3},{3,2},{4,5},{5,4},{6,7},{7,6},{8,9},{9,8},{10,11... | collective-permute-start | bytes 147464 | tf_op jit(solution)/shard_map/ppermute | solution.py:420
  9.5 9.5 %collective-permute-start.3 = (f32[24,512]{1,0:T(8,128)S(1)}, f32[24,512]{1,0:T(8,128)S(1)}, u32[]{:S(2)}, u32[]{:S(2)}) collective-permute-start(f32[24,512]{1,0:T(8,128)S(1)} %get-tuple-element.47), channel_id=1, source_target_pairs={{1,2},{2,1},{3,4},{4,3},{5,6},{6,5},{9,10},{10,9},{11,12},{12,11},... | collective-permute-start | bytes 147464 | tf_op jit(solution)/shard_map/ppermute | solution.py:420
  14.1 3.1 %collective-permute-start = (f32[56,128]{1,0:T(8,128)S(1)}, f32[56,128]{1,0:T(8,128)S(1)}, u32[]{:S(2)}, u32[]{:S(2)}) collective-permute-start(f32[56,128]{1,0:T(8,128)S(1)} %get-tuple-element.44), channel_id=1, source_target_pairs={{0,8},{8,0},{16,24},{24,16},{1,9},{9,1},{17,25},{25,17},{2,10},{10... | collective-permute-start | bytes 86024 | tf_op jit(solution)/shard_map/ppermute | solution.py:417
  15.4 3.6 %collective-permute-start.1 = (f32[56,128]{1,0:T(8,128)S(1)}, f32[56,128]{1,0:T(8,128)S(1)}, u32[]{:S(2)}, u32[]{:S(2)}) collective-permute-start(f32[56,128]{1,0:T(8,128)S(1)} %get-tuple-element.45), channel_id=1, source_target_pairs={{0,24},{8,16},{16,8},{24,0},{1,25},{9,17},{17,9},{25,1},{2,26},{10... | collective-permute-start | bytes 86024 | tf_op jit(solution)/shard_map/ppermute | solution.py:417
  16.6 3.1 %collective-permute-start.4 = (f32[24,128]{1,0:T(8,128)S(1)}, f32[24,128]{1,0:T(8,128)S(1)}, u32[]{:S(2)}, u32[]{:S(2)}) collective-permute-start(f32[24,128]{1,0:T(8,128)S(1)} %get-tuple-element.57), channel_id=1, source_target_pairs={{0,16},{8,24},{16,0},{24,8},{1,17},{9,25},{17,1},{25,9},{2,18},{10... | collective-permute-start | bytes 36872 | tf_op jit(solution)/shard_map/ppermute | solution.py:417
  20.7 8.6 %collective-permute-start.7 = (f32[24,512]{1,0:T(8,128)S(1)}, f32[24,512]{1,0:T(8,128)S(1)}, u32[]{:S(2)}, u32[]{:S(2)}) collective-permute-start(f32[24,512]{1,0:T(8,128)S(1)} %get-tuple-element.62), channel_id=1, source_target_pairs={{0,1},{1,0},{2,3},{3,2},{4,5},{5,4},{6,7},{7,6},{8,9},{9,8},{10,11... | collective-permute-start | bytes 147464 | tf_op jit(solution)/shard_map/ppermute | solution.py:420
  20.8 8.5 %collective-permute-start.8 = (f32[24,512]{1,0:T(8,128)S(1)}, f32[24,512]{1,0:T(8,128)S(1)}, u32[]{:S(2)}, u32[]{:S(2)}) collective-permute-start(f32[24,512]{1,0:T(8,128)S(1)} %get-tuple-element.63), channel_id=1, source_target_pairs={{1,2},{2,1},{3,4},{4,3},{5,6},{6,5},{9,10},{10,9},{11,12},{12,11},... | collective-permute-start | bytes 147464 | tf_op jit(solution)/shard_map/ppermute | solution.py:420
  24.9 2.8 %collective-permute-start.5 = (f32[56,128]{1,0:T(8,128)S(1)}, f32[56,128]{1,0:T(8,128)S(1)}, u32[]{:S(2)}, u32[]{:S(2)}) collective-permute-start(f32[56,128]{1,0:T(8,128)S(1)} %get-tuple-element.60), channel_id=1, source_target_pairs={{0,8},{8,0},{16,24},{24,16},{1,9},{9,1},{17,25},{25,17},{2,10},{10... | collective-permute-start | bytes 86024 | tf_op jit(solution)/shard_map/ppermute | solution.py:417
  25.6 3.6 %collective-permute-start.6 = (f32[56,128]{1,0:T(8,128)S(1)}, f32[56,128]{1,0:T(8,128)S(1)}, u32[]{:S(2)}, u32[]{:S(2)}) collective-permute-start(f32[56,128]{1,0:T(8,128)S(1)} %get-tuple-element.61), channel_id=1, source_target_pairs={{0,24},{8,16},{16,8},{24,0},{1,25},{9,17},{17,9},{25,1},{2,26},{10... | collective-permute-start | bytes 86024 | tf_op jit(solution)/shard_map/ppermute | solution.py:417
  27.3 2.6 %collective-permute-start.9 = (f32[24,128]{1,0:T(8,128)S(1)}, f32[24,128]{1,0:T(8,128)S(1)}, u32[]{:S(2)}, u32[]{:S(2)}) collective-permute-start(f32[24,128]{1,0:T(8,128)S(1)} %get-tuple-element.67), channel_id=1, source_target_pairs={{0,16},{8,24},{16,0},{24,8},{1,17},{9,25},{17,1},{25,9},{2,18},{10... | collective-permute-start | bytes 36872 | tf_op jit(solution)/shard_map/ppermute | solution.py:417
  31.0 8.1 %collective-permute-start.12 = (f32[24,512]{1,0:T(8,128)S(1)}, f32[24,512]{1,0:T(8,128)S(1)}, u32[]{:S(2)}, u32[]{:S(2)}) collective-permute-start(f32[24,512]{1,0:T(8,128)S(1)} %get-tuple-element.72), channel_id=1, source_target_pairs={{0,1},{1,0},{2,3},{3,2},{4,5},{5,4},{6,7},{7,6},{8,9},{9,8},{10,11... | collective-permute-start | bytes 147464 | tf_op jit(solution)/shard_map/ppermute | solution.py:420
  31.0 8.0 %collective-permute-start.13 = (f32[24,512]{1,0:T(8,128)S(1)}, f32[24,512]{1,0:T(8,128)S(1)}, u32[]{:S(2)}, u32[]{:S(2)}) collective-permute-start(f32[24,512]{1,0:T(8,128)S(1)} %get-tuple-element.73), channel_id=1, source_target_pairs={{1,2},{2,1},{3,4},{4,3},{5,6},{6,5},{9,10},{10,9},{11,12},{12,11},... | collective-permute-start | bytes 147464 | tf_op jit(solution)/shard_map/ppermute | solution.py:420
  34.7 3.3 %collective-permute-start.10 = (f32[56,128]{1,0:T(8,128)S(1)}, f32[56,128]{1,0:T(8,128)S(1)}, u32[]{:S(2)}, u32[]{:S(2)}) collective-permute-start(f32[56,128]{1,0:T(8,128)S(1)} %get-tuple-element.70), channel_id=1, source_target_pairs={{0,8},{8,0},{16,24},{24,16},{1,9},{9,1},{17,25},{25,17},{2,10},{10... | collective-permute-start | bytes 86024 | tf_op jit(solution)/shard_map/ppermute | solution.py:417
  35.5 3.6 %collective-permute-start.11 = (f32[56,128]{1,0:T(8,128)S(1)}, f32[56,128]{1,0:T(8,128)S(1)}, u32[]{:S(2)}, u32[]{:S(2)}) collective-permute-start(f32[56,128]{1,0:T(8,128)S(1)} %get-tuple-element.71), channel_id=1, source_target_pairs={{0,24},{8,16},{16,8},{24,0},{1,25},{9,17},{17,9},{25,1},{2,26},{10... | collective-permute-start | bytes 86024 | tf_op jit(solution)/shard_map/ppermute | solution.py:417
  36.7 3.1 %collective-permute-start.14 = (f32[24,128]{1,0:T(8,128)S(1)}, f32[24,128]{1,0:T(8,128)S(1)}, u32[]{:S(2)}, u32[]{:S(2)}) collective-permute-start(f32[24,128]{1,0:T(8,128)S(1)} %get-tuple-element.77), channel_id=1, source_target_pairs={{0,16},{8,24},{16,0},{24,8},{1,17},{9,25},{17,1},{25,9},{2,18},{10... | collective-permute-start | bytes 36872 | tf_op jit(solution)/shard_map/ppermute | solution.py:417

commit v3 on v2

--- a/solution.py
+++ b/solution.py
@@ -433,13 +433,18 @@
             pltpu.VMEM(ocean_target.shape, jnp.int32),
             pltpu.SemaphoreType.DMA((9,)),
         ],
-        spectra,
-        turning,
-        currents,
-        drag_rates,
-        land_mask,
-        ocean_target,
-        *tables,
+        *[
+            pltpu.with_memory_space_constraint(array, pltpu.HBM)
+            for array in (
+                spectra,
+                turning,
+                currents,
+                drag_rates,
+                land_mask,
+                ocean_target,
+                *tables,
+            )
+        ],
         space_in=pltpu.HBM,
     )
     for step in range(STEPS):

time: 41.3 us -> 34 us (0.82)
  local copies, waits for them, and re-layouts: 7.11 us -> 0 us
    unnamed x18 -> x0, local copies, waits for them, and re-layouts: 7.11 us -> none
  transfers between devices with their start and end apart: 15 -> 15, of which waited for: 6 -> 6; matrix products, arithmetic and copies ran while one was open for 0% -> 0% of each run, Pallas kernels for 5% -> 6%
where the time goes in v3:
time: 34 us; the launch traced here: 33.8 us
  starting transfers between devices  20.7 us (61%)
  Pallas kernels  6.81 us (20%)
  waiting for transfers between devices  5.55 us (16%)
  between operations  0.75 us (2%)
    ppermute x3, starting transfers between devices, exchange(): lax.ppermute(sent[-1], axes[0], far)  12.3 us
    ppermute x9, starting transfers between devices, exchange(): lax.ppermute(message, axes[1], list(enumerate(table)))  8.14 us
    pallas_call x7, Pallas kernels, call(): pl.pallas_call(kernel, out_shape=outs, in_specs=[pl.BlockSpec(memory_spac...  6.81 us
    ppermute x9, waiting for transfers between devices, exchange(): lax.ppermute(message, axes[1], list(enumerate(table)))  5.54 us
  transfers between devices with their start and end apart: 15, of which 6 were waited for; matrix products, arithmetic and copies ran while one was open for 0% of the time, Pallas kernels for 6%

profile of v3, /device:TPU:1, one launch (start us, length us, event | category | flops | bytes accessed | tf_op | source)
XLA Modules:
  0.0 33.8 jit_solution(9146824735349705818)
XLA Ops:
  0.6 1.7 %shard_map.104 = (f32[4,24,768]{2,1,0:T(8,128)S(1)}, f32[96,128]{1,0:T(8,128)S(1)}, bf16[96,96]{1,0:T(8,128)(2,1)S(1)}, bf16[96,96]{1,0:T(8,128)(2,1)S(1)}, f32[...) custom-call(f32[4,24,768]{2,1,0:T(8,128)} %refs_0_.1, ...), custom_call_target="tpu_custom_call" | custom-call | tf_op jit(solution)/shard_map/pallas_call | solution.py:404
  2.3 0.1 collective-permute-start.2
  2.5 4.6 %collective-permute-start.3 = (f32[24,512]{1,0:T(8,128)S(1)}, f32[24,512]{1,0:T(8,128)S(1)}, u32[]{:S(2)}, u32[]{:S(2)}) collective-permute-start(f32[24,512]{1,0:T(8,128)S(1)} %get-tuple-element.47), channel_id=1, source_target_pairs={{1,2},{2,1},{3,4},{4,3},{5,6},{6,5},{9,10},{10,9},{11,12},{12,11},... | collective-permute-start | bytes 147464 | tf_op jit(solution)/shard_map/ppermute | solution.py:420
  7.0 1.3 %collective-permute-start = (f32[56,128]{1,0:T(8,128)S(1)}, f32[56,128]{1,0:T(8,128)S(1)}, u32[]{:S(2)}, u32[]{:S(2)}) collective-permute-start(f32[56,128]{1,0:T(8,128)S(1)} %get-tuple-element.44), channel_id=1, source_target_pairs={{0,8},{8,0},{16,24},{24,16},{1,9},{9,1},{17,25},{25,17},{2,10},{10... | collective-permute-start | bytes 86024 | tf_op jit(solution)/shard_map/ppermute | solution.py:417
  8.3 1.2 %collective-permute-start.1 = (f32[56,128]{1,0:T(8,128)S(1)}, f32[56,128]{1,0:T(8,128)S(1)}, u32[]{:S(2)}, u32[]{:S(2)}) collective-permute-start(f32[56,128]{1,0:T(8,128)S(1)} %get-tuple-element.45), channel_id=1, source_target_pairs={{0,24},{8,16},{16,8},{24,0},{1,25},{9,17},{17,9},{25,1},{2,26},{10... | collective-permute-start | bytes 86024 | tf_op jit(solution)/shard_map/ppermute | solution.py:417
  9.5 0.2 collective-permute-start.4
  9.7 0.4 %collective-permute-done.refs_4_.refs_10_ = f32[56,128]{1,0:T(8,128)S(1)} collective-permute-done((f32[56,128]{1,0:T(8,128)S(1)}, f32[56,128]{1,0:T(8,128)S(1)}, u32[]{:S(2)}, u32[]{:S(2)}) %collective-permute-start) | collective-permute-done | bytes 28704 | tf_op jit(solution)/shard_map/ppermute | solution.py:417
  10.1 1.8 %collective-permute-done.1.refs_5_.refs_12_ = f32[56,128]{1,0:T(8,128)S(1)} collective-permute-done((f32[56,128]{1,0:T(8,128)S(1)}, f32[56,128]{1,0:T(8,128)S(1)}, u32[]{:S(2)}, u32[]{:S(2)}) %collective-permute-start.1) | collective-permute-done | bytes 28704 | tf_op jit(solution)/shard_map/ppermute | solution.py:417
  11.9 0.0 collective-permute-done.2.refs_6_
  11.9 0.0 collective-permute-done.3.refs_7_
  11.9 0.6 %shard_map.105 = (f32[4,24,768]{2,1,0:T(8,128)S(1)}, f32[96,128]{1,0:T(8,128)S(1)}) custom-call(f32[4,24,768]{2,1,0:T(8,128)S(1)} %get-tuple-element.40.refs_0_, f32[96,128]{1,0:T(8,128)S(1)} %get-tuple-element.41.refs_1_.refs_2_, f32[96,128]{1,0:T(8,128)S(1)} %get-tuple-element.42.refs_2_, f32[8,768]{1,0:T(8,128)S(1)} %get-tuple-element.43.refs_3_, ...), custom_call_target="tpu_custom_call" | custom-call | tf_op jit(solution)/shard_map/pallas_call | solution.py:404
  12.6 0.0 collective-permute-done.4.refs_11_
  12.6 1.0 %shard_map.106 = (f32[4,24,768]{2,1,0:T(8,128)S(1)}, f32[96,128]{1,0:T(8,128)S(1)}, f32[96,128]{1,0:T(8,128)S(1)}, f32[56,128]{1,0:T(8,128)S(1)}, f32[24,128]{1,...) custom-call(f32[4,24,768]{2,1,0:T(8,128)S(1)} %get-tuple-element.48.refs_0_, ...), custom_call_target="tpu_custom_call" | custom-call | tf_op jit(solution)/shard_map/pallas_call | solution.py:404
  13.6 0.1 collective-permute-start.7
  13.7 4.1 %collective-permute-start.8 = (f32[24,512]{1,0:T(8,128)S(1)}, f32[24,512]{1,0:T(8,128)S(1)}, u32[]{:S(2)}, u32[]{:S(2)}) collective-permute-start(f32[24,512]{1,0:T(8,128)S(1)} %get-tuple-element.63), channel_id=1, source_target_pairs={{1,2},{2,1},{3,4},{4,3},{5,6},{6,5},{9,10},{10,9},{11,12},{12,11},... | collective-permute-start | bytes 147464 | tf_op jit(solution)/shard_map/ppermute | solution.py:420
  17.8 0.8 %collective-permute-start.5 = (f32[56,128]{1,0:T(8,128)S(1)}, f32[56,128]{1,0:T(8,128)S(1)}, u32[]{:S(2)}, u32[]{:S(2)}) collective-permute-start(f32[56,128]{1,0:T(8,128)S(1)} %get-tuple-element.60), channel_id=1, source_target_pairs={{0,8},{8,0},{16,24},{24,16},{1,9},{9,1},{17,25},{25,17},{2,10},{10... | collective-permute-start | bytes 86024 | tf_op jit(solution)/shard_map/ppermute | solution.py:417
  18.6 1.7 %collective-permute-start.6 = (f32[56,128]{1,0:T(8,128)S(1)}, f32[56,128]{1,0:T(8,128)S(1)}, u32[]{:S(2)}, u32[]{:S(2)}) collective-permute-start(f32[56,128]{1,0:T(8,128)S(1)} %get-tuple-element.61), channel_id=1, source_target_pairs={{0,24},{8,16},{16,8},{24,0},{1,25},{9,17},{17,9},{25,1},{2,26},{10... | collective-permute-start | bytes 86024 | tf_op jit(solution)/shard_map/ppermute | solution.py:417
  20.3 0.3 collective-permute-start.9
  20.5 0.1 collective-permute-done.5.refs_4_.refs_10_
  20.6 1.6 %collective-permute-done.6.refs_5_.refs_12_ = f32[56,128]{1,0:T(8,128)S(1)} collective-permute-done((f32[56,128]{1,0:T(8,128)S(1)}, f32[56,128]{1,0:T(8,128)S(1)}, u32[]{:S(2)}, u32[]{:S(2)}) %collective-permute-start.6) | collective-permute-done | bytes 28704 | tf_op jit(solution)/shard_map/ppermute | solution.py:417
  22.2 0.0 collective-permute-done.7.refs_6_
  22.2 0.7 %shard_map.107 = (f32[4,24,768]{2,1,0:T(8,128)S(1)}, f32[96,128]{1,0:T(8,128)S(1)}) custom-call(f32[4,24,768]{2,1,0:T(8,128)S(1)} %get-tuple-element.58.refs_0_, f32[96,128]{1,0:T(8,128)S(1)} %get-tuple-element.59.refs_1_.refs_2_, f32[96,128]{1,0:T(8,128)S(1)} %get-tuple-element.42.refs_2_, f32[8,768]{1,0:T(8,128)S(1)} %get-tuple-element.43.refs_3_, ...), custom_call_target="tpu_custom_call" | custom-call | tf_op jit(solution)/shard_map/pallas_call | solution.py:404
  22.9 1.0 %shard_map.108 = (f32[4,24,768]{2,1,0:T(8,128)S(1)}, f32[96,128]{1,0:T(8,128)S(1)}, f32[96,128]{1,0:T(8,128)S(1)}, f32[56,128]{1,0:T(8,128)S(1)}, f32[24,128]{1,...) custom-call(f32[4,24,768]{2,1,0:T(8,128)S(1)} %get-tuple-element.64.refs_0_, ...), custom_call_target="tpu_custom_call" | custom-call | tf_op jit(solution)/shard_map/pallas_call | solution.py:404
  23.9 0.1 collective-permute-start.12
  24.0 3.6 %collective-permute-start.13 = (f32[24,512]{1,0:T(8,128)S(1)}, f32[24,512]{1,0:T(8,128)S(1)}, u32[]{:S(2)}, u32[]{:S(2)}) collective-permute-start(f32[24,512]{1,0:T(8,128)S(1)} %get-tuple-element.73), channel_id=1, source_target_pairs={{1,2},{2,1},{3,4},{4,3},{5,6},{6,5},{9,10},{10,9},{11,12},{12,11},... | collective-permute-start | bytes 147464 | tf_op jit(solution)/shard_map/ppermute | solution.py:420
  27.6 0.8 %collective-permute-start.10 = (f32[56,128]{1,0:T(8,128)S(1)}, f32[56,128]{1,0:T(8,128)S(1)}, u32[]{:S(2)}, u32[]{:S(2)}) collective-permute-start(f32[56,128]{1,0:T(8,128)S(1)} %get-tuple-element.70), channel_id=1, source_target_pairs={{0,8},{8,0},{16,24},{24,16},{1,9},{9,1},{17,25},{25,17},{2,10},{10... | collective-permute-start | bytes 86024 | tf_op jit(solution)/shard_map/ppermute | solution.py:417
  28.4 1.2 %collective-permute-start.11 = (f32[56,128]{1,0:T(8,128)S(1)}, f32[56,128]{1,0:T(8,128)S(1)}, u32[]{:S(2)}, u32[]{:S(2)}) collective-permute-start(f32[56,128]{1,0:T(8,128)S(1)} %get-tuple-element.71), channel_id=1, source_target_pairs={{0,24},{8,16},{16,8},{24,0},{1,25},{9,17},{17,9},{25,1},{2,26},{10... | collective-permute-start | bytes 86024 | tf_op jit(solution)/shard_map/ppermute | solution.py:417
  29.6 0.7 %collective-permute-start.14 = (f32[24,128]{1,0:T(8,128)S(1)}, f32[24,128]{1,0:T(8,128)S(1)}, u32[]{:S(2)}, u32[]{:S(2)}) collective-permute-start(f32[24,128]{1,0:T(8,128)S(1)} %get-tuple-element.77), channel_id=1, source_target_pairs={{0,16},{8,24},{16,0},{24,8},{1,17},{9,25},{17,1},{25,9},{2,18},{10... | collective-permute-start | bytes 36872 | tf_op jit(solution)/shard_map/ppermute | solution.py:417
  30.4 0.6 %collective-permute-done.10.refs_4_.refs_10_ = f32[56,128]{1,0:T(8,128)S(1)} collective-permute-done((f32[56,128]{1,0:T(8,128)S(1)}, f32[56,128]{1,0:T(8,128)S(1)}, u32[]{:S(2)}, u32[]{:S(2)}) %collective-permute-start.10) | collective-permute-done | bytes 28704 | tf_op jit(solution)/shard_map/ppermute | solution.py:417
  31.0 1.1 %collective-permute-done.11.refs_5_.refs_12_ = f32[56,128]{1,0:T(8,128)S(1)} collective-permute-done((f32[56,128]{1,0:T(8,128)S(1)}, f32[56,128]{1,0:T(8,128)S(1)}, u32[]{:S(2)}, u32[]{:S(2)}) %collective-permute-start.11) | collective-permute-done | bytes 28704 | tf_op jit(solution)/shard_map/ppermute | solution.py:417
  32.0 0.7 %shard_map.109 = (f32[4,24,768]{2,1,0:T(8,128)S(1)}, f32[96,128]{1,0:T(8,128)S(1)}) custom-call(f32[4,24,768]{2,1,0:T(8,128)S(1)} %get-tuple-element.68.refs_0_, f32[96,128]{1,0:T(8,128)S(1)} %get-tuple-element.69.refs_1_.refs_2_, f32[96,128]{1,0:T(8,128)S(1)} %get-tuple-element.42.refs_2_, f32[8,768]{1,0:T(8,128)S(1)} %get-tuple-element.43.refs_3_, ...), custom_call_target="tpu_custom_call" | custom-call | tf_op jit(solution)/shard_map/pallas_call | solution.py:404
  32.7 1.1 %shard_map.110 = (f32[4,24,768]{2,1,0:T(8,128)}, f32[4,24,64]{2,1,0:T(8,128)}) custom-call(f32[4,24,768]{2,1,0:T(8,128)S(1)} %get-tuple-element.74.refs_0_, f32[96,128]{1,0:T(8,128)S(1)} %get-tuple-element.75.refs_1_, f32[96,128]{1,0:T(8,128)S(1)} %get-tuple-element.69.refs_1_.refs_2_, f32[96,128]{1,0:T(8,128)S(1)} %get-tuple-element.76.refs_3_, ...), custom_call_target="tpu_custom_call" | custom-call | tf_op jit(solution)/shard_map/pallas_call | solution.py:404
  (5 shorter events, 0.0 us)
Async XLA Ops:
  2.3 9.6 %collective-permute-start.2 = (f32[24,512]{1,0:T(8,128)S(1)}, f32[24,512]{1,0:T(8,128)S(1)}, u32[]{:S(2)}, u32[]{:S(2)}) collective-permute-start(f32[24,512]{1,0:T(8,128)S(1)} %get-tuple-element.46), channel_id=1, source_target_pairs={{0,1},{1,0},{2,3},{3,2},{4,5},{5,4},{6,7},{7,6},{8,9},{9,8},{10,11... | collective-permute-start | bytes 147464 | tf_op jit(solution)/shard_map/ppermute | solution.py:420
  2.5 9.5 %collective-permute-start.3 = (f32[24,512]{1,0:T(8,128)S(1)}, f32[24,512]{1,0:T(8,128)S(1)}, u32[]{:S(2)}, u32[]{:S(2)}) collective-permute-start(f32[24,512]{1,0:T(8,128)S(1)} %get-tuple-element.47), channel_id=1, source_target_pairs={{1,2},{2,1},{3,4},{4,3},{5,6},{6,5},{9,10},{10,9},{11,12},{12,11},... | collective-permute-start | bytes 147464 | tf_op jit(solution)/shard_map/ppermute | solution.py:420
  7.0 3.1 %collective-permute-start = (f32[56,128]{1,0:T(8,128)S(1)}, f32[56,128]{1,0:T(8,128)S(1)}, u32[]{:S(2)}, u32[]{:S(2)}) collective-permute-start(f32[56,128]{1,0:T(8,128)S(1)} %get-tuple-element.44), channel_id=1, source_target_pairs={{0,8},{8,0},{16,24},{24,16},{1,9},{9,1},{17,25},{25,17},{2,10},{10... | collective-permute-start | bytes 86024 | tf_op jit(solution)/shard_map/ppermute | solution.py:417
  8.3 3.6 %collective-permute-start.1 = (f32[56,128]{1,0:T(8,128)S(1)}, f32[56,128]{1,0:T(8,128)S(1)}, u32[]{:S(2)}, u32[]{:S(2)}) collective-permute-start(f32[56,128]{1,0:T(8,128)S(1)} %get-tuple-element.45), channel_id=1, source_target_pairs={{0,24},{8,16},{16,8},{24,0},{1,25},{9,17},{17,9},{25,1},{2,26},{10... | collective-permute-start | bytes 86024 | tf_op jit(solution)/shard_map/ppermute | solution.py:417
  9.5 3.1 %collective-permute-start.4 = (f32[24,128]{1,0:T(8,128)S(1)}, f32[24,128]{1,0:T(8,128)S(1)}, u32[]{:S(2)}, u32[]{:S(2)}) collective-permute-start(f32[24,128]{1,0:T(8,128)S(1)} %get-tuple-element.57), channel_id=1, source_target_pairs={{0,16},{8,24},{16,0},{24,8},{1,17},{9,25},{17,1},{25,9},{2,18},{10... | collective-permute-start | bytes 36872 | tf_op jit(solution)/shard_map/ppermute | solution.py:417
  13.6 8.6 %collective-permute-start.7 = (f32[24,512]{1,0:T(8,128)S(1)}, f32[24,512]{1,0:T(8,128)S(1)}, u32[]{:S(2)}, u32[]{:S(2)}) collective-permute-start(f32[24,512]{1,0:T(8,128)S(1)} %get-tuple-element.62), channel_id=1, source_target_pairs={{0,1},{1,0},{2,3},{3,2},{4,5},{5,4},{6,7},{7,6},{8,9},{9,8},{10,11... | collective-permute-start | bytes 147464 | tf_op jit(solution)/shard_map/ppermute | solution.py:420
  13.7 8.5 %collective-permute-start.8 = (f32[24,512]{1,0:T(8,128)S(1)}, f32[24,512]{1,0:T(8,128)S(1)}, u32[]{:S(2)}, u32[]{:S(2)}) collective-permute-start(f32[24,512]{1,0:T(8,128)S(1)} %get-tuple-element.63), channel_id=1, source_target_pairs={{1,2},{2,1},{3,4},{4,3},{5,6},{6,5},{9,10},{10,9},{11,12},{12,11},... | collective-permute-start | bytes 147464 | tf_op jit(solution)/shard_map/ppermute | solution.py:420
  17.8 2.8 %collective-permute-start.5 = (f32[56,128]{1,0:T(8,128)S(1)}, f32[56,128]{1,0:T(8,128)S(1)}, u32[]{:S(2)}, u32[]{:S(2)}) collective-permute-start(f32[56,128]{1,0:T(8,128)S(1)} %get-tuple-element.60), channel_id=1, source_target_pairs={{0,8},{8,0},{16,24},{24,16},{1,9},{9,1},{17,25},{25,17},{2,10},{10... | collective-permute-start | bytes 86024 | tf_op jit(solution)/shard_map/ppermute | solution.py:417
  18.6 3.6 %collective-permute-start.6 = (f32[56,128]{1,0:T(8,128)S(1)}, f32[56,128]{1,0:T(8,128)S(1)}, u32[]{:S(2)}, u32[]{:S(2)}) collective-permute-start(f32[56,128]{1,0:T(8,128)S(1)} %get-tuple-element.61), channel_id=1, source_target_pairs={{0,24},{8,16},{16,8},{24,0},{1,25},{9,17},{17,9},{25,1},{2,26},{10... | collective-permute-start | bytes 86024 | tf_op jit(solution)/shard_map/ppermute | solution.py:417
  20.3 2.6 %collective-permute-start.9 = (f32[24,128]{1,0:T(8,128)S(1)}, f32[24,128]{1,0:T(8,128)S(1)}, u32[]{:S(2)}, u32[]{:S(2)}) collective-permute-start(f32[24,128]{1,0:T(8,128)S(1)} %get-tuple-element.67), channel_id=1, source_target_pairs={{0,16},{8,24},{16,0},{24,8},{1,17},{9,25},{17,1},{25,9},{2,18},{10... | collective-permute-start | bytes 36872 | tf_op jit(solution)/shard_map/ppermute | solution.py:417
  23.9 8.1 %collective-permute-start.12 = (f32[24,512]{1,0:T(8,128)S(1)}, f32[24,512]{1,0:T(8,128)S(1)}, u32[]{:S(2)}, u32[]{:S(2)}) collective-permute-start(f32[24,512]{1,0:T(8,128)S(1)} %get-tuple-element.72), channel_id=1, source_target_pairs={{0,1},{1,0},{2,3},{3,2},{4,5},{5,4},{6,7},{7,6},{8,9},{9,8},{10,11... | collective-permute-start | bytes 147464 | tf_op jit(solution)/shard_map/ppermute | solution.py:420
  24.0 8.0 %collective-permute-start.13 = (f32[24,512]{1,0:T(8,128)S(1)}, f32[24,512]{1,0:T(8,128)S(1)}, u32[]{:S(2)}, u32[]{:S(2)}) collective-permute-start(f32[24,512]{1,0:T(8,128)S(1)} %get-tuple-element.73), channel_id=1, source_target_pairs={{1,2},{2,1},{3,4},{4,3},{5,6},{6,5},{9,10},{10,9},{11,12},{12,11},... | collective-permute-start | bytes 147464 | tf_op jit(solution)/shard_map/ppermute | solution.py:420
  27.6 3.3 %collective-permute-start.10 = (f32[56,128]{1,0:T(8,128)S(1)}, f32[56,128]{1,0:T(8,128)S(1)}, u32[]{:S(2)}, u32[]{:S(2)}) collective-permute-start(f32[56,128]{1,0:T(8,128)S(1)} %get-tuple-element.70), channel_id=1, source_target_pairs={{0,8},{8,0},{16,24},{24,16},{1,9},{9,1},{17,25},{25,17},{2,10},{10... | collective-permute-start | bytes 86024 | tf_op jit(solution)/shard_map/ppermute | solution.py:417
  28.4 3.6 %collective-permute-start.11 = (f32[56,128]{1,0:T(8,128)S(1)}, f32[56,128]{1,0:T(8,128)S(1)}, u32[]{:S(2)}, u32[]{:S(2)}) collective-permute-start(f32[56,128]{1,0:T(8,128)S(1)} %get-tuple-element.71), channel_id=1, source_target_pairs={{0,24},{8,16},{16,8},{24,0},{1,25},{9,17},{17,9},{25,1},{2,26},{10... | collective-permute-start | bytes 86024 | tf_op jit(solution)/shard_map/ppermute | solution.py:417
  29.6 3.1 %collective-permute-start.14 = (f32[24,128]{1,0:T(8,128)S(1)}, f32[24,128]{1,0:T(8,128)S(1)}, u32[]{:S(2)}, u32[]{:S(2)}) collective-permute-start(f32[24,128]{1,0:T(8,128)S(1)} %get-tuple-element.77), channel_id=1, source_target_pairs={{0,16},{8,24},{16,0},{24,8},{1,17},{9,25},{17,1},{25,9},{2,18},{10... | collective-permute-start | bytes 36872 | tf_op jit(solution)/shard_map/ppermute | solution.py:417

commit v4 on v3

--- a/solution.py
+++ b/solution.py
@@ -63,14 +63,8 @@
 
 def sec_exchanges(count):
     if count % 4 == 0:
-        far = count // 4
-        return [
-            [((i // 4 + hop) % far) * 4 + ((i % 4) ^ flip) for i in range(count)]
-            for hop in range(far)
-            for flip in range(4)
-            if hop or flip
-        ]
-    return [[(i + hop) % count for i in range(count)] for hop in range(1, count)]
+        return [(hop, flip) for hop in range(count // 4) for flip in (3, 1, 2, 0) if hop or flip]
+    return [(hop, 0) for hop in range(1, count)]
 
 
 class Plan:
@@ -80,7 +74,12 @@
         self.columns = rows * cols
         self.chunk = self.columns // sections
         self.tiles = spectral // LANES
-        self.exchanges = sec_exchanges(sections)
+        self.quad = 4 if sections % 4 == 0 else 1
+        self.hops = sec_exchanges(sections)
+        self.exchanges = [
+            [self.partner(i, number, divmod)[0] for i in range(sections)]
+            for number in range(len(self.hops))
+        ]
         self.edges = [
             any(abs(target - i) == 1 for i, target in enumerate(table)) for table in self.exchanges
         ]
@@ -88,24 +87,16 @@
             self.chunk + (self.tiles * rows + 8 if edge else 0) for edge in self.edges
         ]
 
-    def partner(self, section, number):
-        if self.sections % 4 == 0:
-            far = self.sections // 4
-            hop, flip = divmod(number + 1, 4)
-            high, low = lax.div(section, 4), lax.rem(section, 4)
-            flipped = low
-            if flip & 1:
-                flipped = flipped + 1 - 2 * lax.rem(flipped, 2)
-            if flip & 2:
-                flipped = flipped + 2 - 4 * lax.div(flipped, 2)
-            return (
-                lax.rem(high + hop, far) * 4 + flipped,
-                lax.rem(high + far - hop, far) * 4 + flipped,
-            )
-        hop = number + 1
-        return (
-            lax.rem(section + hop, self.sections),
-            lax.rem(section + self.sections - hop, self.sections),
+    def partner(self, section, number, divide=lambda a, b: (lax.div(a, b), lax.rem(a, b))):
+        hop, flip = self.hops[number]
+        groups = self.sections // self.quad
+        high, low = divide(section, self.quad)
+        if flip & 1:
+            low = low + 1 - 2 * divide(low, 2)[1]
+        if flip & 2:
+            low = low + 2 - 4 * divide(low, 2)[0]
+        return tuple(
+            divide(high + shift, groups)[1] * self.quad + low for shift in (hop, groups - hop)
         )
 
 

time: 34 us -> 33.2 us (0.976)
  waiting for transfers between devices: 5.55 us -> 4.7 us
    ppermute x9, waiting for transfers between devices: 5.54 us -> 4.68 us  [exchange(): lax.ppermute(message, axes[1], list(enumerate(table)))]
  transfers between devices with their start and end apart: 15 -> 15, of which waited for: 6 -> 5; matrix products, arithmetic and copies ran while one was open for 0% -> 0% of each run, Pallas kernels for 6% -> 6%
where the time goes in v4:
time: 33.2 us; the launch traced here: 33 us
  starting transfers between devices  20.7 us (62%)
  Pallas kernels  6.83 us (21%)
  waiting for transfers between devices  4.7 us (14%)
  between operations  0.75 us (2%)
    ppermute x3, starting transfers between devices, exchange(): lax.ppermute(sent[-1], axes[0], far)  12.3 us
    ppermute x9, starting transfers between devices, exchange(): lax.ppermute(message, axes[1], list(enumerate(table)))  8.14 us
    pallas_call x7, Pallas kernels, call(): pl.pallas_call(kernel, out_shape=outs, in_specs=[pl.BlockSpec(memory_spac...  6.83 us
    ppermute x9, waiting for transfers between devices, exchange(): lax.ppermute(message, axes[1], list(enumerate(table)))  4.68 us
  transfers between devices with their start and end apart: 15, of which 5 were waited for; matrix products, arithmetic and copies ran while one was open for 0% of the time, Pallas kernels for 6%

profile of v4, /device:TPU:1, one launch (start us, length us, event | category | flops | bytes accessed | tf_op | source)
XLA Modules:
  0.0 33.0 jit_solution(6739282316258843242)
XLA Ops:
  0.6 1.7 %shard_map.104 = (f32[4,24,768]{2,1,0:T(8,128)S(1)}, f32[96,128]{1,0:T(8,128)S(1)}, bf16[96,96]{1,0:T(8,128)(2,1)S(1)}, bf16[96,96]{1,0:T(8,128)(2,1)S(1)}, f32[...) custom-call(f32[4,24,768]{2,1,0:T(8,128)} %refs_0_.1, ...), custom_call_target="tpu_custom_call" | custom-call | tf_op jit(solution)/shard_map/pallas_call | solution.py:395
  2.3 0.1 collective-permute-start.2
  2.5 4.6 %collective-permute-start.3 = (f32[24,512]{1,0:T(8,128)S(1)}, f32[24,512]{1,0:T(8,128)S(1)}, u32[]{:S(2)}, u32[]{:S(2)}) collective-permute-start(f32[24,512]{1,0:T(8,128)S(1)} %get-tuple-element.47), channel_id=1, source_target_pairs={{1,2},{2,1},{3,4},{4,3},{5,6},{6,5},{9,10},{10,9},{11,12},{12,11},... | collective-permute-start | bytes 147464 | tf_op jit(solution)/shard_map/ppermute | solution.py:411
  7.0 2.2 %collective-permute-start = (f32[56,128]{1,0:T(8,128)S(1)}, f32[56,128]{1,0:T(8,128)S(1)}, u32[]{:S(2)}, u32[]{:S(2)}) collective-permute-start(f32[56,128]{1,0:T(8,128)S(1)} %get-tuple-element.44), channel_id=1, source_target_pairs={{0,24},{8,16},{16,8},{24,0},{1,25},{9,17},{17,9},{25,1},{2,26},{10... | collective-permute-start | bytes 86024 | tf_op jit(solution)/shard_map/ppermute | solution.py:408
  9.2 0.3 collective-permute-start.1
  9.5 0.2 collective-permute-start.4
  9.7 1.0 %collective-permute-done.refs_4_.refs_10_ = f32[56,128]{1,0:T(8,128)S(1)} collective-permute-done((f32[56,128]{1,0:T(8,128)S(1)}, f32[56,128]{1,0:T(8,128)S(1)}, u32[]{:S(2)}, u32[]{:S(2)}) %collective-permute-start) | collective-permute-done | bytes 28704 | tf_op jit(solution)/shard_map/ppermute | solution.py:408
  10.7 1.2 %collective-permute-done.1.refs_5_.refs_11_ = f32[56,128]{1,0:T(8,128)S(1)} collective-permute-done((f32[56,128]{1,0:T(8,128)S(1)}, f32[56,128]{1,0:T(8,128)S(1)}, u32[]{:S(2)}, u32[]{:S(2)}) %collective-permute-start.1) | collective-permute-done | bytes 28704 | tf_op jit(solution)/shard_map/ppermute | solution.py:408
  12.0 0.0 collective-permute-done.2.refs_6_
  12.0 0.0 collective-permute-done.3.refs_7_
  12.0 0.6 %shard_map.105 = (f32[4,24,768]{2,1,0:T(8,128)S(1)}, f32[96,128]{1,0:T(8,128)S(1)}) custom-call(f32[4,24,768]{2,1,0:T(8,128)S(1)} %get-tuple-element.40.refs_0_, f32[96,128]{1,0:T(8,128)S(1)} %get-tuple-element.41.refs_1_.refs_2_, f32[96,128]{1,0:T(8,128)S(1)} %get-tuple-element.42.refs_2_, f32[8,768]{1,0:T(8,128)S(1)} %get-tuple-element.43.refs_3_, ...), custom_call_target="tpu_custom_call" | custom-call | tf_op jit(solution)/shard_map/pallas_call | solution.py:395
  12.6 0.0 collective-permute-done.4.refs_12_
  12.6 1.0 %shard_map.106 = (f32[4,24,768]{2,1,0:T(8,128)S(1)}, f32[96,128]{1,0:T(8,128)S(1)}, f32[96,128]{1,0:T(8,128)S(1)}, f32[56,128]{1,0:T(8,128)S(1)}, f32[56,128]{1,...) custom-call(f32[4,24,768]{2,1,0:T(8,128)S(1)} %get-tuple-element.48.refs_0_, ...), custom_call_target="tpu_custom_call" | custom-call | tf_op jit(solution)/shard_map/pallas_call | solution.py:395
  13.7 0.1 collective-permute-start.7
  13.7 4.1 %collective-permute-start.8 = (f32[24,512]{1,0:T(8,128)S(1)}, f32[24,512]{1,0:T(8,128)S(1)}, u32[]{:S(2)}, u32[]{:S(2)}) collective-permute-start(f32[24,512]{1,0:T(8,128)S(1)} %get-tuple-element.63), channel_id=1, source_target_pairs={{1,2},{2,1},{3,4},{4,3},{5,6},{6,5},{9,10},{10,9},{11,12},{12,11},... | collective-permute-start | bytes 147464 | tf_op jit(solution)/shard_map/ppermute | solution.py:411
  17.8 0.7 %collective-permute-start.5 = (f32[56,128]{1,0:T(8,128)S(1)}, f32[56,128]{1,0:T(8,128)S(1)}, u32[]{:S(2)}, u32[]{:S(2)}) collective-permute-start(f32[56,128]{1,0:T(8,128)S(1)} %get-tuple-element.60), channel_id=1, source_target_pairs={{0,24},{8,16},{16,8},{24,0},{1,25},{9,17},{17,9},{25,1},{2,26},{10... | collective-permute-start | bytes 86024 | tf_op jit(solution)/shard_map/ppermute | solution.py:408
  18.5 0.8 %collective-permute-start.6 = (f32[56,128]{1,0:T(8,128)S(1)}, f32[56,128]{1,0:T(8,128)S(1)}, u32[]{:S(2)}, u32[]{:S(2)}) collective-permute-start(f32[56,128]{1,0:T(8,128)S(1)} %get-tuple-element.61), channel_id=1, source_target_pairs={{0,8},{8,0},{16,24},{24,16},{1,9},{9,1},{17,25},{25,17},{2,10},{10... | collective-permute-start | bytes 86024 | tf_op jit(solution)/shard_map/ppermute | solution.py:408
  19.3 1.2 %collective-permute-start.9 = (f32[24,128]{1,0:T(8,128)S(1)}, f32[24,128]{1,0:T(8,128)S(1)}, u32[]{:S(2)}, u32[]{:S(2)}) collective-permute-start(f32[24,128]{1,0:T(8,128)S(1)} %get-tuple-element.67), channel_id=1, source_target_pairs={{0,16},{8,24},{16,0},{24,8},{1,17},{9,25},{17,1},{25,9},{2,18},{10... | collective-permute-start | bytes 36872 | tf_op jit(solution)/shard_map/ppermute | solution.py:408
  20.6 1.0 %collective-permute-done.5.refs_4_.refs_10_ = f32[56,128]{1,0:T(8,128)S(1)} collective-permute-done((f32[56,128]{1,0:T(8,128)S(1)}, f32[56,128]{1,0:T(8,128)S(1)}, u32[]{:S(2)}, u32[]{:S(2)}) %collective-permute-start.5) | collective-permute-done | bytes 28704 | tf_op jit(solution)/shard_map/ppermute | solution.py:408
  21.5 0.7 %shard_map.107 = (f32[4,24,768]{2,1,0:T(8,128)S(1)}, f32[96,128]{1,0:T(8,128)S(1)}) custom-call(f32[4,24,768]{2,1,0:T(8,128)S(1)} %get-tuple-element.58.refs_0_, f32[96,128]{1,0:T(8,128)S(1)} %get-tuple-element.59.refs_1_.refs_2_, f32[96,128]{1,0:T(8,128)S(1)} %get-tuple-element.42.refs_2_, f32[8,768]{1,0:T(8,128)S(1)} %get-tuple-element.43.refs_3_, ...), custom_call_target="tpu_custom_call" | custom-call | tf_op jit(solution)/shard_map/pallas_call | solution.py:395
  22.2 1.0 %shard_map.108 = (f32[4,24,768]{2,1,0:T(8,128)S(1)}, f32[96,128]{1,0:T(8,128)S(1)}, f32[96,128]{1,0:T(8,128)S(1)}, f32[56,128]{1,0:T(8,128)S(1)}, f32[56,128]{1,...) custom-call(f32[4,24,768]{2,1,0:T(8,128)S(1)} %get-tuple-element.64.refs_0_, ...), custom_call_target="tpu_custom_call" | custom-call | tf_op jit(solution)/shard_map/pallas_call | solution.py:395
  23.2 0.1 collective-permute-start.12
  23.3 3.6 %collective-permute-start.13 = (f32[24,512]{1,0:T(8,128)S(1)}, f32[24,512]{1,0:T(8,128)S(1)}, u32[]{:S(2)}, u32[]{:S(2)}) collective-permute-start(f32[24,512]{1,0:T(8,128)S(1)} %get-tuple-element.73), channel_id=1, source_target_pairs={{1,2},{2,1},{3,4},{4,3},{5,6},{6,5},{9,10},{10,9},{11,12},{12,11},... | collective-permute-start | bytes 147464 | tf_op jit(solution)/shard_map/ppermute | solution.py:411
  27.0 1.5 %collective-permute-start.10 = (f32[56,128]{1,0:T(8,128)S(1)}, f32[56,128]{1,0:T(8,128)S(1)}, u32[]{:S(2)}, u32[]{:S(2)}) collective-permute-start(f32[56,128]{1,0:T(8,128)S(1)} %get-tuple-element.70), channel_id=1, source_target_pairs={{0,24},{8,16},{16,8},{24,0},{1,25},{9,17},{17,9},{25,1},{2,26},{10... | collective-permute-start | bytes 86024 | tf_op jit(solution)/shard_map/ppermute | solution.py:408
  28.4 0.8 %collective-permute-start.11 = (f32[56,128]{1,0:T(8,128)S(1)}, f32[56,128]{1,0:T(8,128)S(1)}, u32[]{:S(2)}, u32[]{:S(2)}) collective-permute-start(f32[56,128]{1,0:T(8,128)S(1)} %get-tuple-element.71), channel_id=1, source_target_pairs={{0,8},{8,0},{16,24},{24,16},{1,9},{9,1},{17,25},{25,17},{2,10},{10... | collective-permute-start | bytes 86024 | tf_op jit(solution)/shard_map/ppermute | solution.py:408
  29.2 0.5 %collective-permute-start.14 = (f32[24,128]{1,0:T(8,128)S(1)}, f32[24,128]{1,0:T(8,128)S(1)}, u32[]{:S(2)}, u32[]{:S(2)}) collective-permute-start(f32[24,128]{1,0:T(8,128)S(1)} %get-tuple-element.77), channel_id=1, source_target_pairs={{0,16},{8,24},{16,0},{24,8},{1,17},{9,25},{17,1},{25,9},{2,18},{10... | collective-permute-start | bytes 36872 | tf_op jit(solution)/shard_map/ppermute | solution.py:408
  29.7 1.0 %collective-permute-done.10.refs_4_.refs_10_ = f32[56,128]{1,0:T(8,128)S(1)} collective-permute-done((f32[56,128]{1,0:T(8,128)S(1)}, f32[56,128]{1,0:T(8,128)S(1)}, u32[]{:S(2)}, u32[]{:S(2)}) %collective-permute-start.10) | collective-permute-done | bytes 28704 | tf_op jit(solution)/shard_map/ppermute | solution.py:408
  30.7 0.5 %collective-permute-done.11.refs_5_.refs_11_ = f32[56,128]{1,0:T(8,128)S(1)} collective-permute-done((f32[56,128]{1,0:T(8,128)S(1)}, f32[56,128]{1,0:T(8,128)S(1)}, u32[]{:S(2)}, u32[]{:S(2)}) %collective-permute-start.11) | collective-permute-done | bytes 28704 | tf_op jit(solution)/shard_map/ppermute | solution.py:408
  31.1 0.0 collective-permute-done.12.refs_6_
  31.2 0.0 collective-permute-done.13.refs_7_
  31.2 0.7 %shard_map.109 = (f32[4,24,768]{2,1,0:T(8,128)S(1)}, f32[96,128]{1,0:T(8,128)S(1)}) custom-call(f32[4,24,768]{2,1,0:T(8,128)S(1)} %get-tuple-element.68.refs_0_, f32[96,128]{1,0:T(8,128)S(1)} %get-tuple-element.69.refs_1_.refs_2_, f32[96,128]{1,0:T(8,128)S(1)} %get-tuple-element.42.refs_2_, f32[8,768]{1,0:T(8,128)S(1)} %get-tuple-element.43.refs_3_, ...), custom_call_target="tpu_custom_call" | custom-call | tf_op jit(solution)/shard_map/pallas_call | solution.py:395
  31.8 1.1 %shard_map.110 = (f32[4,24,768]{2,1,0:T(8,128)}, f32[4,24,64]{2,1,0:T(8,128)}) custom-call(f32[4,24,768]{2,1,0:T(8,128)S(1)} %get-tuple-element.74.refs_0_, f32[96,128]{1,0:T(8,128)S(1)} %get-tuple-element.75.refs_1_, f32[96,128]{1,0:T(8,128)S(1)} %get-tuple-element.69.refs_1_.refs_2_, f32[96,128]{1,0:T(8,128)S(1)} %get-tuple-element.76.refs_3_, ...), custom_call_target="tpu_custom_call" | custom-call | tf_op jit(solution)/shard_map/pallas_call | solution.py:395
  (5 shorter events, 0.0 us)
Async XLA Ops:
  2.3 9.6 %collective-permute-start.2 = (f32[24,512]{1,0:T(8,128)S(1)}, f32[24,512]{1,0:T(8,128)S(1)}, u32[]{:S(2)}, u32[]{:S(2)}) collective-permute-start(f32[24,512]{1,0:T(8,128)S(1)} %get-tuple-element.46), channel_id=1, source_target_pairs={{0,1},{1,0},{2,3},{3,2},{4,5},{5,4},{6,7},{7,6},{8,9},{9,8},{10,11... | collective-permute-start | bytes 147464 | tf_op jit(solution)/shard_map/ppermute | solution.py:411
  2.5 9.5 %collective-permute-start.3 = (f32[24,512]{1,0:T(8,128)S(1)}, f32[24,512]{1,0:T(8,128)S(1)}, u32[]{:S(2)}, u32[]{:S(2)}) collective-permute-start(f32[24,512]{1,0:T(8,128)S(1)} %get-tuple-element.47), channel_id=1, source_target_pairs={{1,2},{2,1},{3,4},{4,3},{5,6},{6,5},{9,10},{10,9},{11,12},{12,11},... | collective-permute-start | bytes 147464 | tf_op jit(solution)/shard_map/ppermute | solution.py:411
  7.0 3.7 %collective-permute-start = (f32[56,128]{1,0:T(8,128)S(1)}, f32[56,128]{1,0:T(8,128)S(1)}, u32[]{:S(2)}, u32[]{:S(2)}) collective-permute-start(f32[56,128]{1,0:T(8,128)S(1)} %get-tuple-element.44), channel_id=1, source_target_pairs={{0,24},{8,16},{16,8},{24,0},{1,25},{9,17},{17,9},{25,1},{2,26},{10... | collective-permute-start | bytes 86024 | tf_op jit(solution)/shard_map/ppermute | solution.py:408
  9.2 2.7 %collective-permute-start.1 = (f32[56,128]{1,0:T(8,128)S(1)}, f32[56,128]{1,0:T(8,128)S(1)}, u32[]{:S(2)}, u32[]{:S(2)}) collective-permute-start(f32[56,128]{1,0:T(8,128)S(1)} %get-tuple-element.45), channel_id=1, source_target_pairs={{0,8},{8,0},{16,24},{24,16},{1,9},{9,1},{17,25},{25,17},{2,10},{10... | collective-permute-start | bytes 86024 | tf_op jit(solution)/shard_map/ppermute | solution.py:408
  9.5 3.1 %collective-permute-start.4 = (f32[24,128]{1,0:T(8,128)S(1)}, f32[24,128]{1,0:T(8,128)S(1)}, u32[]{:S(2)}, u32[]{:S(2)}) collective-permute-start(f32[24,128]{1,0:T(8,128)S(1)} %get-tuple-element.57), channel_id=1, source_target_pairs={{0,16},{8,24},{16,0},{24,8},{1,17},{9,25},{17,1},{25,9},{2,18},{10... | collective-permute-start | bytes 36872 | tf_op jit(solution)/shard_map/ppermute | solution.py:408
  13.7 7.9 %collective-permute-start.7 = (f32[24,512]{1,0:T(8,128)S(1)}, f32[24,512]{1,0:T(8,128)S(1)}, u32[]{:S(2)}, u32[]{:S(2)}) collective-permute-start(f32[24,512]{1,0:T(8,128)S(1)} %get-tuple-element.62), channel_id=1, source_target_pairs={{0,1},{1,0},{2,3},{3,2},{4,5},{5,4},{6,7},{7,6},{8,9},{9,8},{10,11... | collective-permute-start | bytes 147464 | tf_op jit(solution)/shard_map/ppermute | solution.py:411
  13.7 7.8 %collective-permute-start.8 = (f32[24,512]{1,0:T(8,128)S(1)}, f32[24,512]{1,0:T(8,128)S(1)}, u32[]{:S(2)}, u32[]{:S(2)}) collective-permute-start(f32[24,512]{1,0:T(8,128)S(1)} %get-tuple-element.63), channel_id=1, source_target_pairs={{1,2},{2,1},{3,4},{4,3},{5,6},{6,5},{9,10},{10,9},{11,12},{12,11},... | collective-permute-start | bytes 147464 | tf_op jit(solution)/shard_map/ppermute | solution.py:411
  17.8 3.7 %collective-permute-start.5 = (f32[56,128]{1,0:T(8,128)S(1)}, f32[56,128]{1,0:T(8,128)S(1)}, u32[]{:S(2)}, u32[]{:S(2)}) collective-permute-start(f32[56,128]{1,0:T(8,128)S(1)} %get-tuple-element.60), channel_id=1, source_target_pairs={{0,24},{8,16},{16,8},{24,0},{1,25},{9,17},{17,9},{25,1},{2,26},{10... | collective-permute-start | bytes 86024 | tf_op jit(solution)/shard_map/ppermute | solution.py:408
  18.5 3.0 %collective-permute-start.6 = (f32[56,128]{1,0:T(8,128)S(1)}, f32[56,128]{1,0:T(8,128)S(1)}, u32[]{:S(2)}, u32[]{:S(2)}) collective-permute-start(f32[56,128]{1,0:T(8,128)S(1)} %get-tuple-element.61), channel_id=1, source_target_pairs={{0,8},{8,0},{16,24},{24,16},{1,9},{9,1},{17,25},{25,17},{2,10},{10... | collective-permute-start | bytes 86024 | tf_op jit(solution)/shard_map/ppermute | solution.py:408
  19.3 2.9 %collective-permute-start.9 = (f32[24,128]{1,0:T(8,128)S(1)}, f32[24,128]{1,0:T(8,128)S(1)}, u32[]{:S(2)}, u32[]{:S(2)}) collective-permute-start(f32[24,128]{1,0:T(8,128)S(1)} %get-tuple-element.67), channel_id=1, source_target_pairs={{0,16},{8,24},{16,0},{24,8},{1,17},{9,25},{17,1},{25,9},{2,18},{10... | collective-permute-start | bytes 36872 | tf_op jit(solution)/shard_map/ppermute | solution.py:408
  23.2 7.9 %collective-permute-start.12 = (f32[24,512]{1,0:T(8,128)S(1)}, f32[24,512]{1,0:T(8,128)S(1)}, u32[]{:S(2)}, u32[]{:S(2)}) collective-permute-start(f32[24,512]{1,0:T(8,128)S(1)} %get-tuple-element.72), channel_id=1, source_target_pairs={{0,1},{1,0},{2,3},{3,2},{4,5},{5,4},{6,7},{7,6},{8,9},{9,8},{10,11... | collective-permute-start | bytes 147464 | tf_op jit(solution)/shard_map/ppermute | solution.py:411
  23.3 7.8 %collective-permute-start.13 = (f32[24,512]{1,0:T(8,128)S(1)}, f32[24,512]{1,0:T(8,128)S(1)}, u32[]{:S(2)}, u32[]{:S(2)}) collective-permute-start(f32[24,512]{1,0:T(8,128)S(1)} %get-tuple-element.73), channel_id=1, source_target_pairs={{1,2},{2,1},{3,4},{4,3},{5,6},{6,5},{9,10},{10,9},{11,12},{12,11},... | collective-permute-start | bytes 147464 | tf_op jit(solution)/shard_map/ppermute | solution.py:411
  27.0 3.7 %collective-permute-start.10 = (f32[56,128]{1,0:T(8,128)S(1)}, f32[56,128]{1,0:T(8,128)S(1)}, u32[]{:S(2)}, u32[]{:S(2)}) collective-permute-start(f32[56,128]{1,0:T(8,128)S(1)} %get-tuple-element.70), channel_id=1, source_target_pairs={{0,24},{8,16},{16,8},{24,0},{1,25},{9,17},{17,9},{25,1},{2,26},{10... | collective-permute-start | bytes 86024 | tf_op jit(solution)/shard_map/ppermute | solution.py:408
  28.4 2.7 %collective-permute-start.11 = (f32[56,128]{1,0:T(8,128)S(1)}, f32[56,128]{1,0:T(8,128)S(1)}, u32[]{:S(2)}, u32[]{:S(2)}) collective-permute-start(f32[56,128]{1,0:T(8,128)S(1)} %get-tuple-element.71), channel_id=1, source_target_pairs={{0,8},{8,0},{16,24},{24,16},{1,9},{9,1},{17,25},{25,17},{2,10},{10... | collective-permute-start | bytes 86024 | tf_op jit(solution)/shard_map/ppermute | solution.py:408
  29.2 2.6 %collective-permute-start.14 = (f32[24,128]{1,0:T(8,128)S(1)}, f32[24,128]{1,0:T(8,128)S(1)}, u32[]{:S(2)}, u32[]{:S(2)}) collective-permute-start(f32[24,128]{1,0:T(8,128)S(1)} %get-tuple-element.77), channel_id=1, source_target_pairs={{0,16},{8,24},{16,0},{24,8},{1,17},{9,25},{17,1},{25,9},{2,18},{10... | collective-permute-start | bytes 36872 | tf_op jit(solution)/shard_map/ppermute | solution.py:408

commit v5 on v4

--- a/solution.py
+++ b/solution.py
@@ -159,8 +159,8 @@
 def first_kernel(plan, axes, *refs):
     waves_in, turning_in, currents_in, drag_in, mask_in, target_in = refs[:6]
     tables_in, refs = refs[6:9], refs[9:]
-    waves, ocean_out, permute_out, permute_t_out, turn_out, sea_out, keep_out = refs[:7]
-    tables_out, packed_out, refs = refs[7:10], refs[10], refs[11:]
+    waves, ocean_out, permute_out, permute_t_out, turn_out, turn_edge_out = refs[:6]
+    sea_out, keep_out, tables_out, packed_out, refs = refs[6], refs[7], refs[8:11], refs[11], refs[12:]
     count = len(plan.exchanges)
     sec_out, lat_out, refs = refs[:count], refs[count : count + 2], refs[count + 2 :]
     turning, currents, drag, mask, target, done = refs
@@ -205,7 +205,12 @@
     permute_out[...] = jnp.where(slot_col == across.astype(F32), sea, 0.0).astype(BF16)
     permute_t = jnp.where(slot_row == down.astype(F32), 1.0, 0.0).astype(BF16)
     permute_t_out[...] = permute_t
-    turn_out[...] = jnp.broadcast_to(column_of(row_of(turning)), (columns, LANES))
+    turn = jnp.broadcast_to(column_of(row_of(turning)), (columns, LANES))
+    turn_out[...] = turn
+    cols = plan.cols
+    for row in range(rows):
+        turn_edge_out[row : row + 1, :] = turn[row * cols : row * cols + 1, :]
+        turn_edge_out[rows + row : rows + row + 1, :] = turn[(row + 1) * cols - 1 : (row + 1) * cols, :]
     sea_out[...] = jnp.broadcast_to(sea, (columns, LANES))
     keep = 1.0 - drag[...].reshape(1, plan.depth)
     blank = jnp.zeros((1, LANES - 2 * plan.depth), F32)
@@ -227,38 +232,35 @@
         copy.wait()
 
 
+class Directions:
+    def __init__(self, shape):
+        direction = lax.rem(lane_of(shape), NDIR)
+        self.eastward = (direction < NDIR // 4) | (direction >= 3 * NDIR // 4)
+        self.northward = direction < NDIR // 2
+        self.first, self.final = direction == 0, direction == NDIR - 1
+
+    def turned(self, moved, rate, gain):
+        behind = jnp.where(
+            self.first, pltpu.roll(moved, LANES - (NDIR - 1), 1), pltpu.roll(moved, 1, 1)
+        )
+        forward = jnp.where(
+            self.final, pltpu.roll(moved, NDIR - 1, 1), pltpu.roll(moved, LANES - 1, 1)
+        )
+        return moved - jnp.abs(rate) * gain * (moved - jnp.where(rate > 0.0, behind, forward))
+
+
 def move_kernel(plan, axes, *refs):
-    waves, ocean, turn, rates = refs[:4]
-    edge_numbers = [number for number, edge in enumerate(plan.edges) if edge]
-    sec_in, refs = refs[4 : 4 + len(edge_numbers)], refs[4 + len(edge_numbers) :]
-    near, far, turned_out, spin_out, west_edge, east_edge = refs
-    section, band = lax.axis_index(axes[1]), lax.axis_index(axes[0])
-    even = lax.rem(band, 2) == 0
-    rows, cols, tiles, chunk = plan.rows, plan.cols, plan.tiles, plan.chunk
-
-    west_edge[...] = jnp.zeros_like(west_edge)
-    east_edge[...] = jnp.zeros_like(east_edge)
-    for number, message in zip(edge_numbers, sec_in):
-        _, source = plan.partner(section, number)
-
-        @pl.when(source == section + 1)
-        def _():
-            east_edge[...] = message[chunk:, :]
-
-        @pl.when(source == section - 1)
-        def _():
-            west_edge[...] = message[chunk:, :]
-
+    waves, turn, rates, near, far, turned_out = refs
+    even = lax.rem(lax.axis_index(axes[0]), 2) == 0
+    rows, cols, tiles = plan.rows, plan.cols, plan.tiles
     block = (cols, LANES)
-    direction = lax.rem(lane_of(block), NDIR)
-    eastward = (direction < NDIR // 4) | (direction >= 3 * NDIR // 4)
-    northward = direction < NDIR // 2
-    first, final = direction == 0, direction == NDIR - 1
+    masks = Directions(block)
     place = lax.broadcasted_iota(jnp.int32, block, 0)
-    at_west, at_east = place == 0, place == cols - 1
+    outside = place == jnp.where(masks.eastward, 0, cols - 1)
     for tile in range(tiles):
         lanes = slice(tile * LANES, (tile + 1) * LANES)
         stay, along_x, along_y, gain = (rates[k : k + 1, lanes] for k in range(4))
+        along_x = jnp.where(outside, 0.0, along_x)
         half = tile % (tiles // 2)
         half = slice(half * LANES, (half + 1) * LANES)
         south_edge = jnp.where(even, far[:, half], near[:, half])
@@ -267,44 +269,19 @@
             south_edge = pltpu.roll(south_edge, LANES - NDIR // 2, 1)
             north_edge = pltpu.roll(north_edge, NDIR // 2, 1)
         for row in range(rows):
-            edge = slice(tile * rows + row, tile * rows + row + 1)
             center = waves[row, :, lanes]
-            west = jnp.where(at_west, west_edge[edge, :], pltpu.roll(center, 1, 0))
-            east = jnp.where(at_east, east_edge[edge, :], pltpu.roll(center, cols - 1, 0))
             south = waves[row - 1, :, lanes] if row else south_edge
             north = waves[row + 1, :, lanes] if row < rows - 1 else north_edge
             moved = (
                 stay * center
-                + along_x * jnp.where(eastward, west, east)
-                + along_y * jnp.where(northward, south, north)
-            )
-            behind = jnp.where(
-                first, pltpu.roll(moved, LANES - (NDIR - 1), 1), pltpu.roll(moved, 1, 1)
-            )
-            forward = jnp.where(
-                final, pltpu.roll(moved, NDIR - 1, 1), pltpu.roll(moved, LANES - 1, 1)
+                + along_x
+                * jnp.where(
+                    masks.eastward, pltpu.roll(center, 1, 0), pltpu.roll(center, cols - 1, 0)
+                )
+                + along_y * jnp.where(masks.northward, south, north)
             )
             rate = turn[row * cols : (row + 1) * cols, :]
-            turned_out[row, :, lanes] = moved - jnp.abs(rate) * gain * (
-                moved - jnp.where(rate > 0.0, behind, forward)
-            )
-
-    zonal = lane_of(block) < plan.depth
-    half = slice(plan.spectral // 2, plan.spectral // 2 + LANES)
-    south_edge = jnp.where(even, far[:, half], near[:, half])
-    north_edge = jnp.where(even, near[:, half], far[:, half])
-    for row in range(rows):
-        flat = slice(row * cols, (row + 1) * cols)
-        edge = slice(tiles * rows + row, tiles * rows + row + 1)
-        center = ocean[flat, :]
-        west = jnp.where(at_west, west_edge[edge, :], pltpu.roll(center, 1, 0))
-        east = jnp.where(at_east, east_edge[edge, :], pltpu.roll(center, cols - 1, 0))
-        south = ocean[(row - 1) * cols : row * cols, :] if row else south_edge
-        north = ocean[(row + 1) * cols : (row + 2) * cols, :] if row < rows - 1 else north_edge
-        shear = 0.5 * jnp.where(zonal, south - north, east - west)
-        shear = shear + swapped(plan, shear)
-        y = (band * rows + row).astype(F32)
-        spin_out[flat, :] = 0.2 + 0.6 * y / float(plan.bands * rows) + shear
+            turned_out[row, :, lanes] = masks.turned(moved, rate, gain)
 
 
 def swapped(plan, value):
@@ -314,24 +291,37 @@
 
 
 def couple_kernel(plan, axes, last, *refs):
-    turned, spin, ocean_in, packed_in, permute, permute_t, sea, keep, stokes, grow = refs[:10]
-    refs = refs[10:]
+    turned, ocean_in, packed_in, permute, permute_t, turn_edge, sea, keep = refs[:8]
+    stokes, rates, grow, refs = refs[8], refs[9], refs[10], refs[11:]
     count = len(plan.exchanges)
-    sec_in, refs = refs[:count], refs[count:]
+    sec_in, near, far, refs = refs[:count], refs[count], refs[count + 1], refs[count + 2 :]
     if last:
-        waves_far, ocean_far, coupled, waves_out, ocean_out, done = refs
+        waves_far, ocean_far, coupled, west_edge, east_edge, waves_out, ocean_out, done = refs
     else:
         waves_out, ocean_out, packed_out = refs[:3]
-        sec_out, lat_out, coupled = refs[3 : count + 3], refs[count + 3 : count + 5], refs[-1]
+        sec_out, lat_out = refs[3 : count + 3], refs[count + 3 : count + 5]
+        coupled, west_edge, east_edge = refs[count + 5 :]
     section, band = lax.axis_index(axes[1]), lax.axis_index(axes[0])
     even = lax.rem(band, 2) == 0
-    rows, cols, chunk, columns = plan.rows, plan.cols, plan.chunk, plan.columns
+    rows, cols, chunk, columns, tiles = plan.rows, plan.cols, plan.chunk, plan.columns, plan.tiles
 
     own = pl.ds(pl.multiple_of(section * chunk, 8), chunk)
     coupled[own, :] = packed_in[own, :]
+    west_edge[...] = jnp.zeros_like(west_edge)
+    east_edge[...] = jnp.zeros_like(east_edge)
     for number, message in enumerate(sec_in):
         _, source = plan.partner(section, number)
         coupled[pl.ds(pl.multiple_of(source * chunk, 8), chunk), :] = message[0:chunk, :]
+        if plan.edges[number]:
+
+            @pl.when(source == section + 1)
+            def _():
+                east_edge[...] = message[chunk:, :]
+
+            @pl.when(source == section - 1)
+            def _():
+                west_edge[...] = message[chunk:, :]
+
     arrived = coupled[...]
     other = pltpu.roll(arrived, LANES // 2, 1)
     lane = lane_of((columns, LANES))
@@ -339,24 +329,67 @@
     at_waves = dot(permute[...], split_value(both)).astype(BF16)
     at_waves = jnp.concatenate([at_waves, at_waves], axis=1)
 
-    pushed = swapped(plan, ocean_in[...] + other)
-    turn_by = ocean_dt * spin[...] * pushed
-    new = keep[0:1, :] * (ocean_in[...] + jnp.where(lane < plan.depth, turn_by, -turn_by)) * sea[...]
+    masks = Directions((2 * rows, LANES))
+    westmost = lax.broadcasted_iota(jnp.int32, (2 * rows, LANES), 0) < rows
+    reached = jnp.where(masks.eastward, 1, 0) == jnp.where(westmost, 1, 0)
+    extra = []
+    for tile in range(tiles):
+        lanes = slice(tile * LANES, (tile + 1) * LANES)
+        edge = slice(tile * rows, (tile + 1) * rows)
+        came = jnp.concatenate([west_edge[edge, :], east_edge[edge, :]], axis=0)
+        moved = rates[1:2, lanes] * jnp.where(reached, came, 0.0)
+        extra.append(masks.turned(moved, turn_edge[...], rates[3:4, lanes]))
+
+    block = (cols, LANES)
+    zonal = lane_of(block) < plan.depth
+    place = lax.broadcasted_iota(jnp.int32, block, 0)
+    at_west, at_east = place == 0, place == cols - 1
+    half = slice(plan.spectral // 2, plan.spectral // 2 + LANES)
+    south_edge = jnp.where(even, far[:, half], near[:, half])
+    north_edge = jnp.where(even, near[:, half], far[:, half])
+    new = []
+    for row in range(rows):
+        flat = slice(row * cols, (row + 1) * cols)
+        edge = slice(tiles * rows + row, tiles * rows + row + 1)
+        center = ocean_in[flat, :]
+        west = jnp.where(at_west, west_edge[edge, :], pltpu.roll(center, 1, 0))
+        east = jnp.where(at_east, east_edge[edge, :], pltpu.roll(center, cols - 1, 0))
+        south = ocean_in[(row - 1) * cols : row * cols, :] if row else south_edge
+        north = ocean_in[(row + 1) * cols : (row + 2) * cols, :] if row < rows - 1 else north_edge
+        shear = 0.5 * jnp.where(zonal, south - north, east - west)
+        y = (band * rows + row).astype(F32)
+        spin = 0.2 + 0.6 * y / float(plan.bands * rows) + (shear + swapped(plan, shear))
+        turn_by = ocean_dt * spin * swapped(plan, center + other[flat, :])
+        value = keep[0:1, :] * (center + jnp.where(zonal, turn_by, -turn_by)) * sea[flat, :]
+        if last:
+            ocean_out[row] = value[:, : 2 * plan.depth]
+        else:
+            ocean_out[flat, :] = value
+        new.append(value)
     if last:
-        ocean_out[...] = new[:, : 2 * plan.depth].reshape(rows, cols, 2 * plan.depth)
         copies = [pltpu.make_async_copy(ocean_out, ocean_far, done.at[0])]
         copies[0].start()
-    else:
-        ocean_out[...] = new
 
     total = None
     wet = jnp.concatenate([sea[...], sea[...]], axis=1)
+    place = lax.broadcasted_iota(jnp.int32, (8, 256), 0)
+    at_first, at_last = place == 0, place == 7
     for number, start in enumerate(range(0, plan.spectral, 256)):
         lanes = slice(start, start + 256)
         table = jnp.concatenate(
             [grow[(2 * number + k) * 256 : (2 * number + k + 1) * 256, :] for k in range(2)], axis=1
         )
-        grown = turned[:, :, lanes].reshape(columns, 256) * (wet + dot(at_waves, table))
+        from_edges = jnp.concatenate(extra[2 * number : 2 * number + 2], axis=1)
+        parts = []
+        for row in range(rows):
+            west = jnp.where(at_first, from_edges[row : row + 1, :], 0.0)
+            east = jnp.where(at_last, from_edges[rows + row : rows + row + 1, :], 0.0)
+            parts += [
+                turned[row, 0:8, lanes] + west,
+                turned[row, 8 : cols - 8, lanes],
+                turned[row, cols - 8 :, lanes] + east,
+            ]
+        grown = jnp.concatenate(parts, axis=0) * (wet + dot(at_waves, table))
         waves_out[:, :, lanes] = grown.reshape(rows, cols, 256)
         if last:
             copy = pltpu.make_async_copy(
@@ -371,8 +404,9 @@
         for copy in copies:
             copy.wait()
         return
+    ocean = jnp.concatenate(new, axis=0)
     send_parts(
-        plan, section, even, waves_out, new, total, permute_t[...], packed_out, sec_out, lat_out
+        plan, section, even, waves_out, ocean, total, permute_t[...], packed_out, sec_out, lat_out
     )
 
 
@@ -410,9 +444,10 @@
         ]
         return got, lax.ppermute(sent[-2], axes[0], near), lax.ppermute(sent[-1], axes[0], far)
 
-    waves, ocean, permute, permute_t, turn, sea, keep, stokes, rates, grow, packed, *sent = call(
+    waves, ocean, permute, permute_t, turn, turn_edge, sea, keep, stokes, rates, grow, packed, *sent = call(
         functools.partial(first_kernel, plan, axes),
-        [field, state, square, square, state, state, shape((8, LANES), F32)]
+        [field, state, square, square, state, shape((2 * rows, LANES), F32), state]
+        + [shape((8, LANES), F32)]
         + [shape(table.shape, table.dtype) for table in tables]
         + [state]
         + messages,
@@ -441,40 +476,36 @@
     for step in range(STEPS):
         last = step == STEPS - 1
         got, near, far = exchange(sent)
-        turned, spin = call(
-            functools.partial(move_kernel, plan, axes),
-            [field, state],
-            [edge, edge],
-            waves,
-            ocean,
-            turn,
-            rates,
-            *[message for message, edged in zip(got, plan.edges) if edged],
-            near,
-            far,
+        (turned,) = call(
+            functools.partial(move_kernel, plan, axes), [field], [], waves, turn, rates, near, far
         )
         result = call(
             functools.partial(couple_kernel, plan, axes, last),
             [field, shape(currents.shape, F32)] if last else [field, state, state] + messages,
-            [
-                coupled,
-                pltpu.VMEM(spectra.shape, F32),
-                pltpu.VMEM(currents.shape, F32),
-                pltpu.SemaphoreType.DMA((1 + spans,)),
-            ]
-            if last
-            else [coupled],
+            [coupled, edge, edge]
+            + (
+                [
+                    pltpu.VMEM(spectra.shape, F32),
+                    pltpu.VMEM(currents.shape, F32),
+                    pltpu.SemaphoreType.DMA((1 + spans,)),
+                ]
+                if last
+                else []
+            ),
             turned,
-            spin,
             ocean,
             packed,
             permute,
             permute_t,
+            turn_edge,
             sea,
             keep,
             stokes,
+            rates,
             grow,
             *got,
+            near,
+            far,
             space_out=pltpu.HBM if last else pltpu.VMEM,
         )
         waves, ocean = result[:2]

time: 33.2 us -> 32.6 us (0.982)
  waiting for transfers between devices: 4.7 us -> 4.18 us
    ppermute x9, waiting for transfers between devices: 4.68 us -> 4.17 us  [exchange(): lax.ppermute(message, axes[1], list(enumerate(table)))]
  transfers between devices with their start and end apart: 15 -> 15, of which waited for: 5 -> 3; matrix products, arithmetic and copies ran while one was open for 0% -> 0% of each run, Pallas kernels for 6% -> 5%
where the time goes in v5:
time: 32.6 us; the launch traced here: 32.4 us
  starting transfers between devices  20.9 us (64%)
  Pallas kernels  6.59 us (20%)
  waiting for transfers between devices  4.18 us (13%)
  between operations  0.72 us (2%)
    ppermute x3, starting transfers between devices, exchange(): lax.ppermute(sent[-1], axes[0], far)  12.5 us
    ppermute x9, starting transfers between devices, exchange(): lax.ppermute(message, axes[1], list(enumerate(table)))  8.14 us
    pallas_call x7, Pallas kernels, call(): pl.pallas_call(kernel, out_shape=outs, in_specs=[pl.BlockSpec(memory_spac...  6.59 us
    ppermute x9, waiting for transfers between devices, exchange(): lax.ppermute(message, axes[1], list(enumerate(table)))  4.17 us
  transfers between devices with their start and end apart: 15, of which 3 were waited for; matrix products, arithmetic and copies ran while one was open for 0% of the time, Pallas kernels for 5%

profile of v5, /device:TPU:1, one launch (start us, length us, event | category | flops | bytes accessed | tf_op | source)
XLA Modules:
  0.0 32.4 jit_solution(14922714110753786669)
XLA Ops:
  0.6 1.7 %shard_map.104 = (f32[4,24,768]{2,1,0:T(8,128)S(1)}, f32[96,128]{1,0:T(8,128)S(1)}, bf16[96,96]{1,0:T(8,128)(2,1)S(1)}, bf16[96,96]{1,0:T(8,128)(2,1)S(1)}, f32[...) custom-call(f32[4,24,768]{2,1,0:T(8,128)} %refs_0_.1, ...), custom_call_target="tpu_custom_call" | custom-call | tf_op jit(solution)/shard_map/pallas_call | solution.py:429
  2.3 0.1 collective-permute-start
  2.5 4.6 %collective-permute-start.1 = (f32[24,512]{1,0:T(8,128)S(1)}, f32[24,512]{1,0:T(8,128)S(1)}, u32[]{:S(2)}, u32[]{:S(2)}) collective-permute-start(f32[24,512]{1,0:T(8,128)S(1)} %get-tuple-element.39), channel_id=1, source_target_pairs={{1,2},{2,1},{3,4},{4,3},{5,6},{6,5},{9,10},{10,9},{11,12},{12,11},... | collective-permute-start | bytes 147464 | tf_op jit(solution)/shard_map/ppermute | solution.py:445
  7.0 2.2 %collective-permute-start.2 = (f32[56,128]{1,0:T(8,128)S(1)}, f32[56,128]{1,0:T(8,128)S(1)}, u32[]{:S(2)}, u32[]{:S(2)}) collective-permute-start(f32[56,128]{1,0:T(8,128)S(1)} %get-tuple-element.49), channel_id=1, source_target_pairs={{0,24},{8,16},{16,8},{24,0},{1,25},{9,17},{17,9},{25,1},{2,26},{10... | collective-permute-start | bytes 86024 | tf_op jit(solution)/shard_map/ppermute | solution.py:442
  9.2 0.3 collective-permute-start.3
  9.5 0.2 collective-permute-start.4
  9.7 0.0 collective-permute-done.1.refs_4_.refs_15_
  9.7 0.6 %shard_map.105.refs_0_ = f32[4,24,768]{2,1,0:T(8,128)S(1)} custom-call(f32[4,24,768]{2,1,0:T(8,128)S(1)} %get-tuple-element.35.refs_0_, f32[96,128]{1,0:T(8,128)S(1)} %get-tuple-element.36.refs_1_, f32[8,768]{1,0:T(8,128)S(1)} %get-tuple-element.37.refs_2_.refs_9_, f32[24,512]{1,0:T(8,128)S(1)} %collective-permute-done.refs_3_.refs_14_, ...), custom_call_target="tpu_custom_call" | custom-call | tf_op jit(solution)/shard_map/pallas_call | solution.py:429
  10.3 1.7 %collective-permute-done.4.refs_13_ = f32[24,128]{1,0:T(8,128)S(1)} collective-permute-done((f32[24,128]{1,0:T(8,128)S(1)}, f32[24,128]{1,0:T(8,128)S(1)}, u32[]{:S(2)}, u32[]{:S(2)}) %collective-permute-start.4) | collective-permute-done | bytes 12320 | tf_op jit(solution)/shard_map/ppermute | solution.py:442
  12.0 0.0 collective-permute-done.2.refs_11_
  12.1 0.0 collective-permute-done.3.refs_12_
  12.1 1.0 %shard_map.106 = (f32[4,24,768]{2,1,0:T(8,128)S(1)}, f32[96,128]{1,0:T(8,128)S(1)}, f32[96,128]{1,0:T(8,128)S(1)}, f32[56,128]{1,0:T(8,128)S(1)}, f32[56,128]{1,...) custom-call(f32[4,24,768]{2,1,0:T(8,128)S(1)} %shard_map.105.refs_0_, ...), custom_call_target="tpu_custom_call" | custom-call | tf_op jit(solution)/shard_map/pallas_call | solution.py:429
  13.1 0.1 collective-permute-start.5
  13.2 4.2 %collective-permute-start.6 = (f32[24,512]{1,0:T(8,128)S(1)}, f32[24,512]{1,0:T(8,128)S(1)}, u32[]{:S(2)}, u32[]{:S(2)}) collective-permute-start(f32[24,512]{1,0:T(8,128)S(1)} %get-tuple-element.54), channel_id=1, source_target_pairs={{1,2},{2,1},{3,4},{4,3},{5,6},{6,5},{9,10},{10,9},{11,12},{12,11},... | collective-permute-start | bytes 147464 | tf_op jit(solution)/shard_map/ppermute | solution.py:445
  17.3 1.2 %collective-permute-start.7 = (f32[56,128]{1,0:T(8,128)S(1)}, f32[56,128]{1,0:T(8,128)S(1)}, u32[]{:S(2)}, u32[]{:S(2)}) collective-permute-start(f32[56,128]{1,0:T(8,128)S(1)} %get-tuple-element.57), channel_id=1, source_target_pairs={{0,24},{8,16},{16,8},{24,0},{1,25},{9,17},{17,9},{25,1},{2,26},{10... | collective-permute-start | bytes 86024 | tf_op jit(solution)/shard_map/ppermute | solution.py:442
  18.6 0.1 collective-permute-start.8
  18.7 1.4 %collective-permute-start.9 = (f32[24,128]{1,0:T(8,128)S(1)}, f32[24,128]{1,0:T(8,128)S(1)}, u32[]{:S(2)}, u32[]{:S(2)}) collective-permute-start(f32[24,128]{1,0:T(8,128)S(1)} %get-tuple-element.59), channel_id=1, source_target_pairs={{0,16},{8,24},{16,0},{24,8},{1,17},{9,25},{17,1},{25,9},{2,18},{10... | collective-permute-start | bytes 36872 | tf_op jit(solution)/shard_map/ppermute | solution.py:442
  20.1 0.6 %shard_map.107.refs_0_ = f32[4,24,768]{2,1,0:T(8,128)S(1)} custom-call(f32[4,24,768]{2,1,0:T(8,128)S(1)} %get-tuple-element.52.refs_0_, f32[96,128]{1,0:T(8,128)S(1)} %get-tuple-element.36.refs_1_, f32[8,768]{1,0:T(8,128)S(1)} %get-tuple-element.37.refs_2_.refs_9_, f32[24,512]{1,0:T(8,128)S(1)} %collective-permute-done.5.refs_3_.refs_14_, ...), custom_call_target="tpu_custom_call" | custom-call | tf_op jit(solution)/shard_map/pallas_call | solution.py:429
  20.6 0.6 %collective-permute-done.9.refs_13_ = f32[24,128]{1,0:T(8,128)S(1)} collective-permute-done((f32[24,128]{1,0:T(8,128)S(1)}, f32[24,128]{1,0:T(8,128)S(1)}, u32[]{:S(2)}, u32[]{:S(2)}) %collective-permute-start.9) | collective-permute-done | bytes 12320 | tf_op jit(solution)/shard_map/ppermute | solution.py:442
  21.2 0.0 collective-permute-done.7.refs_11_
  21.2 0.0 collective-permute-done.8.refs_12_
  21.3 1.0 %shard_map.108 = (f32[4,24,768]{2,1,0:T(8,128)S(1)}, f32[96,128]{1,0:T(8,128)S(1)}, f32[96,128]{1,0:T(8,128)S(1)}, f32[56,128]{1,0:T(8,128)S(1)}, f32[56,128]{1,...) custom-call(f32[4,24,768]{2,1,0:T(8,128)S(1)} %shard_map.107.refs_0_, ...), custom_call_target="tpu_custom_call" | custom-call | tf_op jit(solution)/shard_map/pallas_call | solution.py:429
  22.3 0.1 collective-permute-start.10
  22.4 3.8 %collective-permute-start.11 = (f32[24,512]{1,0:T(8,128)S(1)}, f32[24,512]{1,0:T(8,128)S(1)}, u32[]{:S(2)}, u32[]{:S(2)}) collective-permute-start(f32[24,512]{1,0:T(8,128)S(1)} %get-tuple-element.62), channel_id=1, source_target_pairs={{1,2},{2,1},{3,4},{4,3},{5,6},{6,5},{9,10},{10,9},{11,12},{12,11},... | collective-permute-start | bytes 147464 | tf_op jit(solution)/shard_map/ppermute | solution.py:445
  26.2 2.3 %collective-permute-start.12 = (f32[56,128]{1,0:T(8,128)S(1)}, f32[56,128]{1,0:T(8,128)S(1)}, u32[]{:S(2)}, u32[]{:S(2)}) collective-permute-start(f32[56,128]{1,0:T(8,128)S(1)} %get-tuple-element.65), channel_id=1, source_target_pairs={{0,24},{8,16},{16,8},{24,0},{1,25},{9,17},{17,9},{25,1},{2,26},{10... | collective-permute-start | bytes 86024 | tf_op jit(solution)/shard_map/ppermute | solution.py:442
  28.4 0.3 collective-permute-start.13
  28.7 0.2 collective-permute-start.14
  28.9 0.0 collective-permute-done.10.refs_3_.refs_14_
  28.9 0.0 collective-permute-done.11.refs_4_.refs_15_
  28.9 0.6 %shard_map.109.refs_0_ = f32[4,24,768]{2,1,0:T(8,128)S(1)} custom-call(f32[4,24,768]{2,1,0:T(8,128)S(1)} %get-tuple-element.60.refs_0_, f32[96,128]{1,0:T(8,128)S(1)} %get-tuple-element.36.refs_1_, f32[8,768]{1,0:T(8,128)S(1)} %get-tuple-element.37.refs_2_.refs_9_, f32[24,512]{1,0:T(8,128)S(1)} %collective-permute-done.10.refs_3_.refs_14_, ...), custom_call_target="tpu_custom_call" | custom-call | tf_op jit(solution)/shard_map/pallas_call | solution.py:429
  29.5 1.8 %collective-permute-done.14.refs_13_ = f32[24,128]{1,0:T(8,128)S(1)} collective-permute-done((f32[24,128]{1,0:T(8,128)S(1)}, f32[24,128]{1,0:T(8,128)S(1)}, u32[]{:S(2)}, u32[]{:S(2)}) %collective-permute-start.14) | collective-permute-done | bytes 12320 | tf_op jit(solution)/shard_map/ppermute | solution.py:442
  31.3 1.1 %shard_map.110 = (f32[4,24,768]{2,1,0:T(8,128)}, f32[4,24,64]{2,1,0:T(8,128)}) custom-call(f32[4,24,768]{2,1,0:T(8,128)S(1)} %shard_map.109.refs_0_, f32[96,128]{1,0:T(8,128)S(1)} %get-tuple-element.63.refs_1_, f32[96,128]{1,0:T(8,128)S(1)} %get-tuple-element.64.refs_2_, bf16[96,96]{1,0:T(8,128)(2,1)S(1)} %get-tuple-element.42.refs_3_, ...), custom_call_target="tpu_custom_call" | custom-call | tf_op jit(solution)/shard_map/pallas_call | solution.py:429
  (5 shorter events, 0.0 us)
Async XLA Ops:
  2.3 7.4 %collective-permute-start = (f32[24,512]{1,0:T(8,128)S(1)}, f32[24,512]{1,0:T(8,128)S(1)}, u32[]{:S(2)}, u32[]{:S(2)}) collective-permute-start(f32[24,512]{1,0:T(8,128)S(1)} %get-tuple-element.38), channel_id=1, source_target_pairs={{0,1},{1,0},{2,3},{3,2},{4,5},{5,4},{6,7},{7,6},{8,9},{9,8},{10,11... | collective-permute-start | bytes 147464 | tf_op jit(solution)/shard_map/ppermute | solution.py:445
  2.5 7.3 %collective-permute-start.1 = (f32[24,512]{1,0:T(8,128)S(1)}, f32[24,512]{1,0:T(8,128)S(1)}, u32[]{:S(2)}, u32[]{:S(2)}) collective-permute-start(f32[24,512]{1,0:T(8,128)S(1)} %get-tuple-element.39), channel_id=1, source_target_pairs={{1,2},{2,1},{3,4},{4,3},{5,6},{6,5},{9,10},{10,9},{11,12},{12,11},... | collective-permute-start | bytes 147464 | tf_op jit(solution)/shard_map/ppermute | solution.py:445
  7.0 5.0 %collective-permute-start.2 = (f32[56,128]{1,0:T(8,128)S(1)}, f32[56,128]{1,0:T(8,128)S(1)}, u32[]{:S(2)}, u32[]{:S(2)}) collective-permute-start(f32[56,128]{1,0:T(8,128)S(1)} %get-tuple-element.49), channel_id=1, source_target_pairs={{0,24},{8,16},{16,8},{24,0},{1,25},{9,17},{17,9},{25,1},{2,26},{10... | collective-permute-start | bytes 86024 | tf_op jit(solution)/shard_map/ppermute | solution.py:442
  9.2 2.8 %collective-permute-start.3 = (f32[56,128]{1,0:T(8,128)S(1)}, f32[56,128]{1,0:T(8,128)S(1)}, u32[]{:S(2)}, u32[]{:S(2)}) collective-permute-start(f32[56,128]{1,0:T(8,128)S(1)} %get-tuple-element.50), channel_id=1, source_target_pairs={{0,8},{8,0},{16,24},{24,16},{1,9},{9,1},{17,25},{25,17},{2,10},{10... | collective-permute-start | bytes 86024 | tf_op jit(solution)/shard_map/ppermute | solution.py:442
  9.5 2.5 %collective-permute-start.4 = (f32[24,128]{1,0:T(8,128)S(1)}, f32[24,128]{1,0:T(8,128)S(1)}, u32[]{:S(2)}, u32[]{:S(2)}) collective-permute-start(f32[24,128]{1,0:T(8,128)S(1)} %get-tuple-element.51), channel_id=1, source_target_pairs={{0,16},{8,24},{16,0},{24,8},{1,17},{9,25},{17,1},{25,9},{2,18},{10... | collective-permute-start | bytes 36872 | tf_op jit(solution)/shard_map/ppermute | solution.py:442
  13.1 7.0 %collective-permute-start.5 = (f32[24,512]{1,0:T(8,128)S(1)}, f32[24,512]{1,0:T(8,128)S(1)}, u32[]{:S(2)}, u32[]{:S(2)}) collective-permute-start(f32[24,512]{1,0:T(8,128)S(1)} %get-tuple-element.53), channel_id=1, source_target_pairs={{0,1},{1,0},{2,3},{3,2},{4,5},{5,4},{6,7},{7,6},{8,9},{9,8},{10,11... | collective-permute-start | bytes 147464 | tf_op jit(solution)/shard_map/ppermute | solution.py:445
  13.2 6.9 %collective-permute-start.6 = (f32[24,512]{1,0:T(8,128)S(1)}, f32[24,512]{1,0:T(8,128)S(1)}, u32[]{:S(2)}, u32[]{:S(2)}) collective-permute-start(f32[24,512]{1,0:T(8,128)S(1)} %get-tuple-element.54), channel_id=1, source_target_pairs={{1,2},{2,1},{3,4},{4,3},{5,6},{6,5},{9,10},{10,9},{11,12},{12,11},... | collective-permute-start | bytes 147464 | tf_op jit(solution)/shard_map/ppermute | solution.py:445
  17.3 3.9 %collective-permute-start.7 = (f32[56,128]{1,0:T(8,128)S(1)}, f32[56,128]{1,0:T(8,128)S(1)}, u32[]{:S(2)}, u32[]{:S(2)}) collective-permute-start(f32[56,128]{1,0:T(8,128)S(1)} %get-tuple-element.57), channel_id=1, source_target_pairs={{0,24},{8,16},{16,8},{24,0},{1,25},{9,17},{17,9},{25,1},{2,26},{10... | collective-permute-start | bytes 86024 | tf_op jit(solution)/shard_map/ppermute | solution.py:442
  18.6 2.7 %collective-permute-start.8 = (f32[56,128]{1,0:T(8,128)S(1)}, f32[56,128]{1,0:T(8,128)S(1)}, u32[]{:S(2)}, u32[]{:S(2)}) collective-permute-start(f32[56,128]{1,0:T(8,128)S(1)} %get-tuple-element.58), channel_id=1, source_target_pairs={{0,8},{8,0},{16,24},{24,16},{1,9},{9,1},{17,25},{25,17},{2,10},{10... | collective-permute-start | bytes 86024 | tf_op jit(solution)/shard_map/ppermute | solution.py:442
  18.7 2.5 %collective-permute-start.9 = (f32[24,128]{1,0:T(8,128)S(1)}, f32[24,128]{1,0:T(8,128)S(1)}, u32[]{:S(2)}, u32[]{:S(2)}) collective-permute-start(f32[24,128]{1,0:T(8,128)S(1)} %get-tuple-element.59), channel_id=1, source_target_pairs={{0,16},{8,24},{16,0},{24,8},{1,17},{9,25},{17,1},{25,9},{2,18},{10... | collective-permute-start | bytes 36872 | tf_op jit(solution)/shard_map/ppermute | solution.py:442
  22.3 6.6 %collective-permute-start.10 = (f32[24,512]{1,0:T(8,128)S(1)}, f32[24,512]{1,0:T(8,128)S(1)}, u32[]{:S(2)}, u32[]{:S(2)}) collective-permute-start(f32[24,512]{1,0:T(8,128)S(1)} %get-tuple-element.61), channel_id=1, source_target_pairs={{0,1},{1,0},{2,3},{3,2},{4,5},{5,4},{6,7},{7,6},{8,9},{9,8},{10,11... | collective-permute-start | bytes 147464 | tf_op jit(solution)/shard_map/ppermute | solution.py:445
  22.4 6.5 %collective-permute-start.11 = (f32[24,512]{1,0:T(8,128)S(1)}, f32[24,512]{1,0:T(8,128)S(1)}, u32[]{:S(2)}, u32[]{:S(2)}) collective-permute-start(f32[24,512]{1,0:T(8,128)S(1)} %get-tuple-element.62), channel_id=1, source_target_pairs={{1,2},{2,1},{3,4},{4,3},{5,6},{6,5},{9,10},{10,9},{11,12},{12,11},... | collective-permute-start | bytes 147464 | tf_op jit(solution)/shard_map/ppermute | solution.py:445
  26.2 5.1 %collective-permute-start.12 = (f32[56,128]{1,0:T(8,128)S(1)}, f32[56,128]{1,0:T(8,128)S(1)}, u32[]{:S(2)}, u32[]{:S(2)}) collective-permute-start(f32[56,128]{1,0:T(8,128)S(1)} %get-tuple-element.65), channel_id=1, source_target_pairs={{0,24},{8,16},{16,8},{24,0},{1,25},{9,17},{17,9},{25,1},{2,26},{10... | collective-permute-start | bytes 86024 | tf_op jit(solution)/shard_map/ppermute | solution.py:442
  28.4 2.8 %collective-permute-start.13 = (f32[56,128]{1,0:T(8,128)S(1)}, f32[56,128]{1,0:T(8,128)S(1)}, u32[]{:S(2)}, u32[]{:S(2)}) collective-permute-start(f32[56,128]{1,0:T(8,128)S(1)} %get-tuple-element.66), channel_id=1, source_target_pairs={{0,8},{8,0},{16,24},{24,16},{1,9},{9,1},{17,25},{25,17},{2,10},{10... | collective-permute-start | bytes 86024 | tf_op jit(solution)/shard_map/ppermute | solution.py:442
  28.7 2.5 %collective-permute-start.14 = (f32[24,128]{1,0:T(8,128)S(1)}, f32[24,128]{1,0:T(8,128)S(1)}, u32[]{:S(2)}, u32[]{:S(2)}) collective-permute-start(f32[24,128]{1,0:T(8,128)S(1)} %get-tuple-element.67), channel_id=1, source_target_pairs={{0,16},{8,24},{16,0},{24,8},{1,17},{9,25},{17,1},{25,9},{2,18},{10... | collective-permute-start | bytes 36872 | tf_op jit(solution)/shard_map/ppermute | solution.py:442

commit v6 on v5

--- a/solution.py
+++ b/solution.py
@@ -61,12 +61,6 @@
     )
 
 
-def sec_exchanges(count):
-    if count % 4 == 0:
-        return [(hop, flip) for hop in range(count // 4) for flip in (3, 1, 2, 0) if hop or flip]
-    return [(hop, 0) for hop in range(1, count)]
-
-
 class Plan:
     def __init__(self, sections, bands, rows, cols, spectral, depth):
         self.sections, self.bands = sections, bands
@@ -74,21 +68,26 @@
         self.columns = rows * cols
         self.chunk = self.columns // sections
         self.tiles = spectral // LANES
-        self.quad = 4 if sections % 4 == 0 else 1
-        self.hops = sec_exchanges(sections)
-        self.exchanges = [
-            [self.partner(i, number, divmod)[0] for i in range(sections)]
-            for number in range(len(self.hops))
+        self.edge = ((self.tiles // 2 + 1) * rows + 7) // 8 * 8
+        self.relay = sections % 4 == 0
+        self.quad = 4 if self.relay else 1
+        self.hops = [
+            (hop, flip)
+            for hop in range(1, sections // self.quad)
+            for flip in ((3, 1, 2, 0) if self.relay else (0,))
         ]
+        self.direct = [self.table(*hop) for hop in self.hops]
         self.edges = [
-            any(abs(target - i) == 1 for i, target in enumerate(table)) for table in self.exchanges
+            any(abs(target - i) == 1 for i, target in table) for table in self.direct
         ]
-        self.sec_rows = [
-            self.chunk + (self.tiles * rows + 8 if edge else 0) for edge in self.edges
-        ]
-
-    def partner(self, section, number, divide=lambda a, b: (lax.div(a, b), lax.rem(a, b))):
-        hop, flip = self.hops[number]
+        self.sizes = [self.chunk + (self.edge if edge else 0) for edge in self.edges]
+        if self.relay:
+            self.sizes = [2 * (self.chunk + self.edge), self.chunk] + self.sizes
+
+    def table(self, hop, flip):
+        return [(i, self.partner(i, hop, flip, divmod)[0]) for i in range(self.sections)]
+
+    def partner(self, section, hop, flip, divide=lambda a, b: (lax.div(a, b), lax.rem(a, b))):
         groups = self.sections // self.quad
         high, low = divide(section, self.quad)
         if flip & 1:
@@ -99,6 +98,39 @@
             divide(high + shift, groups)[1] * self.quad + low for shift in (hop, groups - hop)
         )
 
+    def received(self, section, messages):
+        parts = []
+        if self.relay:
+            from_x, from_y = messages[:2]
+            parts = [
+                (self.partner(section, 0, 1)[1], from_x, 0, self.chunk),
+                (self.partner(section, 0, 2)[1], from_y, 0, None),
+                (self.partner(section, 0, 3)[1], from_y, self.chunk, 2 * self.chunk),
+            ]
+            messages = messages[2:]
+        for message, hop, edge in zip(messages, self.hops, self.edges):
+            parts.append((self.partner(section, *hop)[1], message, 0, self.chunk if edge else None))
+        return parts
+
+    def sent(self, section, messages):
+        parts = []
+        if self.relay:
+            to_x, to_y = messages[:2]
+            parts = [
+                (self.partner(section, 0, 1)[0], to_x, 0, self.chunk),
+                (self.partner(section, 0, 2)[0], to_y, 0, None),
+                (
+                    self.partner(section, 0, 3)[0],
+                    to_x,
+                    self.chunk + self.edge,
+                    2 * self.chunk + self.edge,
+                ),
+            ]
+            messages = messages[2:]
+        for message, hop, edge in zip(messages, self.hops, self.edges):
+            parts.append((self.partner(section, *hop)[0], message, 0, self.chunk if edge else None))
+        return parts
+
 
 def lane_of(shape):
     return lax.broadcasted_iota(jnp.int32, shape, len(shape) - 1)
@@ -117,6 +149,13 @@
     high = part.astype(BF16)
     low = (part - high.astype(F32)).astype(BF16)
     return dot(jnp.concatenate([high, low], axis=0), table)
+
+
+def packed_half(edge, tile, half, ahead, forward):
+    first = edge[:, tile * LANES : (tile + 1) * LANES]
+    second = edge[:, (tile + half) * LANES : (tile + half + 1) * LANES]
+    keep = jnp.where(ahead, 1, 0) == jnp.where(forward, 1, 0)
+    return jnp.where(keep, first, pltpu.roll(second, NDIR // 2, 1))
 
 
 def send_parts(plan, section, even, waves, ocean, total, permute_t, packed_out, sec_out, lat_out):
@@ -124,36 +163,41 @@
     lane = lane_of((plan.columns, LANES))
     near, far = lat_out
     sea_rows = ocean.reshape(rows, cols, LANES)
-    low_half = lax.rem(lane_of((cols, LANES)), NDIR) < NDIR // 2
+    half = tiles // 2
+    masks = Directions((cols, LANES))
     for out, northward in ((far, jnp.logical_not(even)), (near, even)):
         edge = jnp.where(northward, waves[rows - 1], waves[0])
-        for tile in range(tiles // 2):
-            first = edge[:, tile * LANES : (tile + 1) * LANES]
-            second = edge[:, (tile + tiles // 2) * LANES : (tile + tiles // 2 + 1) * LANES]
-            up = jnp.where(low_half, first, pltpu.roll(second, NDIR // 2, 1))
-            down = jnp.where(low_half, pltpu.roll(second, LANES - NDIR // 2, 1), first)
-            out[:, tile * LANES : (tile + 1) * LANES] = jnp.where(northward, up, down)
+        for tile in range(half):
+            out[:, tile * LANES : (tile + 1) * LANES] = packed_half(
+                edge, tile, half, masks.northward, northward
+            )
         out[:, plan.spectral // 2 :] = jnp.where(northward, sea_rows[rows - 1], sea_rows[0])
     moments = total[: plan.columns] + total[plan.columns :]
     moments = moments + pltpu.roll(moments, LANES // 2, 1)
     ordered = dot(permute_t, split_value(moments))
     ordered = ordered + pltpu.roll(ordered, LANES // 2, 1)
     packed_out[...] = jnp.where(lane < LANES // 2, ocean, ordered)
-    for number, out in enumerate(sec_out):
-        target, _ = plan.partner(section, number)
-        out[0:chunk, :] = packed_out[pl.ds(pl.multiple_of(target * chunk, 8), chunk), :]
-        if not plan.edges[number]:
+    for target, out, at, edge_at in plan.sent(section, sec_out):
+        out[at : at + chunk, :] = packed_out[pl.ds(pl.multiple_of(target * chunk, 8), chunk), :]
+        if edge_at is None:
             continue
         eastward = target == section + 1
         for row in range(rows):
             edge = jnp.where(eastward, waves[row, cols - 1 : cols, :], waves[row, 0:1, :])
-            for tile in range(tiles):
-                place = chunk + tile * rows + row
-                out[place : place + 1, :] = edge[:, tile * LANES : (tile + 1) * LANES]
-            place = chunk + tiles * rows + row
+            for tile in range(half):
+                place = edge_at + tile * rows + row
+                out[place : place + 1, :] = packed_half(
+                    edge, tile, half, masks.eastward[0:1, :], eastward
+                )
+            place = edge_at + half * rows + row
             out[place : place + 1, :] = jnp.where(
                 eastward, sea_rows[row, cols - 1 : cols, :], sea_rows[row, 0:1, :]
             )
+
+
+def relay_kernel(plan, from_x, to_y, out):
+    out[0 : plan.chunk, :] = to_y[...]
+    out[plan.chunk :, :] = from_x[plan.chunk + plan.edge :, :]
 
 
 def first_kernel(plan, axes, *refs):
@@ -161,7 +205,7 @@
     tables_in, refs = refs[6:9], refs[9:]
     waves, ocean_out, permute_out, permute_t_out, turn_out, turn_edge_out = refs[:6]
     sea_out, keep_out, tables_out, packed_out, refs = refs[6], refs[7], refs[8:11], refs[11], refs[12:]
-    count = len(plan.exchanges)
+    count = len(plan.sizes)
     sec_out, lat_out, refs = refs[:count], refs[count : count + 2], refs[count + 2 :]
     turning, currents, drag, mask, target, done = refs
     pairs = [
@@ -267,7 +311,7 @@
         north_edge = jnp.where(even, near[:, half], far[:, half])
         if tile >= tiles // 2:
             south_edge = pltpu.roll(south_edge, LANES - NDIR // 2, 1)
-            north_edge = pltpu.roll(north_edge, NDIR // 2, 1)
+            north_edge = pltpu.roll(north_edge, LANES - NDIR // 2, 1)
         for row in range(rows):
             center = waves[row, :, lanes]
             south = waves[row - 1, :, lanes] if row else south_edge
@@ -293,7 +337,7 @@
 def couple_kernel(plan, axes, last, *refs):
     turned, ocean_in, packed_in, permute, permute_t, turn_edge, sea, keep = refs[:8]
     stokes, rates, grow, refs = refs[8], refs[9], refs[10], refs[11:]
-    count = len(plan.exchanges)
+    count = len(plan.sizes)
     sec_in, near, far, refs = refs[:count], refs[count], refs[count + 1], refs[count + 2 :]
     if last:
         waves_far, ocean_far, coupled, west_edge, east_edge, waves_out, ocean_out, done = refs
@@ -309,18 +353,18 @@
     coupled[own, :] = packed_in[own, :]
     west_edge[...] = jnp.zeros_like(west_edge)
     east_edge[...] = jnp.zeros_like(east_edge)
-    for number, message in enumerate(sec_in):
-        _, source = plan.partner(section, number)
-        coupled[pl.ds(pl.multiple_of(source * chunk, 8), chunk), :] = message[0:chunk, :]
-        if plan.edges[number]:
-
-            @pl.when(source == section + 1)
-            def _():
-                east_edge[...] = message[chunk:, :]
-
-            @pl.when(source == section - 1)
-            def _():
-                west_edge[...] = message[chunk:, :]
+    for source, message, at, edge_at in plan.received(section, sec_in):
+        coupled[pl.ds(pl.multiple_of(source * chunk, 8), chunk), :] = message[at : at + chunk, :]
+        if edge_at is None:
+            continue
+
+        @pl.when(source == section + 1)
+        def _():
+            east_edge[...] = message[edge_at : edge_at + plan.edge, :]
+
+        @pl.when(source == section - 1)
+        def _():
+            west_edge[...] = message[edge_at : edge_at + plan.edge, :]
 
     arrived = coupled[...]
     other = pltpu.roll(arrived, LANES // 2, 1)
@@ -335,8 +379,11 @@
     extra = []
     for tile in range(tiles):
         lanes = slice(tile * LANES, (tile + 1) * LANES)
-        edge = slice(tile * rows, (tile + 1) * rows)
+        edge = tile % (tiles // 2)
+        edge = slice(edge * rows, (edge + 1) * rows)
         came = jnp.concatenate([west_edge[edge, :], east_edge[edge, :]], axis=0)
+        if tile >= tiles // 2:
+            came = pltpu.roll(came, LANES - NDIR // 2, 1)
         moved = rates[1:2, lanes] * jnp.where(reached, came, 0.0)
         extra.append(masks.turned(moved, turn_edge[...], rates[3:4, lanes]))
 
@@ -350,7 +397,7 @@
     new = []
     for row in range(rows):
         flat = slice(row * cols, (row + 1) * cols)
-        edge = slice(tiles * rows + row, tiles * rows + row + 1)
+        edge = slice(tiles // 2 * rows + row, tiles // 2 * rows + row + 1)
         center = ocean_in[flat, :]
         west = jnp.where(at_west, west_edge[edge, :], pltpu.roll(center, 1, 0))
         east = jnp.where(at_east, east_edge[edge, :], pltpu.roll(center, cols - 1, 0))
@@ -415,13 +462,13 @@
     columns, rows, cols, spectral = plan.columns, plan.rows, plan.cols, plan.spectral
     shape = jax.ShapeDtypeStruct
     params = pltpu.CompilerParams(vmem_limit_bytes=32 * 1024 * 1024)
-    messages = [shape((size, LANES), F32) for size in plan.sec_rows] + [
+    messages = [shape((size, LANES), F32) for size in plan.sizes] + [
         shape((cols, spectral // 2 + LANES), F32)
     ] * 2
     state = shape((columns, LANES), F32)
     field = shape(spectra.shape, F32)
     square = shape((columns, columns), BF16)
-    edge = pltpu.VMEM((plan.tiles * rows + 8, LANES), F32)
+    edge = pltpu.VMEM((plan.edge, LANES), F32)
     coupled = pltpu.VMEM((columns, LANES), F32)
     spans = spectral // 256
 
@@ -438,11 +485,26 @@
     def exchange(sent):
         near = [(i, i ^ 1) for i in range(plan.bands) if i ^ 1 < plan.bands]
         far = [(i, ((i + 1) ^ 1) - 1) for i in range(1, plan.bands) if ((i + 1) ^ 1) - 1 < plan.bands]
-        got = [
-            lax.ppermute(message, axes[1], list(enumerate(table)))
-            for message, table in zip(sent, plan.exchanges)
+        sent, near_out, far_out = sent[:-2], sent[-2], sent[-1]
+        got = []
+        if plan.relay:
+            to_x, to_y, *sent = sent
+            got.append(lax.ppermute(to_x, axes[1], plan.table(0, 1)))
+        far_in = lax.ppermute(far_out, axes[0], far)
+        near_in = lax.ppermute(near_out, axes[0], near)
+        if plan.relay:
+            (to_y,) = call(
+                functools.partial(relay_kernel, plan),
+                [shape((2 * plan.chunk + plan.edge, LANES), F32)],
+                [],
+                got[0],
+                to_y,
+            )
+            got.append(lax.ppermute(to_y, axes[1], plan.table(0, 2)))
+        got += [
+            lax.ppermute(message, axes[1], table) for message, table in zip(sent, plan.direct)
         ]
-        return got, lax.ppermute(sent[-2], axes[0], near), lax.ppermute(sent[-1], axes[0], far)
+        return got, near_in, far_in
 
     waves, ocean, permute, permute_t, turn, turn_edge, sea, keep, stokes, rates, grow, packed, *sent = call(
         functools.partial(first_kernel, plan, axes),

time: 32.6 us -> 31.1 us (0.954)
  starting transfers between devices: 20.9 us -> 19.7 us
  waiting for transfers between devices: 4.18 us -> 3.68 us
    ppermute x15 -> x12, starting transfers between devices: 20.9 us -> 19.7 us  [the longest x3 9.25 us: exchange(): far_in = lax.ppermute(far_out, axes[0], far)]
    ppermute x15 -> x12, waiting for transfers between devices: 4.18 us -> 3.68 us  [the longest x3 3.66 us: exchange(): far_in = lax.ppermute(far_out, axes[0], far)]
    pallas_call x7 -> x10, Pallas kernels: 6.59 us -> 6.62 us  [call(): pl.pallas_call(kernel, out_shape=outs, in_specs=[pl.BlockSpec(memory_spac...]
  transfers between devices with their start and end apart: 15 -> 12, of which waited for: 3 -> 3; matrix products, arithmetic and copies ran while one was open for 0% -> 0% of each run, Pallas kernels for 5% -> 6%
where the time goes in v6:
time: 31.1 us; the launch traced here: 30.8 us
  starting transfers between devices  19.7 us (63%)
  Pallas kernels  6.62 us (21%)
  waiting for transfers between devices  3.68 us (12%)
  between operations  0.78 us (3%)
    ppermute x3, starting transfers between devices, exchange(): far_in = lax.ppermute(far_out, axes[0], far)  9.25 us
    pallas_call x10, Pallas kernels, call(): pl.pallas_call(kernel, out_shape=outs, in_specs=[pl.BlockSpec(memory_spac...  6.62 us
    ppermute x3, starting transfers between devices, exchange(): near_in = lax.ppermute(near_out, axes[0], near)  4.17 us
    ppermute x3, starting transfers between devices, exchange(): got.append(lax.ppermute(to_y, axes[1], plan.table(0, 2)))  3.91 us
    ppermute x3, waiting for transfers between devices, exchange(): far_in = lax.ppermute(far_out, axes[0], far)  3.66 us
    ppermute x3, starting transfers between devices, exchange(): got.append(lax.ppermute(to_x, axes[1], plan.table(0, 1)))  2.4 us
  transfers between devices with their start and end apart: 12, of which 3 were waited for; matrix products, arithmetic and copies ran while one was open for 0% of the time, Pallas kernels for 6%

profile of v6, /device:TPU:1, one launch (start us, length us, event | category | flops | bytes accessed | tf_op | source)
XLA Modules:
  0.0 30.8 jit_solution(8356044545052451622)
XLA Ops:
  0.6 1.7 %shard_map.104 = (f32[4,24,768]{2,1,0:T(8,128)S(1)}, f32[96,128]{1,0:T(8,128)S(1)}, bf16[96,96]{1,0:T(8,128)(2,1)S(1)}, bf16[96,96]{1,0:T(8,128)(2,1)S(1)}, f32[...) custom-call(f32[4,24,768]{2,1,0:T(8,128)} %refs_0_.1, ...), custom_call_target="tpu_custom_call" | custom-call | tf_op jit(solution)/shard_map/pallas_call | solution.py:476
  2.3 2.1 %collective-permute-start.2 = (f32[80,128]{1,0:T(8,128)S(1)}, f32[80,128]{1,0:T(8,128)S(1)}, u32[]{:S(2)}, u32[]{:S(2)}) collective-permute-start(f32[80,128]{1,0:T(8,128)S(1)} %get-tuple-element.46), channel_id=1, source_target_pairs={{0,8},{8,0},{16,24},{24,16},{1,9},{9,1},{17,25},{25,17},{2,10},{10... | collective-permute-start | bytes 122888 | tf_op jit(solution)/shard_map/ppermute | solution.py:492
  4.4 1.0 %collective-permute-start = (f32[24,512]{1,0:T(8,128)S(1)}, f32[24,512]{1,0:T(8,128)S(1)}, u32[]{:S(2)}, u32[]{:S(2)}) collective-permute-start(f32[24,512]{1,0:T(8,128)S(1)} %get-tuple-element.35), channel_id=1, source_target_pairs={{0,1},{1,0},{2,3},{3,2},{4,5},{5,4},{6,7},{7,6},{8,9},{9,8},{10,11... | collective-permute-start | bytes 147464 | tf_op jit(solution)/shard_map/ppermute | solution.py:494
  5.4 3.1 %collective-permute-start.1 = (f32[24,512]{1,0:T(8,128)S(1)}, f32[24,512]{1,0:T(8,128)S(1)}, u32[]{:S(2)}, u32[]{:S(2)}) collective-permute-start(f32[24,512]{1,0:T(8,128)S(1)} %get-tuple-element.36), channel_id=1, source_target_pairs={{1,2},{2,1},{3,4},{4,3},{5,6},{6,5},{9,10},{10,9},{11,12},{12,11},... | collective-permute-start | bytes 147464 | tf_op jit(solution)/shard_map/ppermute | solution.py:493
  8.5 0.0 collective-permute-done.2.from_x.refs_11_
  8.5 1.3 %collective-permute-start.3 = (f32[64,128]{1,0:T(8,128)S(1)}, f32[64,128]{1,0:T(8,128)S(1)}, u32[]{:S(2)}, u32[]{:S(2)}) collective-permute-start(f32[64,128]{1,0:T(8,128)S(1)} %shard_map.106), channel_id=1, source_target_pairs={{0,16},{8,24},{16,0},{24,8},{1,17},{9,25},{17,1},{25,9},{2,18},{10... | collective-permute-start | bytes 98312 | tf_op jit(solution)/shard_map/ppermute | solution.py:503
  9.8 0.0 collective-permute-done.refs_3_.refs_13_
  9.8 1.1 %collective-permute-done.1.refs_4_.refs_14_ = f32[24,512]{1,0:T(8,128)S(1)} collective-permute-done((f32[24,512]{1,0:T(8,128)S(1)}, f32[24,512]{1,0:T(8,128)S(1)}, u32[]{:S(2)}, u32[]{:S(2)}) %collective-permute-start.1) | collective-permute-done | bytes 49184 | tf_op jit(solution)/shard_map/ppermute | solution.py:493
  10.9 0.6 %shard_map.105.refs_0_ = f32[4,24,768]{2,1,0:T(8,128)S(1)} custom-call(f32[4,24,768]{2,1,0:T(8,128)S(1)} %get-tuple-element.32.refs_0_, f32[96,128]{1,0:T(8,128)S(1)} %get-tuple-element.33.refs_1_, f32[8,768]{1,0:T(8,128)S(1)} %get-tuple-element.34.refs_2_.refs_9_, f32[24,512]{1,0:T(8,128)S(1)} %collective-permute-done.refs_3_.refs_13_, ...), custom_call_target="tpu_custom_call" | custom-call | tf_op jit(solution)/shard_map/pallas_call | solution.py:476
  11.5 0.0 collective-permute-done.3.refs_12_
  11.5 1.0 %shard_map.107 = (f32[4,24,768]{2,1,0:T(8,128)S(1)}, f32[96,128]{1,0:T(8,128)S(1)}, f32[96,128]{1,0:T(8,128)S(1)}, f32[80,128]{1,0:T(8,128)S(1)}, f32[24,128]{1,...) custom-call(f32[4,24,768]{2,1,0:T(8,128)S(1)} %shard_map.105.refs_0_, ...), custom_call_target="tpu_custom_call" | custom-call | tf_op jit(solution)/shard_map/pallas_call | solution.py:476
  12.6 0.1 collective-permute-start.6
  12.7 1.7 %collective-permute-start.4 = (f32[24,512]{1,0:T(8,128)S(1)}, f32[24,512]{1,0:T(8,128)S(1)}, u32[]{:S(2)}, u32[]{:S(2)}) collective-permute-start(f32[24,512]{1,0:T(8,128)S(1)} %get-tuple-element.49), channel_id=1, source_target_pairs={{0,1},{1,0},{2,3},{3,2},{4,5},{5,4},{6,7},{7,6},{8,9},{9,8},{10,11... | collective-permute-start | bytes 147464 | tf_op jit(solution)/shard_map/ppermute | solution.py:494
  14.4 3.1 %collective-permute-start.5 = (f32[24,512]{1,0:T(8,128)S(1)}, f32[24,512]{1,0:T(8,128)S(1)}, u32[]{:S(2)}, u32[]{:S(2)}) collective-permute-start(f32[24,512]{1,0:T(8,128)S(1)} %get-tuple-element.50), channel_id=1, source_target_pairs={{1,2},{2,1},{3,4},{4,3},{5,6},{6,5},{9,10},{10,9},{11,12},{12,11},... | collective-permute-start | bytes 147464 | tf_op jit(solution)/shard_map/ppermute | solution.py:493
  17.5 0.0 collective-permute-done.6.from_x.refs_11_
  17.5 1.3 %collective-permute-start.7 = (f32[64,128]{1,0:T(8,128)S(1)}, f32[64,128]{1,0:T(8,128)S(1)}, u32[]{:S(2)}, u32[]{:S(2)}) collective-permute-start(f32[64,128]{1,0:T(8,128)S(1)} %shard_map.109), channel_id=1, source_target_pairs={{0,16},{8,24},{16,0},{24,8},{1,17},{9,25},{17,1},{25,9},{2,18},{10... | collective-permute-start | bytes 98312 | tf_op jit(solution)/shard_map/ppermute | solution.py:503
  18.8 0.0 collective-permute-done.4.refs_3_.refs_13_
  18.8 1.3 %collective-permute-done.5.refs_4_.refs_14_ = f32[24,512]{1,0:T(8,128)S(1)} collective-permute-done((f32[24,512]{1,0:T(8,128)S(1)}, f32[24,512]{1,0:T(8,128)S(1)}, u32[]{:S(2)}, u32[]{:S(2)}) %collective-permute-start.5) | collective-permute-done | bytes 49184 | tf_op jit(solution)/shard_map/ppermute | solution.py:493
  20.1 0.6 %shard_map.108.refs_0_ = f32[4,24,768]{2,1,0:T(8,128)S(1)} custom-call(f32[4,24,768]{2,1,0:T(8,128)S(1)} %get-tuple-element.48.refs_0_, f32[96,128]{1,0:T(8,128)S(1)} %get-tuple-element.33.refs_1_, f32[8,768]{1,0:T(8,128)S(1)} %get-tuple-element.34.refs_2_.refs_9_, f32[24,512]{1,0:T(8,128)S(1)} %collective-permute-done.4.refs_3_.refs_13_, ...), custom_call_target="tpu_custom_call" | custom-call | tf_op jit(solution)/shard_map/pallas_call | solution.py:476
  20.7 0.0 collective-permute-done.7.refs_12_
  20.7 1.0 %shard_map.110 = (f32[4,24,768]{2,1,0:T(8,128)S(1)}, f32[96,128]{1,0:T(8,128)S(1)}, f32[96,128]{1,0:T(8,128)S(1)}, f32[80,128]{1,0:T(8,128)S(1)}, f32[24,128]{1,...) custom-call(f32[4,24,768]{2,1,0:T(8,128)S(1)} %shard_map.108.refs_0_, ...), custom_call_target="tpu_custom_call" | custom-call | tf_op jit(solution)/shard_map/pallas_call | solution.py:476
  21.7 0.2 collective-permute-start.10
  21.9 1.5 %collective-permute-start.8 = (f32[24,512]{1,0:T(8,128)S(1)}, f32[24,512]{1,0:T(8,128)S(1)}, u32[]{:S(2)}, u32[]{:S(2)}) collective-permute-start(f32[24,512]{1,0:T(8,128)S(1)} %get-tuple-element.56), channel_id=1, source_target_pairs={{0,1},{1,0},{2,3},{3,2},{4,5},{5,4},{6,7},{7,6},{8,9},{9,8},{10,11... | collective-permute-start | bytes 147464 | tf_op jit(solution)/shard_map/ppermute | solution.py:494
  23.4 3.1 %collective-permute-start.9 = (f32[24,512]{1,0:T(8,128)S(1)}, f32[24,512]{1,0:T(8,128)S(1)}, u32[]{:S(2)}, u32[]{:S(2)}) collective-permute-start(f32[24,512]{1,0:T(8,128)S(1)} %get-tuple-element.57), channel_id=1, source_target_pairs={{1,2},{2,1},{3,4},{4,3},{5,6},{6,5},{9,10},{10,9},{11,12},{12,11},... | collective-permute-start | bytes 147464 | tf_op jit(solution)/shard_map/ppermute | solution.py:493
  26.5 0.0 collective-permute-done.10.from_x.refs_11_
  26.5 1.3 %collective-permute-start.11 = (f32[64,128]{1,0:T(8,128)S(1)}, f32[64,128]{1,0:T(8,128)S(1)}, u32[]{:S(2)}, u32[]{:S(2)}) collective-permute-start(f32[64,128]{1,0:T(8,128)S(1)} %shard_map.112), channel_id=1, source_target_pairs={{0,16},{8,24},{16,0},{24,8},{1,17},{9,25},{17,1},{25,9},{2,18},{10... | collective-permute-start | bytes 98312 | tf_op jit(solution)/shard_map/ppermute | solution.py:503
  27.8 0.0 collective-permute-done.8.refs_3_.refs_13_
  27.8 1.3 %collective-permute-done.9.refs_4_.refs_14_ = f32[24,512]{1,0:T(8,128)S(1)} collective-permute-done((f32[24,512]{1,0:T(8,128)S(1)}, f32[24,512]{1,0:T(8,128)S(1)}, u32[]{:S(2)}, u32[]{:S(2)}) %collective-permute-start.9) | collective-permute-done | bytes 49184 | tf_op jit(solution)/shard_map/ppermute | solution.py:493
  29.1 0.6 %shard_map.111.refs_0_ = f32[4,24,768]{2,1,0:T(8,128)S(1)} custom-call(f32[4,24,768]{2,1,0:T(8,128)S(1)} %get-tuple-element.55.refs_0_, f32[96,128]{1,0:T(8,128)S(1)} %get-tuple-element.33.refs_1_, f32[8,768]{1,0:T(8,128)S(1)} %get-tuple-element.34.refs_2_.refs_9_, f32[24,512]{1,0:T(8,128)S(1)} %collective-permute-done.8.refs_3_.refs_13_, ...), custom_call_target="tpu_custom_call" | custom-call | tf_op jit(solution)/shard_map/pallas_call | solution.py:476
  29.6 0.0 collective-permute-done.11.refs_12_
  29.7 1.1 %shard_map.113 = (f32[4,24,768]{2,1,0:T(8,128)}, f32[4,24,64]{2,1,0:T(8,128)}) custom-call(f32[4,24,768]{2,1,0:T(8,128)S(1)} %shard_map.111.refs_0_, f32[96,128]{1,0:T(8,128)S(1)} %get-tuple-element.58.refs_1_, f32[96,128]{1,0:T(8,128)S(1)} %get-tuple-element.59.refs_2_, bf16[96,96]{1,0:T(8,128)(2,1)S(1)} %get-tuple-element.39.refs_3_, ...), custom_call_target="tpu_custom_call" | custom-call | tf_op jit(solution)/shard_map/pallas_call | solution.py:476
  (3 shorter events, 0.0 us)
Async XLA Ops:
  2.3 6.2 %collective-permute-start.2 = (f32[80,128]{1,0:T(8,128)S(1)}, f32[80,128]{1,0:T(8,128)S(1)}, u32[]{:S(2)}, u32[]{:S(2)}) collective-permute-start(f32[80,128]{1,0:T(8,128)S(1)} %get-tuple-element.46), channel_id=1, source_target_pairs={{0,8},{8,0},{16,24},{24,16},{1,9},{9,1},{17,25},{25,17},{2,10},{10... | collective-permute-start | bytes 122888 | tf_op jit(solution)/shard_map/ppermute | solution.py:492
  4.4 5.4 %collective-permute-start = (f32[24,512]{1,0:T(8,128)S(1)}, f32[24,512]{1,0:T(8,128)S(1)}, u32[]{:S(2)}, u32[]{:S(2)}) collective-permute-start(f32[24,512]{1,0:T(8,128)S(1)} %get-tuple-element.35), channel_id=1, source_target_pairs={{0,1},{1,0},{2,3},{3,2},{4,5},{5,4},{6,7},{7,6},{8,9},{9,8},{10,11... | collective-permute-start | bytes 147464 | tf_op jit(solution)/shard_map/ppermute | solution.py:494
  5.4 5.5 %collective-permute-start.1 = (f32[24,512]{1,0:T(8,128)S(1)}, f32[24,512]{1,0:T(8,128)S(1)}, u32[]{:S(2)}, u32[]{:S(2)}) collective-permute-start(f32[24,512]{1,0:T(8,128)S(1)} %get-tuple-element.36), channel_id=1, source_target_pairs={{1,2},{2,1},{3,4},{4,3},{5,6},{6,5},{9,10},{10,9},{11,12},{12,11},... | collective-permute-start | bytes 147464 | tf_op jit(solution)/shard_map/ppermute | solution.py:493
  8.5 3.0 %collective-permute-start.3 = (f32[64,128]{1,0:T(8,128)S(1)}, f32[64,128]{1,0:T(8,128)S(1)}, u32[]{:S(2)}, u32[]{:S(2)}) collective-permute-start(f32[64,128]{1,0:T(8,128)S(1)} %shard_map.106), channel_id=1, source_target_pairs={{0,16},{8,24},{16,0},{24,8},{1,17},{9,25},{17,1},{25,9},{2,18},{10... | collective-permute-start | bytes 98312 | tf_op jit(solution)/shard_map/ppermute | solution.py:503
  12.6 4.9 %collective-permute-start.6 = (f32[80,128]{1,0:T(8,128)S(1)}, f32[80,128]{1,0:T(8,128)S(1)}, u32[]{:S(2)}, u32[]{:S(2)}) collective-permute-start(f32[80,128]{1,0:T(8,128)S(1)} %get-tuple-element.53), channel_id=1, source_target_pairs={{0,8},{8,0},{16,24},{24,16},{1,9},{9,1},{17,25},{25,17},{2,10},{10... | collective-permute-start | bytes 122888 | tf_op jit(solution)/shard_map/ppermute | solution.py:492
  12.7 6.1 %collective-permute-start.4 = (f32[24,512]{1,0:T(8,128)S(1)}, f32[24,512]{1,0:T(8,128)S(1)}, u32[]{:S(2)}, u32[]{:S(2)}) collective-permute-start(f32[24,512]{1,0:T(8,128)S(1)} %get-tuple-element.49), channel_id=1, source_target_pairs={{0,1},{1,0},{2,3},{3,2},{4,5},{5,4},{6,7},{7,6},{8,9},{9,8},{10,11... | collective-permute-start | bytes 147464 | tf_op jit(solution)/shard_map/ppermute | solution.py:494
  14.4 5.7 %collective-permute-start.5 = (f32[24,512]{1,0:T(8,128)S(1)}, f32[24,512]{1,0:T(8,128)S(1)}, u32[]{:S(2)}, u32[]{:S(2)}) collective-permute-start(f32[24,512]{1,0:T(8,128)S(1)} %get-tuple-element.50), channel_id=1, source_target_pairs={{1,2},{2,1},{3,4},{4,3},{5,6},{6,5},{9,10},{10,9},{11,12},{12,11},... | collective-permute-start | bytes 147464 | tf_op jit(solution)/shard_map/ppermute | solution.py:493
  17.5 3.2 %collective-permute-start.7 = (f32[64,128]{1,0:T(8,128)S(1)}, f32[64,128]{1,0:T(8,128)S(1)}, u32[]{:S(2)}, u32[]{:S(2)}) collective-permute-start(f32[64,128]{1,0:T(8,128)S(1)} %shard_map.109), channel_id=1, source_target_pairs={{0,16},{8,24},{16,0},{24,8},{1,17},{9,25},{17,1},{25,9},{2,18},{10... | collective-permute-start | bytes 98312 | tf_op jit(solution)/shard_map/ppermute | solution.py:503
  21.7 4.8 %collective-permute-start.10 = (f32[80,128]{1,0:T(8,128)S(1)}, f32[80,128]{1,0:T(8,128)S(1)}, u32[]{:S(2)}, u32[]{:S(2)}) collective-permute-start(f32[80,128]{1,0:T(8,128)S(1)} %get-tuple-element.60), channel_id=1, source_target_pairs={{0,8},{8,0},{16,24},{24,16},{1,9},{9,1},{17,25},{25,17},{2,10},{10... | collective-permute-start | bytes 122888 | tf_op jit(solution)/shard_map/ppermute | solution.py:492
  21.9 5.9 %collective-permute-start.8 = (f32[24,512]{1,0:T(8,128)S(1)}, f32[24,512]{1,0:T(8,128)S(1)}, u32[]{:S(2)}, u32[]{:S(2)}) collective-permute-start(f32[24,512]{1,0:T(8,128)S(1)} %get-tuple-element.56), channel_id=1, source_target_pairs={{0,1},{1,0},{2,3},{3,2},{4,5},{5,4},{6,7},{7,6},{8,9},{9,8},{10,11... | collective-permute-start | bytes 147464 | tf_op jit(solution)/shard_map/ppermute | solution.py:494
  23.4 5.7 %collective-permute-start.9 = (f32[24,512]{1,0:T(8,128)S(1)}, f32[24,512]{1,0:T(8,128)S(1)}, u32[]{:S(2)}, u32[]{:S(2)}) collective-permute-start(f32[24,512]{1,0:T(8,128)S(1)} %get-tuple-element.57), channel_id=1, source_target_pairs={{1,2},{2,1},{3,4},{4,3},{5,6},{6,5},{9,10},{10,9},{11,12},{12,11},... | collective-permute-start | bytes 147464 | tf_op jit(solution)/shard_map/ppermute | solution.py:493
  26.5 3.2 %collective-permute-start.11 = (f32[64,128]{1,0:T(8,128)S(1)}, f32[64,128]{1,0:T(8,128)S(1)}, u32[]{:S(2)}, u32[]{:S(2)}) collective-permute-start(f32[64,128]{1,0:T(8,128)S(1)} %shard_map.112), channel_id=1, source_target_pairs={{0,16},{8,24},{16,0},{24,8},{1,17},{9,25},{17,1},{25,9},{2,18},{10... | collective-permute-start | bytes 98312 | tf_op jit(solution)/shard_map/ppermute | solution.py:503

commit v7 on v6

v7 whole, which is shorter than its diff:
```python
import functools
import math

import jax
import jax.numpy as jnp
import ml_dtypes
import numpy as np
from jax import lax
from jax.experimental import pallas as pl
from jax.experimental.pallas import tpu as pltpu
from jax.sharding import PartitionSpec as P

NFREQ = 24
NDIR = 32
STEPS = 3

stokes_scale = 0.1
ocean_dt = 0.3
current_gain = 0.2

LANES = 128
F32 = jnp.float32
BF16 = jnp.bfloat16


def split_halves(table):
    high = table.astype(ml_dtypes.bfloat16)
    low = (table - high.astype(np.float64)).astype(ml_dtypes.bfloat16)
    return high, low


def build_tables(nfreq, ndir, ndepth):
    fraction = np.arange(nfreq) / (nfreq - 1)
    angles = (np.arange(ndir) + 0.5) * (2.0 * math.pi / ndir)
    east_part, north_part = np.cos(angles), np.sin(angles)
    courant = 0.1 + 0.3 * fraction
    depth_level = 0.5 + (ndepth - 2) * (1.0 - fraction)
    weights = np.maximum(1.0 - np.abs(np.arange(ndepth)[None, :] - depth_level[:, None]), 0.0)
    mean_weights = weights / weights.sum(axis=1, keepdims=True)
    x_rate = np.abs(courant[:, None] * east_part[None, :]).reshape(-1)
    y_rate = np.abs(courant[:, None] * north_part[None, :]).reshape(-1)
    turn_gain = np.repeat(1.0 - 0.5 * fraction, ndir)
    rates = np.stack([1.0 - x_rate - y_rate, x_rate, y_rate, turn_gain] * 2).astype(np.float32)
    compass = np.stack([east_part, north_part])
    stokes = (stokes_scale * weights[:, None, None, :] * compass.T[None, :, :, None]).reshape(
        nfreq * ndir, 2 * ndepth
    )
    growth = current_gain * (1.0 + fraction)
    grow = (
        growth[None, None, :, None] * mean_weights.T[None, :, :, None] * compass[:, None, None, :]
    ).reshape(2 * ndepth, nfreq * ndir)
    stokes_high, stokes_low = split_halves(stokes)
    grow_high, grow_low = split_halves(grow)
    return (
        np.concatenate([stokes_high, stokes_low], axis=1),
        rates,
        np.concatenate([grow_high, grow_high, grow_low, grow_low], axis=0)
        .reshape(8 * ndepth, -1, LANES)
        .transpose(1, 0, 2)
        .reshape(-1, LANES),
    )


class Plan:
    def __init__(self, sections, bands, rows, cols, spectral, depth):
        self.sections, self.bands = sections, bands
        self.rows, self.cols, self.spectral, self.depth = rows, cols, spectral, depth
        self.columns = rows * cols
        self.chunk = self.columns // sections
        self.tiles = spectral // LANES
        self.edge = ((self.tiles // 2 + 1) * rows + 7) // 8 * 8
        self.relay = sections % 4 == 0
        self.quad = 4 if self.relay else 1
        self.hops = [
            (hop, flip)
            for hop in range(1, sections // self.quad)
            for flip in ((3, 1, 2, 0) if self.relay else (0,))
        ]
        self.direct = [self.table(*hop) for hop in self.hops]
        self.edges = [
            any(abs(target - i) == 1 for i, target in table) for table in self.direct
        ]
        self.sizes = [self.chunk + (self.edge if edge else 0) for edge in self.edges]
        if self.relay:
            self.sizes = [2 * (self.chunk + self.edge), self.chunk] + self.sizes

    def table(self, hop, flip):
        return [(i, self.partner(i, hop, flip, divmod)[0]) for i in range(self.sections)]

    def partner(self, section, hop, flip, divide=lambda a, b: (lax.div(a, b), lax.rem(a, b))):
        groups = self.sections // self.quad
        high, low = divide(section, self.quad)
        if flip & 1:
            low = low + 1 - 2 * divide(low, 2)[1]
        if flip & 2:
            low = low + 2 - 4 * divide(low, 2)[0]
        return tuple(
            divide(high + shift, groups)[1] * self.quad + low for shift in (hop, groups - hop)
        )

    def received(self, section, messages):
        parts = []
        if self.relay:
            from_x, from_y = messages[:2]
            parts = [
                (self.partner(section, 0, 1)[1], from_x, 0, self.chunk),
                (self.partner(section, 0, 2)[1], from_y, 0, None),
                (self.partner(section, 0, 3)[1], from_y, self.chunk, 2 * self.chunk),
            ]
            messages = messages[2:]
        for message, hop, edge in zip(messages, self.hops, self.edges):
            parts.append((self.partner(section, *hop)[1], message, 0, self.chunk if edge else None))
        return parts

    def sent(self, section, messages):
        parts = []
        if self.relay:
            to_x, to_y = messages[:2]
            parts = [
                (self.partner(section, 0, 1)[0], to_x, 0, self.chunk),
                (self.partner(section, 0, 2)[0], to_y, 0, None),
                (
                    self.partner(section, 0, 3)[0],
                    to_x,
                    self.chunk + self.edge,
                    2 * self.chunk + self.edge,
                ),
            ]
            messages = messages[2:]
        for message, hop, edge in zip(messages, self.hops, self.edges):
            parts.append((self.partner(section, *hop)[0], message, 0, self.chunk if edge else None))
        return parts


def lane_of(shape):
    return lax.broadcasted_iota(jnp.int32, shape, len(shape) - 1)


def dot(a, b):
    return jnp.dot(a, b, preferred_element_type=F32)


def split_value(value):
    high = value.astype(BF16).astype(F32)
    return jnp.where(lane_of(value.shape) < LANES // 2, high, value - high).astype(BF16)


def stokes_product(part, table):
    high = part.astype(BF16)
    low = (part - high.astype(F32)).astype(BF16)
    return dot(jnp.concatenate([high, low], axis=0), table)


def packed_half(edge, tile, half, ahead, forward):
    first = edge[:, tile * LANES : (tile + 1) * LANES]
    second = edge[:, (tile + half) * LANES : (tile + half + 1) * LANES]
    keep = jnp.where(ahead, 1, 0) == jnp.where(forward, 1, 0)
    return jnp.where(keep, first, pltpu.roll(second, NDIR // 2, 1))


def fill_lat(plan, even, waves, sea_rows, lat_out):
    half = plan.tiles // 2
    masks = Directions((plan.cols, LANES))
    near, far = lat_out
    for out, northward in ((far, jnp.logical_not(even)), (near, even)):
        edge = jnp.where(northward, waves[plan.rows - 1], waves[0])
        for tile in range(half):
            out[:, tile * LANES : (tile + 1) * LANES] = packed_half(
                edge, tile, half, masks.northward, northward
            )
        out[:, plan.spectral // 2 :] = jnp.where(northward, sea_rows[plan.rows - 1], sea_rows[0])


def fill_sections(plan, section, edges, ocean, ordered, packed_out, sec_out):
    chunk, rows, cols, half = plan.chunk, plan.rows, plan.cols, plan.tiles // 2
    lane = lane_of((plan.columns, LANES))
    packed_out[...] = jnp.where(lane < LANES // 2, ocean, ordered)
    sea_rows = ocean.reshape(rows, cols, LANES)
    masks = Directions((rows, LANES))
    for target, out, at, edge_at in plan.sent(section, sec_out):
        out[at : at + chunk, :] = packed_out[pl.ds(pl.multiple_of(target * chunk, 8), chunk), :]
        if edge_at is None:
            continue
        eastward = target == section + 1
        edge = jnp.where(eastward, edges[rows:, :], edges[:rows, :])
        for tile in range(half):
            place = edge_at + tile * rows
            out[place : place + rows, :] = packed_half(edge, tile, half, masks.eastward, eastward)
        for row in range(rows):
            place = edge_at + half * rows + row
            out[place : place + 1, :] = jnp.where(
                eastward, sea_rows[row, cols - 1 : cols, :], sea_rows[row, 0:1, :]
            )


def take_sections(plan, section, packed_in, sec_in, coupled, west_edge, east_edge):
    chunk = plan.chunk
    own = pl.ds(pl.multiple_of(section * chunk, 8), chunk)
    coupled[own, :] = packed_in[own, :]
    west_edge[...] = jnp.zeros_like(west_edge)
    east_edge[...] = jnp.zeros_like(east_edge)
    for source, message, at, edge_at in plan.received(section, sec_in):
        coupled[pl.ds(pl.multiple_of(source * chunk, 8), chunk), :] = message[at : at + chunk, :]
        if edge_at is None:
            continue

        @pl.when(source == section + 1)
        def _():
            east_edge[...] = message[edge_at : edge_at + plan.edge, :]

        @pl.when(source == section - 1)
        def _():
            west_edge[...] = message[edge_at : edge_at + plan.edge, :]


def edge_part(plan, rates, turn_edge, west_edge, east_edge):
    rows, half = plan.rows, plan.tiles // 2
    shape = (2 * rows, LANES)
    masks = Directions(shape)
    westmost = lax.broadcasted_iota(jnp.int32, shape, 0) < rows
    reached = jnp.where(masks.eastward, 1, 0) == jnp.where(westmost, 1, 0)
    parts = []
    for tile in range(plan.tiles):
        lanes = slice(tile * LANES, (tile + 1) * LANES)
        edge = slice(tile % half * rows, (tile % half + 1) * rows)
        came = jnp.concatenate([west_edge[edge, :], east_edge[edge, :]], axis=0)
        if tile >= half:
            came = pltpu.roll(came, LANES - NDIR // 2, 1)
        moved = rates[1:2, lanes] * jnp.where(reached, came, 0.0)
        parts.append(masks.turned(moved, turn_edge[...], rates[3:4, lanes]))
    return parts


def ocean_step(plan, band, even, ocean_in, stokes, near, far, west_edge, east_edge, keep, sea):
    rows, cols, half = plan.rows, plan.cols, plan.tiles // 2
    block = (cols, LANES)
    zonal = lane_of(block) < plan.depth
    place = lax.broadcasted_iota(jnp.int32, block, 0)
    at_west, at_east = place == 0, place == cols - 1
    lanes = slice(plan.spectral // 2, plan.spectral // 2 + LANES)
    south_edge = jnp.where(even, far[:, lanes], near[:, lanes])
    north_edge = jnp.where(even, near[:, lanes], far[:, lanes])
    new = []
    for row in range(rows):
        flat = slice(row * cols, (row + 1) * cols)
        edge = slice(half * rows + row, half * rows + row + 1)
        center = ocean_in[flat, :]
        west = jnp.where(at_west, west_edge[edge, :], pltpu.roll(center, 1, 0))
        east = jnp.where(at_east, east_edge[edge, :], pltpu.roll(center, cols - 1, 0))
        south = ocean_in[(row - 1) * cols : row * cols, :] if row else south_edge
        north = ocean_in[(row + 1) * cols : (row + 2) * cols, :] if row < rows - 1 else north_edge
        shear = 0.5 * jnp.where(zonal, south - north, east - west)
        y = (band * rows + row).astype(F32)
        spin = 0.2 + 0.6 * y / float(plan.bands * rows) + (shear + swapped(plan, shear))
        turn_by = ocean_dt * spin * swapped(plan, center + stokes[flat, :])
        new.append(keep[0:1, :] * (center + jnp.where(zonal, turn_by, -turn_by)) * sea[flat, :])
    return new


def twice(value, axis=1):
    return jnp.concatenate([value, value], axis=axis)


def growth_table(grow, number):
    return jnp.concatenate(
        [grow[(2 * number + k) * 256 : (2 * number + k + 1) * 256, :] for k in range(2)], axis=1
    )


def currents_twice(arrived):
    other = pltpu.roll(arrived, LANES // 2, 1)
    return jnp.where(lane_of(arrived.shape) < LANES // 2, arrived, other), other


def grown_part(plan, turned, from_edges, factor, lanes):
    rows, cols = plan.rows, plan.cols
    place = lax.broadcasted_iota(jnp.int32, (8, 256), 0)
    at_first, at_last = place == 0, place == 7
    parts = []
    for row in range(rows):
        west = jnp.where(at_first, from_edges[row : row + 1, :], 0.0)
        east = jnp.where(at_last, from_edges[rows + row : rows + row + 1, :], 0.0)
        parts += [
            turned[row, 0:8, lanes] + west,
            turned[row, 8 : cols - 8, lanes],
            turned[row, cols - 8 :, lanes] + east,
        ]
    return jnp.concatenate(parts, axis=0) * factor


def relay_kernel(plan, axes, from_x, to_y, out):
    out[0 : plan.chunk, :] = to_y[...]
    out[plan.chunk :, :] = from_x[plan.chunk + plan.edge :, :]


def first_kernel(plan, axes, *refs):
    waves_in, turning_in, currents_in, drag_in, mask_in, target_in = refs[:6]
    tables_in, refs = refs[6:9], refs[9:]
    waves, ocean_out, packed_out, permute_out, order_out, permute_edge_out, order_edge_out = refs[:7]
    turn_out, turn_edge_out, sea_out, sea_order_out, sea_edge_out, keep_out = refs[7:13]
    tables_out, refs = refs[13:16], refs[16:]
    count = len(plan.sizes)
    sec_out, lat_out, refs = refs[:count], refs[count : count + 2], refs[count + 2 :]
    turning, currents, drag, mask, target, done = refs
    pairs = [
        (target_in, target),
        (turning_in, turning),
        (mask_in, mask),
        (drag_in, drag),
        (waves_in, waves),
        (tables_in[0], tables_out[0]),
        (currents_in, currents),
        (tables_in[1], tables_out[1]),
        (tables_in[2], tables_out[2]),
    ]
    copies = [pltpu.make_async_copy(a, b, done.at[k]) for k, (a, b) in enumerate(pairs)]
    for copy in copies:
        copy.start()
    section, band = lax.axis_index(axes[1]), lax.axis_index(axes[0])
    even = lax.rem(band, 2) == 0
    columns, rows, cols = plan.columns, plan.rows, plan.cols
    across = lane_of((columns, columns))
    down = lax.broadcasted_iota(jnp.int32, (columns, columns), 0)
    here = across == down

    def row_of(ref):
        return jnp.concatenate([ref[row : row + 1, :] for row in range(rows)], axis=1)

    def column_of(row):
        spread = jnp.broadcast_to(row, (columns, columns))
        return jnp.sum(jnp.where(here, spread, jnp.zeros_like(spread)), axis=1, keepdims=True)

    def edges_of(value):
        west = [value[row * cols : row * cols + 1, :] for row in range(rows)]
        east = [value[(row + 1) * cols - 1 : (row + 1) * cols, :] for row in range(rows)]
        return jnp.concatenate(west + east, axis=0)

    for copy in copies[:4]:
        copy.wait()
    sea_row = row_of(mask).astype(F32)
    sea = column_of(sea_row)
    target_row = row_of(target).astype(F32)
    target_col = column_of(target_row)
    same = target_col == target_row
    rank_col = jnp.sum(jnp.where(same & (across < down), 1.0, 0.0), axis=1, keepdims=True)
    rank_row = jnp.sum(jnp.where(same & (down < across), 1.0, 0.0), axis=0, keepdims=True)
    slot_col = target_col * float(plan.chunk) + rank_col
    slot_row = target_row * float(plan.chunk) + rank_row
    permute = jnp.where(slot_col == across.astype(F32), sea, 0.0)
    order = jnp.where(slot_row == down.astype(F32), 1.0, 0.0)
    permute_out[...] = permute.astype(BF16)
    order_out[...] = twice(order).astype(BF16)
    sea_order = jnp.sum(order * sea_row, axis=1, keepdims=True)
    sea_order_out[...] = jnp.broadcast_to(sea_order, (columns, LANES))
    edge_count = 4 * rows
    number = lax.rem(lane_of((columns, edge_count)), 2 * rows)
    wanted = lax.rem(number, rows) * cols + lax.div(number, rows) * (cols - 1)
    chosen = lax.broadcasted_iota(jnp.int32, (columns, edge_count), 0) == wanted
    order_edge_out[...] = dot(
        order.astype(BF16), jnp.where(chosen, 1.0, 0.0).astype(BF16)
    ).astype(BF16)
    number = lax.rem(lax.broadcasted_iota(jnp.int32, (edge_count, columns), 0), 2 * rows)
    wanted = lax.rem(number, rows) * cols + lax.div(number, rows) * (cols - 1)
    chosen = lane_of((edge_count, columns)) == wanted
    permute_edge_out[...] = dot(
        jnp.where(chosen, 1.0, 0.0).astype(BF16), permute.astype(BF16)
    ).astype(BF16)
    sea_out[...] = jnp.broadcast_to(sea, (columns, LANES))
    sea_edge_out[...] = edges_of(jnp.broadcast_to(sea, (columns, LANES)))
    turn = jnp.broadcast_to(column_of(row_of(turning)), (columns, LANES))
    turn_out[...] = turn
    turn_edge_out[...] = edges_of(turn)
    keep = 1.0 - drag[...].reshape(1, plan.depth)
    blank = jnp.zeros((1, LANES - 2 * plan.depth), F32)
    keep_out[...] = jnp.broadcast_to(jnp.concatenate([keep, keep, blank], axis=1), (8, LANES))
    for copy in copies[4:7]:
        copy.wait()
    flat = currents[...].reshape(columns, 2 * plan.depth)
    ocean = jnp.concatenate([flat, jnp.zeros((columns, LANES - 2 * plan.depth), F32)], axis=1)
    ocean_out[...] = ocean
    total = None
    for start in range(0, plan.spectral, 256):
        part = waves[:, :, start : start + 256].reshape(columns, 256)
        product = stokes_product(part, tables_out[0][start : start + 256, :])
        total = product if total is None else total + product
    moments = total[:columns] + total[columns:]
    moments = moments + pltpu.roll(moments, LANES // 2, 1)
    ordered = dot(order.astype(BF16), split_value(moments))
    ordered = ordered + pltpu.roll(ordered, LANES // 2, 1)
    west = [waves[row, 0:1, :] for row in range(rows)]
    east = [waves[row, cols - 1 : cols, :] for row in range(rows)]
    edges = jnp.concatenate(west + east, axis=0)
    fill_sections(plan, section, edges, ocean, ordered, packed_out, sec_out)
    fill_lat(plan, even, waves, ocean.reshape(rows, cols, LANES), lat_out)
    for copy in copies[7:]:
        copy.wait()


class Directions:
    def __init__(self, shape):
        direction = lax.rem(lane_of(shape), NDIR)
        self.eastward = (direction < NDIR // 4) | (direction >= 3 * NDIR // 4)
        self.northward = direction < NDIR // 2
        self.first, self.final = direction == 0, direction == NDIR - 1

    def turned(self, moved, rate, gain):
        behind = jnp.where(
            self.first, pltpu.roll(moved, LANES - (NDIR - 1), 1), pltpu.roll(moved, 1, 1)
        )
        forward = jnp.where(
            self.final, pltpu.roll(moved, NDIR - 1, 1), pltpu.roll(moved, LANES - 1, 1)
        )
        return moved - jnp.abs(rate) * gain * (moved - jnp.where(rate > 0.0, behind, forward))


def move_kernel(plan, axes, *refs):
    waves, turn, rates, near, far, refs = *refs[:5], refs[5:]
    if len(refs) > 1:
        order, turned_out, edge_out, sorted_out = refs
    else:
        (turned_out,) = refs
    even = lax.rem(lax.axis_index(axes[0]), 2) == 0
    rows, cols, tiles = plan.rows, plan.cols, plan.tiles
    block = (cols, LANES)
    masks = Directions(block)
    place = lax.broadcasted_iota(jnp.int32, block, 0)
    outside = place == jnp.where(masks.eastward, 0, cols - 1)
    for tile in range(tiles):
        lanes = slice(tile * LANES, (tile + 1) * LANES)
        stay, along_x, along_y, gain = (rates[k : k + 1, lanes] for k in range(4))
        along_x = jnp.where(outside, 0.0, along_x)
        half = tile % (tiles // 2)
        half = slice(half * LANES, (half + 1) * LANES)
        south_edge = jnp.where(even, far[:, half], near[:, half])
        north_edge = jnp.where(even, near[:, half], far[:, half])
        if tile >= tiles // 2:
            south_edge = pltpu.roll(south_edge, LANES - NDIR // 2, 1)
            north_edge = pltpu.roll(north_edge, LANES - NDIR // 2, 1)
        for row in range(rows):
            center = waves[row, :, lanes]
            south = waves[row - 1, :, lanes] if row else south_edge
            north = waves[row + 1, :, lanes] if row < rows - 1 else north_edge
            moved = (
                stay * center
                + along_x
                * jnp.where(
                    masks.eastward, pltpu.roll(center, 1, 0), pltpu.roll(center, cols - 1, 0)
                )
                + along_y * jnp.where(masks.northward, south, north)
            )
            rate = turn[row * cols : (row + 1) * cols, :]
            turned = masks.turned(moved, rate, gain)
            turned_out[row, :, lanes] = turned
            if len(refs) > 1:
                edge_out[row : row + 1, lanes] = turned[0:1, :]
                edge_out[rows + row : rows + row + 1, lanes] = turned[cols - 1 : cols, :]
    if len(refs) > 1:
        for start in range(0, plan.spectral, 256):
            part = turned_out[:, :, start : start + 256].reshape(plan.columns, 256)
            high = part.astype(BF16)
            low = (part - high.astype(F32)).astype(BF16)
            sorted_out[:, start : start + 256] = dot(
                order[...], jnp.concatenate([high, low], axis=0)
            )


def swapped(plan, value):
    half = plan.depth
    zonal = lane_of(value.shape) < half
    return jnp.where(zonal, pltpu.roll(value, LANES - half, 1), pltpu.roll(value, half, 1))


def send_kernel(plan, axes, *refs):
    turned_order, turned_edge, ocean_in, packed_in, permute_edge, order_edge, turn_edge = refs[:7]
    sea, sea_order, sea_edge, keep, stokes, rates, grow = refs[7:14]
    count = len(plan.sizes)
    near, far, sec_in, refs = refs[14], refs[15], refs[16 : 16 + count], refs[16 + count :]
    ocean_out, packed_out, coupled, extra_out, sec_out = *refs[:4], refs[4 : 4 + count]
    west_edge, east_edge = refs[4 + count :]
    section, band = lax.axis_index(axes[1]), lax.axis_index(axes[0])
    even = lax.rem(band, 2) == 0
    columns, rows = plan.columns, plan.rows

    take_sections(plan, section, packed_in, sec_in, coupled, west_edge, east_edge)
    both, drift = currents_twice(coupled[...])
    in_order = twice(split_value(both * sea_order[...]))
    at_edge = twice(dot(permute_edge[...], split_value(both)).astype(BF16))
    extra = edge_part(plan, rates, turn_edge, west_edge, east_edge)
    total = None
    edges = []
    wet, wet_edge = twice(sea_order[...]), twice(sea_edge[...])
    for number, start in enumerate(range(0, plan.spectral, 256)):
        lanes = slice(start, start + 256)
        table = growth_table(grow, number)
        from_edges = jnp.concatenate(extra[2 * number : 2 * number + 2], axis=1)
        extra_out[:, lanes] = from_edges
        high = from_edges.astype(BF16).astype(F32)
        halves = jnp.concatenate([high, from_edges - high], axis=0).astype(BF16)
        turned = turned_order[:, lanes] + dot(order_edge[...], halves)
        grown = turned * (wet + dot(in_order, table))
        product = stokes_product(grown, stokes[lanes, :])
        total = product if total is None else total + product
        edges.append(
            (turned_edge[:, lanes] + from_edges)
            * (wet_edge + dot(at_edge, table)[: 2 * rows, :])
        )
    new = ocean_step(
        plan, band, even, ocean_in, drift, near, far, west_edge, east_edge, keep, sea
    )
    ocean = jnp.concatenate(new, axis=0)
    ocean_out[...] = ocean
    moments = total[:columns] + total[columns:]
    moments = moments + pltpu.roll(moments, LANES // 2, 1)
    fill_sections(
        plan, section, jnp.concatenate(edges, axis=1), ocean, moments, packed_out, sec_out
    )


def grow_kernel(plan, axes, *refs):
    turned, extra, coupled, permute, sea, grow, ocean, waves_out, *lat_out = refs
    even = lax.rem(lax.axis_index(axes[0]), 2) == 0
    both, _ = currents_twice(coupled[...])
    at_waves = twice(dot(permute[...], split_value(both)).astype(BF16))
    wet = twice(sea[...])
    for number, start in enumerate(range(0, plan.spectral, 256)):
        lanes = slice(start, start + 256)
        factor = wet + dot(at_waves, growth_table(grow, number))
        grown = grown_part(plan, turned, extra[:, lanes], factor, lanes)
        waves_out[:, :, lanes] = grown.reshape(plan.rows, plan.cols, 256)
    sea_rows = ocean[...].reshape(plan.rows, plan.cols, LANES)
    fill_lat(plan, even, waves_out, sea_rows, lat_out)


def last_kernel(plan, axes, *refs):
    turned, ocean_in, packed_in, permute, turn_edge, sea, keep, rates, grow = refs[:9]
    count = len(plan.sizes)
    near, far, sec_in, refs = refs[9], refs[10], refs[11 : 11 + count], refs[11 + count :]
    waves_far, ocean_far, coupled, west_edge, east_edge, waves_out, ocean_out, done = refs
    section, band = lax.axis_index(axes[1]), lax.axis_index(axes[0])
    even = lax.rem(band, 2) == 0

    take_sections(plan, section, packed_in, sec_in, coupled, west_edge, east_edge)
    both, drift = currents_twice(coupled[...])
    at_waves = twice(dot(permute[...], split_value(both)).astype(BF16))
    extra = edge_part(plan, rates, turn_edge, west_edge, east_edge)
    new = ocean_step(
        plan, band, even, ocean_in, drift, near, far, west_edge, east_edge, keep, sea
    )
    for row, value in enumerate(new):
        ocean_out[row] = value[:, : 2 * plan.depth]
    copies = [pltpu.make_async_copy(ocean_out, ocean_far, done.at[0])]
    copies[0].start()
    wet = twice(sea[...])
    for number, start in enumerate(range(0, plan.spectral, 256)):
        lanes = slice(start, start + 256)
        factor = wet + dot(at_waves, growth_table(grow, number))
        from_edges = jnp.concatenate(extra[2 * number : 2 * number + 2], axis=1)
        grown = grown_part(plan, turned, from_edges, factor, lanes)
        waves_out[:, :, lanes] = grown.reshape(plan.rows, plan.cols, 256)
        copy = pltpu.make_async_copy(
            waves_out.at[:, :, lanes], waves_far.at[:, :, lanes], done.at[number + 1]
        )
        copy.start()
        copies.append(copy)
    for copy in copies:
        copy.wait()


def per_device(plan, axes, spectra, turning, currents, drag_rates, land_mask, ocean_target):
    tables = [jnp.asarray(table) for table in build_tables(NFREQ, NDIR, drag_rates.shape[0])]
    columns, rows, cols, spectral = plan.columns, plan.rows, plan.cols, plan.spectral
    shape = jax.ShapeDtypeStruct
    params = pltpu.CompilerParams(vmem_limit_bytes=32 * 1024 * 1024)
    to_sections = [shape((size, LANES), F32) for size in plan.sizes]
    to_bands = [shape((cols, spectral // 2 + LANES), F32)] * 2
    state = shape((columns, LANES), F32)
    field = shape(spectra.shape, F32)
    at_edges = shape((2 * rows, LANES), F32)
    edge_field = shape((2 * rows, spectral), F32)
    edge = pltpu.VMEM((plan.edge, LANES), F32)
    spans = spectral // 256

    def call(kernel, outs, scratch, *args, space_in=pltpu.VMEM, space_out=pltpu.VMEM):
        return pl.pallas_call(
            functools.partial(kernel, plan, axes),
            out_shape=outs,
            in_specs=[pl.BlockSpec(memory_space=space_in)] * len(args),
            out_specs=[pl.BlockSpec(memory_space=space_out)] * len(outs),
            scratch_shapes=scratch,
            compiler_params=params,
        )(*args)

    pairs = [(i, i ^ 1) for i in range(plan.bands) if i ^ 1 < plan.bands]
    others = [(i, ((i + 1) ^ 1) - 1) for i in range(1, plan.bands)]
    others = [(i, j) for i, j in others if j < plan.bands]

    def exchange(to_sections, make_to_bands):
        got = []
        if plan.relay:
            to_x, to_y, *to_sections = to_sections
            got.append(lax.ppermute(to_x, axes[1], plan.table(0, 1)))
        kept, near_out, far_out = make_to_bands()
        far_in = lax.ppermute(far_out, axes[0], others)
        near_in = lax.ppermute(near_out, axes[0], pairs)
        if plan.relay:
            (to_y,) = call(
                relay_kernel,
                [shape((2 * plan.chunk + plan.edge, LANES), F32)],
                [],
                got[0],
                to_y,
            )
            got.append(lax.ppermute(to_y, axes[1], plan.table(0, 2)))
        got += [
            lax.ppermute(message, axes[1], table)
            for message, table in zip(to_sections, plan.direct)
        ]
        return kept, [near_in, far_in, *got]

    started = call(
        first_kernel,
        [
            field,
            state,
            state,
            shape((columns, columns), BF16),
            shape((columns, 2 * columns), BF16),
            shape((4 * rows, columns), BF16),
            shape((columns, 4 * rows), BF16),
            state,
            at_edges,
            state,
            state,
            at_edges,
            shape((8, LANES), F32),
        ]
        + [shape(table.shape, table.dtype) for table in tables]
        + to_sections
        + to_bands,
        [
            pltpu.VMEM(turning.shape, F32),
            pltpu.VMEM(currents.shape, F32),
            pltpu.VMEM(drag_rates.shape, F32),
            pltpu.VMEM(land_mask.shape, jnp.int32),
            pltpu.VMEM(ocean_target.shape, jnp.int32),
            pltpu.SemaphoreType.DMA((9,)),
        ],
        *[
            pltpu.with_memory_space_constraint(array, pltpu.HBM)
            for array in (
                spectra,
                turning,
                currents,
                drag_rates,
                land_mask,
                ocean_target,
                *tables,
            )
        ],
        space_in=pltpu.HBM,
    )
    waves, ocean, packed, permute, order, permute_edge, order_edge = started[:7]
    turn, turn_edge, sea, sea_order, sea_edge, keep, stokes, rates, grow = started[7:16]
    sent, lat = started[16:-2], started[-2:]
    waves, came = exchange(sent, lambda: (waves, *lat))
    for step in range(STEPS - 1):
        turned, turned_edge, turned_order = call(
            move_kernel,
            [field, edge_field, shape((columns, spectral), F32)],
            [],
            waves,
            turn,
            rates,
            *came[:2],
            order,
        )
        ocean, packed, coupled, extra, *sent = call(
            send_kernel,
            [state, state, state, edge_field] + to_sections,
            [edge, edge],
            turned_order,
            turned_edge,
            ocean,
            packed,
            permute_edge,
            order_edge,
            turn_edge,
            sea,
            sea_order,
            sea_edge,
            keep,
            stokes,
            rates,
            grow,
            *came,
        )

        def grown():
            return call(
                grow_kernel,
                [field] + to_bands,
                [],
                turned,
                extra,
                coupled,
                permute,
                sea,
                grow,
                ocean,
            )

        waves, came = exchange(sent, grown)
    (turned,) = call(move_kernel, [field], [], waves, turn, rates, *came[:2])
    return call(
        last_kernel,
        [field, shape(currents.shape, F32)],
        [
            pltpu.VMEM((columns, LANES), F32),
            edge,
            edge,
            pltpu.VMEM(spectra.shape, F32),
            pltpu.VMEM(currents.shape, F32),
            pltpu.SemaphoreType.DMA((1 + spans,)),
        ],
        turned,
        ocean,
        packed,
        permute,
        turn_edge,
        sea,
        keep,
        rates,
        grow,
        *came,
        space_out=pltpu.HBM,
    )


def solution(mesh):
    sections, bands = mesh.shape["sec"], mesh.shape["lat"]

    def local(spectra, turning, currents, drag_rates, land_mask, ocean_target):
        rows, cols, spectral = spectra.shape
        plan = Plan(sections, bands, rows, cols, spectral, drag_rates.shape[0])
        return per_device(
            plan, ("lat", "sec"), spectra, turning, currents, drag_rates, land_mask, ocean_target
        )

    return jax.shard_map(
        local,
        mesh=mesh,
        in_specs=(
            P("lat", "sec", None),
            P("lat", "sec"),
            P("lat", "sec", None),
            P(),
            P("lat", "sec"),
            P("lat", "sec"),
        ),
        out_specs=(P("lat", "sec", None), P("lat", "sec", None)),
        check_vma=False,
    )
```

time: 31.1 us -> 31.1 us (level)
  waiting for transfers between devices: 3.68 us -> 3.04 us
  Pallas kernels: 6.62 us -> 7.16 us
    ppermute x3, starting transfers between devices: 2.4 us -> 3.3 us  [exchange(): got.append(lax.ppermute(to_x, axes[1], plan.table(0, 1)))]
    ppermute x6, starting transfers between devices: 13.4 us -> 12.8 us  [the longest x3 9.29 us: exchange(): far_in = lax.ppermute(far_out, axes[0], others)]
    ppermute x6, waiting for transfers between devices: 3.66 us -> 3.03 us  [the longest x3 3.02 us: exchange(): far_in = lax.ppermute(far_out, axes[0], others)]
    pallas_call x10 -> x12, Pallas kernels: 6.62 us -> 7.16 us  [call(): pl.pallas_call(functools.partial(kernel, plan, axes), out_shape=outs, in_...]
  transfers between devices with their start and end apart: 12 -> 12, of which waited for: 3 -> 3; matrix products, arithmetic and copies ran while one was open for 0% -> 0% of each run, Pallas kernels for 6% -> 9%
where the time goes in v7:
time: 31.1 us; the launch traced here: 30.9 us
  starting transfers between devices  20 us (64%)
  Pallas kernels  7.16 us (23%)
  waiting for transfers between devices  3.04 us (10%)
  between operations  0.76 us (2%)
    ppermute x3, starting transfers between devices, exchange(): far_in = lax.ppermute(far_out, axes[0], others)  9.29 us
    pallas_call x12, Pallas kernels, call(): pl.pallas_call(functools.partial(kernel, plan, axes), out_shape=outs, in_...  7.16 us
    ppermute x3, starting transfers between devices, exchange(): got.append(lax.ppermute(to_y, axes[1], plan.table(0, 2)))  3.92 us
    ppermute x3, starting transfers between devices, exchange(): near_in = lax.ppermute(near_out, axes[0], pairs)  3.48 us
    ppermute x3, starting transfers between devices, exchange(): got.append(lax.ppermute(to_x, axes[1], plan.table(0, 1)))  3.3 us
    ppermute x3, waiting for transfers between devices, exchange(): far_in = lax.ppermute(far_out, axes[0], others)  3.02 us
  transfers between devices with their start and end apart: 12, of which 3 were waited for; matrix products, arithmetic and copies ran while one was open for 0% of the time, Pallas kernels for 9%

profile of v7, /device:TPU:1, one launch (start us, length us, event | category | flops | bytes accessed | tf_op | source)
XLA Modules:
  0.0 30.9 jit_solution(501708966491088055)
XLA Ops:
  0.6 1.7 %shard_map.104 = (f32[4,24,768]{2,1,0:T(8,128)S(1)}, f32[96,128]{1,0:T(8,128)S(1)}, f32[96,128]{1,0:T(8,128)S(1)}, bf16[96,96]{1,0:T(8,128)(2,1)S(1)}, bf16[96,1...) custom-call(f32[4,24,768]{2,1,0:T(8,128)} %refs_0_.1, ...), custom_call_target="tpu_custom_call" | custom-call | tf_op jit(solution)/shard_map/pallas_call | solution.py:584
  2.4 2.1 %collective-permute-start.2 = (f32[80,128]{1,0:T(8,128)S(1)}, f32[80,128]{1,0:T(8,128)S(1)}, u32[]{:S(2)}, u32[]{:S(2)}) collective-permute-start(f32[80,128]{1,0:T(8,128)S(1)} %get-tuple-element.66), channel_id=1, source_target_pairs={{0,8},{8,0},{16,24},{24,16},{1,9},{9,1},{17,25},{25,17},{2,10},{10... | collective-permute-start | bytes 122888 | tf_op jit(solution)/shard_map/ppermute | solution.py:601
  4.5 1.0 %collective-permute-start = (f32[24,512]{1,0:T(8,128)S(1)}, f32[24,512]{1,0:T(8,128)S(1)}, u32[]{:S(2)}, u32[]{:S(2)}) collective-permute-start(f32[24,512]{1,0:T(8,128)S(1)} %get-tuple-element.49), channel_id=1, source_target_pairs={{0,1},{1,0},{2,3},{3,2},{4,5},{5,4},{6,7},{7,6},{8,9},{9,8},{10,11... | collective-permute-start | bytes 147464 | tf_op jit(solution)/shard_map/ppermute | solution.py:604
  5.4 3.1 %collective-permute-start.1 = (f32[24,512]{1,0:T(8,128)S(1)}, f32[24,512]{1,0:T(8,128)S(1)}, u32[]{:S(2)}, u32[]{:S(2)}) collective-permute-start(f32[24,512]{1,0:T(8,128)S(1)} %get-tuple-element.50), channel_id=1, source_target_pairs={{1,2},{2,1},{3,4},{4,3},{5,6},{6,5},{9,10},{10,9},{11,12},{12,11},... | collective-permute-start | bytes 147464 | tf_op jit(solution)/shard_map/ppermute | solution.py:603
  8.5 0.0 collective-permute-done.2.from_x.refs_16_
  8.5 1.3 %collective-permute-start.3 = (f32[64,128]{1,0:T(8,128)S(1)}, f32[64,128]{1,0:T(8,128)S(1)}, u32[]{:S(2)}, u32[]{:S(2)}) collective-permute-start(f32[64,128]{1,0:T(8,128)S(1)} %shard_map.106), channel_id=1, source_target_pairs={{0,16},{8,24},{16,0},{24,8},{1,17},{9,25},{17,1},{25,9},{2,18},{10... | collective-permute-start | bytes 98312 | tf_op jit(solution)/shard_map/ppermute | solution.py:613
  9.9 0.0 collective-permute-done.refs_3_.refs_14_
  9.9 1.1 %collective-permute-done.1.refs_4_.refs_15_ = f32[24,512]{1,0:T(8,128)S(1)} collective-permute-done((f32[24,512]{1,0:T(8,128)S(1)}, f32[24,512]{1,0:T(8,128)S(1)}, u32[]{:S(2)}, u32[]{:S(2)}) %collective-permute-start.1) | collective-permute-done | bytes 49184 | tf_op jit(solution)/shard_map/ppermute | solution.py:603
  11.0 0.6 %shard_map.105 = (f32[4,24,768]{2,1,0:T(8,128)S(1)}, f32[8,768]{1,0:T(8,128)S(1)}, f32[96,768]{1,0:T(8,128)S(1)}) custom-call(f32[4,24,768]{2,1,0:T(8,128)S(1)} %get-tuple-element.46.refs_0_, f32[96,128]{1,0:T(8,128)S(1)} %get-tuple-element.47.refs_1_, f32[8,768]{1,0:T(8,128)S(1)} %get-tuple-element.48.refs_2_.refs_12_.refs_7_, ...), custom_call_target="tpu_custom_call" | custom-call | tf_op jit(solution)/shard_map/pallas_call | solution.py:584
  11.6 0.0 collective-permute-done.3.refs_17_
  11.6 0.8 %shard_map.107 = (f32[96,128]{1,0:T(8,128)S(1)}, f32[96,128]{1,0:T(8,128)S(1)}, f32[96,128]{1,0:T(8,128)S(1)}, f32[8,768]{1,0:T(8,128)S(1)}, f32[80,128]{1,0:T(8,128)S(1)}, /*index=5*/f32[24,128]{1,0:T(8,128)S(1)}) custom-call(f32[96,768]{1,0:T(8,128)S(1)} %get-tuple-element.53.refs_0_, f32[8,768]{1,0:T(8,128)S(1)} %get-tuple-element.54.refs_1_, ...), custom_call_target="tpu_custom_call" | custom-call | tf_op jit(solution)/shard_map/pallas_call | solution.py:584
  12.4 0.1 collective-permute-start.6
  12.5 0.5 %shard_map.108 = (f32[4,24,768]{2,1,0:T(8,128)S(1)}, f32[24,512]{1,0:T(8,128)S(1)}, f32[24,512]{1,0:T(8,128)S(1)}) custom-call(f32[4,24,768]{2,1,0:T(8,128)S(1)} %get-tuple-element.52.refs_0_, f32[8,768]{1,0:T(8,128)S(1)} %get-tuple-element.68.refs_1_, f32[96,128]{1,0:T(8,128)S(1)} %get-tuple-element.69.refs_2_, ...), custom_call_target="tpu_custom_call" | custom-call | tf_op jit(solution)/shard_map/pallas_call | solution.py:584
  12.9 1.8 %collective-permute-start.4 = (f32[24,512]{1,0:T(8,128)S(1)}, f32[24,512]{1,0:T(8,128)S(1)}, u32[]{:S(2)}, u32[]{:S(2)}) collective-permute-start(f32[24,512]{1,0:T(8,128)S(1)} %get-tuple-element.73), channel_id=1, source_target_pairs={{0,1},{1,0},{2,3},{3,2},{4,5},{5,4},{6,7},{7,6},{8,9},{9,8},{10,11... | collective-permute-start | bytes 147464 | tf_op jit(solution)/shard_map/ppermute | solution.py:604
  14.7 3.1 %collective-permute-start.5 = (f32[24,512]{1,0:T(8,128)S(1)}, f32[24,512]{1,0:T(8,128)S(1)}, u32[]{:S(2)}, u32[]{:S(2)}) collective-permute-start(f32[24,512]{1,0:T(8,128)S(1)} %get-tuple-element.74), channel_id=1, source_target_pairs={{1,2},{2,1},{3,4},{4,3},{5,6},{6,5},{9,10},{10,9},{11,12},{12,11},... | collective-permute-start | bytes 147464 | tf_op jit(solution)/shard_map/ppermute | solution.py:603
  17.8 0.0 collective-permute-done.6.from_x.refs_16_
  17.9 1.3 %collective-permute-start.7 = (f32[64,128]{1,0:T(8,128)S(1)}, f32[64,128]{1,0:T(8,128)S(1)}, u32[]{:S(2)}, u32[]{:S(2)}) collective-permute-start(f32[64,128]{1,0:T(8,128)S(1)} %shard_map.110), channel_id=1, source_target_pairs={{0,16},{8,24},{16,0},{24,8},{1,17},{9,25},{17,1},{25,9},{2,18},{10... | collective-permute-start | bytes 98312 | tf_op jit(solution)/shard_map/ppermute | solution.py:613
  19.2 0.0 collective-permute-done.4.refs_3_.refs_14_
  19.2 1.0 %collective-permute-done.5.refs_4_.refs_15_ = f32[24,512]{1,0:T(8,128)S(1)} collective-permute-done((f32[24,512]{1,0:T(8,128)S(1)}, f32[24,512]{1,0:T(8,128)S(1)}, u32[]{:S(2)}, u32[]{:S(2)}) %collective-permute-start.5) | collective-permute-done | bytes 49184 | tf_op jit(solution)/shard_map/ppermute | solution.py:603
  20.1 0.6 %shard_map.109 = (f32[4,24,768]{2,1,0:T(8,128)S(1)}, f32[8,768]{1,0:T(8,128)S(1)}, f32[96,768]{1,0:T(8,128)S(1)}) custom-call(f32[4,24,768]{2,1,0:T(8,128)S(1)} %get-tuple-element.72.refs_0_, f32[96,128]{1,0:T(8,128)S(1)} %get-tuple-element.47.refs_1_, f32[8,768]{1,0:T(8,128)S(1)} %get-tuple-element.48.refs_2_.refs_12_.refs_7_, ...), custom_call_target="tpu_custom_call" | custom-call | tf_op jit(solution)/shard_map/pallas_call | solution.py:584
  20.7 0.0 collective-permute-done.7.refs_17_
  20.7 0.8 %shard_map.111 = (f32[96,128]{1,0:T(8,128)S(1)}, f32[96,128]{1,0:T(8,128)S(1)}, f32[96,128]{1,0:T(8,128)S(1)}, f32[8,768]{1,0:T(8,128)S(1)}, f32[80,128]{1,0:T(8,128)S(1)}, /*index=5*/f32[24,128]{1,0:T(8,128)S(1)}) custom-call(f32[96,768]{1,0:T(8,128)S(1)} %get-tuple-element.76.refs_0_, f32[8,768]{1,0:T(8,128)S(1)} %get-tuple-element.77.refs_1_, ...), custom_call_target="tpu_custom_call" | custom-call | tf_op jit(solution)/shard_map/pallas_call | solution.py:584
  21.5 1.1 %collective-permute-start.10 = (f32[80,128]{1,0:T(8,128)S(1)}, f32[80,128]{1,0:T(8,128)S(1)}, u32[]{:S(2)}, u32[]{:S(2)}) collective-permute-start(f32[80,128]{1,0:T(8,128)S(1)} %get-tuple-element.88), channel_id=1, source_target_pairs={{0,8},{8,0},{16,24},{24,16},{1,9},{9,1},{17,25},{25,17},{2,10},{10... | collective-permute-start | bytes 122888 | tf_op jit(solution)/shard_map/ppermute | solution.py:601
  22.6 0.5 %shard_map.112 = (f32[4,24,768]{2,1,0:T(8,128)S(1)}, f32[24,512]{1,0:T(8,128)S(1)}, f32[24,512]{1,0:T(8,128)S(1)}) custom-call(f32[4,24,768]{2,1,0:T(8,128)S(1)} %get-tuple-element.75.refs_0_, f32[8,768]{1,0:T(8,128)S(1)} %get-tuple-element.81.refs_1_, f32[96,128]{1,0:T(8,128)S(1)} %get-tuple-element.82.refs_2_, ...), custom_call_target="tpu_custom_call" | custom-call | tf_op jit(solution)/shard_map/pallas_call | solution.py:584
  23.1 0.7 %collective-permute-start.8 = (f32[24,512]{1,0:T(8,128)S(1)}, f32[24,512]{1,0:T(8,128)S(1)}, u32[]{:S(2)}, u32[]{:S(2)}) collective-permute-start(f32[24,512]{1,0:T(8,128)S(1)} %get-tuple-element.85), channel_id=1, source_target_pairs={{0,1},{1,0},{2,3},{3,2},{4,5},{5,4},{6,7},{7,6},{8,9},{9,8},{10,11... | collective-permute-start | bytes 147464 | tf_op jit(solution)/shard_map/ppermute | solution.py:604
  23.8 3.1 %collective-permute-start.9 = (f32[24,512]{1,0:T(8,128)S(1)}, f32[24,512]{1,0:T(8,128)S(1)}, u32[]{:S(2)}, u32[]{:S(2)}) collective-permute-start(f32[24,512]{1,0:T(8,128)S(1)} %get-tuple-element.86), channel_id=1, source_target_pairs={{1,2},{2,1},{3,4},{4,3},{5,6},{6,5},{9,10},{10,9},{11,12},{12,11},... | collective-permute-start | bytes 147464 | tf_op jit(solution)/shard_map/ppermute | solution.py:603
  26.9 1.3 %collective-permute-start.11 = (f32[64,128]{1,0:T(8,128)S(1)}, f32[64,128]{1,0:T(8,128)S(1)}, u32[]{:S(2)}, u32[]{:S(2)}) collective-permute-start(f32[64,128]{1,0:T(8,128)S(1)} %shard_map.114), channel_id=1, source_target_pairs={{0,16},{8,24},{16,0},{24,8},{1,17},{9,25},{17,1},{25,9},{2,18},{10... | collective-permute-start | bytes 98312 | tf_op jit(solution)/shard_map/ppermute | solution.py:613
  28.3 0.0 collective-permute-done.8.refs_3_.refs_9_
  28.3 1.0 %collective-permute-done.9.refs_4_.refs_10_ = f32[24,512]{1,0:T(8,128)S(1)} collective-permute-done((f32[24,512]{1,0:T(8,128)S(1)}, f32[24,512]{1,0:T(8,128)S(1)}, u32[]{:S(2)}, u32[]{:S(2)}) %collective-permute-start.9) | collective-permute-done | bytes 49184 | tf_op jit(solution)/shard_map/ppermute | solution.py:603
  29.2 0.6 %shard_map.113.refs_0_ = f32[4,24,768]{2,1,0:T(8,128)S(1)} custom-call(f32[4,24,768]{2,1,0:T(8,128)S(1)} %get-tuple-element.84.refs_0_, f32[96,128]{1,0:T(8,128)S(1)} %get-tuple-element.47.refs_1_, f32[8,768]{1,0:T(8,128)S(1)} %get-tuple-element.48.refs_2_.refs_12_.refs_7_, f32[24,512]{1,0:T(8,128)S(1)} %collective-permute-done.8.refs_3_.refs_9_, ...), custom_call_target="tpu_custom_call" | custom-call | tf_op jit(solution)/shard_map/pallas_call | solution.py:584
  29.8 0.0 collective-permute-done.11.refs_12_
  29.8 1.1 %shard_map.115 = (f32[4,24,768]{2,1,0:T(8,128)}, f32[4,24,64]{2,1,0:T(8,128)}) custom-call(f32[4,24,768]{2,1,0:T(8,128)S(1)} %shard_map.113.refs_0_, f32[96,128]{1,0:T(8,128)S(1)} %get-tuple-element.83.refs_6_.refs_1_, f32[96,128]{1,0:T(8,128)S(1)} %get-tuple-element.87.refs_2_, bf16[96,96]{1,0:T(8,128)(2,1)S(1)} %get-tuple-element.70.refs_3_, ...), custom_call_target="tpu_custom_call" | custom-call | tf_op jit(solution)/shard_map/pallas_call | solution.py:584
  (4 shorter events, 0.0 us)
Async XLA Ops:
  2.4 6.2 %collective-permute-start.2 = (f32[80,128]{1,0:T(8,128)S(1)}, f32[80,128]{1,0:T(8,128)S(1)}, u32[]{:S(2)}, u32[]{:S(2)}) collective-permute-start(f32[80,128]{1,0:T(8,128)S(1)} %get-tuple-element.66), channel_id=1, source_target_pairs={{0,8},{8,0},{16,24},{24,16},{1,9},{9,1},{17,25},{25,17},{2,10},{10... | collective-permute-start | bytes 122888 | tf_op jit(solution)/shard_map/ppermute | solution.py:601
  4.5 5.4 %collective-permute-start = (f32[24,512]{1,0:T(8,128)S(1)}, f32[24,512]{1,0:T(8,128)S(1)}, u32[]{:S(2)}, u32[]{:S(2)}) collective-permute-start(f32[24,512]{1,0:T(8,128)S(1)} %get-tuple-element.49), channel_id=1, source_target_pairs={{0,1},{1,0},{2,3},{3,2},{4,5},{5,4},{6,7},{7,6},{8,9},{9,8},{10,11... | collective-permute-start | bytes 147464 | tf_op jit(solution)/shard_map/ppermute | solution.py:604
  5.4 5.5 %collective-permute-start.1 = (f32[24,512]{1,0:T(8,128)S(1)}, f32[24,512]{1,0:T(8,128)S(1)}, u32[]{:S(2)}, u32[]{:S(2)}) collective-permute-start(f32[24,512]{1,0:T(8,128)S(1)} %get-tuple-element.50), channel_id=1, source_target_pairs={{1,2},{2,1},{3,4},{4,3},{5,6},{6,5},{9,10},{10,9},{11,12},{12,11},... | collective-permute-start | bytes 147464 | tf_op jit(solution)/shard_map/ppermute | solution.py:603
  8.5 3.0 %collective-permute-start.3 = (f32[64,128]{1,0:T(8,128)S(1)}, f32[64,128]{1,0:T(8,128)S(1)}, u32[]{:S(2)}, u32[]{:S(2)}) collective-permute-start(f32[64,128]{1,0:T(8,128)S(1)} %shard_map.106), channel_id=1, source_target_pairs={{0,16},{8,24},{16,0},{24,8},{1,17},{9,25},{17,1},{25,9},{2,18},{10... | collective-permute-start | bytes 98312 | tf_op jit(solution)/shard_map/ppermute | solution.py:613
  12.4 5.5 %collective-permute-start.6 = (f32[80,128]{1,0:T(8,128)S(1)}, f32[80,128]{1,0:T(8,128)S(1)}, u32[]{:S(2)}, u32[]{:S(2)}) collective-permute-start(f32[80,128]{1,0:T(8,128)S(1)} %get-tuple-element.79), channel_id=1, source_target_pairs={{0,8},{8,0},{16,24},{24,16},{1,9},{9,1},{17,25},{25,17},{2,10},{10... | collective-permute-start | bytes 122888 | tf_op jit(solution)/shard_map/ppermute | solution.py:601
  12.9 6.2 %collective-permute-start.4 = (f32[24,512]{1,0:T(8,128)S(1)}, f32[24,512]{1,0:T(8,128)S(1)}, u32[]{:S(2)}, u32[]{:S(2)}) collective-permute-start(f32[24,512]{1,0:T(8,128)S(1)} %get-tuple-element.73), channel_id=1, source_target_pairs={{0,1},{1,0},{2,3},{3,2},{4,5},{5,4},{6,7},{7,6},{8,9},{9,8},{10,11... | collective-permute-start | bytes 147464 | tf_op jit(solution)/shard_map/ppermute | solution.py:604
  14.7 5.4 %collective-permute-start.5 = (f32[24,512]{1,0:T(8,128)S(1)}, f32[24,512]{1,0:T(8,128)S(1)}, u32[]{:S(2)}, u32[]{:S(2)}) collective-permute-start(f32[24,512]{1,0:T(8,128)S(1)} %get-tuple-element.74), channel_id=1, source_target_pairs={{1,2},{2,1},{3,4},{4,3},{5,6},{6,5},{9,10},{10,9},{11,12},{12,11},... | collective-permute-start | bytes 147464 | tf_op jit(solution)/shard_map/ppermute | solution.py:603
  17.9 2.9 %collective-permute-start.7 = (f32[64,128]{1,0:T(8,128)S(1)}, f32[64,128]{1,0:T(8,128)S(1)}, u32[]{:S(2)}, u32[]{:S(2)}) collective-permute-start(f32[64,128]{1,0:T(8,128)S(1)} %shard_map.110), channel_id=1, source_target_pairs={{0,16},{8,24},{16,0},{24,8},{1,17},{9,25},{17,1},{25,9},{2,18},{10... | collective-permute-start | bytes 98312 | tf_op jit(solution)/shard_map/ppermute | solution.py:613
  21.5 5.4 %collective-permute-start.10 = (f32[80,128]{1,0:T(8,128)S(1)}, f32[80,128]{1,0:T(8,128)S(1)}, u32[]{:S(2)}, u32[]{:S(2)}) collective-permute-start(f32[80,128]{1,0:T(8,128)S(1)} %get-tuple-element.88), channel_id=1, source_target_pairs={{0,8},{8,0},{16,24},{24,16},{1,9},{9,1},{17,25},{25,17},{2,10},{10... | collective-permute-start | bytes 122888 | tf_op jit(solution)/shard_map/ppermute | solution.py:601
  23.1 5.2 %collective-permute-start.8 = (f32[24,512]{1,0:T(8,128)S(1)}, f32[24,512]{1,0:T(8,128)S(1)}, u32[]{:S(2)}, u32[]{:S(2)}) collective-permute-start(f32[24,512]{1,0:T(8,128)S(1)} %get-tuple-element.85), channel_id=1, source_target_pairs={{0,1},{1,0},{2,3},{3,2},{4,5},{5,4},{6,7},{7,6},{8,9},{9,8},{10,11... | collective-permute-start | bytes 147464 | tf_op jit(solution)/shard_map/ppermute | solution.py:604
  23.8 5.4 %collective-permute-start.9 = (f32[24,512]{1,0:T(8,128)S(1)}, f32[24,512]{1,0:T(8,128)S(1)}, u32[]{:S(2)}, u32[]{:S(2)}) collective-permute-start(f32[24,512]{1,0:T(8,128)S(1)} %get-tuple-element.86), channel_id=1, source_target_pairs={{1,2},{2,1},{3,4},{4,3},{5,6},{6,5},{9,10},{10,9},{11,12},{12,11},... | collective-permute-start | bytes 147464 | tf_op jit(solution)/shard_map/ppermute | solution.py:603
  26.9 2.8 %collective-permute-start.11 = (f32[64,128]{1,0:T(8,128)S(1)}, f32[64,128]{1,0:T(8,128)S(1)}, u32[]{:S(2)}, u32[]{:S(2)}) collective-permute-start(f32[64,128]{1,0:T(8,128)S(1)} %shard_map.114), channel_id=1, source_target_pairs={{0,16},{8,24},{16,0},{24,8},{1,17},{9,25},{17,1},{25,9},{2,18},{10... | collective-permute-start | bytes 98312 | tf_op jit(solution)/shard_map/ppermute | solution.py:613

commit v8 on v7

--- a/solution.py
+++ b/solution.py
@@ -158,17 +158,20 @@
     return jnp.where(keep, first, pltpu.roll(second, NDIR // 2, 1))
 
 
-def fill_lat(plan, even, waves, sea_rows, lat_out):
+def fill_band(plan, northward, edge, sea_row, out):
     half = plan.tiles // 2
     masks = Directions((plan.cols, LANES))
-    near, far = lat_out
+    for tile in range(half):
+        out[:, tile * LANES : (tile + 1) * LANES] = packed_half(
+            edge, tile, half, masks.northward, northward
+        )
+    out[:, plan.spectral // 2 :] = sea_row
+
+
+def fill_bands(plan, even, edges, sea_rows, far, near):
     for out, northward in ((far, jnp.logical_not(even)), (near, even)):
-        edge = jnp.where(northward, waves[plan.rows - 1], waves[0])
-        for tile in range(half):
-            out[:, tile * LANES : (tile + 1) * LANES] = packed_half(
-                edge, tile, half, masks.northward, northward
-            )
-        out[:, plan.spectral // 2 :] = jnp.where(northward, sea_rows[plan.rows - 1], sea_rows[0])
+        edge = jnp.where(northward, edges[1], edges[0])
+        fill_band(plan, northward, edge, jnp.where(northward, sea_rows[1], sea_rows[0]), out)
 
 
 def fill_sections(plan, section, edges, ocean, ordered, packed_out, sec_out):
@@ -272,19 +275,21 @@
     return jnp.where(lane_of(arrived.shape) < LANES // 2, arrived, other), other
 
 
+def with_edges(plan, turned, west, east):
+    place = lax.broadcasted_iota(jnp.int32, (8, 256), 0)
+    return [
+        turned[0:8, :] + jnp.where(place == 0, west, 0.0),
+        turned[8 : plan.cols - 8, :],
+        turned[plan.cols - 8 :, :] + jnp.where(place == 7, east, 0.0),
+    ]
+
+
 def grown_part(plan, turned, from_edges, factor, lanes):
-    rows, cols = plan.rows, plan.cols
-    place = lax.broadcasted_iota(jnp.int32, (8, 256), 0)
-    at_first, at_last = place == 0, place == 7
+    rows = plan.rows
     parts = []
     for row in range(rows):
-        west = jnp.where(at_first, from_edges[row : row + 1, :], 0.0)
-        east = jnp.where(at_last, from_edges[rows + row : rows + row + 1, :], 0.0)
-        parts += [
-            turned[row, 0:8, lanes] + west,
-            turned[row, 8 : cols - 8, lanes],
-            turned[row, cols - 8 :, lanes] + east,
-        ]
+        west, east = from_edges[row : row + 1, :], from_edges[rows + row : rows + row + 1, :]
+        parts += with_edges(plan, turned[row, :, lanes], west, east)
     return jnp.concatenate(parts, axis=0) * factor
 
 
@@ -296,8 +301,8 @@
 def first_kernel(plan, axes, *refs):
     waves_in, turning_in, currents_in, drag_in, mask_in, target_in = refs[:6]
     tables_in, refs = refs[6:9], refs[9:]
-    waves, ocean_out, packed_out, permute_out, order_out, permute_edge_out, order_edge_out = refs[:7]
-    turn_out, turn_edge_out, sea_out, sea_order_out, sea_edge_out, keep_out = refs[7:13]
+    waves, ocean_out, packed_out, permute_out, order_out, permute_some_out, order_edge_out = refs[:7]
+    turn_out, turn_edge_out, sea_out, sea_order_out, sea_some_out, keep_out = refs[7:13]
     tables_out, refs = refs[13:16], refs[16:]
     count = len(plan.sizes)
     sec_out, lat_out, refs = refs[:count], refs[count : count + 2], refs[count + 2 :]
@@ -335,8 +340,15 @@
         east = [value[(row + 1) * cols - 1 : (row + 1) * cols, :] for row in range(rows)]
         return jnp.concatenate(west + east, axis=0)
 
-    for copy in copies[:4]:
+    for copy in copies[:7]:
         copy.wait()
+    total = None
+    for start in range(0, plan.spectral, 256):
+        part = waves[:, :, start : start + 256].reshape(columns, 256)
+        product = stokes_product(part, tables_out[0][start : start + 256, :])
+        total = product if total is None else total + product
+    moments = total[:columns] + total[columns:]
+    moments = moments + pltpu.roll(moments, LANES // 2, 1)
     sea_row = row_of(mask).astype(F32)
     sea = column_of(sea_row)
     target_row = row_of(target).astype(F32)
@@ -359,39 +371,37 @@
     order_edge_out[...] = dot(
         order.astype(BF16), jnp.where(chosen, 1.0, 0.0).astype(BF16)
     ).astype(BF16)
-    number = lax.rem(lax.broadcasted_iota(jnp.int32, (edge_count, columns), 0), 2 * rows)
-    wanted = lax.rem(number, rows) * cols + lax.div(number, rows) * (cols - 1)
-    chosen = lane_of((edge_count, columns)) == wanted
-    permute_edge_out[...] = dot(
-        jnp.where(chosen, 1.0, 0.0).astype(BF16), permute.astype(BF16)
-    ).astype(BF16)
-    sea_out[...] = jnp.broadcast_to(sea, (columns, LANES))
-    sea_edge_out[...] = edges_of(jnp.broadcast_to(sea, (columns, LANES)))
+    shape = (2 * cols + 2 * rows, columns)
+    place = lax.broadcasted_iota(jnp.int32, shape, 0)
+    number = place - 2 * cols
+    wanted = jnp.where(
+        place < 2 * cols,
+        place + jnp.where(place < cols, 0, (rows - 2) * cols),
+        lax.rem(number, rows) * cols + lax.div(number, rows) * (cols - 1),
+    )
+    chosen = jnp.where(lane_of(shape) == wanted, 1.0, 0.0).astype(BF16)
+    permute_some_out[...] = dot(chosen, permute.astype(BF16)).astype(BF16)
+    sea_wide = jnp.broadcast_to(sea, (columns, LANES))
+    sea_some_out[...] = dot(chosen, sea_wide.astype(BF16))
+    sea_out[...] = sea_wide
     turn = jnp.broadcast_to(column_of(row_of(turning)), (columns, LANES))
     turn_out[...] = turn
     turn_edge_out[...] = edges_of(turn)
     keep = 1.0 - drag[...].reshape(1, plan.depth)
     blank = jnp.zeros((1, LANES - 2 * plan.depth), F32)
     keep_out[...] = jnp.broadcast_to(jnp.concatenate([keep, keep, blank], axis=1), (8, LANES))
-    for copy in copies[4:7]:
-        copy.wait()
     flat = currents[...].reshape(columns, 2 * plan.depth)
     ocean = jnp.concatenate([flat, jnp.zeros((columns, LANES - 2 * plan.depth), F32)], axis=1)
     ocean_out[...] = ocean
-    total = None
-    for start in range(0, plan.spectral, 256):
-        part = waves[:, :, start : start + 256].reshape(columns, 256)
-        product = stokes_product(part, tables_out[0][start : start + 256, :])
-        total = product if total is None else total + product
-    moments = total[:columns] + total[columns:]
-    moments = moments + pltpu.roll(moments, LANES // 2, 1)
     ordered = dot(order.astype(BF16), split_value(moments))
     ordered = ordered + pltpu.roll(ordered, LANES // 2, 1)
     west = [waves[row, 0:1, :] for row in range(rows)]
     east = [waves[row, cols - 1 : cols, :] for row in range(rows)]
     edges = jnp.concatenate(west + east, axis=0)
     fill_sections(plan, section, edges, ocean, ordered, packed_out, sec_out)
-    fill_lat(plan, even, waves, ocean.reshape(rows, cols, LANES), lat_out)
+    sea_rows = ocean.reshape(rows, cols, LANES)
+    ends = (waves[0], waves[rows - 1]), (sea_rows[0], sea_rows[rows - 1])
+    fill_bands(plan, even, *ends, *lat_out)
     for copy in copies[7:]:
         copy.wait()
 
@@ -453,7 +463,7 @@
             turned_out[row, :, lanes] = turned
             if len(refs) > 1:
                 edge_out[row : row + 1, lanes] = turned[0:1, :]
-                edge_out[rows + row : rows + row + 1, lanes] = turned[cols - 1 : cols, :]
+                edge_out[rows + row : rows + row + 1, lanes] = turned[cols - 1 :, :]
     if len(refs) > 1:
         for start in range(0, plan.spectral, 256):
             part = turned_out[:, :, start : start + 256].reshape(plan.columns, 256)
@@ -471,24 +481,24 @@
 
 
 def send_kernel(plan, axes, *refs):
-    turned_order, turned_edge, ocean_in, packed_in, permute_edge, order_edge, turn_edge = refs[:7]
-    sea, sea_order, sea_edge, keep, stokes, rates, grow = refs[7:14]
+    turned, turned_edge, turned_order, ocean_in, packed_in, permute_some, order_edge = refs[:7]
+    turn_edge, sea, sea_order, sea_some, keep, stokes, rates, grow, refs = *refs[7:15], refs[15:]
     count = len(plan.sizes)
-    near, far, sec_in, refs = refs[14], refs[15], refs[16 : 16 + count], refs[16 + count :]
-    ocean_out, packed_out, coupled, extra_out, sec_out = *refs[:4], refs[4 : 4 + count]
-    west_edge, east_edge = refs[4 + count :]
+    near, far, sec_in, refs = refs[0], refs[1], refs[2 : 2 + count], refs[2 + count :]
+    ocean_out, packed_out, coupled, extra_out, far_out, near_out = refs[:6]
+    sec_out, (west_edge, east_edge) = refs[6 : 6 + count], refs[6 + count :]
     section, band = lax.axis_index(axes[1]), lax.axis_index(axes[0])
     even = lax.rem(band, 2) == 0
-    columns, rows = plan.columns, plan.rows
+    columns, rows, cols = plan.columns, plan.rows, plan.cols
 
     take_sections(plan, section, packed_in, sec_in, coupled, west_edge, east_edge)
     both, drift = currents_twice(coupled[...])
     in_order = twice(split_value(both * sea_order[...]))
-    at_edge = twice(dot(permute_edge[...], split_value(both)).astype(BF16))
+    at_some = twice(dot(permute_some[...], split_value(both)).astype(BF16))
     extra = edge_part(plan, rates, turn_edge, west_edge, east_edge)
     total = None
-    edges = []
-    wet, wet_edge = twice(sea_order[...]), twice(sea_edge[...])
+    some = []
+    wet, wet_some = twice(sea_order[...]), twice(sea_some[...])
     for number, start in enumerate(range(0, plan.spectral, 256)):
         lanes = slice(start, start + 256)
         table = growth_table(grow, number)
@@ -496,14 +506,16 @@
         extra_out[:, lanes] = from_edges
         high = from_edges.astype(BF16).astype(F32)
         halves = jnp.concatenate([high, from_edges - high], axis=0).astype(BF16)
-        turned = turned_order[:, lanes] + dot(order_edge[...], halves)
-        grown = turned * (wet + dot(in_order, table))
+        grown = turned_order[:, lanes] + dot(order_edge[...], halves)
+        grown = grown * (wet + dot(in_order, table))
         product = stokes_product(grown, stokes[lanes, :])
         total = product if total is None else total + product
-        edges.append(
-            (turned_edge[:, lanes] + from_edges)
-            * (wet_edge + dot(at_edge, table)[: 2 * rows, :])
-        )
+        parts = []
+        for row in (0, rows - 1):
+            west, east = from_edges[row : row + 1, :], from_edges[rows + row : rows + row + 1, :]
+            parts += with_edges(plan, turned[row, :, lanes], west, east)
+        parts.append(turned_edge[:, lanes] + from_edges)
+        some.append(jnp.concatenate(parts, axis=0) * (wet_some + dot(at_some, table)))
     new = ocean_step(
         plan, band, even, ocean_in, drift, near, far, west_edge, east_edge, keep, sea
     )
@@ -511,14 +523,14 @@
     ocean_out[...] = ocean
     moments = total[:columns] + total[columns:]
     moments = moments + pltpu.roll(moments, LANES // 2, 1)
-    fill_sections(
-        plan, section, jnp.concatenate(edges, axis=1), ocean, moments, packed_out, sec_out
-    )
+    some = jnp.concatenate(some, axis=1)
+    fill_sections(plan, section, some[2 * cols :, :], ocean, moments, packed_out, sec_out)
+    ends = (some[:cols, :], some[cols : 2 * cols, :]), (new[0], new[rows - 1])
+    fill_bands(plan, even, *ends, far_out, near_out)
 
 
 def grow_kernel(plan, axes, *refs):
-    turned, extra, coupled, permute, sea, grow, ocean, waves_out, *lat_out = refs
-    even = lax.rem(lax.axis_index(axes[0]), 2) == 0
+    turned, extra, coupled, permute, sea, grow, _, waves_out = refs
     both, _ = currents_twice(coupled[...])
     at_waves = twice(dot(permute[...], split_value(both)).astype(BF16))
     wet = twice(sea[...])
@@ -527,8 +539,6 @@
         factor = wet + dot(at_waves, growth_table(grow, number))
         grown = grown_part(plan, turned, extra[:, lanes], factor, lanes)
         waves_out[:, :, lanes] = grown.reshape(plan.rows, plan.cols, 256)
-    sea_rows = ocean[...].reshape(plan.rows, plan.cols, LANES)
-    fill_lat(plan, even, waves_out, sea_rows, lat_out)
 
 
 def last_kernel(plan, axes, *refs):
@@ -572,11 +582,12 @@
     shape = jax.ShapeDtypeStruct
     params = pltpu.CompilerParams(vmem_limit_bytes=32 * 1024 * 1024)
     to_sections = [shape((size, LANES), F32) for size in plan.sizes]
-    to_bands = [shape((cols, spectral // 2 + LANES), F32)] * 2
+    to_band = shape((cols, spectral // 2 + LANES), F32)
     state = shape((columns, LANES), F32)
     field = shape(spectra.shape, F32)
     at_edges = shape((2 * rows, LANES), F32)
     edge_field = shape((2 * rows, spectral), F32)
+    some = 2 * cols + 2 * rows
     edge = pltpu.VMEM((plan.edge, LANES), F32)
     spans = spectral // 256
 
@@ -594,28 +605,28 @@
     others = [(i, ((i + 1) ^ 1) - 1) for i in range(1, plan.bands)]
     others = [(i, j) for i, j in others if j < plan.bands]
 
-    def exchange(to_sections, make_to_bands):
+    def exchange(to_far, to_near, to_sections, waves):
         got = []
         if plan.relay:
             to_x, to_y, *to_sections = to_sections
             got.append(lax.ppermute(to_x, axes[1], plan.table(0, 1)))
-        kept, near_out, far_out = make_to_bands()
-        far_in = lax.ppermute(far_out, axes[0], others)
-        near_in = lax.ppermute(near_out, axes[0], pairs)
+        far_in = lax.ppermute(to_far, axes[0], others)
+        near_in = lax.ppermute(to_near, axes[0], pairs)
+        first = to_far
         if plan.relay:
-            (to_y,) = call(
+            (first,) = call(
                 relay_kernel,
                 [shape((2 * plan.chunk + plan.edge, LANES), F32)],
                 [],
                 got[0],
                 to_y,
             )
-            got.append(lax.ppermute(to_y, axes[1], plan.table(0, 2)))
+            got.append(lax.ppermute(first, axes[1], plan.table(0, 2)))
         got += [
             lax.ppermute(message, axes[1], table)
             for message, table in zip(to_sections, plan.direct)
         ]
-        return kept, [near_in, far_in, *got]
+        return waves(first), [near_in, far_in, *got]
 
     started = call(
         first_kernel,
@@ -625,18 +636,18 @@
             state,
             shape((columns, columns), BF16),
             shape((columns, 2 * columns), BF16),
-            shape((4 * rows, columns), BF16),
+            shape((some, columns), BF16),
             shape((columns, 4 * rows), BF16),
             state,
             at_edges,
             state,
             state,
-            at_edges,
+            shape((some, LANES), F32),
             shape((8, LANES), F32),
         ]
         + [shape(table.shape, table.dtype) for table in tables]
         + to_sections
-        + to_bands,
+        + [to_band] * 2,
         [
             pltpu.VMEM(turning.shape, F32),
             pltpu.VMEM(currents.shape, F32),
@@ -659,10 +670,9 @@
         ],
         space_in=pltpu.HBM,
     )
-    waves, ocean, packed, permute, order, permute_edge, order_edge = started[:7]
-    turn, turn_edge, sea, sea_order, sea_edge, keep, stokes, rates, grow = started[7:16]
-    sent, lat = started[16:-2], started[-2:]
-    waves, came = exchange(sent, lambda: (waves, *lat))
+    waves, ocean, packed, permute, order, permute_some, order_edge = started[:7]
+    turn, turn_edge, sea, sea_order, sea_some, keep, stokes, rates, grow = started[7:16]
+    waves, came = exchange(*started[-2:], started[16:-2], lambda _: waves)
     for step in range(STEPS - 1):
         turned, turned_edge, turned_order = call(
             move_kernel,
@@ -674,20 +684,21 @@
             *came[:2],
             order,
         )
-        ocean, packed, coupled, extra, *sent = call(
+        ocean, packed, coupled, extra, to_far, to_near, *sent = call(
             send_kernel,
-            [state, state, state, edge_field] + to_sections,
+            [state, state, state, edge_field, to_band, to_band] + to_sections,
             [edge, edge],
+            turned,
+            turned_edge,
             turned_order,
-            turned_edge,
             ocean,
             packed,
-            permute_edge,
+            permute_some,
             order_edge,
             turn_edge,
             sea,
             sea_order,
-            sea_edge,
+            sea_some,
             keep,
             stokes,
             rates,
@@ -695,21 +706,13 @@
             *came,
         )
 
-        def grown():
-            return call(
-                grow_kernel,
-                [field] + to_bands,
-                [],
-                turned,
-                extra,
-                coupled,
-                permute,
-                sea,
-                grow,
-                ocean,
+        def grown(first):
+            (waves,) = call(
+                grow_kernel, [field], [], turned, extra, coupled, permute, sea, grow, first
             )
-
-        waves, came = exchange(sent, grown)
+            return waves
+
+        waves, came = exchange(to_far, to_near, sent, grown)
     (turned,) = call(move_kernel, [field], [], waves, turn, rates, *came[:2])
     return call(
         last_kernel,

time: 31.1 us -> 30.8 us (level)
    ppermute x3, starting transfers between devices: 3.3 us -> 2.38 us  [exchange(): got.append(lax.ppermute(to_x, axes[1], plan.table(0, 1)))]
    ppermute x9, starting transfers between devices: 16.7 us -> 17.3 us  [the longest x3 9.25 us: exchange(): far_in = lax.ppermute(to_far, axes[0], others)]
  transfers between devices with their start and end apart: 12 -> 12, of which waited for: 3 -> 3; matrix products, arithmetic and copies ran while one was open for 0% -> 0% of each run, Pallas kernels for 9% -> 8%
where the time goes in v8:
time: 30.8 us; the launch traced here: 30.5 us
  starting transfers between devices  19.7 us (64%)
  Pallas kernels  7.12 us (23%)
  waiting for transfers between devices  2.88 us (9%)
  between operations  0.79 us (3%)
    ppermute x3, starting transfers between devices, exchange(): far_in = lax.ppermute(to_far, axes[0], others)  9.25 us
    pallas_call x12, Pallas kernels, call(): pl.pallas_call(functools.partial(kernel, plan, axes), out_shape=outs, in_...  7.12 us
    ppermute x3, starting transfers between devices, exchange(): near_in = lax.ppermute(to_near, axes[0], pairs)  4.17 us
    ppermute x3, starting transfers between devices, exchange(): got.append(lax.ppermute(first, axes[1], plan.table(0, 2)))  3.91 us
    ppermute x3, waiting for transfers between devices, exchange(): far_in = lax.ppermute(to_far, axes[0], others)  2.85 us
    ppermute x3, starting transfers between devices, exchange(): got.append(lax.ppermute(to_x, axes[1], plan.table(0, 1)))  2.38 us
  transfers between devices with their start and end apart: 12, of which 3 were waited for; matrix products, arithmetic and copies ran while one was open for 0% of the time, Pallas kernels for 8%

profile of v8, /device:TPU:1, one launch (start us, length us, event | category | flops | bytes accessed | tf_op | source)
XLA Modules:
  0.0 30.5 jit_solution(432110472833209661)
XLA Ops:
  0.6 1.7 %shard_map.104 = (f32[4,24,768]{2,1,0:T(8,128)S(1)}, f32[96,128]{1,0:T(8,128)S(1)}, f32[96,128]{1,0:T(8,128)S(1)}, bf16[96,96]{1,0:T(8,128)(2,1)S(1)}, bf16[96,1...) custom-call(f32[4,24,768]{2,1,0:T(8,128)} %refs_0_.1, ...), custom_call_target="tpu_custom_call" | custom-call | tf_op jit(solution)/shard_map/pallas_call | solution.py:595
  2.3 2.1 %collective-permute-start.2 = (f32[80,128]{1,0:T(8,128)S(1)}, f32[80,128]{1,0:T(8,128)S(1)}, u32[]{:S(2)}, u32[]{:S(2)}) collective-permute-start(f32[80,128]{1,0:T(8,128)S(1)} %get-tuple-element.64), channel_id=1, source_target_pairs={{0,8},{8,0},{16,24},{24,16},{1,9},{9,1},{17,25},{25,17},{2,10},{10... | collective-permute-start | bytes 122888 | tf_op jit(solution)/shard_map/ppermute | solution.py:612
  4.5 1.0 %collective-permute-start = (f32[24,512]{1,0:T(8,128)S(1)}, f32[24,512]{1,0:T(8,128)S(1)}, u32[]{:S(2)}, u32[]{:S(2)}) collective-permute-start(f32[24,512]{1,0:T(8,128)S(1)} %get-tuple-element.47), channel_id=1, source_target_pairs={{0,1},{1,0},{2,3},{3,2},{4,5},{5,4},{6,7},{7,6},{8,9},{9,8},{10,11... | collective-permute-start | bytes 147464 | tf_op jit(solution)/shard_map/ppermute | solution.py:614
  5.4 3.1 %collective-permute-start.1 = (f32[24,512]{1,0:T(8,128)S(1)}, f32[24,512]{1,0:T(8,128)S(1)}, u32[]{:S(2)}, u32[]{:S(2)}) collective-permute-start(f32[24,512]{1,0:T(8,128)S(1)} %get-tuple-element.48), channel_id=1, source_target_pairs={{1,2},{2,1},{3,4},{4,3},{5,6},{6,5},{9,10},{10,9},{11,12},{12,11},... | collective-permute-start | bytes 147464 | tf_op jit(solution)/shard_map/ppermute | solution.py:613
  8.5 0.0 collective-permute-done.2.from_x.refs_17_
  8.5 1.3 %collective-permute-start.3 = (f32[64,128]{1,0:T(8,128)S(1)}, f32[64,128]{1,0:T(8,128)S(1)}, u32[]{:S(2)}, u32[]{:S(2)}) collective-permute-start(f32[64,128]{1,0:T(8,128)S(1)} %shard_map.106), channel_id=1, source_target_pairs={{0,16},{8,24},{16,0},{24,8},{1,17},{9,25},{17,1},{25,9},{2,18},{10... | collective-permute-start | bytes 98312 | tf_op jit(solution)/shard_map/ppermute | solution.py:624
  9.8 0.0 collective-permute-done.refs_3_.refs_15_
  9.8 1.1 %collective-permute-done.1.refs_4_.refs_16_ = f32[24,512]{1,0:T(8,128)S(1)} collective-permute-done((f32[24,512]{1,0:T(8,128)S(1)}, f32[24,512]{1,0:T(8,128)S(1)}, u32[]{:S(2)}, u32[]{:S(2)}) %collective-permute-start.1) | collective-permute-done | bytes 49184 | tf_op jit(solution)/shard_map/ppermute | solution.py:613
  10.9 0.6 %shard_map.105 = (f32[4,24,768]{2,1,0:T(8,128)S(1)}, f32[8,768]{1,0:T(8,128)S(1)}, f32[96,768]{1,0:T(8,128)S(1)}) custom-call(f32[4,24,768]{2,1,0:T(8,128)S(1)} %get-tuple-element.44.refs_0_, f32[96,128]{1,0:T(8,128)S(1)} %get-tuple-element.45.refs_1_, f32[8,768]{1,0:T(8,128)S(1)} %get-tuple-element.46.refs_2_.refs_13_.refs_7_, ...), custom_call_target="tpu_custom_call" | custom-call | tf_op jit(solution)/shard_map/pallas_call | solution.py:595
  11.5 0.0 collective-permute-done.3.refs_18_
  11.5 0.9 %shard_map.107 = (f32[96,128]{1,0:T(8,128)S(1)}, f32[96,128]{1,0:T(8,128)S(1)}, f32[96,128]{1,0:T(8,128)S(1)}, f32[8,768]{1,0:T(8,128)S(1)}, f32[24,512]{1,0:T(8...) custom-call(f32[4,24,768]{2,1,0:T(8,128)S(1)} %get-tuple-element.50.refs_0_, ...), custom_call_target="tpu_custom_call" | custom-call | tf_op jit(solution)/shard_map/pallas_call | solution.py:595
  12.4 0.1 collective-permute-start.4
  12.5 1.7 %collective-permute-start.5 = (f32[24,512]{1,0:T(8,128)S(1)}, f32[24,512]{1,0:T(8,128)S(1)}, u32[]{:S(2)}, u32[]{:S(2)}) collective-permute-start(f32[24,512]{1,0:T(8,128)S(1)} %get-tuple-element.71), channel_id=1, source_target_pairs={{0,1},{1,0},{2,3},{3,2},{4,5},{5,4},{6,7},{7,6},{8,9},{9,8},{10,11... | collective-permute-start | bytes 147464 | tf_op jit(solution)/shard_map/ppermute | solution.py:614
  14.2 3.1 %collective-permute-start.6 = (f32[24,512]{1,0:T(8,128)S(1)}, f32[24,512]{1,0:T(8,128)S(1)}, u32[]{:S(2)}, u32[]{:S(2)}) collective-permute-start(f32[24,512]{1,0:T(8,128)S(1)} %get-tuple-element.72), channel_id=1, source_target_pairs={{1,2},{2,1},{3,4},{4,3},{5,6},{6,5},{9,10},{10,9},{11,12},{12,11},... | collective-permute-start | bytes 147464 | tf_op jit(solution)/shard_map/ppermute | solution.py:613
  17.3 0.0 collective-permute-done.4.from_x.refs_17_
  17.4 1.3 %collective-permute-start.7 = (f32[64,128]{1,0:T(8,128)S(1)}, f32[64,128]{1,0:T(8,128)S(1)}, u32[]{:S(2)}, u32[]{:S(2)}) collective-permute-start(f32[64,128]{1,0:T(8,128)S(1)} %shard_map.108.refs_6_), channel_id=1, source_target_pairs={{0,16},{8,24},{16,0},{24,8},{1,17},{9,25},{17,1},{25,9},{2,18},{10... | collective-permute-start | bytes 98312 | tf_op jit(solution)/shard_map/ppermute | solution.py:624
  18.7 0.4 %shard_map.109.refs_0_ = f32[4,24,768]{2,1,0:T(8,128)S(1)} custom-call(f32[4,24,768]{2,1,0:T(8,128)S(1)} %get-tuple-element.50.refs_0_, f32[8,768]{1,0:T(8,128)S(1)} %get-tuple-element.66.refs_1_, f32[96,128]{1,0:T(8,128)S(1)} %get-tuple-element.67.refs_2_, bf16[96,96]{1,0:T(8,128)(2,1)S(1)} %get-tuple-element.68.refs_3_, ...), custom_call_target="tpu_custom_call" | custom-call | tf_op jit(solution)/shard_map/pallas_call | solution.py:595
  19.1 0.0 collective-permute-done.5.refs_3_.refs_15_
  19.1 0.9 %collective-permute-done.6.refs_4_.refs_16_ = f32[24,512]{1,0:T(8,128)S(1)} collective-permute-done((f32[24,512]{1,0:T(8,128)S(1)}, f32[24,512]{1,0:T(8,128)S(1)}, u32[]{:S(2)}, u32[]{:S(2)}) %collective-permute-start.6) | collective-permute-done | bytes 49184 | tf_op jit(solution)/shard_map/ppermute | solution.py:613
  19.9 0.6 %shard_map.110 = (f32[4,24,768]{2,1,0:T(8,128)S(1)}, f32[8,768]{1,0:T(8,128)S(1)}, f32[96,768]{1,0:T(8,128)S(1)}) custom-call(f32[4,24,768]{2,1,0:T(8,128)S(1)} %shard_map.109.refs_0_, f32[96,128]{1,0:T(8,128)S(1)} %get-tuple-element.45.refs_1_, f32[8,768]{1,0:T(8,128)S(1)} %get-tuple-element.46.refs_2_.refs_13_.refs_7_, ...), custom_call_target="tpu_custom_call" | custom-call | tf_op jit(solution)/shard_map/pallas_call | solution.py:595
  20.5 0.0 collective-permute-done.7.refs_18_
  20.5 0.9 %shard_map.111 = (f32[96,128]{1,0:T(8,128)S(1)}, f32[96,128]{1,0:T(8,128)S(1)}, f32[96,128]{1,0:T(8,128)S(1)}, f32[8,768]{1,0:T(8,128)S(1)}, f32[24,512]{1,0:T(8...) custom-call(f32[4,24,768]{2,1,0:T(8,128)S(1)} %get-tuple-element.73.refs_0_, ...), custom_call_target="tpu_custom_call" | custom-call | tf_op jit(solution)/shard_map/pallas_call | solution.py:595
  21.4 0.2 collective-permute-start.8
  21.6 1.5 %collective-permute-start.9 = (f32[24,512]{1,0:T(8,128)S(1)}, f32[24,512]{1,0:T(8,128)S(1)}, u32[]{:S(2)}, u32[]{:S(2)}) collective-permute-start(f32[24,512]{1,0:T(8,128)S(1)} %get-tuple-element.82), channel_id=1, source_target_pairs={{0,1},{1,0},{2,3},{3,2},{4,5},{5,4},{6,7},{7,6},{8,9},{9,8},{10,11... | collective-permute-start | bytes 147464 | tf_op jit(solution)/shard_map/ppermute | solution.py:614
  23.1 3.1 %collective-permute-start.10 = (f32[24,512]{1,0:T(8,128)S(1)}, f32[24,512]{1,0:T(8,128)S(1)}, u32[]{:S(2)}, u32[]{:S(2)}) collective-permute-start(f32[24,512]{1,0:T(8,128)S(1)} %get-tuple-element.83), channel_id=1, source_target_pairs={{1,2},{2,1},{3,4},{4,3},{5,6},{6,5},{9,10},{10,9},{11,12},{12,11},... | collective-permute-start | bytes 147464 | tf_op jit(solution)/shard_map/ppermute | solution.py:613
  26.2 1.3 %collective-permute-start.11 = (f32[64,128]{1,0:T(8,128)S(1)}, f32[64,128]{1,0:T(8,128)S(1)}, u32[]{:S(2)}, u32[]{:S(2)}) collective-permute-start(f32[64,128]{1,0:T(8,128)S(1)} %shard_map.112.refs_6_), channel_id=1, source_target_pairs={{0,16},{8,24},{16,0},{24,8},{1,17},{9,25},{17,1},{25,9},{2,18},{10... | collective-permute-start | bytes 98312 | tf_op jit(solution)/shard_map/ppermute | solution.py:624
  27.5 0.4 %shard_map.113.refs_0_ = f32[4,24,768]{2,1,0:T(8,128)S(1)} custom-call(f32[4,24,768]{2,1,0:T(8,128)S(1)} %get-tuple-element.73.refs_0_, f32[8,768]{1,0:T(8,128)S(1)} %get-tuple-element.78.refs_1_, f32[96,128]{1,0:T(8,128)S(1)} %get-tuple-element.79.refs_2_, bf16[96,96]{1,0:T(8,128)(2,1)S(1)} %get-tuple-element.68.refs_3_, ...), custom_call_target="tpu_custom_call" | custom-call | tf_op jit(solution)/shard_map/pallas_call | solution.py:595
  27.9 0.0 collective-permute-done.9.refs_3_.refs_9_
  27.9 0.9 %collective-permute-done.10.refs_4_.refs_10_ = f32[24,512]{1,0:T(8,128)S(1)} collective-permute-done((f32[24,512]{1,0:T(8,128)S(1)}, f32[24,512]{1,0:T(8,128)S(1)}, u32[]{:S(2)}, u32[]{:S(2)}) %collective-permute-start.10) | collective-permute-done | bytes 49184 | tf_op jit(solution)/shard_map/ppermute | solution.py:613
  28.8 0.6 %shard_map.114.refs_0_ = f32[4,24,768]{2,1,0:T(8,128)S(1)} custom-call(f32[4,24,768]{2,1,0:T(8,128)S(1)} %shard_map.113.refs_0_, f32[96,128]{1,0:T(8,128)S(1)} %get-tuple-element.45.refs_1_, f32[8,768]{1,0:T(8,128)S(1)} %get-tuple-element.46.refs_2_.refs_13_.refs_7_, f32[24,512]{1,0:T(8,128)S(1)} %collective-permute-done.9.refs_3_.refs_9_, ...), custom_call_target="tpu_custom_call" | custom-call | tf_op jit(solution)/shard_map/pallas_call | solution.py:595
  29.4 0.0 collective-permute-done.11.refs_12_
  29.4 1.1 %shard_map.115 = (f32[4,24,768]{2,1,0:T(8,128)}, f32[4,24,64]{2,1,0:T(8,128)}) custom-call(f32[4,24,768]{2,1,0:T(8,128)S(1)} %shard_map.114.refs_0_, f32[96,128]{1,0:T(8,128)S(1)} %get-tuple-element.84.refs_1_, f32[96,128]{1,0:T(8,128)S(1)} %get-tuple-element.85.refs_2_, bf16[96,96]{1,0:T(8,128)(2,1)S(1)} %get-tuple-element.68.refs_3_, ...), custom_call_target="tpu_custom_call" | custom-call | tf_op jit(solution)/shard_map/pallas_call | solution.py:595
  (4 shorter events, 0.0 us)
Async XLA Ops:
  2.3 6.2 %collective-permute-start.2 = (f32[80,128]{1,0:T(8,128)S(1)}, f32[80,128]{1,0:T(8,128)S(1)}, u32[]{:S(2)}, u32[]{:S(2)}) collective-permute-start(f32[80,128]{1,0:T(8,128)S(1)} %get-tuple-element.64), channel_id=1, source_target_pairs={{0,8},{8,0},{16,24},{24,16},{1,9},{9,1},{17,25},{25,17},{2,10},{10... | collective-permute-start | bytes 122888 | tf_op jit(solution)/shard_map/ppermute | solution.py:612
  4.5 5.4 %collective-permute-start = (f32[24,512]{1,0:T(8,128)S(1)}, f32[24,512]{1,0:T(8,128)S(1)}, u32[]{:S(2)}, u32[]{:S(2)}) collective-permute-start(f32[24,512]{1,0:T(8,128)S(1)} %get-tuple-element.47), channel_id=1, source_target_pairs={{0,1},{1,0},{2,3},{3,2},{4,5},{5,4},{6,7},{7,6},{8,9},{9,8},{10,11... | collective-permute-start | bytes 147464 | tf_op jit(solution)/shard_map/ppermute | solution.py:614
  5.4 5.5 %collective-permute-start.1 = (f32[24,512]{1,0:T(8,128)S(1)}, f32[24,512]{1,0:T(8,128)S(1)}, u32[]{:S(2)}, u32[]{:S(2)}) collective-permute-start(f32[24,512]{1,0:T(8,128)S(1)} %get-tuple-element.48), channel_id=1, source_target_pairs={{1,2},{2,1},{3,4},{4,3},{5,6},{6,5},{9,10},{10,9},{11,12},{12,11},... | collective-permute-start | bytes 147464 | tf_op jit(solution)/shard_map/ppermute | solution.py:613
  8.5 3.0 %collective-permute-start.3 = (f32[64,128]{1,0:T(8,128)S(1)}, f32[64,128]{1,0:T(8,128)S(1)}, u32[]{:S(2)}, u32[]{:S(2)}) collective-permute-start(f32[64,128]{1,0:T(8,128)S(1)} %shard_map.106), channel_id=1, source_target_pairs={{0,16},{8,24},{16,0},{24,8},{1,17},{9,25},{17,1},{25,9},{2,18},{10... | collective-permute-start | bytes 98312 | tf_op jit(solution)/shard_map/ppermute | solution.py:624
  12.4 4.9 %collective-permute-start.4 = (f32[80,128]{1,0:T(8,128)S(1)}, f32[80,128]{1,0:T(8,128)S(1)}, u32[]{:S(2)}, u32[]{:S(2)}) collective-permute-start(f32[80,128]{1,0:T(8,128)S(1)} %get-tuple-element.69), channel_id=1, source_target_pairs={{0,8},{8,0},{16,24},{24,16},{1,9},{9,1},{17,25},{25,17},{2,10},{10... | collective-permute-start | bytes 122888 | tf_op jit(solution)/shard_map/ppermute | solution.py:612
  12.5 6.5 %collective-permute-start.5 = (f32[24,512]{1,0:T(8,128)S(1)}, f32[24,512]{1,0:T(8,128)S(1)}, u32[]{:S(2)}, u32[]{:S(2)}) collective-permute-start(f32[24,512]{1,0:T(8,128)S(1)} %get-tuple-element.71), channel_id=1, source_target_pairs={{0,1},{1,0},{2,3},{3,2},{4,5},{5,4},{6,7},{7,6},{8,9},{9,8},{10,11... | collective-permute-start | bytes 147464 | tf_op jit(solution)/shard_map/ppermute | solution.py:614
  14.2 5.7 %collective-permute-start.6 = (f32[24,512]{1,0:T(8,128)S(1)}, f32[24,512]{1,0:T(8,128)S(1)}, u32[]{:S(2)}, u32[]{:S(2)}) collective-permute-start(f32[24,512]{1,0:T(8,128)S(1)} %get-tuple-element.72), channel_id=1, source_target_pairs={{1,2},{2,1},{3,4},{4,3},{5,6},{6,5},{9,10},{10,9},{11,12},{12,11},... | collective-permute-start | bytes 147464 | tf_op jit(solution)/shard_map/ppermute | solution.py:613
  17.4 3.2 %collective-permute-start.7 = (f32[64,128]{1,0:T(8,128)S(1)}, f32[64,128]{1,0:T(8,128)S(1)}, u32[]{:S(2)}, u32[]{:S(2)}) collective-permute-start(f32[64,128]{1,0:T(8,128)S(1)} %shard_map.108.refs_6_), channel_id=1, source_target_pairs={{0,16},{8,24},{16,0},{24,8},{1,17},{9,25},{17,1},{25,9},{2,18},{10... | collective-permute-start | bytes 98312 | tf_op jit(solution)/shard_map/ppermute | solution.py:624
  21.4 4.8 %collective-permute-start.8 = (f32[80,128]{1,0:T(8,128)S(1)}, f32[80,128]{1,0:T(8,128)S(1)}, u32[]{:S(2)}, u32[]{:S(2)}) collective-permute-start(f32[80,128]{1,0:T(8,128)S(1)} %get-tuple-element.80), channel_id=1, source_target_pairs={{0,8},{8,0},{16,24},{24,16},{1,9},{9,1},{17,25},{25,17},{2,10},{10... | collective-permute-start | bytes 122888 | tf_op jit(solution)/shard_map/ppermute | solution.py:612
  21.6 6.3 %collective-permute-start.9 = (f32[24,512]{1,0:T(8,128)S(1)}, f32[24,512]{1,0:T(8,128)S(1)}, u32[]{:S(2)}, u32[]{:S(2)}) collective-permute-start(f32[24,512]{1,0:T(8,128)S(1)} %get-tuple-element.82), channel_id=1, source_target_pairs={{0,1},{1,0},{2,3},{3,2},{4,5},{5,4},{6,7},{7,6},{8,9},{9,8},{10,11... | collective-permute-start | bytes 147464 | tf_op jit(solution)/shard_map/ppermute | solution.py:614
  23.1 5.7 %collective-permute-start.10 = (f32[24,512]{1,0:T(8,128)S(1)}, f32[24,512]{1,0:T(8,128)S(1)}, u32[]{:S(2)}, u32[]{:S(2)}) collective-permute-start(f32[24,512]{1,0:T(8,128)S(1)} %get-tuple-element.83), channel_id=1, source_target_pairs={{1,2},{2,1},{3,4},{4,3},{5,6},{6,5},{9,10},{10,9},{11,12},{12,11},... | collective-permute-start | bytes 147464 | tf_op jit(solution)/shard_map/ppermute | solution.py:613
  26.2 3.2 %collective-permute-start.11 = (f32[64,128]{1,0:T(8,128)S(1)}, f32[64,128]{1,0:T(8,128)S(1)}, u32[]{:S(2)}, u32[]{:S(2)}) collective-permute-start(f32[64,128]{1,0:T(8,128)S(1)} %shard_map.112.refs_6_), channel_id=1, source_target_pairs={{0,16},{8,24},{16,0},{24,8},{1,17},{9,25},{17,1},{25,9},{2,18},{10... | collective-permute-start | bytes 98312 | tf_op jit(solution)/shard_map/ppermute | solution.py:624

commit v9 on v8

--- a/solution.py
+++ b/solution.py
@@ -196,24 +196,18 @@
             )
 
 
-def take_sections(plan, section, packed_in, sec_in, coupled, west_edge, east_edge):
+def take_sections(plan, section, packed_in, sec_in, coupled):
     chunk = plan.chunk
     own = pl.ds(pl.multiple_of(section * chunk, 8), chunk)
     coupled[own, :] = packed_in[own, :]
-    west_edge[...] = jnp.zeros_like(west_edge)
-    east_edge[...] = jnp.zeros_like(east_edge)
+    west = east = jnp.zeros((plan.edge, LANES), F32)
     for source, message, at, edge_at in plan.received(section, sec_in):
         coupled[pl.ds(pl.multiple_of(source * chunk, 8), chunk), :] = message[at : at + chunk, :]
-        if edge_at is None:
-            continue
-
-        @pl.when(source == section + 1)
-        def _():
-            east_edge[...] = message[edge_at : edge_at + plan.edge, :]
-
-        @pl.when(source == section - 1)
-        def _():
-            west_edge[...] = message[edge_at : edge_at + plan.edge, :]
+        if edge_at is not None:
+            edge = message[edge_at : edge_at + plan.edge, :]
+            west = jnp.where(source == section - 1, edge, west)
+            east = jnp.where(source == section + 1, edge, east)
+    return west, east
 
 
 def edge_part(plan, rates, turn_edge, west_edge, east_edge):
@@ -298,102 +292,55 @@
     out[plan.chunk :, :] = from_x[plan.chunk + plan.edge :, :]
 
 
+def square_places(plan):
+    shape = (plan.columns, plan.columns)
+    return lax.broadcasted_iota(jnp.int32, shape, 0), lax.broadcasted_iota(jnp.int32, shape, 1)
+
+
+def row_of(plan, ref):
+    return jnp.concatenate([ref[row : row + 1, :] for row in range(plan.rows)], axis=1)
+
+
+def column_of(plan, row):
+    down, across = square_places(plan)
+    spread = jnp.broadcast_to(row, down.shape)
+    return jnp.sum(jnp.where(down == across, spread, 0.0), axis=1, keepdims=True)
+
+
 def first_kernel(plan, axes, *refs):
-    waves_in, turning_in, currents_in, drag_in, mask_in, target_in = refs[:6]
-    tables_in, refs = refs[6:9], refs[9:]
-    waves, ocean_out, packed_out, permute_out, order_out, permute_some_out, order_edge_out = refs[:7]
-    turn_out, turn_edge_out, sea_out, sea_order_out, sea_some_out, keep_out = refs[7:13]
-    tables_out, refs = refs[13:16], refs[16:]
+    waves_in, currents_in, target_in, stokes_in, refs = *refs[:4], refs[4:]
+    waves, ocean_out, packed_out, order_out, stokes, refs = *refs[:5], refs[5:]
     count = len(plan.sizes)
     sec_out, lat_out, refs = refs[:count], refs[count : count + 2], refs[count + 2 :]
-    turning, currents, drag, mask, target, done = refs
-    pairs = [
-        (target_in, target),
-        (turning_in, turning),
-        (mask_in, mask),
-        (drag_in, drag),
-        (waves_in, waves),
-        (tables_in[0], tables_out[0]),
-        (currents_in, currents),
-        (tables_in[1], tables_out[1]),
-        (tables_in[2], tables_out[2]),
-    ]
+    currents, target, done = refs
+    pairs = [(target_in, target), (waves_in, waves), (stokes_in, stokes), (currents_in, currents)]
     copies = [pltpu.make_async_copy(a, b, done.at[k]) for k, (a, b) in enumerate(pairs)]
     for copy in copies:
         copy.start()
     section, band = lax.axis_index(axes[1]), lax.axis_index(axes[0])
     even = lax.rem(band, 2) == 0
     columns, rows, cols = plan.columns, plan.rows, plan.cols
-    across = lane_of((columns, columns))
-    down = lax.broadcasted_iota(jnp.int32, (columns, columns), 0)
-    here = across == down
-
-    def row_of(ref):
-        return jnp.concatenate([ref[row : row + 1, :] for row in range(rows)], axis=1)
-
-    def column_of(row):
-        spread = jnp.broadcast_to(row, (columns, columns))
-        return jnp.sum(jnp.where(here, spread, jnp.zeros_like(spread)), axis=1, keepdims=True)
-
-    def edges_of(value):
-        west = [value[row * cols : row * cols + 1, :] for row in range(rows)]
-        east = [value[(row + 1) * cols - 1 : (row + 1) * cols, :] for row in range(rows)]
-        return jnp.concatenate(west + east, axis=0)
-
-    for copy in copies[:7]:
+    copies[0].wait()
+    down, across = square_places(plan)
+    target_row = row_of(plan, target).astype(F32)
+    same = column_of(plan, target_row) == target_row
+    rank = jnp.sum(jnp.where(same & (down < across), 1.0, 0.0), axis=0, keepdims=True)
+    slot = target_row * float(plan.chunk) + rank
+    order = jnp.where(slot == down.astype(F32), 1.0, 0.0).astype(BF16)
+    order_out[...] = twice(order)
+    for copy in copies[1:]:
         copy.wait()
     total = None
     for start in range(0, plan.spectral, 256):
         part = waves[:, :, start : start + 256].reshape(columns, 256)
-        product = stokes_product(part, tables_out[0][start : start + 256, :])
+        product = stokes_product(part, stokes[start : start + 256, :])
         total = product if total is None else total + product
     moments = total[:columns] + total[columns:]
     moments = moments + pltpu.roll(moments, LANES // 2, 1)
-    sea_row = row_of(mask).astype(F32)
-    sea = column_of(sea_row)
-    target_row = row_of(target).astype(F32)
-    target_col = column_of(target_row)
-    same = target_col == target_row
-    rank_col = jnp.sum(jnp.where(same & (across < down), 1.0, 0.0), axis=1, keepdims=True)
-    rank_row = jnp.sum(jnp.where(same & (down < across), 1.0, 0.0), axis=0, keepdims=True)
-    slot_col = target_col * float(plan.chunk) + rank_col
-    slot_row = target_row * float(plan.chunk) + rank_row
-    permute = jnp.where(slot_col == across.astype(F32), sea, 0.0)
-    order = jnp.where(slot_row == down.astype(F32), 1.0, 0.0)
-    permute_out[...] = permute.astype(BF16)
-    order_out[...] = twice(order).astype(BF16)
-    sea_order = jnp.sum(order * sea_row, axis=1, keepdims=True)
-    sea_order_out[...] = jnp.broadcast_to(sea_order, (columns, LANES))
-    edge_count = 4 * rows
-    number = lax.rem(lane_of((columns, edge_count)), 2 * rows)
-    wanted = lax.rem(number, rows) * cols + lax.div(number, rows) * (cols - 1)
-    chosen = lax.broadcasted_iota(jnp.int32, (columns, edge_count), 0) == wanted
-    order_edge_out[...] = dot(
-        order.astype(BF16), jnp.where(chosen, 1.0, 0.0).astype(BF16)
-    ).astype(BF16)
-    shape = (2 * cols + 2 * rows, columns)
-    place = lax.broadcasted_iota(jnp.int32, shape, 0)
-    number = place - 2 * cols
-    wanted = jnp.where(
-        place < 2 * cols,
-        place + jnp.where(place < cols, 0, (rows - 2) * cols),
-        lax.rem(number, rows) * cols + lax.div(number, rows) * (cols - 1),
-    )
-    chosen = jnp.where(lane_of(shape) == wanted, 1.0, 0.0).astype(BF16)
-    permute_some_out[...] = dot(chosen, permute.astype(BF16)).astype(BF16)
-    sea_wide = jnp.broadcast_to(sea, (columns, LANES))
-    sea_some_out[...] = dot(chosen, sea_wide.astype(BF16))
-    sea_out[...] = sea_wide
-    turn = jnp.broadcast_to(column_of(row_of(turning)), (columns, LANES))
-    turn_out[...] = turn
-    turn_edge_out[...] = edges_of(turn)
-    keep = 1.0 - drag[...].reshape(1, plan.depth)
-    blank = jnp.zeros((1, LANES - 2 * plan.depth), F32)
-    keep_out[...] = jnp.broadcast_to(jnp.concatenate([keep, keep, blank], axis=1), (8, LANES))
     flat = currents[...].reshape(columns, 2 * plan.depth)
     ocean = jnp.concatenate([flat, jnp.zeros((columns, LANES - 2 * plan.depth), F32)], axis=1)
     ocean_out[...] = ocean
-    ordered = dot(order.astype(BF16), split_value(moments))
+    ordered = dot(order, split_value(moments))
     ordered = ordered + pltpu.roll(ordered, LANES // 2, 1)
     west = [waves[row, 0:1, :] for row in range(rows)]
     east = [waves[row, cols - 1 : cols, :] for row in range(rows)]
@@ -402,8 +349,48 @@
     sea_rows = ocean.reshape(rows, cols, LANES)
     ends = (waves[0], waves[rows - 1]), (sea_rows[0], sea_rows[rows - 1])
     fill_bands(plan, even, *ends, *lat_out)
-    for copy in copies[7:]:
-        copy.wait()
+
+
+def map_kernel(plan, axes, *refs):
+    turning, drag, mask, order_twice, _, refs = *refs[:5], refs[5:]
+    permute_out, permute_some_out, order_edge_out, turn_out, turn_edge_out = refs[:5]
+    sea_out, sea_order_out, sea_some_out, keep_out = refs[5:]
+    columns, rows, cols = plan.columns, plan.rows, plan.cols
+    order = order_twice[:, :columns]
+    sea = jnp.broadcast_to(column_of(plan, row_of(plan, mask).astype(F32)), (columns, LANES))
+    turn = jnp.broadcast_to(column_of(plan, row_of(plan, turning)), (columns, LANES))
+    sea_out[...] = sea
+    turn_out[...] = turn
+    west = [turn[row * cols : row * cols + 1, :] for row in range(rows)]
+    east = [turn[(row + 1) * cols - 1 : (row + 1) * cols, :] for row in range(rows)]
+    turn_edge_out[...] = jnp.concatenate(west + east, axis=0)
+    sea_order_out[...] = dot(order, sea.astype(BF16))
+    down, across = square_places(plan)
+    same = jnp.where(down == across, 1.0, 0.0).astype(BF16)
+    back = lax.dot_general(
+        order, same, (((0,), (0,)), ((), ())), preferred_element_type=F32
+    )
+    permute = (back * sea[:, :columns]).astype(BF16)
+    permute_out[...] = permute
+    shape = (columns, 4 * rows)
+    number = lax.rem(lane_of(shape), 2 * rows)
+    wanted = lax.rem(number, rows) * cols + lax.div(number, rows) * (cols - 1)
+    chosen = lax.broadcasted_iota(jnp.int32, shape, 0) == wanted
+    order_edge_out[...] = dot(order, jnp.where(chosen, 1.0, 0.0).astype(BF16)).astype(BF16)
+    shape = (2 * cols + 2 * rows, columns)
+    place = lax.broadcasted_iota(jnp.int32, shape, 0)
+    number = place - 2 * cols
+    wanted = jnp.where(
+        place < 2 * cols,
+        place + jnp.where(place < cols, 0, (rows - 2) * cols),
+        lax.rem(number, rows) * cols + lax.div(number, rows) * (cols - 1),
+    )
+    chosen = jnp.where(lane_of(shape) == wanted, 1.0, 0.0).astype(BF16)
+    permute_some_out[...] = dot(chosen, permute).astype(BF16)
+    sea_some_out[...] = dot(chosen, sea.astype(BF16))
+    keep = 1.0 - drag[...].reshape(1, plan.depth)
+    blank = jnp.zeros((1, LANES - 2 * plan.depth), F32)
+    keep_out[...] = jnp.broadcast_to(jnp.concatenate([keep, keep, blank], axis=1), (8, LANES))
 
 
 class Directions:
@@ -486,12 +473,12 @@
     count = len(plan.sizes)
     near, far, sec_in, refs = refs[0], refs[1], refs[2 : 2 + count], refs[2 + count :]
     ocean_out, packed_out, coupled, extra_out, far_out, near_out = refs[:6]
-    sec_out, (west_edge, east_edge) = refs[6 : 6 + count], refs[6 + count :]
+    sec_out = refs[6:]
     section, band = lax.axis_index(axes[1]), lax.axis_index(axes[0])
     even = lax.rem(band, 2) == 0
     columns, rows, cols = plan.columns, plan.rows, plan.cols
 
-    take_sections(plan, section, packed_in, sec_in, coupled, west_edge, east_edge)
+    west_edge, east_edge = take_sections(plan, section, packed_in, sec_in, coupled)
     both, drift = currents_twice(coupled[...])
     in_order = twice(split_value(both * sea_order[...]))
     at_some = twice(dot(permute_some[...], split_value(both)).astype(BF16))
@@ -545,11 +532,11 @@
     turned, ocean_in, packed_in, permute, turn_edge, sea, keep, rates, grow = refs[:9]
     count = len(plan.sizes)
     near, far, sec_in, refs = refs[9], refs[10], refs[11 : 11 + count], refs[11 + count :]
-    waves_far, ocean_far, coupled, west_edge, east_edge, waves_out, ocean_out, done = refs
+    waves_far, ocean_far, coupled, waves_out, ocean_out, done = refs
     section, band = lax.axis_index(axes[1]), lax.axis_index(axes[0])
     even = lax.rem(band, 2) == 0
 
-    take_sections(plan, section, packed_in, sec_in, coupled, west_edge, east_edge)
+    west_edge, east_edge = take_sections(plan, section, packed_in, sec_in, coupled)
     both, drift = currents_twice(coupled[...])
     at_waves = twice(dot(permute[...], split_value(both)).astype(BF16))
     extra = edge_part(plan, rates, turn_edge, west_edge, east_edge)
@@ -577,7 +564,9 @@
 
 
 def per_device(plan, axes, spectra, turning, currents, drag_rates, land_mask, ocean_target):
-    tables = [jnp.asarray(table) for table in build_tables(NFREQ, NDIR, drag_rates.shape[0])]
+    stokes, rates, grow = (
+        jnp.asarray(table) for table in build_tables(NFREQ, NDIR, drag_rates.shape[0])
+    )
     columns, rows, cols, spectral = plan.columns, plan.rows, plan.cols, plan.spectral
     shape = jax.ShapeDtypeStruct
     params = pltpu.CompilerParams(vmem_limit_bytes=32 * 1024 * 1024)
@@ -588,7 +577,6 @@
     at_edges = shape((2 * rows, LANES), F32)
     edge_field = shape((2 * rows, spectral), F32)
     some = 2 * cols + 2 * rows
-    edge = pltpu.VMEM((plan.edge, LANES), F32)
     spans = spectral // 256
 
     def call(kernel, outs, scratch, *args, space_in=pltpu.VMEM, space_out=pltpu.VMEM):
@@ -605,7 +593,7 @@
     others = [(i, ((i + 1) ^ 1) - 1) for i in range(1, plan.bands)]
     others = [(i, j) for i, j in others if j < plan.bands]
 
-    def exchange(to_far, to_near, to_sections, waves):
+    def exchange(to_far, to_near, to_sections, meanwhile):
         got = []
         if plan.relay:
             to_x, to_y, *to_sections = to_sections
@@ -626,53 +614,56 @@
             lax.ppermute(message, axes[1], table)
             for message, table in zip(to_sections, plan.direct)
         ]
-        return waves(first), [near_in, far_in, *got]
-
-    started = call(
+        return meanwhile(first), [near_in, far_in, *got]
+
+    waves, ocean, packed, order, stokes, *sent = call(
         first_kernel,
         [
             field,
             state,
             state,
-            shape((columns, columns), BF16),
             shape((columns, 2 * columns), BF16),
-            shape((some, columns), BF16),
-            shape((columns, 4 * rows), BF16),
-            state,
-            at_edges,
-            state,
-            state,
-            shape((some, LANES), F32),
-            shape((8, LANES), F32),
-        ]
-        + [shape(table.shape, table.dtype) for table in tables]
-        + to_sections
-        + [to_band] * 2,
+            shape(stokes.shape, stokes.dtype),
+            *to_sections,
+            to_band,
+            to_band,
+        ],
         [
-            pltpu.VMEM(turning.shape, F32),
             pltpu.VMEM(currents.shape, F32),
-            pltpu.VMEM(drag_rates.shape, F32),
-            pltpu.VMEM(land_mask.shape, jnp.int32),
             pltpu.VMEM(ocean_target.shape, jnp.int32),
-            pltpu.SemaphoreType.DMA((9,)),
+            pltpu.SemaphoreType.DMA((4,)),
         ],
         *[
             pltpu.with_memory_space_constraint(array, pltpu.HBM)
-            for array in (
-                spectra,
-                turning,
-                currents,
-                drag_rates,
-                land_mask,
-                ocean_target,
-                *tables,
-            )
+            for array in (spectra, currents, ocean_target, stokes)
         ],
         space_in=pltpu.HBM,
     )
-    waves, ocean, packed, permute, order, permute_some, order_edge = started[:7]
-    turn, turn_edge, sea, sea_order, sea_some, keep, stokes, rates, grow = started[7:16]
-    waves, came = exchange(*started[-2:], started[16:-2], lambda _: waves)
+
+    def maps(first):
+        return call(
+            map_kernel,
+            [
+                shape((columns, columns), BF16),
+                shape((some, columns), BF16),
+                shape((columns, 4 * rows), BF16),
+                state,
+                at_edges,
+                state,
+                state,
+                shape((some, LANES), F32),
+                shape((8, LANES), F32),
+            ],
+            [],
+            turning,
+            drag_rates,
+            land_mask,
+            order,
+            first,
+        )
+
+    made, came = exchange(*sent[-2:], sent[:-2], maps)
+    permute, permute_some, order_edge, turn, turn_edge, sea, sea_order, sea_some, keep = made
     for step in range(STEPS - 1):
         turned, turned_edge, turned_order = call(
             move_kernel,
@@ -687,7 +678,7 @@
         ocean, packed, coupled, extra, to_far, to_near, *sent = call(
             send_kernel,
             [state, state, state, edge_field, to_band, to_band] + to_sections,
-            [edge, edge],
+            [],
             turned,
             turned_edge,
             turned_order,
@@ -719,8 +710,6 @@
         [field, shape(currents.shape, F32)],
         [
             pltpu.VMEM((columns, LANES), F32),
-            edge,
-            edge,
             pltpu.VMEM(spectra.shape, F32),
             pltpu.VMEM(currents.shape, F32),
             pltpu.SemaphoreType.DMA((1 + spans,)),

time: 30.8 us -> 30.7 us (level)
  waiting for transfers between devices: 2.88 us -> 2.55 us
    ppermute x3, waiting for transfers between devices: 2.85 us -> 2.52 us  [exchange(): far_in = lax.ppermute(to_far, axes[0], others)]
    pallas_call x12 -> x13, Pallas kernels: 7.12 us -> 7.31 us  [call(): pl.pallas_call(functools.partial(kernel, plan, axes), out_shape=outs, in_...]
  transfers between devices with their start and end apart: 12 -> 12, of which waited for: 3 -> 3; matrix products, arithmetic and copies ran while one was open for 0% -> 0% of each run, Pallas kernels for 8% -> 9%
where the time goes in v9:
time: 30.7 us; the launch traced here: 30.5 us
  starting transfers between devices  19.7 us (64%)
  Pallas kernels  7.31 us (24%)
  waiting for transfers between devices  2.55 us (8%)
  between operations  0.85 us (3%)
    ppermute x3, starting transfers between devices, exchange(): far_in = lax.ppermute(to_far, axes[0], others)  9.24 us
    pallas_call x13, Pallas kernels, call(): pl.pallas_call(functools.partial(kernel, plan, axes), out_shape=outs, in_...  7.31 us
    ppermute x3, starting transfers between devices, exchange(): near_in = lax.ppermute(to_near, axes[0], pairs)  4.17 us
    ppermute x3, starting transfers between devices, exchange(): got.append(lax.ppermute(first, axes[1], plan.table(0, 2)))  3.91 us
    ppermute x3, waiting for transfers between devices, exchange(): far_in = lax.ppermute(to_far, axes[0], others)  2.52 us
    ppermute x3, starting transfers between devices, exchange(): got.append(lax.ppermute(to_x, axes[1], plan.table(0, 1)))  2.41 us
  transfers between devices with their start and end apart: 12, of which 3 were waited for; matrix products, arithmetic and copies ran while one was open for 0% of the time, Pallas kernels for 9%

profile of v9, /device:TPU:1, one launch (start us, length us, event | category | flops | bytes accessed | tf_op | source)
XLA Modules:
  0.0 30.5 jit_solution(14737659452748706822)
XLA Ops:
  0.7 0.0 copy-start.1
  0.7 1.6 %shard_map.104 = (f32[4,24,768]{2,1,0:T(8,128)S(1)}, f32[96,128]{1,0:T(8,128)S(1)}, f32[96,128]{1,0:T(8,128)S(1)}, bf16[96,192]{1,0:T(8,128)(2,1)S(1)}, bf16[768...) custom-call(f32[4,24,768]{2,1,0:T(8,128)} %refs_0_.2, ...), custom_call_target="tpu_custom_call" | custom-call | tf_op jit(solution)/shard_map/pallas_call | solution.py:583
  2.3 0.0 copy-start
  2.3 2.1 %collective-permute-start = (f32[80,128]{1,0:T(8,128)S(1)}, f32[80,128]{1,0:T(8,128)S(1)}, u32[]{:S(2)}, u32[]{:S(2)}) collective-permute-start(f32[80,128]{1,0:T(8,128)S(1)} %get-tuple-element.44), channel_id=1, source_target_pairs={{0,8},{8,0},{16,24},{24,16},{1,9},{9,1},{17,25},{25,17},{2,10},{10... | collective-permute-start | bytes 122888 | tf_op jit(solution)/shard_map/ppermute | solution.py:600
  4.4 1.0 %collective-permute-start.1 = (f32[24,512]{1,0:T(8,128)S(1)}, f32[24,512]{1,0:T(8,128)S(1)}, u32[]{:S(2)}, u32[]{:S(2)}) collective-permute-start(f32[24,512]{1,0:T(8,128)S(1)} %get-tuple-element.47), channel_id=1, source_target_pairs={{0,1},{1,0},{2,3},{3,2},{4,5},{5,4},{6,7},{7,6},{8,9},{9,8},{10,11... | collective-permute-start | bytes 147464 | tf_op jit(solution)/shard_map/ppermute | solution.py:602
  5.4 3.1 %collective-permute-start.2 = (f32[24,512]{1,0:T(8,128)S(1)}, f32[24,512]{1,0:T(8,128)S(1)}, u32[]{:S(2)}, u32[]{:S(2)}) collective-permute-start(f32[24,512]{1,0:T(8,128)S(1)} %get-tuple-element.48), channel_id=1, source_target_pairs={{1,2},{2,1},{3,4},{4,3},{5,6},{6,5},{9,10},{10,9},{11,12},{12,11},... | collective-permute-start | bytes 147464 | tf_op jit(solution)/shard_map/ppermute | solution.py:601
  8.5 0.0 collective-permute-done.from_x.refs_17_
  8.5 1.3 %collective-permute-start.3 = (f32[64,128]{1,0:T(8,128)S(1)}, f32[64,128]{1,0:T(8,128)S(1)}, u32[]{:S(2)}, u32[]{:S(2)}) collective-permute-start(f32[64,128]{1,0:T(8,128)S(1)} %shard_map.105.refs_4_), channel_id=1, source_target_pairs={{0,16},{8,24},{16,0},{24,8},{1,17},{9,25},{17,1},{25,9},{2,18},{10... | collective-permute-start | bytes 98312 | tf_op jit(solution)/shard_map/ppermute | solution.py:612
  9.8 0.3 %shard_map.106 = (bf16[96,96]{1,0:T(8,128)(2,1)S(1)}, bf16[56,96]{1,0:T(8,128)(2,1)S(1)}, bf16[96,16]{1,0:T(8,128)(2,1)S(1)}, f32[96,128]{1,0:T(8,128)S(1)}, f32...) custom-call(f32[4,24]{1,0:T(4,128)S(1)} %copy-done.2, ...), custom_call_target="tpu_custom_call" | custom-call | tf_op jit(solution)/shard_map/pallas_call | solution.py:583
  10.1 0.0 collective-permute-done.1.refs_3_.refs_15_
  10.1 0.8 %collective-permute-done.2.refs_4_.refs_16_ = f32[24,512]{1,0:T(8,128)S(1)} collective-permute-done((f32[24,512]{1,0:T(8,128)S(1)}, f32[24,512]{1,0:T(8,128)S(1)}, u32[]{:S(2)}, u32[]{:S(2)}) %collective-permute-start.2) | collective-permute-done | bytes 49184 | tf_op jit(solution)/shard_map/ppermute | solution.py:601
  10.9 0.6 %shard_map.107 = (f32[4,24,768]{2,1,0:T(8,128)S(1)}, f32[8,768]{1,0:T(8,128)S(1)}, f32[96,768]{1,0:T(8,128)S(1)}) custom-call(f32[4,24,768]{2,1,0:T(8,128)S(1)} %get-tuple-element.42.refs_0_, f32[96,128]{1,0:T(8,128)S(1)} %get-tuple-element.46.refs_1_, f32[8,768]{1,0:T(8,128)S(1)} %copy-done.1, f32[24,512]{1,0:T(8,128)S(1)} %collective-permute-done.1.refs_3_.refs_15_, ...), custom_call_target="tpu_custom_call" | custom-call | tf_op jit(solution)/shard_map/pallas_call | solution.py:583
  11.5 0.0 collective-permute-done.3.refs_18_
  11.5 0.9 %shard_map.108 = (f32[96,128]{1,0:T(8,128)S(1)}, f32[96,128]{1,0:T(8,128)S(1)}, f32[96,128]{1,0:T(8,128)S(1)}, f32[8,768]{1,0:T(8,128)S(1)}, f32[24,512]{1,0:T(8...) custom-call(f32[4,24,768]{2,1,0:T(8,128)S(1)} %get-tuple-element.49.refs_0_, ...), custom_call_target="tpu_custom_call" | custom-call | tf_op jit(solution)/shard_map/pallas_call | solution.py:583
  12.4 0.1 collective-permute-start.4
  12.5 1.7 %collective-permute-start.5 = (f32[24,512]{1,0:T(8,128)S(1)}, f32[24,512]{1,0:T(8,128)S(1)}, u32[]{:S(2)}, u32[]{:S(2)}) collective-permute-start(f32[24,512]{1,0:T(8,128)S(1)} %get-tuple-element.67), channel_id=1, source_target_pairs={{0,1},{1,0},{2,3},{3,2},{4,5},{5,4},{6,7},{7,6},{8,9},{9,8},{10,11... | collective-permute-start | bytes 147464 | tf_op jit(solution)/shard_map/ppermute | solution.py:602
  14.2 3.1 %collective-permute-start.6 = (f32[24,512]{1,0:T(8,128)S(1)}, f32[24,512]{1,0:T(8,128)S(1)}, u32[]{:S(2)}, u32[]{:S(2)}) collective-permute-start(f32[24,512]{1,0:T(8,128)S(1)} %get-tuple-element.68), channel_id=1, source_target_pairs={{1,2},{2,1},{3,4},{4,3},{5,6},{6,5},{9,10},{10,9},{11,12},{12,11},... | collective-permute-start | bytes 147464 | tf_op jit(solution)/shard_map/ppermute | solution.py:601
  17.3 0.0 collective-permute-done.4.from_x.refs_17_
  17.3 1.3 %collective-permute-start.7 = (f32[64,128]{1,0:T(8,128)S(1)}, f32[64,128]{1,0:T(8,128)S(1)}, u32[]{:S(2)}, u32[]{:S(2)}) collective-permute-start(f32[64,128]{1,0:T(8,128)S(1)} %shard_map.109.refs_6_), channel_id=1, source_target_pairs={{0,16},{8,24},{16,0},{24,8},{1,17},{9,25},{17,1},{25,9},{2,18},{10... | collective-permute-start | bytes 98312 | tf_op jit(solution)/shard_map/ppermute | solution.py:612
  18.6 0.4 %shard_map.110.refs_0_ = f32[4,24,768]{2,1,0:T(8,128)S(1)} custom-call(f32[4,24,768]{2,1,0:T(8,128)S(1)} %get-tuple-element.49.refs_0_, f32[8,768]{1,0:T(8,128)S(1)} %get-tuple-element.62.refs_1_, f32[96,128]{1,0:T(8,128)S(1)} %get-tuple-element.63.refs_2_, bf16[96,96]{1,0:T(8,128)(2,1)S(1)} %get-tuple-element.64.refs_3_, ...), custom_call_target="tpu_custom_call" | custom-call | tf_op jit(solution)/shard_map/pallas_call | solution.py:583
  19.0 0.0 collective-permute-done.5.refs_3_.refs_15_
  19.0 0.9 %collective-permute-done.6.refs_4_.refs_16_ = f32[24,512]{1,0:T(8,128)S(1)} collective-permute-done((f32[24,512]{1,0:T(8,128)S(1)}, f32[24,512]{1,0:T(8,128)S(1)}, u32[]{:S(2)}, u32[]{:S(2)}) %collective-permute-start.6) | collective-permute-done | bytes 49184 | tf_op jit(solution)/shard_map/ppermute | solution.py:601
  19.9 0.6 %shard_map.111 = (f32[4,24,768]{2,1,0:T(8,128)S(1)}, f32[8,768]{1,0:T(8,128)S(1)}, f32[96,768]{1,0:T(8,128)S(1)}) custom-call(f32[4,24,768]{2,1,0:T(8,128)S(1)} %shard_map.110.refs_0_, f32[96,128]{1,0:T(8,128)S(1)} %get-tuple-element.46.refs_1_, f32[8,768]{1,0:T(8,128)S(1)} %copy-done.1, f32[24,512]{1,0:T(8,128)S(1)} %collective-permute-done.5.refs_3_.refs_15_, ...), custom_call_target="tpu_custom_call" | custom-call | tf_op jit(solution)/shard_map/pallas_call | solution.py:583
  20.5 0.9 %shard_map.112 = (f32[96,128]{1,0:T(8,128)S(1)}, f32[96,128]{1,0:T(8,128)S(1)}, f32[96,128]{1,0:T(8,128)S(1)}, f32[8,768]{1,0:T(8,128)S(1)}, f32[24,512]{1,0:T(8...) custom-call(f32[4,24,768]{2,1,0:T(8,128)S(1)} %get-tuple-element.69.refs_0_, ...), custom_call_target="tpu_custom_call" | custom-call | tf_op jit(solution)/shard_map/pallas_call | solution.py:583
  21.4 0.2 collective-permute-start.8
  21.6 1.5 %collective-permute-start.9 = (f32[24,512]{1,0:T(8,128)S(1)}, f32[24,512]{1,0:T(8,128)S(1)}, u32[]{:S(2)}, u32[]{:S(2)}) collective-permute-start(f32[24,512]{1,0:T(8,128)S(1)} %get-tuple-element.78), channel_id=1, source_target_pairs={{0,1},{1,0},{2,3},{3,2},{4,5},{5,4},{6,7},{7,6},{8,9},{9,8},{10,11... | collective-permute-start | bytes 147464 | tf_op jit(solution)/shard_map/ppermute | solution.py:602
  23.1 3.1 %collective-permute-start.10 = (f32[24,512]{1,0:T(8,128)S(1)}, f32[24,512]{1,0:T(8,128)S(1)}, u32[]{:S(2)}, u32[]{:S(2)}) collective-permute-start(f32[24,512]{1,0:T(8,128)S(1)} %get-tuple-element.79), channel_id=1, source_target_pairs={{1,2},{2,1},{3,4},{4,3},{5,6},{6,5},{9,10},{10,9},{11,12},{12,11},... | collective-permute-start | bytes 147464 | tf_op jit(solution)/shard_map/ppermute | solution.py:601
  26.2 1.3 %collective-permute-start.11 = (f32[64,128]{1,0:T(8,128)S(1)}, f32[64,128]{1,0:T(8,128)S(1)}, u32[]{:S(2)}, u32[]{:S(2)}) collective-permute-start(f32[64,128]{1,0:T(8,128)S(1)} %shard_map.113.refs_6_), channel_id=1, source_target_pairs={{0,16},{8,24},{16,0},{24,8},{1,17},{9,25},{17,1},{25,9},{2,18},{10... | collective-permute-start | bytes 98312 | tf_op jit(solution)/shard_map/ppermute | solution.py:612
  27.5 0.4 %shard_map.114.refs_0_ = f32[4,24,768]{2,1,0:T(8,128)S(1)} custom-call(f32[4,24,768]{2,1,0:T(8,128)S(1)} %get-tuple-element.69.refs_0_, f32[8,768]{1,0:T(8,128)S(1)} %get-tuple-element.74.refs_1_, f32[96,128]{1,0:T(8,128)S(1)} %get-tuple-element.75.refs_2_, bf16[96,96]{1,0:T(8,128)(2,1)S(1)} %get-tuple-element.64.refs_3_, ...), custom_call_target="tpu_custom_call" | custom-call | tf_op jit(solution)/shard_map/pallas_call | solution.py:583
  27.9 0.9 %collective-permute-done.10.refs_4_.refs_10_ = f32[24,512]{1,0:T(8,128)S(1)} collective-permute-done((f32[24,512]{1,0:T(8,128)S(1)}, f32[24,512]{1,0:T(8,128)S(1)}, u32[]{:S(2)}, u32[]{:S(2)}) %collective-permute-start.10) | collective-permute-done | bytes 49184 | tf_op jit(solution)/shard_map/ppermute | solution.py:601
  28.7 0.6 %shard_map.115.refs_0_ = f32[4,24,768]{2,1,0:T(8,128)S(1)} custom-call(f32[4,24,768]{2,1,0:T(8,128)S(1)} %shard_map.114.refs_0_, f32[96,128]{1,0:T(8,128)S(1)} %get-tuple-element.46.refs_1_, f32[8,768]{1,0:T(8,128)S(1)} %copy-done.1, f32[24,512]{1,0:T(8,128)S(1)} %collective-permute-done.9.refs_3_.refs_9_, f32[24,512]{1,0:T(8,128)S(1)} %collective-permute-done.10.refs_4_.refs_10_), custom_call_target="tpu_custom_call" | custom-call | tf_op jit(solution)/shard_map/pallas_call | solution.py:583
  29.3 1.1 %shard_map.116 = (f32[4,24,768]{2,1,0:T(8,128)}, f32[4,24,64]{2,1,0:T(8,128)}) custom-call(f32[4,24,768]{2,1,0:T(8,128)S(1)} %shard_map.115.refs_0_, f32[96,128]{1,0:T(8,128)S(1)} %get-tuple-element.80.refs_1_, f32[96,128]{1,0:T(8,128)S(1)} %get-tuple-element.81.refs_2_, bf16[96,96]{1,0:T(8,128)(2,1)S(1)} %get-tuple-element.64.refs_3_, ...), custom_call_target="tpu_custom_call" | custom-call | tf_op jit(solution)/shard_map/pallas_call | solution.py:583
  (15 shorter events, 0.0 us)
Async XLA Ops:
  0.6 9.2 %copy-start.2 = (f32[4,24]{1,0:T(4,128)S(1)}, f32[4,24]{1,0:T(4,128)}, u32[]{:S(2)}) copy-start(f32[4,24]{1,0:T(4,128)} %refs_0_.3) | copy-start | bytes 1156
  0.6 9.1 %copy-start.3 = (s32[4,24]{1,0:T(4,128)S(1)}, s32[4,24]{1,0:T(4,128)}, u32[]{:S(2)}) copy-start(s32[4,24]{1,0:T(4,128)} %refs_2_.6) | copy-start | bytes 1156
  0.7 9.1 %copy-start.4 = (f32[32]{0:T(128)S(1)}, f32[32]{0:T(128)}, u32[]{:S(2)}) copy-start(f32[32]{0:T(128)} %refs_1_.3) | copy-start | bytes 388
  0.7 10.2 %copy-start.1 = (f32[8,768]{1,0:T(8,128)S(1)}, f32[8,768]{1,0:T(8,128)}, u32[]{:S(2)}) copy-start(f32[8,768]{1,0:T(8,128)} %constant.7.clone.refs_2_.refs_13_.refs_7_) | copy-start | bytes 73732
  2.3 9.2 %copy-start = (bf16[1536,128]{1,0:T(8,128)(2,1)S(1)}, bf16[1536,128]{1,0:T(8,128)(2,1)}, u32[]{:S(2)}) copy-start(bf16[1536,128]{1,0:T(8,128)(2,1)} %constant.8.clone.refs_14_.refs_5_.refs_8_) | copy-start | bytes 1179652
  2.3 6.2 %collective-permute-start = (f32[80,128]{1,0:T(8,128)S(1)}, f32[80,128]{1,0:T(8,128)S(1)}, u32[]{:S(2)}, u32[]{:S(2)}) collective-permute-start(f32[80,128]{1,0:T(8,128)S(1)} %get-tuple-element.44), channel_id=1, source_target_pairs={{0,8},{8,0},{16,24},{24,16},{1,9},{9,1},{17,25},{25,17},{2,10},{10... | collective-permute-start | bytes 122888 | tf_op jit(solution)/shard_map/ppermute | solution.py:600
  4.4 5.7 %collective-permute-start.1 = (f32[24,512]{1,0:T(8,128)S(1)}, f32[24,512]{1,0:T(8,128)S(1)}, u32[]{:S(2)}, u32[]{:S(2)}) collective-permute-start(f32[24,512]{1,0:T(8,128)S(1)} %get-tuple-element.47), channel_id=1, source_target_pairs={{0,1},{1,0},{2,3},{3,2},{4,5},{5,4},{6,7},{7,6},{8,9},{9,8},{10,11... | collective-permute-start | bytes 147464 | tf_op jit(solution)/shard_map/ppermute | solution.py:602
  5.4 5.5 %collective-permute-start.2 = (f32[24,512]{1,0:T(8,128)S(1)}, f32[24,512]{1,0:T(8,128)S(1)}, u32[]{:S(2)}, u32[]{:S(2)}) collective-permute-start(f32[24,512]{1,0:T(8,128)S(1)} %get-tuple-element.48), channel_id=1, source_target_pairs={{1,2},{2,1},{3,4},{4,3},{5,6},{6,5},{9,10},{10,9},{11,12},{12,11},... | collective-permute-start | bytes 147464 | tf_op jit(solution)/shard_map/ppermute | solution.py:601
  8.5 3.0 %collective-permute-start.3 = (f32[64,128]{1,0:T(8,128)S(1)}, f32[64,128]{1,0:T(8,128)S(1)}, u32[]{:S(2)}, u32[]{:S(2)}) collective-permute-start(f32[64,128]{1,0:T(8,128)S(1)} %shard_map.105.refs_4_), channel_id=1, source_target_pairs={{0,16},{8,24},{16,0},{24,8},{1,17},{9,25},{17,1},{25,9},{2,18},{10... | collective-permute-start | bytes 98312 | tf_op jit(solution)/shard_map/ppermute | solution.py:612
  12.4 4.9 %collective-permute-start.4 = (f32[80,128]{1,0:T(8,128)S(1)}, f32[80,128]{1,0:T(8,128)S(1)}, u32[]{:S(2)}, u32[]{:S(2)}) collective-permute-start(f32[80,128]{1,0:T(8,128)S(1)} %get-tuple-element.65), channel_id=1, source_target_pairs={{0,8},{8,0},{16,24},{24,16},{1,9},{9,1},{17,25},{25,17},{2,10},{10... | collective-permute-start | bytes 122888 | tf_op jit(solution)/shard_map/ppermute | solution.py:600
  12.5 6.5 %collective-permute-start.5 = (f32[24,512]{1,0:T(8,128)S(1)}, f32[24,512]{1,0:T(8,128)S(1)}, u32[]{:S(2)}, u32[]{:S(2)}) collective-permute-start(f32[24,512]{1,0:T(8,128)S(1)} %get-tuple-element.67), channel_id=1, source_target_pairs={{0,1},{1,0},{2,3},{3,2},{4,5},{5,4},{6,7},{7,6},{8,9},{9,8},{10,11... | collective-permute-start | bytes 147464 | tf_op jit(solution)/shard_map/ppermute | solution.py:602
  14.2 5.7 %collective-permute-start.6 = (f32[24,512]{1,0:T(8,128)S(1)}, f32[24,512]{1,0:T(8,128)S(1)}, u32[]{:S(2)}, u32[]{:S(2)}) collective-permute-start(f32[24,512]{1,0:T(8,128)S(1)} %get-tuple-element.68), channel_id=1, source_target_pairs={{1,2},{2,1},{3,4},{4,3},{5,6},{6,5},{9,10},{10,9},{11,12},{12,11},... | collective-permute-start | bytes 147464 | tf_op jit(solution)/shard_map/ppermute | solution.py:601
  17.3 3.2 %collective-permute-start.7 = (f32[64,128]{1,0:T(8,128)S(1)}, f32[64,128]{1,0:T(8,128)S(1)}, u32[]{:S(2)}, u32[]{:S(2)}) collective-permute-start(f32[64,128]{1,0:T(8,128)S(1)} %shard_map.109.refs_6_), channel_id=1, source_target_pairs={{0,16},{8,24},{16,0},{24,8},{1,17},{9,25},{17,1},{25,9},{2,18},{10... | collective-permute-start | bytes 98312 | tf_op jit(solution)/shard_map/ppermute | solution.py:612
  21.4 4.8 %collective-permute-start.8 = (f32[80,128]{1,0:T(8,128)S(1)}, f32[80,128]{1,0:T(8,128)S(1)}, u32[]{:S(2)}, u32[]{:S(2)}) collective-permute-start(f32[80,128]{1,0:T(8,128)S(1)} %get-tuple-element.76), channel_id=1, source_target_pairs={{0,8},{8,0},{16,24},{24,16},{1,9},{9,1},{17,25},{25,17},{2,10},{10... | collective-permute-start | bytes 122888 | tf_op jit(solution)/shard_map/ppermute | solution.py:600
  21.6 6.3 %collective-permute-start.9 = (f32[24,512]{1,0:T(8,128)S(1)}, f32[24,512]{1,0:T(8,128)S(1)}, u32[]{:S(2)}, u32[]{:S(2)}) collective-permute-start(f32[24,512]{1,0:T(8,128)S(1)} %get-tuple-element.78), channel_id=1, source_target_pairs={{0,1},{1,0},{2,3},{3,2},{4,5},{5,4},{6,7},{7,6},{8,9},{9,8},{10,11... | collective-permute-start | bytes 147464 | tf_op jit(solution)/shard_map/ppermute | solution.py:602
  23.1 5.7 %collective-permute-start.10 = (f32[24,512]{1,0:T(8,128)S(1)}, f32[24,512]{1,0:T(8,128)S(1)}, u32[]{:S(2)}, u32[]{:S(2)}) collective-permute-start(f32[24,512]{1,0:T(8,128)S(1)} %get-tuple-element.79), channel_id=1, source_target_pairs={{1,2},{2,1},{3,4},{4,3},{5,6},{6,5},{9,10},{10,9},{11,12},{12,11},... | collective-permute-start | bytes 147464 | tf_op jit(solution)/shard_map/ppermute | solution.py:601
  26.2 3.2 %collective-permute-start.11 = (f32[64,128]{1,0:T(8,128)S(1)}, f32[64,128]{1,0:T(8,128)S(1)}, u32[]{:S(2)}, u32[]{:S(2)}) collective-permute-start(f32[64,128]{1,0:T(8,128)S(1)} %shard_map.113.refs_6_), channel_id=1, source_target_pairs={{0,16},{8,24},{16,0},{24,8},{1,17},{9,25},{17,1},{25,9},{2,18},{10... | collective-permute-start | bytes 98312 | tf_op jit(solution)/shard_map/ppermute | solution.py:612

commit v10 on v9

--- a/solution.py
+++ b/solution.py
@@ -49,15 +49,17 @@
     grow = (
         growth[None, None, :, None] * mean_weights.T[None, :, :, None] * compass[:, None, None, :]
     ).reshape(2 * ndepth, nfreq * ndir)
-    stokes_high, stokes_low = split_halves(stokes)
-    grow_high, grow_low = split_halves(grow)
+    high, low = split_halves(stokes)
+    blank = np.zeros_like(high)
+    stokes_once = np.concatenate([high, low], axis=1)
+    stokes_upper = np.concatenate([blank, high, blank, low], axis=1)
+    high, low = split_halves(grow)
+    grow = np.concatenate([high, high, low, low], axis=0)
     return (
-        np.concatenate([stokes_high, stokes_low], axis=1),
+        stokes_once,
+        stokes_upper,
         rates,
-        np.concatenate([grow_high, grow_high, grow_low, grow_low], axis=0)
-        .reshape(8 * ndepth, -1, LANES)
-        .transpose(1, 0, 2)
-        .reshape(-1, LANES),
+        grow.reshape(2 * LANES, -1, LANES).transpose(1, 0, 2).reshape(-1, LANES),
     )
 
 
@@ -68,6 +70,7 @@
         self.columns = rows * cols
         self.chunk = self.columns // sections
         self.tiles = spectral // LANES
+        self.some = -(-(2 * cols + 2 * rows) // 16) * 16
         self.edge = ((self.tiles // 2 + 1) * rows + 7) // 8 * 8
         self.relay = sections % 4 == 0
         self.quad = 4 if self.relay else 1
@@ -141,14 +144,12 @@
 
 
 def split_value(value):
-    high = value.astype(BF16).astype(F32)
-    return jnp.where(lane_of(value.shape) < LANES // 2, high, value - high).astype(BF16)
+    high = value.astype(BF16)
+    return high, (value - high.astype(F32)).astype(BF16)
 
 
 def stokes_product(part, table):
-    high = part.astype(BF16)
-    low = (part - high.astype(F32)).astype(BF16)
-    return dot(jnp.concatenate([high, low], axis=0), table)
+    return dot(jnp.concatenate(split_value(part), axis=0), table)
 
 
 def packed_half(edge, tile, half, ahead, forward):
@@ -259,14 +260,16 @@
 
 
 def growth_table(grow, number):
+    size = 2 * LANES
     return jnp.concatenate(
-        [grow[(2 * number + k) * 256 : (2 * number + k + 1) * 256, :] for k in range(2)], axis=1
-    )
-
-
-def currents_twice(arrived):
-    other = pltpu.roll(arrived, LANES // 2, 1)
-    return jnp.where(lane_of(arrived.shape) < LANES // 2, arrived, other), other
+        [grow[(2 * number + k) * size : (2 * number + k + 1) * size, :] for k in range(2)], axis=1
+    )
+
+
+def growth_halves(arrived):
+    high = arrived.astype(BF16).astype(F32)
+    lower = lane_of(arrived.shape) < LANES // 2
+    return jnp.where(lower, high, pltpu.roll(arrived - high, LANES // 2, 1)).astype(BF16)
 
 
 def with_edges(plan, turned, west, east):
@@ -309,10 +312,10 @@
 
 def first_kernel(plan, axes, *refs):
     waves_in, currents_in, target_in, stokes_in, refs = *refs[:4], refs[4:]
-    waves, ocean_out, packed_out, order_out, stokes, refs = *refs[:5], refs[5:]
+    waves, ocean_out, packed_out, order_out, refs = *refs[:4], refs[4:]
     count = len(plan.sizes)
     sec_out, lat_out, refs = refs[:count], refs[count : count + 2], refs[count + 2 :]
-    currents, target, done = refs
+    currents, target, stokes, done = refs
     pairs = [(target_in, target), (waves_in, waves), (stokes_in, stokes), (currents_in, currents)]
     copies = [pltpu.make_async_copy(a, b, done.at[k]) for k, (a, b) in enumerate(pairs)]
     for copy in copies:
@@ -326,8 +329,8 @@
     same = column_of(plan, target_row) == target_row
     rank = jnp.sum(jnp.where(same & (down < across), 1.0, 0.0), axis=0, keepdims=True)
     slot = target_row * float(plan.chunk) + rank
-    order = jnp.where(slot == down.astype(F32), 1.0, 0.0).astype(BF16)
-    order_out[...] = twice(order)
+    order = twice(jnp.where(slot == down.astype(F32), 1.0, 0.0)).astype(BF16)
+    order_out[...] = order
     for copy in copies[1:]:
         copy.wait()
     total = None
@@ -336,11 +339,10 @@
         product = stokes_product(part, stokes[start : start + 256, :])
         total = product if total is None else total + product
     moments = total[:columns] + total[columns:]
-    moments = moments + pltpu.roll(moments, LANES // 2, 1)
     flat = currents[...].reshape(columns, 2 * plan.depth)
     ocean = jnp.concatenate([flat, jnp.zeros((columns, LANES - 2 * plan.depth), F32)], axis=1)
     ocean_out[...] = ocean
-    ordered = dot(order, split_value(moments))
+    ordered = dot(order, jnp.concatenate(split_value(moments), axis=0))
     ordered = ordered + pltpu.roll(ordered, LANES // 2, 1)
     west = [waves[row, 0:1, :] for row in range(rows)]
     east = [waves[row, cols - 1 : cols, :] for row in range(rows)]
@@ -353,7 +355,7 @@
 
 def map_kernel(plan, axes, *refs):
     turning, drag, mask, order_twice, _, refs = *refs[:5], refs[5:]
-    permute_out, permute_some_out, order_edge_out, turn_out, turn_edge_out = refs[:5]
+    permute_out, permute_some_out, slots_out, turn_out, turn_edge_out = refs[:5]
     sea_out, sea_order_out, sea_some_out, keep_out = refs[5:]
     columns, rows, cols = plan.columns, plan.rows, plan.cols
     order = order_twice[:, :columns]
@@ -372,12 +374,7 @@
     )
     permute = (back * sea[:, :columns]).astype(BF16)
     permute_out[...] = permute
-    shape = (columns, 4 * rows)
-    number = lax.rem(lane_of(shape), 2 * rows)
-    wanted = lax.rem(number, rows) * cols + lax.div(number, rows) * (cols - 1)
-    chosen = lax.broadcasted_iota(jnp.int32, shape, 0) == wanted
-    order_edge_out[...] = dot(order, jnp.where(chosen, 1.0, 0.0).astype(BF16)).astype(BF16)
-    shape = (2 * cols + 2 * rows, columns)
+    shape = (plan.some, columns)
     place = lax.broadcasted_iota(jnp.int32, shape, 0)
     number = place - 2 * cols
     wanted = jnp.where(
@@ -385,9 +382,13 @@
         place + jnp.where(place < cols, 0, (rows - 2) * cols),
         lax.rem(number, rows) * cols + lax.div(number, rows) * (cols - 1),
     )
+    wanted = jnp.where(number < 2 * rows, wanted, -1)
     chosen = jnp.where(lane_of(shape) == wanted, 1.0, 0.0).astype(BF16)
     permute_some_out[...] = dot(chosen, permute).astype(BF16)
     sea_some_out[...] = dot(chosen, sea.astype(BF16))
+    slot = jnp.sum(order.astype(F32) * down.astype(F32), axis=0, keepdims=True)
+    slot = jnp.broadcast_to(column_of(plan, slot), (columns, LANES)).astype(BF16)
+    slots_out[...] = dot(chosen, slot)[2 * cols : 2 * cols + 2 * rows, :].astype(jnp.int32)
     keep = 1.0 - drag[...].reshape(1, plan.depth)
     blank = jnp.zeros((1, LANES - 2 * plan.depth), F32)
     keep_out[...] = jnp.broadcast_to(jnp.concatenate([keep, keep, blank], axis=1), (8, LANES))
@@ -454,10 +455,8 @@
     if len(refs) > 1:
         for start in range(0, plan.spectral, 256):
             part = turned_out[:, :, start : start + 256].reshape(plan.columns, 256)
-            high = part.astype(BF16)
-            low = (part - high.astype(F32)).astype(BF16)
             sorted_out[:, start : start + 256] = dot(
-                order[...], jnp.concatenate([high, low], axis=0)
+                order[...], jnp.concatenate(split_value(part), axis=0)
             )
 
 
@@ -468,58 +467,64 @@
 
 
 def send_kernel(plan, axes, *refs):
-    turned, turned_edge, turned_order, ocean_in, packed_in, permute_some, order_edge = refs[:7]
+    turned, turned_edge, turned_order, ocean_in, packed_in, permute_some, slots = refs[:7]
     turn_edge, sea, sea_order, sea_some, keep, stokes, rates, grow, refs = *refs[7:15], refs[15:]
     count = len(plan.sizes)
     near, far, sec_in, refs = refs[0], refs[1], refs[2 : 2 + count], refs[2 + count :]
     ocean_out, packed_out, coupled, extra_out, far_out, near_out = refs[:6]
-    sec_out = refs[6:]
+    sec_out, in_order = refs[6 : 6 + count], refs[6 + count]
     section, band = lax.axis_index(axes[1]), lax.axis_index(axes[0])
     even = lax.rem(band, 2) == 0
     columns, rows, cols = plan.columns, plan.rows, plan.cols
 
     west_edge, east_edge = take_sections(plan, section, packed_in, sec_in, coupled)
-    both, drift = currents_twice(coupled[...])
-    in_order = twice(split_value(both * sea_order[...]))
-    at_some = twice(dot(permute_some[...], split_value(both)).astype(BF16))
     extra = edge_part(plan, rates, turn_edge, west_edge, east_edge)
+    in_order[...] = turned_order[...]
+    for number in range(2 * rows):
+        slot = pl.ds(slots[number, 0], 1)
+        part = jnp.concatenate([tile[number : number + 1, :] for tile in extra], axis=1)
+        in_order[slot, :] = in_order[slot, :] + part
+    arrived = coupled[...]
+    halves = growth_halves(arrived)
+    wet, wet_some = sea_order[...], twice(sea_some[...])
+    rows_of = twice(halves * wet.astype(BF16))
+    some_of = twice(dot(permute_some[...], halves).astype(BF16))
+    wet = twice(wet)
     total = None
     some = []
-    wet, wet_some = twice(sea_order[...]), twice(sea_some[...])
+    filler = jnp.zeros((plan.some - 2 * cols - 2 * rows, 256), F32)
     for number, start in enumerate(range(0, plan.spectral, 256)):
         lanes = slice(start, start + 256)
         table = growth_table(grow, number)
         from_edges = jnp.concatenate(extra[2 * number : 2 * number + 2], axis=1)
         extra_out[:, lanes] = from_edges
-        high = from_edges.astype(BF16).astype(F32)
-        halves = jnp.concatenate([high, from_edges - high], axis=0).astype(BF16)
-        grown = turned_order[:, lanes] + dot(order_edge[...], halves)
-        grown = grown * (wet + dot(in_order, table))
+        grown = in_order[:, lanes] * (wet + dot(rows_of, table))
         product = stokes_product(grown, stokes[lanes, :])
         total = product if total is None else total + product
         parts = []
         for row in (0, rows - 1):
             west, east = from_edges[row : row + 1, :], from_edges[rows + row : rows + row + 1, :]
             parts += with_edges(plan, turned[row, :, lanes], west, east)
-        parts.append(turned_edge[:, lanes] + from_edges)
-        some.append(jnp.concatenate(parts, axis=0) * (wet_some + dot(at_some, table)))
+        parts += [turned_edge[:, lanes] + from_edges, filler]
+        some.append(jnp.concatenate(parts, axis=0) * (wet_some + dot(some_of, table)))
+    drift = pltpu.roll(arrived, LANES // 2, 1)
     new = ocean_step(
         plan, band, even, ocean_in, drift, near, far, west_edge, east_edge, keep, sea
     )
     ocean = jnp.concatenate(new, axis=0)
     ocean_out[...] = ocean
-    moments = total[:columns] + total[columns:]
-    moments = moments + pltpu.roll(moments, LANES // 2, 1)
+    total = total[:, :LANES] + total[:, LANES:]
+    moments = total[:columns, :] + total[columns:, :]
     some = jnp.concatenate(some, axis=1)
-    fill_sections(plan, section, some[2 * cols :, :], ocean, moments, packed_out, sec_out)
+    edges = some[2 * cols : 2 * cols + 2 * rows, :]
+    fill_sections(plan, section, edges, ocean, moments, packed_out, sec_out)
     ends = (some[:cols, :], some[cols : 2 * cols, :]), (new[0], new[rows - 1])
     fill_bands(plan, even, *ends, far_out, near_out)
 
 
 def grow_kernel(plan, axes, *refs):
     turned, extra, coupled, permute, sea, grow, _, waves_out = refs
-    both, _ = currents_twice(coupled[...])
-    at_waves = twice(dot(permute[...], split_value(both)).astype(BF16))
+    at_waves = twice(dot(permute[...], growth_halves(coupled[...])).astype(BF16))
     wet = twice(sea[...])
     for number, start in enumerate(range(0, plan.spectral, 256)):
         lanes = slice(start, start + 256)
@@ -537,8 +542,9 @@
     even = lax.rem(band, 2) == 0
 
     west_edge, east_edge = take_sections(plan, section, packed_in, sec_in, coupled)
-    both, drift = currents_twice(coupled[...])
-    at_waves = twice(dot(permute[...], split_value(both)).astype(BF16))
+    arrived = coupled[...]
+    at_waves = twice(dot(permute[...], growth_halves(arrived)).astype(BF16))
+    drift = pltpu.roll(arrived, LANES // 2, 1)
     extra = edge_part(plan, rates, turn_edge, west_edge, east_edge)
     new = ocean_step(
         plan, band, even, ocean_in, drift, near, far, west_edge, east_edge, keep, sea
@@ -564,7 +570,7 @@
 
 
 def per_device(plan, axes, spectra, turning, currents, drag_rates, land_mask, ocean_target):
-    stokes, rates, grow = (
+    stokes_once, stokes, rates, grow = (
         jnp.asarray(table) for table in build_tables(NFREQ, NDIR, drag_rates.shape[0])
     )
     columns, rows, cols, spectral = plan.columns, plan.rows, plan.cols, plan.spectral
@@ -576,7 +582,7 @@
     field = shape(spectra.shape, F32)
     at_edges = shape((2 * rows, LANES), F32)
     edge_field = shape((2 * rows, spectral), F32)
-    some = 2 * cols + 2 * rows
+    some = plan.some
     spans = spectral // 256
 
     def call(kernel, outs, scratch, *args, space_in=pltpu.VMEM, space_out=pltpu.VMEM):
@@ -616,14 +622,13 @@
         ]
         return meanwhile(first), [near_in, far_in, *got]
 
-    waves, ocean, packed, order, stokes, *sent = call(
+    waves, ocean, packed, order, *sent = call(
         first_kernel,
         [
             field,
             state,
             state,
             shape((columns, 2 * columns), BF16),
-            shape(stokes.shape, stokes.dtype),
             *to_sections,
             to_band,
             to_band,
@@ -631,11 +636,12 @@
         [
             pltpu.VMEM(currents.shape, F32),
             pltpu.VMEM(ocean_target.shape, jnp.int32),
+            pltpu.VMEM(stokes_once.shape, BF16),
             pltpu.SemaphoreType.DMA((4,)),
         ],
         *[
             pltpu.with_memory_space_constraint(array, pltpu.HBM)
-            for array in (spectra, currents, ocean_target, stokes)
+            for array in (spectra, currents, ocean_target, stokes_once)
         ],
         space_in=pltpu.HBM,
     )
@@ -646,7 +652,7 @@
             [
                 shape((columns, columns), BF16),
                 shape((some, columns), BF16),
-                shape((columns, 4 * rows), BF16),
+                shape((2 * rows, LANES), jnp.int32),
                 state,
                 at_edges,
                 state,
@@ -663,7 +669,7 @@
         )
 
     made, came = exchange(*sent[-2:], sent[:-2], maps)
-    permute, permute_some, order_edge, turn, turn_edge, sea, sea_order, sea_some, keep = made
+    permute, permute_some, slots, turn, turn_edge, sea, sea_order, sea_some, keep = made
     for step in range(STEPS - 1):
         turned, turned_edge, turned_order = call(
             move_kernel,
@@ -678,14 +684,14 @@
         ocean, packed, coupled, extra, to_far, to_near, *sent = call(
             send_kernel,
             [state, state, state, edge_field, to_band, to_band] + to_sections,
-            [],
+            [pltpu.VMEM((columns, spectral), F32)],
             turned,
             turned_edge,
             turned_order,
             ocean,
             packed,
             permute_some,
-            order_edge,
+            slots,
             turn_edge,
             sea,
             sea_order,

time: 30.7 us -> 30.2 us (0.984)
  Pallas kernels: 7.31 us -> 6.81 us
    pallas_call x13, Pallas kernels: 7.31 us -> 6.81 us  [call(): pl.pallas_call(functools.partial(kernel, plan, axes), out_shape=outs, in_...]
where the time goes in v10:
time: 30.2 us; the launch traced here: 30 us
  starting transfers between devices  19.7 us (65%)
  Pallas kernels  6.81 us (23%)
  waiting for transfers between devices  2.54 us (8%)
  between operations  0.86 us (3%)
    ppermute x3, starting transfers between devices, exchange(): far_in = lax.ppermute(to_far, axes[0], others)  9.24 us
    pallas_call x13, Pallas kernels, call(): pl.pallas_call(functools.partial(kernel, plan, axes), out_shape=outs, in_...  6.81 us
    ppermute x3, starting transfers between devices, exchange(): near_in = lax.ppermute(to_near, axes[0], pairs)  4.17 us
    ppermute x3, starting transfers between devices, exchange(): got.append(lax.ppermute(first, axes[1], plan.table(0, 2)))  3.92 us
    ppermute x3, waiting for transfers between devices, exchange(): far_in = lax.ppermute(to_far, axes[0], others)  2.52 us
    ppermute x3, starting transfers between devices, exchange(): got.append(lax.ppermute(to_x, axes[1], plan.table(0, 1)))  2.4 us
  transfers between devices with their start and end apart: 12, of which 3 were waited for; matrix products, arithmetic and copies ran while one was open for 0% of the time, Pallas kernels for 9%

profile of v10, /device:TPU:1, one launch (start us, length us, event | category | flops | bytes accessed | tf_op | source)
XLA Modules:
  0.0 30.0 jit_solution(10461341789202958328)
XLA Ops:
  0.7 0.0 copy-start.2
  0.7 0.0 copy-start.1
  0.7 1.6 %shard_map.113 = (f32[4,24,768]{2,1,0:T(8,128)S(1)}, f32[96,128]{1,0:T(8,128)S(1)}, f32[96,128]{1,0:T(8,128)S(1)}, bf16[96,192]{1,0:T(8,128)(2,1)S(1)}, f32[80,1...) custom-call(f32[4,24,768]{2,1,0:T(8,128)} %refs_0_.2, ...), custom_call_target="tpu_custom_call" | custom-call | tf_op jit(solution)/shard_map/pallas_call | solution.py:589
  2.3 0.0 copy-start
  2.3 2.1 %collective-permute-start = (f32[80,128]{1,0:T(8,128)S(1)}, f32[80,128]{1,0:T(8,128)S(1)}, u32[]{:S(2)}, u32[]{:S(2)}) collective-permute-start(f32[80,128]{1,0:T(8,128)S(1)} %get-tuple-element.43), channel_id=1, source_target_pairs={{0,8},{8,0},{16,24},{24,16},{1,9},{9,1},{17,25},{25,17},{2,10},{10... | collective-permute-start | bytes 122888 | tf_op jit(solution)/shard_map/ppermute | solution.py:606
  4.4 1.0 %collective-permute-start.1 = (f32[24,512]{1,0:T(8,128)S(1)}, f32[24,512]{1,0:T(8,128)S(1)}, u32[]{:S(2)}, u32[]{:S(2)}) collective-permute-start(f32[24,512]{1,0:T(8,128)S(1)} %get-tuple-element.46), channel_id=1, source_target_pairs={{0,1},{1,0},{2,3},{3,2},{4,5},{5,4},{6,7},{7,6},{8,9},{9,8},{10,11... | collective-permute-start | bytes 147464 | tf_op jit(solution)/shard_map/ppermute | solution.py:608
  5.4 3.1 %collective-permute-start.2 = (f32[24,512]{1,0:T(8,128)S(1)}, f32[24,512]{1,0:T(8,128)S(1)}, u32[]{:S(2)}, u32[]{:S(2)}) collective-permute-start(f32[24,512]{1,0:T(8,128)S(1)} %get-tuple-element.47), channel_id=1, source_target_pairs={{1,2},{2,1},{3,4},{4,3},{5,6},{6,5},{9,10},{10,9},{11,12},{12,11},... | collective-permute-start | bytes 147464 | tf_op jit(solution)/shard_map/ppermute | solution.py:607
  8.5 1.3 %collective-permute-start.3 = (f32[64,128]{1,0:T(8,128)S(1)}, f32[64,128]{1,0:T(8,128)S(1)}, u32[]{:S(2)}, u32[]{:S(2)}) collective-permute-start(f32[64,128]{1,0:T(8,128)S(1)} %shard_map.114.refs_4_), channel_id=1, source_target_pairs={{0,16},{8,24},{16,0},{24,8},{1,17},{9,25},{17,1},{25,9},{2,18},{10... | collective-permute-start | bytes 98312 | tf_op jit(solution)/shard_map/ppermute | solution.py:618
  9.8 0.3 %shard_map.115 = (bf16[96,96]{1,0:T(8,128)(2,1)S(1)}, bf16[64,96]{1,0:T(8,128)(2,1)S(1)}, s32[8,128]{1,0:T(8,128)S(1)}, f32[96,128]{1,0:T(8,128)S(1)}, f32[8,128...) custom-call(f32[4,24]{1,0:T(4,128)S(1)} %copy-done.3, ...), custom_call_target="tpu_custom_call" | custom-call | tf_op jit(solution)/shard_map/pallas_call | solution.py:589
  10.1 0.0 collective-permute-done.1.refs_3_.refs_15_
  10.1 0.8 %collective-permute-done.2.refs_4_.refs_16_ = f32[24,512]{1,0:T(8,128)S(1)} collective-permute-done((f32[24,512]{1,0:T(8,128)S(1)}, f32[24,512]{1,0:T(8,128)S(1)}, u32[]{:S(2)}, u32[]{:S(2)}) %collective-permute-start.2) | collective-permute-done | bytes 49184 | tf_op jit(solution)/shard_map/ppermute | solution.py:607
  10.9 0.6 %shard_map.116 = (f32[4,24,768]{2,1,0:T(8,128)S(1)}, f32[8,768]{1,0:T(8,128)S(1)}, f32[96,768]{1,0:T(8,128)S(1)}) custom-call(f32[4,24,768]{2,1,0:T(8,128)S(1)} %get-tuple-element.41.refs_0_, f32[96,128]{1,0:T(8,128)S(1)} %get-tuple-element.45.refs_1_, f32[8,768]{1,0:T(8,128)S(1)} %copy-done.2, f32[24,512]{1,0:T(8,128)S(1)} %collective-permute-done.1.refs_3_.refs_15_, ...), custom_call_target="tpu_custom_call" | custom-call | tf_op jit(solution)/shard_map/pallas_call | solution.py:589
  11.5 0.0 collective-permute-done.3.refs_18_
  11.5 0.6 %shard_map.117 = (f32[96,128]{1,0:T(8,128)S(1)}, f32[96,128]{1,0:T(8,128)S(1)}, f32[96,128]{1,0:T(8,128)S(1)}, f32[8,768]{1,0:T(8,128)S(1)}, f32[24,512]{1,0:T(8...) custom-call(f32[4,24,768]{2,1,0:T(8,128)S(1)} %get-tuple-element.48.refs_0_, ...), custom_call_target="tpu_custom_call" | custom-call | tf_op jit(solution)/shard_map/pallas_call | solution.py:589
  12.1 0.1 collective-permute-start.4
  12.3 1.7 %collective-permute-start.5 = (f32[24,512]{1,0:T(8,128)S(1)}, f32[24,512]{1,0:T(8,128)S(1)}, u32[]{:S(2)}, u32[]{:S(2)}) collective-permute-start(f32[24,512]{1,0:T(8,128)S(1)} %get-tuple-element.65), channel_id=1, source_target_pairs={{0,1},{1,0},{2,3},{3,2},{4,5},{5,4},{6,7},{7,6},{8,9},{9,8},{10,11... | collective-permute-start | bytes 147464 | tf_op jit(solution)/shard_map/ppermute | solution.py:608
  14.0 3.1 %collective-permute-start.6 = (f32[24,512]{1,0:T(8,128)S(1)}, f32[24,512]{1,0:T(8,128)S(1)}, u32[]{:S(2)}, u32[]{:S(2)}) collective-permute-start(f32[24,512]{1,0:T(8,128)S(1)} %get-tuple-element.66), channel_id=1, source_target_pairs={{1,2},{2,1},{3,4},{4,3},{5,6},{6,5},{9,10},{10,9},{11,12},{12,11},... | collective-permute-start | bytes 147464 | tf_op jit(solution)/shard_map/ppermute | solution.py:607
  17.1 0.0 collective-permute-done.4.from_x.refs_17_
  17.1 1.3 %collective-permute-start.7 = (f32[64,128]{1,0:T(8,128)S(1)}, f32[64,128]{1,0:T(8,128)S(1)}, u32[]{:S(2)}, u32[]{:S(2)}) collective-permute-start(f32[64,128]{1,0:T(8,128)S(1)} %shard_map.118.refs_6_), channel_id=1, source_target_pairs={{0,16},{8,24},{16,0},{24,8},{1,17},{9,25},{17,1},{25,9},{2,18},{10... | collective-permute-start | bytes 98312 | tf_op jit(solution)/shard_map/ppermute | solution.py:618
  18.4 0.4 %shard_map.119.refs_0_ = f32[4,24,768]{2,1,0:T(8,128)S(1)} custom-call(f32[4,24,768]{2,1,0:T(8,128)S(1)} %get-tuple-element.48.refs_0_, f32[8,768]{1,0:T(8,128)S(1)} %get-tuple-element.60.refs_1_, f32[96,128]{1,0:T(8,128)S(1)} %get-tuple-element.61.refs_2_, bf16[96,96]{1,0:T(8,128)(2,1)S(1)} %get-tuple-element.62.refs_3_, ...), custom_call_target="tpu_custom_call" | custom-call | tf_op jit(solution)/shard_map/pallas_call | solution.py:589
  18.8 0.9 %collective-permute-done.6.refs_4_.refs_16_ = f32[24,512]{1,0:T(8,128)S(1)} collective-permute-done((f32[24,512]{1,0:T(8,128)S(1)}, f32[24,512]{1,0:T(8,128)S(1)}, u32[]{:S(2)}, u32[]{:S(2)}) %collective-permute-start.6) | collective-permute-done | bytes 49184 | tf_op jit(solution)/shard_map/ppermute | solution.py:607
  19.7 0.6 %shard_map.120 = (f32[4,24,768]{2,1,0:T(8,128)S(1)}, f32[8,768]{1,0:T(8,128)S(1)}, f32[96,768]{1,0:T(8,128)S(1)}) custom-call(f32[4,24,768]{2,1,0:T(8,128)S(1)} %shard_map.119.refs_0_, f32[96,128]{1,0:T(8,128)S(1)} %get-tuple-element.45.refs_1_, f32[8,768]{1,0:T(8,128)S(1)} %copy-done.2, f32[24,512]{1,0:T(8,128)S(1)} %collective-permute-done.5.refs_3_.refs_15_, ...), custom_call_target="tpu_custom_call" | custom-call | tf_op jit(solution)/shard_map/pallas_call | solution.py:589
  20.3 0.0 collective-permute-done.7.refs_18_
  20.3 0.6 %shard_map.121 = (f32[96,128]{1,0:T(8,128)S(1)}, f32[96,128]{1,0:T(8,128)S(1)}, f32[96,128]{1,0:T(8,128)S(1)}, f32[8,768]{1,0:T(8,128)S(1)}, f32[24,512]{1,0:T(8...) custom-call(f32[4,24,768]{2,1,0:T(8,128)S(1)} %get-tuple-element.67.refs_0_, ...), custom_call_target="tpu_custom_call" | custom-call | tf_op jit(solution)/shard_map/pallas_call | solution.py:589
  20.9 0.2 collective-permute-start.8
  21.1 1.5 %collective-permute-start.9 = (f32[24,512]{1,0:T(8,128)S(1)}, f32[24,512]{1,0:T(8,128)S(1)}, u32[]{:S(2)}, u32[]{:S(2)}) collective-permute-start(f32[24,512]{1,0:T(8,128)S(1)} %get-tuple-element.76), channel_id=1, source_target_pairs={{0,1},{1,0},{2,3},{3,2},{4,5},{5,4},{6,7},{7,6},{8,9},{9,8},{10,11... | collective-permute-start | bytes 147464 | tf_op jit(solution)/shard_map/ppermute | solution.py:608
  22.6 3.1 %collective-permute-start.10 = (f32[24,512]{1,0:T(8,128)S(1)}, f32[24,512]{1,0:T(8,128)S(1)}, u32[]{:S(2)}, u32[]{:S(2)}) collective-permute-start(f32[24,512]{1,0:T(8,128)S(1)} %get-tuple-element.77), channel_id=1, source_target_pairs={{1,2},{2,1},{3,4},{4,3},{5,6},{6,5},{9,10},{10,9},{11,12},{12,11},... | collective-permute-start | bytes 147464 | tf_op jit(solution)/shard_map/ppermute | solution.py:607
  25.7 1.3 %collective-permute-start.11 = (f32[64,128]{1,0:T(8,128)S(1)}, f32[64,128]{1,0:T(8,128)S(1)}, u32[]{:S(2)}, u32[]{:S(2)}) collective-permute-start(f32[64,128]{1,0:T(8,128)S(1)} %shard_map.122.refs_6_), channel_id=1, source_target_pairs={{0,16},{8,24},{16,0},{24,8},{1,17},{9,25},{17,1},{25,9},{2,18},{10... | collective-permute-start | bytes 98312 | tf_op jit(solution)/shard_map/ppermute | solution.py:618
  27.0 0.4 %shard_map.123.refs_0_ = f32[4,24,768]{2,1,0:T(8,128)S(1)} custom-call(f32[4,24,768]{2,1,0:T(8,128)S(1)} %get-tuple-element.67.refs_0_, f32[8,768]{1,0:T(8,128)S(1)} %get-tuple-element.72.refs_1_, f32[96,128]{1,0:T(8,128)S(1)} %get-tuple-element.73.refs_2_, bf16[96,96]{1,0:T(8,128)(2,1)S(1)} %get-tuple-element.62.refs_3_, ...), custom_call_target="tpu_custom_call" | custom-call | tf_op jit(solution)/shard_map/pallas_call | solution.py:589
  27.4 0.9 %collective-permute-done.10.refs_4_.refs_10_ = f32[24,512]{1,0:T(8,128)S(1)} collective-permute-done((f32[24,512]{1,0:T(8,128)S(1)}, f32[24,512]{1,0:T(8,128)S(1)}, u32[]{:S(2)}, u32[]{:S(2)}) %collective-permute-start.10) | collective-permute-done | bytes 49184 | tf_op jit(solution)/shard_map/ppermute | solution.py:607
  28.3 0.6 %shard_map.124.refs_0_ = f32[4,24,768]{2,1,0:T(8,128)S(1)} custom-call(f32[4,24,768]{2,1,0:T(8,128)S(1)} %shard_map.123.refs_0_, f32[96,128]{1,0:T(8,128)S(1)} %get-tuple-element.45.refs_1_, f32[8,768]{1,0:T(8,128)S(1)} %copy-done.2, f32[24,512]{1,0:T(8,128)S(1)} %collective-permute-done.9.refs_3_.refs_9_, f32[24,512]{1,0:T(8,128)S(1)} %collective-permute-done.10.refs_4_.refs_10_), custom_call_target="tpu_custom_call" | custom-call | tf_op jit(solution)/shard_map/pallas_call | solution.py:589
  28.9 1.1 %shard_map.125 = (f32[4,24,768]{2,1,0:T(8,128)}, f32[4,24,64]{2,1,0:T(8,128)}) custom-call(f32[4,24,768]{2,1,0:T(8,128)S(1)} %shard_map.124.refs_0_, f32[96,128]{1,0:T(8,128)S(1)} %get-tuple-element.78.refs_1_, f32[96,128]{1,0:T(8,128)S(1)} %get-tuple-element.79.refs_2_, bf16[96,96]{1,0:T(8,128)(2,1)S(1)} %get-tuple-element.62.refs_3_, ...), custom_call_target="tpu_custom_call" | custom-call | tf_op jit(solution)/shard_map/pallas_call | solution.py:589
  (17 shorter events, 0.0 us)
Async XLA Ops:
  0.6 9.2 %copy-start.3 = (f32[4,24]{1,0:T(4,128)S(1)}, f32[4,24]{1,0:T(4,128)}, u32[]{:S(2)}) copy-start(f32[4,24]{1,0:T(4,128)} %refs_0_.3) | copy-start | bytes 1156
  0.6 9.2 %copy-start.4 = (s32[4,24]{1,0:T(4,128)S(1)}, s32[4,24]{1,0:T(4,128)}, u32[]{:S(2)}) copy-start(s32[4,24]{1,0:T(4,128)} %refs_2_.6) | copy-start | bytes 1156
  0.7 9.2 %copy-start.5 = (f32[32]{0:T(128)S(1)}, f32[32]{0:T(128)}, u32[]{:S(2)}) copy-start(f32[32]{0:T(128)} %refs_1_.3) | copy-start | bytes 388
  0.7 10.2 %copy-start.2 = (f32[8,768]{1,0:T(8,128)S(1)}, f32[8,768]{1,0:T(8,128)}, u32[]{:S(2)}) copy-start(f32[8,768]{1,0:T(8,128)} %constant.10.clone.refs_2_.refs_13_.refs_7_) | copy-start | bytes 73732
  0.7 10.8 %copy-start.1 = (bf16[768,256]{1,0:T(8,128)(2,1)S(1)}, bf16[768,256]{1,0:T(8,128)(2,1)}, u32[]{:S(2)}) copy-start(bf16[768,256]{1,0:T(8,128)(2,1)} %constant.9.clone.refs_12_) | copy-start | bytes 1179652
  2.3 9.2 %copy-start = (bf16[1536,128]{1,0:T(8,128)(2,1)S(1)}, bf16[1536,128]{1,0:T(8,128)(2,1)}, u32[]{:S(2)}) copy-start(bf16[1536,128]{1,0:T(8,128)(2,1)} %constant.11.clone.refs_14_.refs_5_.refs_8_) | copy-start | bytes 1179652
  2.3 6.2 %collective-permute-start = (f32[80,128]{1,0:T(8,128)S(1)}, f32[80,128]{1,0:T(8,128)S(1)}, u32[]{:S(2)}, u32[]{:S(2)}) collective-permute-start(f32[80,128]{1,0:T(8,128)S(1)} %get-tuple-element.43), channel_id=1, source_target_pairs={{0,8},{8,0},{16,24},{24,16},{1,9},{9,1},{17,25},{25,17},{2,10},{10... | collective-permute-start | bytes 122888 | tf_op jit(solution)/shard_map/ppermute | solution.py:606
  4.4 5.7 %collective-permute-start.1 = (f32[24,512]{1,0:T(8,128)S(1)}, f32[24,512]{1,0:T(8,128)S(1)}, u32[]{:S(2)}, u32[]{:S(2)}) collective-permute-start(f32[24,512]{1,0:T(8,128)S(1)} %get-tuple-element.46), channel_id=1, source_target_pairs={{0,1},{1,0},{2,3},{3,2},{4,5},{5,4},{6,7},{7,6},{8,9},{9,8},{10,11... | collective-permute-start | bytes 147464 | tf_op jit(solution)/shard_map/ppermute | solution.py:608
  5.4 5.5 %collective-permute-start.2 = (f32[24,512]{1,0:T(8,128)S(1)}, f32[24,512]{1,0:T(8,128)S(1)}, u32[]{:S(2)}, u32[]{:S(2)}) collective-permute-start(f32[24,512]{1,0:T(8,128)S(1)} %get-tuple-element.47), channel_id=1, source_target_pairs={{1,2},{2,1},{3,4},{4,3},{5,6},{6,5},{9,10},{10,9},{11,12},{12,11},... | collective-permute-start | bytes 147464 | tf_op jit(solution)/shard_map/ppermute | solution.py:607
  8.5 3.0 %collective-permute-start.3 = (f32[64,128]{1,0:T(8,128)S(1)}, f32[64,128]{1,0:T(8,128)S(1)}, u32[]{:S(2)}, u32[]{:S(2)}) collective-permute-start(f32[64,128]{1,0:T(8,128)S(1)} %shard_map.114.refs_4_), channel_id=1, source_target_pairs={{0,16},{8,24},{16,0},{24,8},{1,17},{9,25},{17,1},{25,9},{2,18},{10... | collective-permute-start | bytes 98312 | tf_op jit(solution)/shard_map/ppermute | solution.py:618
  12.1 4.9 %collective-permute-start.4 = (f32[80,128]{1,0:T(8,128)S(1)}, f32[80,128]{1,0:T(8,128)S(1)}, u32[]{:S(2)}, u32[]{:S(2)}) collective-permute-start(f32[80,128]{1,0:T(8,128)S(1)} %get-tuple-element.63), channel_id=1, source_target_pairs={{0,8},{8,0},{16,24},{24,16},{1,9},{9,1},{17,25},{25,17},{2,10},{10... | collective-permute-start | bytes 122888 | tf_op jit(solution)/shard_map/ppermute | solution.py:606
  12.3 6.5 %collective-permute-start.5 = (f32[24,512]{1,0:T(8,128)S(1)}, f32[24,512]{1,0:T(8,128)S(1)}, u32[]{:S(2)}, u32[]{:S(2)}) collective-permute-start(f32[24,512]{1,0:T(8,128)S(1)} %get-tuple-element.65), channel_id=1, source_target_pairs={{0,1},{1,0},{2,3},{3,2},{4,5},{5,4},{6,7},{7,6},{8,9},{9,8},{10,11... | collective-permute-start | bytes 147464 | tf_op jit(solution)/shard_map/ppermute | solution.py:608
  14.0 5.7 %collective-permute-start.6 = (f32[24,512]{1,0:T(8,128)S(1)}, f32[24,512]{1,0:T(8,128)S(1)}, u32[]{:S(2)}, u32[]{:S(2)}) collective-permute-start(f32[24,512]{1,0:T(8,128)S(1)} %get-tuple-element.66), channel_id=1, source_target_pairs={{1,2},{2,1},{3,4},{4,3},{5,6},{6,5},{9,10},{10,9},{11,12},{12,11},... | collective-permute-start | bytes 147464 | tf_op jit(solution)/shard_map/ppermute | solution.py:607
  17.1 3.2 %collective-permute-start.7 = (f32[64,128]{1,0:T(8,128)S(1)}, f32[64,128]{1,0:T(8,128)S(1)}, u32[]{:S(2)}, u32[]{:S(2)}) collective-permute-start(f32[64,128]{1,0:T(8,128)S(1)} %shard_map.118.refs_6_), channel_id=1, source_target_pairs={{0,16},{8,24},{16,0},{24,8},{1,17},{9,25},{17,1},{25,9},{2,18},{10... | collective-permute-start | bytes 98312 | tf_op jit(solution)/shard_map/ppermute | solution.py:618
  20.9 4.8 %collective-permute-start.8 = (f32[80,128]{1,0:T(8,128)S(1)}, f32[80,128]{1,0:T(8,128)S(1)}, u32[]{:S(2)}, u32[]{:S(2)}) collective-permute-start(f32[80,128]{1,0:T(8,128)S(1)} %get-tuple-element.74), channel_id=1, source_target_pairs={{0,8},{8,0},{16,24},{24,16},{1,9},{9,1},{17,25},{25,17},{2,10},{10... | collective-permute-start | bytes 122888 | tf_op jit(solution)/shard_map/ppermute | solution.py:606
  21.1 6.3 %collective-permute-start.9 = (f32[24,512]{1,0:T(8,128)S(1)}, f32[24,512]{1,0:T(8,128)S(1)}, u32[]{:S(2)}, u32[]{:S(2)}) collective-permute-start(f32[24,512]{1,0:T(8,128)S(1)} %get-tuple-element.76), channel_id=1, source_target_pairs={{0,1},{1,0},{2,3},{3,2},{4,5},{5,4},{6,7},{7,6},{8,9},{9,8},{10,11... | collective-permute-start | bytes 147464 | tf_op jit(solution)/shard_map/ppermute | solution.py:608
  22.6 5.7 %collective-permute-start.10 = (f32[24,512]{1,0:T(8,128)S(1)}, f32[24,512]{1,0:T(8,128)S(1)}, u32[]{:S(2)}, u32[]{:S(2)}) collective-permute-start(f32[24,512]{1,0:T(8,128)S(1)} %get-tuple-element.77), channel_id=1, source_target_pairs={{1,2},{2,1},{3,4},{4,3},{5,6},{6,5},{9,10},{10,9},{11,12},{12,11},... | collective-permute-start | bytes 147464 | tf_op jit(solution)/shard_map/ppermute | solution.py:607
  25.7 3.2 %collective-permute-start.11 = (f32[64,128]{1,0:T(8,128)S(1)}, f32[64,128]{1,0:T(8,128)S(1)}, u32[]{:S(2)}, u32[]{:S(2)}) collective-permute-start(f32[64,128]{1,0:T(8,128)S(1)} %shard_map.122.refs_6_), channel_id=1, source_target_pairs={{0,16},{8,24},{16,0},{24,8},{1,17},{9,25},{17,1},{25,9},{2,18},{10... | collective-permute-start | bytes 98312 | tf_op jit(solution)/shard_map/ppermute | solution.py:618

commit v11 on v10

--- a/solution.py
+++ b/solution.py
@@ -72,23 +72,30 @@
         self.tiles = spectral // LANES
         self.some = -(-(2 * cols + 2 * rows) // 16) * 16
         self.edge = ((self.tiles // 2 + 1) * rows + 7) // 8 * 8
-        self.relay = sections % 4 == 0
+        self.relay = sections % 4 == 0 and bands % 2 == 0 and self.chunk <= cols
         self.quad = 4 if self.relay else 1
         self.hops = [
             (hop, flip)
             for hop in range(1, sections // self.quad)
             for flip in ((3, 1, 2, 0) if self.relay else (0,))
         ]
-        self.direct = [self.table(*hop) for hop in self.hops]
-        self.edges = [
-            any(abs(target - i) == 1 for i, target in table) for table in self.direct
+        self.direct = [
+            [(i, self.partner(i, *hop, divmod)[0]) for i in range(sections)] for hop in self.hops
         ]
+        self.edges = [any(abs(target - i) == 1 for i, target in table) for table in self.direct]
         self.sizes = [self.chunk + (self.edge if edge else 0) for edge in self.edges]
         if self.relay:
-            self.sizes = [2 * (self.chunk + self.edge), self.chunk] + self.sizes
-
-    def table(self, hop, flip):
-        return [(i, self.partner(i, hop, flip, divmod)[0]) for i in range(self.sections)]
+            self.sizes = [2 * (self.chunk + self.edge)] + self.sizes
+        self.row_lanes = slice(spectral // 2, spectral // 2 + LANES)
+        self.chunk_lanes = slice(spectral // 2 + LANES, spectral // 2 + 2 * LANES)
+
+    def crossing(self, flip):
+        bands = self.bands
+        return [
+            (i * bands + band, (i ^ flip) * bands + (band ^ 1))
+            for i in range(self.sections)
+            for band in range(bands)
+        ]
 
     def partner(self, section, hop, flip, divide=lambda a, b: (lax.div(a, b), lax.rem(a, b))):
         groups = self.sections // self.quad
@@ -115,23 +122,21 @@
             parts.append((self.partner(section, *hop)[1], message, 0, self.chunk if edge else None))
         return parts
 
-    def sent(self, section, messages):
+    def sent(self, section, messages, near):
         parts = []
+        lanes = slice(0, LANES)
         if self.relay:
-            to_x, to_y = messages[:2]
+            to_x = messages[0]
+            second = self.chunk + self.edge
             parts = [
-                (self.partner(section, 0, 1)[0], to_x, 0, self.chunk),
-                (self.partner(section, 0, 2)[0], to_y, 0, None),
-                (
-                    self.partner(section, 0, 3)[0],
-                    to_x,
-                    self.chunk + self.edge,
-                    2 * self.chunk + self.edge,
-                ),
+                (self.partner(section, 0, 1)[0], to_x, 0, lanes, self.chunk),
+                (self.partner(section, 0, 2)[0], near, 0, self.chunk_lanes, None),
+                (self.partner(section, 0, 3)[0], to_x, second, lanes, second + self.chunk),
             ]
-            messages = messages[2:]
+            messages = messages[1:]
         for message, hop, edge in zip(messages, self.hops, self.edges):
-            parts.append((self.partner(section, *hop)[0], message, 0, self.chunk if edge else None))
+            target = self.partner(section, *hop)[0]
+            parts.append((target, message, 0, lanes, self.chunk if edge else None))
         return parts
 
 
@@ -166,7 +171,7 @@
         out[:, tile * LANES : (tile + 1) * LANES] = packed_half(
             edge, tile, half, masks.northward, northward
         )
-    out[:, plan.spectral // 2 :] = sea_row
+    out[:, plan.row_lanes] = sea_row
 
 
 def fill_bands(plan, even, edges, sea_rows, far, near):
@@ -175,14 +180,15 @@
         fill_band(plan, northward, edge, jnp.where(northward, sea_rows[1], sea_rows[0]), out)
 
 
-def fill_sections(plan, section, edges, ocean, ordered, packed_out, sec_out):
+def fill_sections(plan, section, edges, ocean, ordered, packed_out, sec_out, near):
     chunk, rows, cols, half = plan.chunk, plan.rows, plan.cols, plan.tiles // 2
     lane = lane_of((plan.columns, LANES))
     packed_out[...] = jnp.where(lane < LANES // 2, ocean, ordered)
     sea_rows = ocean.reshape(rows, cols, LANES)
     masks = Directions((rows, LANES))
-    for target, out, at, edge_at in plan.sent(section, sec_out):
-        out[at : at + chunk, :] = packed_out[pl.ds(pl.multiple_of(target * chunk, 8), chunk), :]
+    for target, out, at, lanes, edge_at in plan.sent(section, sec_out, near):
+        part = packed_out[pl.ds(pl.multiple_of(target * chunk, 8), chunk), :]
+        out[at : at + chunk, lanes] = part
         if edge_at is None:
             continue
         eastward = target == section + 1
@@ -235,7 +241,7 @@
     zonal = lane_of(block) < plan.depth
     place = lax.broadcasted_iota(jnp.int32, block, 0)
     at_west, at_east = place == 0, place == cols - 1
-    lanes = slice(plan.spectral // 2, plan.spectral // 2 + LANES)
+    lanes = plan.row_lanes
     south_edge = jnp.where(even, far[:, lanes], near[:, lanes])
     north_edge = jnp.where(even, near[:, lanes], far[:, lanes])
     new = []
@@ -290,9 +296,11 @@
     return jnp.concatenate(parts, axis=0) * factor
 
 
-def relay_kernel(plan, axes, from_x, to_y, out):
-    out[0 : plan.chunk, :] = to_y[...]
-    out[plan.chunk :, :] = from_x[plan.chunk + plan.edge :, :]
+def relay_kernel(plan, axes, from_x, near, to_y, to_mate):
+    own = plan.chunk + plan.edge
+    to_y[0 : plan.chunk, :] = near[0 : plan.chunk, plan.chunk_lanes]
+    to_y[plan.chunk :, :] = from_x[own:, :]
+    to_mate[...] = from_x[:own, :]
 
 
 def square_places(plan):
@@ -347,7 +355,7 @@
     west = [waves[row, 0:1, :] for row in range(rows)]
     east = [waves[row, cols - 1 : cols, :] for row in range(rows)]
     edges = jnp.concatenate(west + east, axis=0)
-    fill_sections(plan, section, edges, ocean, ordered, packed_out, sec_out)
+    fill_sections(plan, section, edges, ocean, ordered, packed_out, sec_out, lat_out[1])
     sea_rows = ocean.reshape(rows, cols, LANES)
     ends = (waves[0], waves[rows - 1]), (sea_rows[0], sea_rows[rows - 1])
     fill_bands(plan, even, *ends, *lat_out)
@@ -470,7 +478,8 @@
     turned, turned_edge, turned_order, ocean_in, packed_in, permute_some, slots = refs[:7]
     turn_edge, sea, sea_order, sea_some, keep, stokes, rates, grow, refs = *refs[7:15], refs[15:]
     count = len(plan.sizes)
-    near, far, sec_in, refs = refs[0], refs[1], refs[2 : 2 + count], refs[2 + count :]
+    got = count + plan.relay
+    near, far, sec_in, refs = refs[0], refs[1], refs[2 : 2 + got], refs[2 + got :]
     ocean_out, packed_out, coupled, extra_out, far_out, near_out = refs[:6]
     sec_out, in_order = refs[6 : 6 + count], refs[6 + count]
     section, band = lax.axis_index(axes[1]), lax.axis_index(axes[0])
@@ -517,7 +526,7 @@
     moments = total[:columns, :] + total[columns:, :]
     some = jnp.concatenate(some, axis=1)
     edges = some[2 * cols : 2 * cols + 2 * rows, :]
-    fill_sections(plan, section, edges, ocean, moments, packed_out, sec_out)
+    fill_sections(plan, section, edges, ocean, moments, packed_out, sec_out, near_out)
     ends = (some[:cols, :], some[cols : 2 * cols, :]), (new[0], new[rows - 1])
     fill_bands(plan, even, *ends, far_out, near_out)
 
@@ -535,8 +544,8 @@
 
 def last_kernel(plan, axes, *refs):
     turned, ocean_in, packed_in, permute, turn_edge, sea, keep, rates, grow = refs[:9]
-    count = len(plan.sizes)
-    near, far, sec_in, refs = refs[9], refs[10], refs[11 : 11 + count], refs[11 + count :]
+    got = len(plan.sizes) + plan.relay
+    near, far, sec_in, refs = refs[9], refs[10], refs[11 : 11 + got], refs[11 + got :]
     waves_far, ocean_far, coupled, waves_out, ocean_out, done = refs
     section, band = lax.axis_index(axes[1]), lax.axis_index(axes[0])
     even = lax.rem(band, 2) == 0
@@ -577,7 +586,8 @@
     shape = jax.ShapeDtypeStruct
     params = pltpu.CompilerParams(vmem_limit_bytes=32 * 1024 * 1024)
     to_sections = [shape((size, LANES), F32) for size in plan.sizes]
-    to_band = shape((cols, spectral // 2 + LANES), F32)
+    to_far = shape((cols, plan.row_lanes.stop), F32)
+    to_near = shape((cols, plan.chunk_lanes.stop), F32)
     state = shape((columns, LANES), F32)
     field = shape(spectra.shape, F32)
     at_edges = shape((2 * rows, LANES), F32)
@@ -595,6 +605,7 @@
             compiler_params=params,
         )(*args)
 
+    both_axes = (axes[1], axes[0])
     pairs = [(i, i ^ 1) for i in range(plan.bands) if i ^ 1 < plan.bands]
     others = [(i, ((i + 1) ^ 1) - 1) for i in range(1, plan.bands)]
     others = [(i, j) for i, j in others if j < plan.bands]
@@ -602,20 +613,22 @@
     def exchange(to_far, to_near, to_sections, meanwhile):
         got = []
         if plan.relay:
-            to_x, to_y, *to_sections = to_sections
-            got.append(lax.ppermute(to_x, axes[1], plan.table(0, 1)))
+            to_x, *to_sections = to_sections
+            from_x = lax.ppermute(to_x, both_axes, plan.crossing(1))
         far_in = lax.ppermute(to_far, axes[0], others)
         near_in = lax.ppermute(to_near, axes[0], pairs)
         first = to_far
         if plan.relay:
-            (first,) = call(
+            part = plan.chunk + plan.edge
+            first, to_mate = call(
                 relay_kernel,
-                [shape((2 * plan.chunk + plan.edge, LANES), F32)],
+                [shape((plan.chunk + part, LANES), F32), shape((part, LANES), F32)],
                 [],
-                got[0],
-                to_y,
+                from_x,
+                near_in,
             )
-            got.append(lax.ppermute(first, axes[1], plan.table(0, 2)))
+            from_y = lax.ppermute(first, both_axes, plan.crossing(2))
+            got = [lax.ppermute(to_mate, axes[0], pairs), from_y]
         got += [
             lax.ppermute(message, axes[1], table)
             for message, table in zip(to_sections, plan.direct)
@@ -630,8 +643,8 @@
             state,
             shape((columns, 2 * columns), BF16),
             *to_sections,
-            to_band,
-            to_band,
+            to_far,
+            to_near,
         ],
         [
             pltpu.VMEM(currents.shape, F32),
@@ -681,9 +694,9 @@
             *came[:2],
             order,
         )
-        ocean, packed, coupled, extra, to_far, to_near, *sent = call(
+        ocean, packed, coupled, extra, *sent = call(
             send_kernel,
-            [state, state, state, edge_field, to_band, to_band] + to_sections,
+            [state, state, state, edge_field, to_far, to_near] + to_sections,
             [pltpu.VMEM((columns, spectral), F32)],
             turned,
             turned_edge,
@@ -709,7 +722,7 @@
             )
             return waves
 
-        waves, came = exchange(to_far, to_near, sent, grown)
+        waves, came = exchange(*sent[:2], sent[2:], grown)
     (turned,) = call(move_kernel, [field], [], waves, turn, rates, *came[:2])
     return call(
         last_kernel,

time: 30.2 us -> 30.1 us (level)
  starting transfers between devices: 19.7 us -> 20.1 us
  waiting for transfers between devices: 2.54 us -> 2.23 us
    ppermute x3, starting transfers between devices: 4.17 us -> 0.53 us  [exchange(): near_in = lax.ppermute(to_near, axes[0], pairs)]
    ppermute x6 -> x9, starting transfers between devices: 6.32 us -> 9.69 us  [the longest x3 4.6 us: exchange(): from_x = lax.ppermute(to_x, both_axes, plan.crossing(1))]
    ppermute x3, waiting for transfers between devices: 2.52 us -> 0.21 us  [exchange(): far_in = lax.ppermute(to_far, axes[0], others)]
    ppermute x6 -> x9, waiting for transfers between devices: 0.02 us -> 2 us  [the longest x3 1.99 us: exchange(): from_y = lax.ppermute(first, both_axes, plan.crossing(2))]
    ppermute x3, starting transfers between devices: 9.24 us -> 9.83 us  [exchange(): far_in = lax.ppermute(to_far, axes[0], others)]
  transfers between devices with their start and end apart: 12 -> 15, of which waited for: 3 -> 5; matrix products, arithmetic and copies ran while one was open for 0% -> 0% of each run, Pallas kernels for 9% -> 9%
where the time goes in v11:
time: 30.1 us; the launch traced here: 30 us
  starting transfers between devices  20.1 us (67%)
  Pallas kernels  6.76 us (22%)
  waiting for transfers between devices  2.23 us (7%)
  between operations  0.88 us (3%)
    ppermute x3, starting transfers between devices, exchange(): far_in = lax.ppermute(to_far, axes[0], others)  9.83 us
    pallas_call x13, Pallas kernels, call(): pl.pallas_call(functools.partial(kernel, plan, axes), out_shape=outs, in_...  6.76 us
    ppermute x3, starting transfers between devices, exchange(): from_x = lax.ppermute(to_x, both_axes, plan.crossing(1))  4.6 us
    ppermute x3, starting transfers between devices, exchange(): got = [lax.ppermute(to_mate, axes[0], pairs), from_y]  3.22 us
    ppermute x3, waiting for transfers between devices, exchange(): from_y = lax.ppermute(first, both_axes, plan.crossing(2))  1.99 us
    ppermute x3, starting transfers between devices, exchange(): from_y = lax.ppermute(first, both_axes, plan.crossing(2))  1.87 us
  transfers between devices with their start and end apart: 15, of which 5 were waited for; matrix products, arithmetic and copies ran while one was open for 0% of the time, Pallas kernels for 9%

profile of v11, /device:TPU:1, one launch (start us, length us, event | category | flops | bytes accessed | tf_op | source)
XLA Modules:
  0.0 30.0 jit_solution(5531424322788059892)
XLA Ops:
  0.7 0.0 copy-start.2
  0.7 0.0 copy-start.1
  0.7 1.6 %shard_map.113 = (f32[4,24,768]{2,1,0:T(8,128)S(1)}, f32[96,128]{1,0:T(8,128)S(1)}, f32[96,128]{1,0:T(8,128)S(1)}, bf16[96,192]{1,0:T(8,128)(2,1)S(1)}, f32[80,1...) custom-call(f32[4,24,768]{2,1,0:T(8,128)} %refs_0_.2, f32[4,24,64]{2,1,0:T(8,128)} %refs_1_.2, ...), custom_call_target="tpu_custom_call" | custom-call | tf_op jit(solution)/shard_map/pallas_call | solution.py:599
  2.3 0.1 collective-permute-start.1
  2.4 2.6 %collective-permute-start = (f32[80,128]{1,0:T(8,128)S(1)}, f32[80,128]{1,0:T(8,128)S(1)}, u32[]{:S(2)}, u32[]{:S(2)}) collective-permute-start(f32[80,128]{1,0:T(8,128)S(1)} %get-tuple-element.46), channel_id=1, source_target_pairs={{0,9},{1,8},{2,11},{3,10},{4,13},{5,12},{6,15},{7,14},{8,1},{9,0},... | collective-permute-start | bytes 122888 | tf_op jit(solution)/shard_map/ppermute | solution.py:617
  5.1 3.5 %collective-permute-start.2 = (f32[24,512]{1,0:T(8,128)S(1)}, f32[24,512]{1,0:T(8,128)S(1)}, u32[]{:S(2)}, u32[]{:S(2)}) collective-permute-start(f32[24,512]{1,0:T(8,128)S(1)} %get-tuple-element.50), channel_id=1, source_target_pairs={{1,2},{2,1},{3,4},{4,3},{5,6},{6,5},{9,10},{10,9},{11,12},{12,11},... | collective-permute-start | bytes 147464 | tf_op jit(solution)/shard_map/ppermute | solution.py:618
  8.6 0.1 collective-permute-start.4
  8.7 1.6 %collective-permute-start.3 = (f32[40,128]{1,0:T(8,128)S(1)}, f32[40,128]{1,0:T(8,128)S(1)}, u32[]{:S(2)}, u32[]{:S(2)}) collective-permute-start(f32[40,128]{1,0:T(8,128)S(1)} %get-tuple-element.63), channel_id=1, source_target_pairs={{0,1},{1,0},{2,3},{3,2},{4,5},{5,4},{6,7},{7,6},{8,9},{9,8},{10,11... | collective-permute-start | bytes 61448 | tf_op jit(solution)/shard_map/ppermute | solution.py:631
  10.3 0.3 %shard_map.115 = (bf16[96,96]{1,0:T(8,128)(2,1)S(1)}, bf16[64,96]{1,0:T(8,128)(2,1)S(1)}, s32[8,128]{1,0:T(8,128)S(1)}, f32[96,128]{1,0:T(8,128)S(1)}, f32[8,128...) custom-call(f32[4,24]{1,0:T(4,128)S(1)} %copy-done.3, ...), custom_call_target="tpu_custom_call" | custom-call | tf_op jit(solution)/shard_map/pallas_call | solution.py:599
  10.7 0.6 %shard_map.116 = (f32[4,24,768]{2,1,0:T(8,128)S(1)}, f32[8,768]{1,0:T(8,128)S(1)}, f32[96,768]{1,0:T(8,128)S(1)}) custom-call(f32[4,24,768]{2,1,0:T(8,128)S(1)} %get-tuple-element.44.refs_0_, f32[96,128]{1,0:T(8,128)S(1)} %get-tuple-element.49.refs_1_, f32[8,768]{1,0:T(8,128)S(1)} %copy-done.2, f32[24,640]{1,0:T(8,128)S(1)} %collective-permute-done.1.near.refs_3_.refs_15_, ...), custom_call_target="tpu_custom_call" | custom-call | tf_op jit(solution)/shard_map/pallas_call | solution.py:599
  11.3 0.8 %collective-permute-done.4.refs_18_ = f32[64,128]{1,0:T(8,128)S(1)} collective-permute-done((f32[64,128]{1,0:T(8,128)S(1)}, f32[64,128]{1,0:T(8,128)S(1)}, u32[]{:S(2)}, u32[]{:S(2)}) %collective-permute-start.4) | collective-permute-done | bytes 32800 | tf_op jit(solution)/shard_map/ppermute | solution.py:630
  12.0 0.6 %shard_map.117 = (f32[96,128]{1,0:T(8,128)S(1)}, f32[96,128]{1,0:T(8,128)S(1)}, f32[96,128]{1,0:T(8,128)S(1)}, f32[8,768]{1,0:T(8,128)S(1)}, f32[24,512]{1,0:T(8...) custom-call(f32[4,24,768]{2,1,0:T(8,128)S(1)} %get-tuple-element.51.refs_0_, ...), custom_call_target="tpu_custom_call" | custom-call | tf_op jit(solution)/shard_map/pallas_call | solution.py:599
  12.7 0.1 collective-permute-start.6
  12.7 0.6 %collective-permute-start.5 = (f32[80,128]{1,0:T(8,128)S(1)}, f32[80,128]{1,0:T(8,128)S(1)}, u32[]{:S(2)}, u32[]{:S(2)}) collective-permute-start(f32[80,128]{1,0:T(8,128)S(1)} %get-tuple-element.67), channel_id=1, source_target_pairs={{0,9},{1,8},{2,11},{3,10},{4,13},{5,12},{6,15},{7,14},{8,1},{9,0},... | collective-permute-start | bytes 122888 | tf_op jit(solution)/shard_map/ppermute | solution.py:617
  13.4 3.2 %collective-permute-start.7 = (f32[24,512]{1,0:T(8,128)S(1)}, f32[24,512]{1,0:T(8,128)S(1)}, u32[]{:S(2)}, u32[]{:S(2)}) collective-permute-start(f32[24,512]{1,0:T(8,128)S(1)} %get-tuple-element.70), channel_id=1, source_target_pairs={{1,2},{2,1},{3,4},{4,3},{5,6},{6,5},{9,10},{10,9},{11,12},{12,11},... | collective-permute-start | bytes 147464 | tf_op jit(solution)/shard_map/ppermute | solution.py:618
  16.6 1.5 %collective-permute-start.9 = (f32[64,128]{1,0:T(8,128)S(1)}, f32[64,128]{1,0:T(8,128)S(1)}, u32[]{:S(2)}, u32[]{:S(2)}) collective-permute-start(f32[64,128]{1,0:T(8,128)S(1)} %get-tuple-element.69.refs_6_), channel_id=1, source_target_pairs={{0,17},{1,16},{2,19},{3,18},{4,21},{5,20},{6,23},{7,22},{8,25},{9,... | collective-permute-start | bytes 98312 | tf_op jit(solution)/shard_map/ppermute | solution.py:630
  18.0 0.2 collective-permute-start.8
  18.3 0.4 %shard_map.119.refs_0_ = f32[4,24,768]{2,1,0:T(8,128)S(1)} custom-call(f32[4,24,768]{2,1,0:T(8,128)S(1)} %get-tuple-element.51.refs_0_, f32[8,768]{1,0:T(8,128)S(1)} %get-tuple-element.64.refs_1_, f32[96,128]{1,0:T(8,128)S(1)} %get-tuple-element.65.refs_2_, bf16[96,96]{1,0:T(8,128)(2,1)S(1)} %get-tuple-element.66.refs_3_, ...), custom_call_target="tpu_custom_call" | custom-call | tf_op jit(solution)/shard_map/pallas_call | solution.py:599
  18.7 0.1 collective-permute-done.7.refs_4_.refs_16_
  18.8 0.6 %shard_map.120 = (f32[4,24,768]{2,1,0:T(8,128)S(1)}, f32[8,768]{1,0:T(8,128)S(1)}, f32[96,768]{1,0:T(8,128)S(1)}) custom-call(f32[4,24,768]{2,1,0:T(8,128)S(1)} %shard_map.119.refs_0_, f32[96,128]{1,0:T(8,128)S(1)} %get-tuple-element.49.refs_1_, f32[8,768]{1,0:T(8,128)S(1)} %copy-done.2, f32[24,640]{1,0:T(8,128)S(1)} %collective-permute-done.6.near.refs_3_.refs_15_, ...), custom_call_target="tpu_custom_call" | custom-call | tf_op jit(solution)/shard_map/pallas_call | solution.py:599
  19.4 0.6 %collective-permute-done.9.refs_18_ = f32[64,128]{1,0:T(8,128)S(1)} collective-permute-done((f32[64,128]{1,0:T(8,128)S(1)}, f32[64,128]{1,0:T(8,128)S(1)}, u32[]{:S(2)}, u32[]{:S(2)}) %collective-permute-start.9) | collective-permute-done | bytes 32800 | tf_op jit(solution)/shard_map/ppermute | solution.py:630
  20.0 0.6 %shard_map.121 = (f32[96,128]{1,0:T(8,128)S(1)}, f32[96,128]{1,0:T(8,128)S(1)}, f32[96,128]{1,0:T(8,128)S(1)}, f32[8,768]{1,0:T(8,128)S(1)}, f32[24,512]{1,0:T(8...) custom-call(f32[4,24,768]{2,1,0:T(8,128)S(1)} %get-tuple-element.71.refs_0_, ...), custom_call_target="tpu_custom_call" | custom-call | tf_op jit(solution)/shard_map/pallas_call | solution.py:599
  20.6 0.3 %collective-permute-start.11 = (f32[24,640]{1,0:T(8,128)S(1)}, f32[24,640]{1,0:T(8,128)S(1)}, u32[]{:S(2)}, u32[]{:S(2)}) collective-permute-start(f32[24,640]{1,0:T(8,128)S(1)} %get-tuple-element.80), channel_id=1, source_target_pairs={{0,1},{1,0},{2,3},{3,2},{4,5},{5,4},{6,7},{7,6},{8,9},{9,8},{10,11... | collective-permute-start | bytes 184328 | tf_op jit(solution)/shard_map/ppermute | solution.py:619
  20.9 1.3 %collective-permute-start.10 = (f32[80,128]{1,0:T(8,128)S(1)}, f32[80,128]{1,0:T(8,128)S(1)}, u32[]{:S(2)}, u32[]{:S(2)}) collective-permute-start(f32[80,128]{1,0:T(8,128)S(1)} %get-tuple-element.79), channel_id=1, source_target_pairs={{0,9},{1,8},{2,11},{3,10},{4,13},{5,12},{6,15},{7,14},{8,1},{9,0},... | collective-permute-start | bytes 122888 | tf_op jit(solution)/shard_map/ppermute | solution.py:617
  22.2 3.2 %collective-permute-start.12 = (f32[24,512]{1,0:T(8,128)S(1)}, f32[24,512]{1,0:T(8,128)S(1)}, u32[]{:S(2)}, u32[]{:S(2)}) collective-permute-start(f32[24,512]{1,0:T(8,128)S(1)} %get-tuple-element.82), channel_id=1, source_target_pairs={{1,2},{2,1},{3,4},{4,3},{5,6},{6,5},{9,10},{10,9},{11,12},{12,11},... | collective-permute-start | bytes 147464 | tf_op jit(solution)/shard_map/ppermute | solution.py:618
  25.4 0.3 %collective-permute-start.14 = (f32[64,128]{1,0:T(8,128)S(1)}, f32[64,128]{1,0:T(8,128)S(1)}, u32[]{:S(2)}, u32[]{:S(2)}) collective-permute-start(f32[64,128]{1,0:T(8,128)S(1)} %get-tuple-element.81.refs_6_), channel_id=1, source_target_pairs={{0,17},{1,16},{2,19},{3,18},{4,21},{5,20},{6,23},{7,22},{8,25},{9,... | collective-permute-start | bytes 98312 | tf_op jit(solution)/shard_map/ppermute | solution.py:630
  25.8 1.4 %collective-permute-start.13 = (f32[40,128]{1,0:T(8,128)S(1)}, f32[40,128]{1,0:T(8,128)S(1)}, u32[]{:S(2)}, u32[]{:S(2)}) collective-permute-start(f32[40,128]{1,0:T(8,128)S(1)} %get-tuple-element.85), channel_id=1, source_target_pairs={{0,1},{1,0},{2,3},{3,2},{4,5},{5,4},{6,7},{7,6},{8,9},{9,8},{10,11... | collective-permute-start | bytes 61448 | tf_op jit(solution)/shard_map/ppermute | solution.py:631
  27.1 0.4 %shard_map.123.refs_0_ = f32[4,24,768]{2,1,0:T(8,128)S(1)} custom-call(f32[4,24,768]{2,1,0:T(8,128)S(1)} %get-tuple-element.71.refs_0_, f32[8,768]{1,0:T(8,128)S(1)} %get-tuple-element.77.refs_1_, f32[96,128]{1,0:T(8,128)S(1)} %get-tuple-element.78.refs_2_, bf16[96,96]{1,0:T(8,128)(2,1)S(1)} %get-tuple-element.66.refs_3_, ...), custom_call_target="tpu_custom_call" | custom-call | tf_op jit(solution)/shard_map/pallas_call | solution.py:599
  27.5 0.1 collective-permute-done.12.refs_4_.refs_10_
  27.6 0.6 %shard_map.124.refs_0_ = f32[4,24,768]{2,1,0:T(8,128)S(1)} custom-call(f32[4,24,768]{2,1,0:T(8,128)S(1)} %shard_map.123.refs_0_, f32[96,128]{1,0:T(8,128)S(1)} %get-tuple-element.49.refs_1_, f32[8,768]{1,0:T(8,128)S(1)} %copy-done.2, f32[24,640]{1,0:T(8,128)S(1)} %collective-permute-done.11.near.refs_3_.refs_9_, ...), custom_call_target="tpu_custom_call" | custom-call | tf_op jit(solution)/shard_map/pallas_call | solution.py:599
  28.2 0.6 %collective-permute-done.14.refs_12_ = f32[64,128]{1,0:T(8,128)S(1)} collective-permute-done((f32[64,128]{1,0:T(8,128)S(1)}, f32[64,128]{1,0:T(8,128)S(1)}, u32[]{:S(2)}, u32[]{:S(2)}) %collective-permute-start.14) | collective-permute-done | bytes 32800 | tf_op jit(solution)/shard_map/ppermute | solution.py:630
  28.9 1.1 %shard_map.125 = (f32[4,24,768]{2,1,0:T(8,128)}, f32[4,24,64]{2,1,0:T(8,128)}) custom-call(f32[4,24,768]{2,1,0:T(8,128)S(1)} %shard_map.124.refs_0_, f32[96,128]{1,0:T(8,128)S(1)} %get-tuple-element.83.refs_1_, f32[96,128]{1,0:T(8,128)S(1)} %get-tuple-element.84.refs_2_, bf16[96,96]{1,0:T(8,128)(2,1)S(1)} %get-tuple-element.66.refs_3_, ...), custom_call_target="tpu_custom_call" | custom-call | tf_op jit(solution)/shard_map/pallas_call | solution.py:599
  (23 shorter events, 0.1 us)
Async XLA Ops:
  0.6 9.7 %copy-start.3 = (f32[4,24]{1,0:T(4,128)S(1)}, f32[4,24]{1,0:T(4,128)}, u32[]{:S(2)}) copy-start(f32[4,24]{1,0:T(4,128)} %refs_0_.3) | copy-start | bytes 1156
  0.6 9.7 %copy-start.4 = (s32[4,24]{1,0:T(4,128)S(1)}, s32[4,24]{1,0:T(4,128)}, u32[]{:S(2)}) copy-start(s32[4,24]{1,0:T(4,128)} %refs_2_.6) | copy-start | bytes 1156
  0.7 9.7 %copy-start.5 = (f32[32]{0:T(128)S(1)}, f32[32]{0:T(128)}, u32[]{:S(2)}) copy-start(f32[32]{0:T(128)} %refs_1_.3) | copy-start | bytes 388
  0.7 10.0 %copy-start.2 = (f32[8,768]{1,0:T(8,128)S(1)}, f32[8,768]{1,0:T(8,128)}, u32[]{:S(2)}) copy-start(f32[8,768]{1,0:T(8,128)} %constant.10.clone.refs_2_.refs_13_.refs_7_) | copy-start | bytes 73732
  0.7 11.4 %copy-start.1 = (bf16[768,256]{1,0:T(8,128)(2,1)S(1)}, bf16[768,256]{1,0:T(8,128)(2,1)}, u32[]{:S(2)}) copy-start(bf16[768,256]{1,0:T(8,128)(2,1)} %constant.9.clone.refs_12_) | copy-start | bytes 1179652
  2.3 9.7 %copy-start = (bf16[1536,128]{1,0:T(8,128)(2,1)S(1)}, bf16[1536,128]{1,0:T(8,128)(2,1)}, u32[]{:S(2)}) copy-start(bf16[1536,128]{1,0:T(8,128)(2,1)} %constant.11.clone.refs_14_.refs_5_.refs_8_) | copy-start | bytes 1179652
  2.3 6.3 %collective-permute-start.1 = (f32[24,640]{1,0:T(8,128)S(1)}, f32[24,640]{1,0:T(8,128)S(1)}, u32[]{:S(2)}, u32[]{:S(2)}) collective-permute-start(f32[24,640]{1,0:T(8,128)S(1)} %get-tuple-element.47), channel_id=1, source_target_pairs={{0,1},{1,0},{2,3},{3,2},{4,5},{5,4},{6,7},{7,6},{8,9},{9,8},{10,11... | collective-permute-start | bytes 184328 | tf_op jit(solution)/shard_map/ppermute | solution.py:619
  2.4 6.2 %collective-permute-start = (f32[80,128]{1,0:T(8,128)S(1)}, f32[80,128]{1,0:T(8,128)S(1)}, u32[]{:S(2)}, u32[]{:S(2)}) collective-permute-start(f32[80,128]{1,0:T(8,128)S(1)} %get-tuple-element.46), channel_id=1, source_target_pairs={{0,9},{1,8},{2,11},{3,10},{4,13},{5,12},{6,15},{7,14},{8,1},{9,0},... | collective-permute-start | bytes 122888 | tf_op jit(solution)/shard_map/ppermute | solution.py:617
  5.1 5.6 %collective-permute-start.2 = (f32[24,512]{1,0:T(8,128)S(1)}, f32[24,512]{1,0:T(8,128)S(1)}, u32[]{:S(2)}, u32[]{:S(2)}) collective-permute-start(f32[24,512]{1,0:T(8,128)S(1)} %get-tuple-element.50), channel_id=1, source_target_pairs={{1,2},{2,1},{3,4},{4,3},{5,6},{6,5},{9,10},{10,9},{11,12},{12,11},... | collective-permute-start | bytes 147464 | tf_op jit(solution)/shard_map/ppermute | solution.py:618
  8.6 3.4 %collective-permute-start.4 = (f32[64,128]{1,0:T(8,128)S(1)}, f32[64,128]{1,0:T(8,128)S(1)}, u32[]{:S(2)}, u32[]{:S(2)}) collective-permute-start(f32[64,128]{1,0:T(8,128)S(1)} %get-tuple-element.48.refs_4_), channel_id=1, source_target_pairs={{0,17},{1,16},{2,19},{3,18},{4,21},{5,20},{6,23},{7,22},{8,25},{9,... | collective-permute-start | bytes 98312 | tf_op jit(solution)/shard_map/ppermute | solution.py:630
  8.7 2.6 %collective-permute-start.3 = (f32[40,128]{1,0:T(8,128)S(1)}, f32[40,128]{1,0:T(8,128)S(1)}, u32[]{:S(2)}, u32[]{:S(2)}) collective-permute-start(f32[40,128]{1,0:T(8,128)S(1)} %get-tuple-element.63), channel_id=1, source_target_pairs={{0,1},{1,0},{2,3},{3,2},{4,5},{5,4},{6,7},{7,6},{8,9},{9,8},{10,11... | collective-permute-start | bytes 61448 | tf_op jit(solution)/shard_map/ppermute | solution.py:631
  12.7 3.9 %collective-permute-start.6 = (f32[24,640]{1,0:T(8,128)S(1)}, f32[24,640]{1,0:T(8,128)S(1)}, u32[]{:S(2)}, u32[]{:S(2)}) collective-permute-start(f32[24,640]{1,0:T(8,128)S(1)} %get-tuple-element.68), channel_id=1, source_target_pairs={{0,1},{1,0},{2,3},{3,2},{4,5},{5,4},{6,7},{7,6},{8,9},{9,8},{10,11... | collective-permute-start | bytes 184328 | tf_op jit(solution)/shard_map/ppermute | solution.py:619
  12.7 3.8 %collective-permute-start.5 = (f32[80,128]{1,0:T(8,128)S(1)}, f32[80,128]{1,0:T(8,128)S(1)}, u32[]{:S(2)}, u32[]{:S(2)}) collective-permute-start(f32[80,128]{1,0:T(8,128)S(1)} %get-tuple-element.67), channel_id=1, source_target_pairs={{0,9},{1,8},{2,11},{3,10},{4,13},{5,12},{6,15},{7,14},{8,1},{9,0},... | collective-permute-start | bytes 122888 | tf_op jit(solution)/shard_map/ppermute | solution.py:617
  13.4 5.4 %collective-permute-start.7 = (f32[24,512]{1,0:T(8,128)S(1)}, f32[24,512]{1,0:T(8,128)S(1)}, u32[]{:S(2)}, u32[]{:S(2)}) collective-permute-start(f32[24,512]{1,0:T(8,128)S(1)} %get-tuple-element.70), channel_id=1, source_target_pairs={{1,2},{2,1},{3,4},{4,3},{5,6},{6,5},{9,10},{10,9},{11,12},{12,11},... | collective-permute-start | bytes 147464 | tf_op jit(solution)/shard_map/ppermute | solution.py:618
  16.6 3.4 %collective-permute-start.9 = (f32[64,128]{1,0:T(8,128)S(1)}, f32[64,128]{1,0:T(8,128)S(1)}, u32[]{:S(2)}, u32[]{:S(2)}) collective-permute-start(f32[64,128]{1,0:T(8,128)S(1)} %get-tuple-element.69.refs_6_), channel_id=1, source_target_pairs={{0,17},{1,16},{2,19},{3,18},{4,21},{5,20},{6,23},{7,22},{8,25},{9,... | collective-permute-start | bytes 98312 | tf_op jit(solution)/shard_map/ppermute | solution.py:630
  18.0 1.3 %collective-permute-start.8 = (f32[40,128]{1,0:T(8,128)S(1)}, f32[40,128]{1,0:T(8,128)S(1)}, u32[]{:S(2)}, u32[]{:S(2)}) collective-permute-start(f32[40,128]{1,0:T(8,128)S(1)} %get-tuple-element.76), channel_id=1, source_target_pairs={{0,1},{1,0},{2,3},{3,2},{4,5},{5,4},{6,7},{7,6},{8,9},{9,8},{10,11... | collective-permute-start | bytes 61448 | tf_op jit(solution)/shard_map/ppermute | solution.py:631
  20.6 4.9 %collective-permute-start.11 = (f32[24,640]{1,0:T(8,128)S(1)}, f32[24,640]{1,0:T(8,128)S(1)}, u32[]{:S(2)}, u32[]{:S(2)}) collective-permute-start(f32[24,640]{1,0:T(8,128)S(1)} %get-tuple-element.80), channel_id=1, source_target_pairs={{0,1},{1,0},{2,3},{3,2},{4,5},{5,4},{6,7},{7,6},{8,9},{9,8},{10,11... | collective-permute-start | bytes 184328 | tf_op jit(solution)/shard_map/ppermute | solution.py:619
  20.9 4.5 %collective-permute-start.10 = (f32[80,128]{1,0:T(8,128)S(1)}, f32[80,128]{1,0:T(8,128)S(1)}, u32[]{:S(2)}, u32[]{:S(2)}) collective-permute-start(f32[80,128]{1,0:T(8,128)S(1)} %get-tuple-element.79), channel_id=1, source_target_pairs={{0,9},{1,8},{2,11},{3,10},{4,13},{5,12},{6,15},{7,14},{8,1},{9,0},... | collective-permute-start | bytes 122888 | tf_op jit(solution)/shard_map/ppermute | solution.py:617
  22.2 5.4 %collective-permute-start.12 = (f32[24,512]{1,0:T(8,128)S(1)}, f32[24,512]{1,0:T(8,128)S(1)}, u32[]{:S(2)}, u32[]{:S(2)}) collective-permute-start(f32[24,512]{1,0:T(8,128)S(1)} %get-tuple-element.82), channel_id=1, source_target_pairs={{1,2},{2,1},{3,4},{4,3},{5,6},{6,5},{9,10},{10,9},{11,12},{12,11},... | collective-permute-start | bytes 147464 | tf_op jit(solution)/shard_map/ppermute | solution.py:618
  25.4 3.4 %collective-permute-start.14 = (f32[64,128]{1,0:T(8,128)S(1)}, f32[64,128]{1,0:T(8,128)S(1)}, u32[]{:S(2)}, u32[]{:S(2)}) collective-permute-start(f32[64,128]{1,0:T(8,128)S(1)} %get-tuple-element.81.refs_6_), channel_id=1, source_target_pairs={{0,17},{1,16},{2,19},{3,18},{4,21},{5,20},{6,23},{7,22},{8,25},{9,... | collective-permute-start | bytes 98312 | tf_op jit(solution)/shard_map/ppermute | solution.py:630
  25.8 2.4 %collective-permute-start.13 = (f32[40,128]{1,0:T(8,128)S(1)}, f32[40,128]{1,0:T(8,128)S(1)}, u32[]{:S(2)}, u32[]{:S(2)}) collective-permute-start(f32[40,128]{1,0:T(8,128)S(1)} %get-tuple-element.85), channel_id=1, source_target_pairs={{0,1},{1,0},{2,3},{3,2},{4,5},{5,4},{6,7},{7,6},{8,9},{9,8},{10,11... | collective-permute-start | bytes 61448 | tf_op jit(solution)/shard_map/ppermute | solution.py:631

commit v12 on v11

--- a/solution.py
+++ b/solution.py
@@ -49,7 +49,9 @@
     grow = (
         growth[None, None, :, None] * mean_weights.T[None, :, :, None] * compass[:, None, None, :]
     ).reshape(2 * ndepth, nfreq * ndir)
-    high, low = split_halves(stokes)
+    pairs = stokes.reshape(-1, 2, LANES // ndir, ndir, 2 * ndepth)
+    stokes = np.concatenate([pairs[:, 0, :, : ndir // 2], pairs[:, 1, :, ndir // 2 :]], axis=2)
+    high, low = split_halves(stokes.reshape(nfreq * ndir // 2, 2 * ndepth))
     blank = np.zeros_like(high)
     stokes_once = np.concatenate([high, low], axis=1)
     stokes_upper = np.concatenate([blank, high, blank, low], axis=1)
@@ -153,8 +155,17 @@
     return high, (value - high.astype(F32)).astype(BF16)
 
 
+def opposed(part):
+    first, second = part[:, :LANES], part[:, LANES:]
+    lower = lax.rem(lane_of(first.shape), NDIR) < NDIR // 2
+    shift = NDIR // 2
+    return jnp.where(lower, first, second) - jnp.where(
+        lower, pltpu.roll(first, LANES - shift, 1), pltpu.roll(second, shift, 1)
+    )
+
+
 def stokes_product(part, table):
-    return dot(jnp.concatenate(split_value(part), axis=0), table)
+    return dot(jnp.concatenate(split_value(opposed(part)), axis=1), twice(table, 0))
 
 
 def packed_half(edge, tile, half, ahead, forward):
@@ -344,9 +355,9 @@
     total = None
     for start in range(0, plan.spectral, 256):
         part = waves[:, :, start : start + 256].reshape(columns, 256)
-        product = stokes_product(part, stokes[start : start + 256, :])
+        product = stokes_product(part, stokes[start // 2 : start // 2 + LANES, :])
         total = product if total is None else total + product
-    moments = total[:columns] + total[columns:]
+    moments = total
     flat = currents[...].reshape(columns, 2 * plan.depth)
     ocean = jnp.concatenate([flat, jnp.zeros((columns, LANES - 2 * plan.depth), F32)], axis=1)
     ocean_out[...] = ocean
@@ -500,30 +511,31 @@
     some_of = twice(dot(permute_some[...], halves).astype(BF16))
     wet = twice(wet)
     total = None
-    some = []
+    some, grown = [], []
     filler = jnp.zeros((plan.some - 2 * cols - 2 * rows, 256), F32)
     for number, start in enumerate(range(0, plan.spectral, 256)):
         lanes = slice(start, start + 256)
         table = growth_table(grow, number)
         from_edges = jnp.concatenate(extra[2 * number : 2 * number + 2], axis=1)
         extra_out[:, lanes] = from_edges
-        grown = in_order[:, lanes] * (wet + dot(rows_of, table))
-        product = stokes_product(grown, stokes[lanes, :])
-        total = product if total is None else total + product
+        grown.append(in_order[:, lanes] * (wet + dot(rows_of, table)))
         parts = []
         for row in (0, rows - 1):
             west, east = from_edges[row : row + 1, :], from_edges[rows + row : rows + row + 1, :]
             parts += with_edges(plan, turned[row, :, lanes], west, east)
         parts += [turned_edge[:, lanes] + from_edges, filler]
         some.append(jnp.concatenate(parts, axis=0) * (wet_some + dot(some_of, table)))
+    for number, start in enumerate(range(0, plan.spectral, 256)):
+        lanes = slice(start, start + 256)
+        product = stokes_product(grown[number], stokes[start // 2 : start // 2 + LANES, :])
+        total = product if total is None else total + product
     drift = pltpu.roll(arrived, LANES // 2, 1)
     new = ocean_step(
         plan, band, even, ocean_in, drift, near, far, west_edge, east_edge, keep, sea
     )
     ocean = jnp.concatenate(new, axis=0)
     ocean_out[...] = ocean
-    total = total[:, :LANES] + total[:, LANES:]
-    moments = total[:columns, :] + total[columns:, :]
+    moments = total[:, :LANES] + total[:, LANES:]
     some = jnp.concatenate(some, axis=1)
     edges = some[2 * cols : 2 * cols + 2 * rows, :]
     fill_sections(plan, section, edges, ocean, moments, packed_out, sec_out, near_out)

time: 30.1 us -> 30 us (level)
  transfers between devices with their start and end apart: 15 -> 15, of which waited for: 5 -> 5; matrix products, arithmetic and copies ran while one was open for 0% -> 0% of each run, Pallas kernels for 9% -> 10%
where the time goes in v12:
time: 30 us; the launch traced here: 29.8 us
  starting transfers between devices  20.1 us (67%)
  Pallas kernels  6.64 us (22%)
  waiting for transfers between devices  2.22 us (7%)
  between operations  0.89 us (3%)
    ppermute x3, starting transfers between devices, exchange(): far_in = lax.ppermute(to_far, axes[0], others)  9.83 us
    pallas_call x13, Pallas kernels, call(): pl.pallas_call(functools.partial(kernel, plan, axes), out_shape=outs, in_...  6.64 us
    ppermute x3, starting transfers between devices, exchange(): from_x = lax.ppermute(to_x, both_axes, plan.crossing(1))  4.59 us
    ppermute x3, starting transfers between devices, exchange(): got = [lax.ppermute(to_mate, axes[0], pairs), from_y]  3.22 us
    ppermute x3, waiting for transfers between devices, exchange(): from_y = lax.ppermute(first, both_axes, plan.crossing(2))  1.98 us
    ppermute x3, starting transfers between devices, exchange(): from_y = lax.ppermute(first, both_axes, plan.crossing(2))  1.87 us
  transfers between devices with their start and end apart: 15, of which 5 were waited for; matrix products, arithmetic and copies ran while one was open for 0% of the time, Pallas kernels for 10%

profile of v12, /device:TPU:1, one launch (start us, length us, event | category | flops | bytes accessed | tf_op | source)
XLA Modules:
  0.0 29.8 jit_solution(467051879212484272)
XLA Ops:
  0.7 0.0 copy-start.1
  0.7 1.6 %shard_map.113 = (f32[4,24,768]{2,1,0:T(8,128)S(1)}, f32[96,128]{1,0:T(8,128)S(1)}, f32[96,128]{1,0:T(8,128)S(1)}, bf16[96,192]{1,0:T(8,128)(2,1)S(1)}, f32[80,1...) custom-call(f32[4,24,768]{2,1,0:T(8,128)} %refs_0_.2, f32[4,24,64]{2,1,0:T(8,128)} %refs_1_.2, ...), custom_call_target="tpu_custom_call" | custom-call | tf_op jit(solution)/shard_map/pallas_call | solution.py:611
  2.2 0.0 copy-start
  2.3 0.1 collective-permute-start.1
  2.4 2.6 %collective-permute-start = (f32[80,128]{1,0:T(8,128)S(1)}, f32[80,128]{1,0:T(8,128)S(1)}, u32[]{:S(2)}, u32[]{:S(2)}) collective-permute-start(f32[80,128]{1,0:T(8,128)S(1)} %get-tuple-element.46), channel_id=1, source_target_pairs={{0,9},{1,8},{2,11},{3,10},{4,13},{5,12},{6,15},{7,14},{8,1},{9,0},... | collective-permute-start | bytes 122888 | tf_op jit(solution)/shard_map/ppermute | solution.py:629
  5.0 3.5 %collective-permute-start.2 = (f32[24,512]{1,0:T(8,128)S(1)}, f32[24,512]{1,0:T(8,128)S(1)}, u32[]{:S(2)}, u32[]{:S(2)}) collective-permute-start(f32[24,512]{1,0:T(8,128)S(1)} %get-tuple-element.50), channel_id=1, source_target_pairs={{1,2},{2,1},{3,4},{4,3},{5,6},{6,5},{9,10},{10,9},{11,12},{12,11},... | collective-permute-start | bytes 147464 | tf_op jit(solution)/shard_map/ppermute | solution.py:630
  8.6 0.1 collective-permute-start.4
  8.6 1.6 %collective-permute-start.3 = (f32[40,128]{1,0:T(8,128)S(1)}, f32[40,128]{1,0:T(8,128)S(1)}, u32[]{:S(2)}, u32[]{:S(2)}) collective-permute-start(f32[40,128]{1,0:T(8,128)S(1)} %get-tuple-element.63), channel_id=1, source_target_pairs={{0,1},{1,0},{2,3},{3,2},{4,5},{5,4},{6,7},{7,6},{8,9},{9,8},{10,11... | collective-permute-start | bytes 61448 | tf_op jit(solution)/shard_map/ppermute | solution.py:643
  10.3 0.3 %shard_map.115 = (bf16[96,96]{1,0:T(8,128)(2,1)S(1)}, bf16[64,96]{1,0:T(8,128)(2,1)S(1)}, s32[8,128]{1,0:T(8,128)S(1)}, f32[96,128]{1,0:T(8,128)S(1)}, f32[8,128...) custom-call(f32[4,24]{1,0:T(4,128)S(1)} %copy-done.3, ...), custom_call_target="tpu_custom_call" | custom-call | tf_op jit(solution)/shard_map/pallas_call | solution.py:611
  10.6 0.6 %shard_map.116 = (f32[4,24,768]{2,1,0:T(8,128)S(1)}, f32[8,768]{1,0:T(8,128)S(1)}, f32[96,768]{1,0:T(8,128)S(1)}) custom-call(f32[4,24,768]{2,1,0:T(8,128)S(1)} %get-tuple-element.44.refs_0_, f32[96,128]{1,0:T(8,128)S(1)} %get-tuple-element.49.refs_1_, f32[8,768]{1,0:T(8,128)S(1)} %copy-done.1, f32[24,640]{1,0:T(8,128)S(1)} %collective-permute-done.1.near.refs_3_.refs_15_, ...), custom_call_target="tpu_custom_call" | custom-call | tf_op jit(solution)/shard_map/pallas_call | solution.py:611
  11.2 0.7 %collective-permute-done.4.refs_18_ = f32[64,128]{1,0:T(8,128)S(1)} collective-permute-done((f32[64,128]{1,0:T(8,128)S(1)}, f32[64,128]{1,0:T(8,128)S(1)}, u32[]{:S(2)}, u32[]{:S(2)}) %collective-permute-start.4) | collective-permute-done | bytes 32800 | tf_op jit(solution)/shard_map/ppermute | solution.py:642
  12.0 0.6 %shard_map.117 = (f32[96,128]{1,0:T(8,128)S(1)}, f32[96,128]{1,0:T(8,128)S(1)}, f32[96,128]{1,0:T(8,128)S(1)}, f32[8,768]{1,0:T(8,128)S(1)}, f32[24,512]{1,0:T(8...) custom-call(f32[4,24,768]{2,1,0:T(8,128)S(1)} %get-tuple-element.51.refs_0_, ...), custom_call_target="tpu_custom_call" | custom-call | tf_op jit(solution)/shard_map/pallas_call | solution.py:611
  12.6 0.1 collective-permute-start.6
  12.6 0.6 %collective-permute-start.5 = (f32[80,128]{1,0:T(8,128)S(1)}, f32[80,128]{1,0:T(8,128)S(1)}, u32[]{:S(2)}, u32[]{:S(2)}) collective-permute-start(f32[80,128]{1,0:T(8,128)S(1)} %get-tuple-element.67), channel_id=1, source_target_pairs={{0,9},{1,8},{2,11},{3,10},{4,13},{5,12},{6,15},{7,14},{8,1},{9,0},... | collective-permute-start | bytes 122888 | tf_op jit(solution)/shard_map/ppermute | solution.py:629
  13.3 3.2 %collective-permute-start.7 = (f32[24,512]{1,0:T(8,128)S(1)}, f32[24,512]{1,0:T(8,128)S(1)}, u32[]{:S(2)}, u32[]{:S(2)}) collective-permute-start(f32[24,512]{1,0:T(8,128)S(1)} %get-tuple-element.70), channel_id=1, source_target_pairs={{1,2},{2,1},{3,4},{4,3},{5,6},{6,5},{9,10},{10,9},{11,12},{12,11},... | collective-permute-start | bytes 147464 | tf_op jit(solution)/shard_map/ppermute | solution.py:630
  16.5 1.5 %collective-permute-start.9 = (f32[64,128]{1,0:T(8,128)S(1)}, f32[64,128]{1,0:T(8,128)S(1)}, u32[]{:S(2)}, u32[]{:S(2)}) collective-permute-start(f32[64,128]{1,0:T(8,128)S(1)} %get-tuple-element.69.refs_6_), channel_id=1, source_target_pairs={{0,17},{1,16},{2,19},{3,18},{4,21},{5,20},{6,23},{7,22},{8,25},{9,... | collective-permute-start | bytes 98312 | tf_op jit(solution)/shard_map/ppermute | solution.py:642
  17.9 0.2 collective-permute-start.8
  18.2 0.4 %shard_map.119.refs_0_ = f32[4,24,768]{2,1,0:T(8,128)S(1)} custom-call(f32[4,24,768]{2,1,0:T(8,128)S(1)} %get-tuple-element.51.refs_0_, f32[8,768]{1,0:T(8,128)S(1)} %get-tuple-element.64.refs_1_, f32[96,128]{1,0:T(8,128)S(1)} %get-tuple-element.65.refs_2_, bf16[96,96]{1,0:T(8,128)(2,1)S(1)} %get-tuple-element.66.refs_3_, ...), custom_call_target="tpu_custom_call" | custom-call | tf_op jit(solution)/shard_map/pallas_call | solution.py:611
  18.6 0.1 collective-permute-done.7.refs_4_.refs_16_
  18.7 0.6 %shard_map.120 = (f32[4,24,768]{2,1,0:T(8,128)S(1)}, f32[8,768]{1,0:T(8,128)S(1)}, f32[96,768]{1,0:T(8,128)S(1)}) custom-call(f32[4,24,768]{2,1,0:T(8,128)S(1)} %shard_map.119.refs_0_, f32[96,128]{1,0:T(8,128)S(1)} %get-tuple-element.49.refs_1_, f32[8,768]{1,0:T(8,128)S(1)} %copy-done.1, f32[24,640]{1,0:T(8,128)S(1)} %collective-permute-done.6.near.refs_3_.refs_15_, ...), custom_call_target="tpu_custom_call" | custom-call | tf_op jit(solution)/shard_map/pallas_call | solution.py:611
  19.3 0.6 %collective-permute-done.9.refs_18_ = f32[64,128]{1,0:T(8,128)S(1)} collective-permute-done((f32[64,128]{1,0:T(8,128)S(1)}, f32[64,128]{1,0:T(8,128)S(1)}, u32[]{:S(2)}, u32[]{:S(2)}) %collective-permute-start.9) | collective-permute-done | bytes 32800 | tf_op jit(solution)/shard_map/ppermute | solution.py:642
  19.9 0.6 %shard_map.121 = (f32[96,128]{1,0:T(8,128)S(1)}, f32[96,128]{1,0:T(8,128)S(1)}, f32[96,128]{1,0:T(8,128)S(1)}, f32[8,768]{1,0:T(8,128)S(1)}, f32[24,512]{1,0:T(8...) custom-call(f32[4,24,768]{2,1,0:T(8,128)S(1)} %get-tuple-element.71.refs_0_, ...), custom_call_target="tpu_custom_call" | custom-call | tf_op jit(solution)/shard_map/pallas_call | solution.py:611
  20.5 0.3 %collective-permute-start.11 = (f32[24,640]{1,0:T(8,128)S(1)}, f32[24,640]{1,0:T(8,128)S(1)}, u32[]{:S(2)}, u32[]{:S(2)}) collective-permute-start(f32[24,640]{1,0:T(8,128)S(1)} %get-tuple-element.80), channel_id=1, source_target_pairs={{0,1},{1,0},{2,3},{3,2},{4,5},{5,4},{6,7},{7,6},{8,9},{9,8},{10,11... | collective-permute-start | bytes 184328 | tf_op jit(solution)/shard_map/ppermute | solution.py:631
  20.8 1.3 %collective-permute-start.10 = (f32[80,128]{1,0:T(8,128)S(1)}, f32[80,128]{1,0:T(8,128)S(1)}, u32[]{:S(2)}, u32[]{:S(2)}) collective-permute-start(f32[80,128]{1,0:T(8,128)S(1)} %get-tuple-element.79), channel_id=1, source_target_pairs={{0,9},{1,8},{2,11},{3,10},{4,13},{5,12},{6,15},{7,14},{8,1},{9,0},... | collective-permute-start | bytes 122888 | tf_op jit(solution)/shard_map/ppermute | solution.py:629
  22.1 3.2 %collective-permute-start.12 = (f32[24,512]{1,0:T(8,128)S(1)}, f32[24,512]{1,0:T(8,128)S(1)}, u32[]{:S(2)}, u32[]{:S(2)}) collective-permute-start(f32[24,512]{1,0:T(8,128)S(1)} %get-tuple-element.82), channel_id=1, source_target_pairs={{1,2},{2,1},{3,4},{4,3},{5,6},{6,5},{9,10},{10,9},{11,12},{12,11},... | collective-permute-start | bytes 147464 | tf_op jit(solution)/shard_map/ppermute | solution.py:630
  25.3 0.3 %collective-permute-start.14 = (f32[64,128]{1,0:T(8,128)S(1)}, f32[64,128]{1,0:T(8,128)S(1)}, u32[]{:S(2)}, u32[]{:S(2)}) collective-permute-start(f32[64,128]{1,0:T(8,128)S(1)} %get-tuple-element.81.refs_6_), channel_id=1, source_target_pairs={{0,17},{1,16},{2,19},{3,18},{4,21},{5,20},{6,23},{7,22},{8,25},{9,... | collective-permute-start | bytes 98312 | tf_op jit(solution)/shard_map/ppermute | solution.py:642
  25.7 1.4 %collective-permute-start.13 = (f32[40,128]{1,0:T(8,128)S(1)}, f32[40,128]{1,0:T(8,128)S(1)}, u32[]{:S(2)}, u32[]{:S(2)}) collective-permute-start(f32[40,128]{1,0:T(8,128)S(1)} %get-tuple-element.85), channel_id=1, source_target_pairs={{0,1},{1,0},{2,3},{3,2},{4,5},{5,4},{6,7},{7,6},{8,9},{9,8},{10,11... | collective-permute-start | bytes 61448 | tf_op jit(solution)/shard_map/ppermute | solution.py:643
  27.0 0.4 %shard_map.123.refs_0_ = f32[4,24,768]{2,1,0:T(8,128)S(1)} custom-call(f32[4,24,768]{2,1,0:T(8,128)S(1)} %get-tuple-element.71.refs_0_, f32[8,768]{1,0:T(8,128)S(1)} %get-tuple-element.77.refs_1_, f32[96,128]{1,0:T(8,128)S(1)} %get-tuple-element.78.refs_2_, bf16[96,96]{1,0:T(8,128)(2,1)S(1)} %get-tuple-element.66.refs_3_, ...), custom_call_target="tpu_custom_call" | custom-call | tf_op jit(solution)/shard_map/pallas_call | solution.py:611
  27.4 0.1 collective-permute-done.12.refs_4_.refs_10_
  27.5 0.6 %shard_map.124.refs_0_ = f32[4,24,768]{2,1,0:T(8,128)S(1)} custom-call(f32[4,24,768]{2,1,0:T(8,128)S(1)} %shard_map.123.refs_0_, f32[96,128]{1,0:T(8,128)S(1)} %get-tuple-element.49.refs_1_, f32[8,768]{1,0:T(8,128)S(1)} %copy-done.1, f32[24,640]{1,0:T(8,128)S(1)} %collective-permute-done.11.near.refs_3_.refs_9_, ...), custom_call_target="tpu_custom_call" | custom-call | tf_op jit(solution)/shard_map/pallas_call | solution.py:611
  28.1 0.6 %collective-permute-done.14.refs_12_ = f32[64,128]{1,0:T(8,128)S(1)} collective-permute-done((f32[64,128]{1,0:T(8,128)S(1)}, f32[64,128]{1,0:T(8,128)S(1)}, u32[]{:S(2)}, u32[]{:S(2)}) %collective-permute-start.14) | collective-permute-done | bytes 32800 | tf_op jit(solution)/shard_map/ppermute | solution.py:642
  28.7 1.1 %shard_map.125 = (f32[4,24,768]{2,1,0:T(8,128)}, f32[4,24,64]{2,1,0:T(8,128)}) custom-call(f32[4,24,768]{2,1,0:T(8,128)S(1)} %shard_map.124.refs_0_, f32[96,128]{1,0:T(8,128)S(1)} %get-tuple-element.83.refs_1_, f32[96,128]{1,0:T(8,128)S(1)} %get-tuple-element.84.refs_2_, bf16[96,96]{1,0:T(8,128)(2,1)S(1)} %get-tuple-element.66.refs_3_, ...), custom_call_target="tpu_custom_call" | custom-call | tf_op jit(solution)/shard_map/pallas_call | solution.py:611
  (23 shorter events, 0.1 us)
Async XLA Ops:
  0.6 9.6 %copy-start.3 = (f32[4,24]{1,0:T(4,128)S(1)}, f32[4,24]{1,0:T(4,128)}, u32[]{:S(2)}) copy-start(f32[4,24]{1,0:T(4,128)} %refs_0_.3) | copy-start | bytes 1156
  0.6 9.6 %copy-start.4 = (s32[4,24]{1,0:T(4,128)S(1)}, s32[4,24]{1,0:T(4,128)}, u32[]{:S(2)}) copy-start(s32[4,24]{1,0:T(4,128)} %refs_2_.6) | copy-start | bytes 1156
  0.7 9.6 %copy-start.5 = (f32[32]{0:T(128)S(1)}, f32[32]{0:T(128)}, u32[]{:S(2)}) copy-start(f32[32]{0:T(128)} %refs_1_.3) | copy-start | bytes 388
  0.7 9.9 %copy-start.1 = (f32[8,768]{1,0:T(8,128)S(1)}, f32[8,768]{1,0:T(8,128)}, u32[]{:S(2)}) copy-start(f32[8,768]{1,0:T(8,128)} %constant.10.clone.refs_2_.refs_13_.refs_7_) | copy-start | bytes 73732
  2.2 9.7 %copy-start = (bf16[1536,128]{1,0:T(8,128)(2,1)S(1)}, bf16[1536,128]{1,0:T(8,128)(2,1)}, u32[]{:S(2)}) copy-start(bf16[1536,128]{1,0:T(8,128)(2,1)} %constant.11.clone.refs_14_.refs_5_.refs_8_) | copy-start | bytes 1179652
  2.3 6.3 %collective-permute-start.1 = (f32[24,640]{1,0:T(8,128)S(1)}, f32[24,640]{1,0:T(8,128)S(1)}, u32[]{:S(2)}, u32[]{:S(2)}) collective-permute-start(f32[24,640]{1,0:T(8,128)S(1)} %get-tuple-element.47), channel_id=1, source_target_pairs={{0,1},{1,0},{2,3},{3,2},{4,5},{5,4},{6,7},{7,6},{8,9},{9,8},{10,11... | collective-permute-start | bytes 184328 | tf_op jit(solution)/shard_map/ppermute | solution.py:631
  2.4 6.2 %collective-permute-start = (f32[80,128]{1,0:T(8,128)S(1)}, f32[80,128]{1,0:T(8,128)S(1)}, u32[]{:S(2)}, u32[]{:S(2)}) collective-permute-start(f32[80,128]{1,0:T(8,128)S(1)} %get-tuple-element.46), channel_id=1, source_target_pairs={{0,9},{1,8},{2,11},{3,10},{4,13},{5,12},{6,15},{7,14},{8,1},{9,0},... | collective-permute-start | bytes 122888 | tf_op jit(solution)/shard_map/ppermute | solution.py:629
  5.0 5.6 %collective-permute-start.2 = (f32[24,512]{1,0:T(8,128)S(1)}, f32[24,512]{1,0:T(8,128)S(1)}, u32[]{:S(2)}, u32[]{:S(2)}) collective-permute-start(f32[24,512]{1,0:T(8,128)S(1)} %get-tuple-element.50), channel_id=1, source_target_pairs={{1,2},{2,1},{3,4},{4,3},{5,6},{6,5},{9,10},{10,9},{11,12},{12,11},... | collective-permute-start | bytes 147464 | tf_op jit(solution)/shard_map/ppermute | solution.py:630
  8.6 3.4 %collective-permute-start.4 = (f32[64,128]{1,0:T(8,128)S(1)}, f32[64,128]{1,0:T(8,128)S(1)}, u32[]{:S(2)}, u32[]{:S(2)}) collective-permute-start(f32[64,128]{1,0:T(8,128)S(1)} %get-tuple-element.48.refs_4_), channel_id=1, source_target_pairs={{0,17},{1,16},{2,19},{3,18},{4,21},{5,20},{6,23},{7,22},{8,25},{9,... | collective-permute-start | bytes 98312 | tf_op jit(solution)/shard_map/ppermute | solution.py:642
  8.6 2.6 %collective-permute-start.3 = (f32[40,128]{1,0:T(8,128)S(1)}, f32[40,128]{1,0:T(8,128)S(1)}, u32[]{:S(2)}, u32[]{:S(2)}) collective-permute-start(f32[40,128]{1,0:T(8,128)S(1)} %get-tuple-element.63), channel_id=1, source_target_pairs={{0,1},{1,0},{2,3},{3,2},{4,5},{5,4},{6,7},{7,6},{8,9},{9,8},{10,11... | collective-permute-start | bytes 61448 | tf_op jit(solution)/shard_map/ppermute | solution.py:643
  10.6 1.4 %copy-start.2 = (bf16[384,256]{1,0:T(8,128)(2,1)S(1)}, bf16[384,256]{1,0:T(8,128)(2,1)}, u32[]{:S(2)}) copy-start(bf16[384,256]{1,0:T(8,128)(2,1)} %constant.9.clone.refs_12_) | copy-start | bytes 589828
  12.6 3.9 %collective-permute-start.6 = (f32[24,640]{1,0:T(8,128)S(1)}, f32[24,640]{1,0:T(8,128)S(1)}, u32[]{:S(2)}, u32[]{:S(2)}) collective-permute-start(f32[24,640]{1,0:T(8,128)S(1)} %get-tuple-element.68), channel_id=1, source_target_pairs={{0,1},{1,0},{2,3},{3,2},{4,5},{5,4},{6,7},{7,6},{8,9},{9,8},{10,11... | collective-permute-start | bytes 184328 | tf_op jit(solution)/shard_map/ppermute | solution.py:631
  12.6 3.8 %collective-permute-start.5 = (f32[80,128]{1,0:T(8,128)S(1)}, f32[80,128]{1,0:T(8,128)S(1)}, u32[]{:S(2)}, u32[]{:S(2)}) collective-permute-start(f32[80,128]{1,0:T(8,128)S(1)} %get-tuple-element.67), channel_id=1, source_target_pairs={{0,9},{1,8},{2,11},{3,10},{4,13},{5,12},{6,15},{7,14},{8,1},{9,0},... | collective-permute-start | bytes 122888 | tf_op jit(solution)/shard_map/ppermute | solution.py:629
  13.3 5.4 %collective-permute-start.7 = (f32[24,512]{1,0:T(8,128)S(1)}, f32[24,512]{1,0:T(8,128)S(1)}, u32[]{:S(2)}, u32[]{:S(2)}) collective-permute-start(f32[24,512]{1,0:T(8,128)S(1)} %get-tuple-element.70), channel_id=1, source_target_pairs={{1,2},{2,1},{3,4},{4,3},{5,6},{6,5},{9,10},{10,9},{11,12},{12,11},... | collective-permute-start | bytes 147464 | tf_op jit(solution)/shard_map/ppermute | solution.py:630
  16.5 3.4 %collective-permute-start.9 = (f32[64,128]{1,0:T(8,128)S(1)}, f32[64,128]{1,0:T(8,128)S(1)}, u32[]{:S(2)}, u32[]{:S(2)}) collective-permute-start(f32[64,128]{1,0:T(8,128)S(1)} %get-tuple-element.69.refs_6_), channel_id=1, source_target_pairs={{0,17},{1,16},{2,19},{3,18},{4,21},{5,20},{6,23},{7,22},{8,25},{9,... | collective-permute-start | bytes 98312 | tf_op jit(solution)/shard_map/ppermute | solution.py:642
  17.9 1.3 %collective-permute-start.8 = (f32[40,128]{1,0:T(8,128)S(1)}, f32[40,128]{1,0:T(8,128)S(1)}, u32[]{:S(2)}, u32[]{:S(2)}) collective-permute-start(f32[40,128]{1,0:T(8,128)S(1)} %get-tuple-element.76), channel_id=1, source_target_pairs={{0,1},{1,0},{2,3},{3,2},{4,5},{5,4},{6,7},{7,6},{8,9},{9,8},{10,11... | collective-permute-start | bytes 61448 | tf_op jit(solution)/shard_map/ppermute | solution.py:643
  20.5 4.8 %collective-permute-start.11 = (f32[24,640]{1,0:T(8,128)S(1)}, f32[24,640]{1,0:T(8,128)S(1)}, u32[]{:S(2)}, u32[]{:S(2)}) collective-permute-start(f32[24,640]{1,0:T(8,128)S(1)} %get-tuple-element.80), channel_id=1, source_target_pairs={{0,1},{1,0},{2,3},{3,2},{4,5},{5,4},{6,7},{7,6},{8,9},{9,8},{10,11... | collective-permute-start | bytes 184328 | tf_op jit(solution)/shard_map/ppermute | solution.py:631
  20.8 4.5 %collective-permute-start.10 = (f32[80,128]{1,0:T(8,128)S(1)}, f32[80,128]{1,0:T(8,128)S(1)}, u32[]{:S(2)}, u32[]{:S(2)}) collective-permute-start(f32[80,128]{1,0:T(8,128)S(1)} %get-tuple-element.79), channel_id=1, source_target_pairs={{0,9},{1,8},{2,11},{3,10},{4,13},{5,12},{6,15},{7,14},{8,1},{9,0},... | collective-permute-start | bytes 122888 | tf_op jit(solution)/shard_map/ppermute | solution.py:629
  22.1 5.4 %collective-permute-start.12 = (f32[24,512]{1,0:T(8,128)S(1)}, f32[24,512]{1,0:T(8,128)S(1)}, u32[]{:S(2)}, u32[]{:S(2)}) collective-permute-start(f32[24,512]{1,0:T(8,128)S(1)} %get-tuple-element.82), channel_id=1, source_target_pairs={{1,2},{2,1},{3,4},{4,3},{5,6},{6,5},{9,10},{10,9},{11,12},{12,11},... | collective-permute-start | bytes 147464 | tf_op jit(solution)/shard_map/ppermute | solution.py:630
  25.3 3.4 %collective-permute-start.14 = (f32[64,128]{1,0:T(8,128)S(1)}, f32[64,128]{1,0:T(8,128)S(1)}, u32[]{:S(2)}, u32[]{:S(2)}) collective-permute-start(f32[64,128]{1,0:T(8,128)S(1)} %get-tuple-element.81.refs_6_), channel_id=1, source_target_pairs={{0,17},{1,16},{2,19},{3,18},{4,21},{5,20},{6,23},{7,22},{8,25},{9,... | collective-permute-start | bytes 98312 | tf_op jit(solution)/shard_map/ppermute | solution.py:642
  25.7 2.4 %collective-permute-start.13 = (f32[40,128]{1,0:T(8,128)S(1)}, f32[40,128]{1,0:T(8,128)S(1)}, u32[]{:S(2)}, u32[]{:S(2)}) collective-permute-start(f32[40,128]{1,0:T(8,128)S(1)} %get-tuple-element.85), channel_id=1, source_target_pairs={{0,1},{1,0},{2,3},{3,2},{4,5},{5,4},{6,7},{7,6},{8,9},{9,8},{10,11... | collective-permute-start | bytes 61448 | tf_op jit(solution)/shard_map/ppermute | solution.py:643

commit v13 on v12

--- a/solution.py
+++ b/solution.py
@@ -86,10 +86,14 @@
         ]
         self.edges = [any(abs(target - i) == 1 for i, target in table) for table in self.direct]
         self.sizes = [self.chunk + (self.edge if edge else 0) for edge in self.edges]
+        near_rows = cols * (spectral // 2 + LANES + depth) // LANES
+        self.x_rows = max(2 * (self.chunk + self.edge), (near_rows + 8) // 8 * 8)
         if self.relay:
-            self.sizes = [2 * (self.chunk + self.edge)] + self.sizes
-        self.row_lanes = slice(spectral // 2, spectral // 2 + LANES)
-        self.chunk_lanes = slice(spectral // 2 + LANES, spectral // 2 + 2 * LANES)
+            self.sizes = [self.x_rows] + self.sizes
+        start = spectral // 2
+        self.far_lanes = slice(start, start + depth)
+        self.chunk_lanes = slice(start, start + LANES)
+        self.near_lanes = slice(start + LANES, start + LANES + depth)
 
     def crossing(self, flip):
         bands = self.bands
@@ -175,20 +179,24 @@
     return jnp.where(keep, first, pltpu.roll(second, NDIR // 2, 1))
 
 
-def fill_band(plan, northward, edge, sea_row, out):
+def fill_band(plan, northward, edge, sea_row, out, lanes):
     half = plan.tiles // 2
     masks = Directions((plan.cols, LANES))
     for tile in range(half):
         out[:, tile * LANES : (tile + 1) * LANES] = packed_half(
             edge, tile, half, masks.northward, northward
         )
-    out[:, plan.row_lanes] = sea_row
+    out[:, lanes] = sea_row[:, : plan.depth]
 
 
 def fill_bands(plan, even, edges, sea_rows, far, near):
-    for out, northward in ((far, jnp.logical_not(even)), (near, even)):
+    for out, northward, lanes in (
+        (far, jnp.logical_not(even), plan.far_lanes),
+        (near, even, plan.near_lanes),
+    ):
         edge = jnp.where(northward, edges[1], edges[0])
-        fill_band(plan, northward, edge, jnp.where(northward, sea_rows[1], sea_rows[0]), out)
+        sea_row = jnp.where(northward, sea_rows[1], sea_rows[0])
+        fill_band(plan, northward, edge, sea_row, out, lanes)
 
 
 def fill_sections(plan, section, edges, ocean, ordered, packed_out, sec_out, near):
@@ -197,6 +205,9 @@
     packed_out[...] = jnp.where(lane < LANES // 2, ocean, ordered)
     sea_rows = ocean.reshape(rows, cols, LANES)
     masks = Directions((rows, LANES))
+    if plan.relay:
+        used = 2 * (chunk + plan.edge)
+        sec_out[0][used:, :] = jnp.zeros((plan.x_rows - used, LANES), F32)
     for target, out, at, lanes, edge_at in plan.sent(section, sec_out, near):
         part = packed_out[pl.ds(pl.multiple_of(target * chunk, 8), chunk), :]
         out[at : at + chunk, lanes] = part
@@ -252,9 +263,10 @@
     zonal = lane_of(block) < plan.depth
     place = lax.broadcasted_iota(jnp.int32, block, 0)
     at_west, at_east = place == 0, place == cols - 1
-    lanes = plan.row_lanes
-    south_edge = jnp.where(even, far[:, lanes], near[:, lanes])
-    north_edge = jnp.where(even, near[:, lanes], far[:, lanes])
+    blank = jnp.zeros((cols, LANES - plan.depth), F32)
+    far = jnp.concatenate([far[:, plan.far_lanes], blank], axis=1)
+    near = jnp.concatenate([near[:, plan.near_lanes], blank], axis=1)
+    south_edge, north_edge = jnp.where(even, far, near), jnp.where(even, near, far)
     new = []
     for row in range(rows):
         flat = slice(row * cols, (row + 1) * cols)
@@ -310,7 +322,7 @@
 def relay_kernel(plan, axes, from_x, near, to_y, to_mate):
     own = plan.chunk + plan.edge
     to_y[0 : plan.chunk, :] = near[0 : plan.chunk, plan.chunk_lanes]
-    to_y[plan.chunk :, :] = from_x[own:, :]
+    to_y[plan.chunk :, :] = from_x[own : 2 * own, :]
     to_mate[...] = from_x[:own, :]
 
 
@@ -598,8 +610,8 @@
     shape = jax.ShapeDtypeStruct
     params = pltpu.CompilerParams(vmem_limit_bytes=32 * 1024 * 1024)
     to_sections = [shape((size, LANES), F32) for size in plan.sizes]
-    to_far = shape((cols, plan.row_lanes.stop), F32)
-    to_near = shape((cols, plan.chunk_lanes.stop), F32)
+    to_far = shape((cols, plan.far_lanes.stop), F32)
+    to_near = shape((cols, plan.near_lanes.stop), F32)
     state = shape((columns, LANES), F32)
     field = shape(spectra.shape, F32)
     at_edges = shape((2 * rows, LANES), F32)

time: 30 us -> 29.9 us (level)
    ppermute x3, starting transfers between devices: 1.87 us -> 0.63 us  [exchange(): from_y = lax.ppermute(first, both_axes, plan.crossing(2))]
    ppermute x3, starting transfers between devices: 3.22 us -> 4.46 us  [exchange(): got = [lax.ppermute(to_mate, axes[0], pairs), from_y]]
    ppermute x3, starting transfers between devices: 4.59 us -> 3.93 us  [exchange(): from_x = lax.ppermute(to_x, both_axes, plan.crossing(1))]
    ppermute x3, starting transfers between devices: 0.53 us -> 0.84 us  [exchange(): near_in = lax.ppermute(to_near, axes[0], pairs)]
  transfers between devices with their start and end apart: 15 -> 15, of which waited for: 5 -> 4; matrix products, arithmetic and copies ran while one was open for 0% -> 0% of each run, Pallas kernels for 10% -> 10%
where the time goes in v13:
time: 29.9 us; the launch traced here: 29.7 us
  starting transfers between devices  19.9 us (67%)
  Pallas kernels  6.66 us (22%)
  waiting for transfers between devices  2.2 us (7%)
  between operations  0.89 us (3%)
    ppermute x3, starting transfers between devices, exchange(): far_in = lax.ppermute(to_far, axes[0], others)  10 us
    pallas_call x13, Pallas kernels, call(): pl.pallas_call(functools.partial(kernel, plan, axes), out_shape=outs, in_...  6.66 us
    ppermute x3, starting transfers between devices, exchange(): got = [lax.ppermute(to_mate, axes[0], pairs), from_y]  4.46 us
    ppermute x3, starting transfers between devices, exchange(): from_x = lax.ppermute(to_x, both_axes, plan.crossing(1))  3.93 us
    ppermute x3, waiting for transfers between devices, exchange(): from_y = lax.ppermute(first, both_axes, plan.crossing(2))  1.7 us
    ppermute x3, starting transfers between devices, exchange(): near_in = lax.ppermute(to_near, axes[0], pairs)  0.84 us
    ppermute x3, starting transfers between devices, exchange(): from_y = lax.ppermute(first, both_axes, plan.crossing(2))  0.63 us
  transfers between devices with their start and end apart: 15, of which 4 were waited for; matrix products, arithmetic and copies ran while one was open for 0% of the time, Pallas kernels for 10%

profile of v13, /device:TPU:1, one launch (start us, length us, event | category | flops | bytes accessed | tf_op | source)
XLA Modules:
  0.0 29.7 jit_solution(16513623986118941192)
XLA Ops:
  0.7 0.0 copy-start.1
  0.7 1.6 %shard_map.113 = (f32[4,24,768]{2,1,0:T(8,128)S(1)}, f32[96,128]{1,0:T(8,128)S(1)}, f32[96,128]{1,0:T(8,128)S(1)}, bf16[96,192]{1,0:T(8,128)(2,1)S(1)}, f32[104,...) custom-call(f32[4,24,768]{2,1,0:T(8,128)} %refs_0_.2, f32[4,24,64]{2,1,0:T(8,128)} %refs_1_.2, ...), custom_call_target="tpu_custom_call" | custom-call | tf_op jit(solution)/shard_map/pallas_call | solution.py:623
  2.2 0.0 copy-start
  2.2 2.7 %collective-permute-start = (f32[104,128]{1,0:T(8,128)S(1)}, f32[104,128]{1,0:T(8,128)S(1)}, u32[]{:S(2)}, u32[]{:S(2)}) collective-permute-start(f32[104,128]{1,0:T(8,128)S(1)} %get-tuple-element.46), channel_id=1, source_target_pairs={{0,9},{1,8},{2,11},{3,10},{4,13},{5,12},{6,15},{7,14},{8,1},{9,0},... | collective-permute-start | bytes 159752 | tf_op jit(solution)/shard_map/ppermute | solution.py:641
  4.9 0.0 collective-permute-start.1
  4.9 3.6 %collective-permute-start.2 = (f32[24,416]{1,0:T(8,128)S(1)}, f32[24,416]{1,0:T(8,128)S(1)}, u32[]{:S(2)}, u32[]{:S(2)}) collective-permute-start(f32[24,416]{1,0:T(8,128)S(1)} %get-tuple-element.50), channel_id=1, source_target_pairs={{1,2},{2,1},{3,4},{4,3},{5,6},{6,5},{9,10},{10,9},{11,12},{12,11},... | collective-permute-start | bytes 119816 | tf_op jit(solution)/shard_map/ppermute | solution.py:642
  8.5 0.5 %collective-permute-start.4 = (f32[64,128]{1,0:T(8,128)S(1)}, f32[64,128]{1,0:T(8,128)S(1)}, u32[]{:S(2)}, u32[]{:S(2)}) collective-permute-start(f32[64,128]{1,0:T(8,128)S(1)} %get-tuple-element.48.refs_4_), channel_id=1, source_target_pairs={{0,17},{1,16},{2,19},{3,18},{4,21},{5,20},{6,23},{7,22},{8,25},{9,... | collective-permute-start | bytes 98312 | tf_op jit(solution)/shard_map/ppermute | solution.py:654
  9.0 1.2 %collective-permute-start.3 = (f32[40,128]{1,0:T(8,128)S(1)}, f32[40,128]{1,0:T(8,128)S(1)}, u32[]{:S(2)}, u32[]{:S(2)}) collective-permute-start(f32[40,128]{1,0:T(8,128)S(1)} %get-tuple-element.63), channel_id=1, source_target_pairs={{0,1},{1,0},{2,3},{3,2},{4,5},{5,4},{6,7},{7,6},{8,9},{9,8},{10,11... | collective-permute-start | bytes 61448 | tf_op jit(solution)/shard_map/ppermute | solution.py:655
  10.3 0.3 %shard_map.115 = (bf16[96,96]{1,0:T(8,128)(2,1)S(1)}, bf16[64,96]{1,0:T(8,128)(2,1)S(1)}, s32[8,128]{1,0:T(8,128)S(1)}, f32[96,128]{1,0:T(8,128)S(1)}, f32[8,128...) custom-call(f32[4,24]{1,0:T(4,128)S(1)} %copy-done.3, ...), custom_call_target="tpu_custom_call" | custom-call | tf_op jit(solution)/shard_map/pallas_call | solution.py:623
  10.6 0.0 copy-start.2
  10.6 0.6 %shard_map.116 = (f32[4,24,768]{2,1,0:T(8,128)S(1)}, f32[8,768]{1,0:T(8,128)S(1)}, f32[96,768]{1,0:T(8,128)S(1)}) custom-call(f32[4,24,768]{2,1,0:T(8,128)S(1)} %get-tuple-element.44.refs_0_, f32[96,128]{1,0:T(8,128)S(1)} %get-tuple-element.49.refs_1_, f32[8,768]{1,0:T(8,128)S(1)} %copy-done.1, f32[24,544]{1,0:T(8,128)S(1)} %collective-permute-done.1.near.refs_3_.refs_15_, ...), custom_call_target="tpu_custom_call" | custom-call | tf_op jit(solution)/shard_map/pallas_call | solution.py:623
  11.2 0.7 %collective-permute-done.4.refs_18_ = f32[64,128]{1,0:T(8,128)S(1)} collective-permute-done((f32[64,128]{1,0:T(8,128)S(1)}, f32[64,128]{1,0:T(8,128)S(1)}, u32[]{:S(2)}, u32[]{:S(2)}) %collective-permute-start.4) | collective-permute-done | bytes 32800 | tf_op jit(solution)/shard_map/ppermute | solution.py:654
  12.0 0.6 %shard_map.117 = (f32[96,128]{1,0:T(8,128)S(1)}, f32[96,128]{1,0:T(8,128)S(1)}, f32[96,128]{1,0:T(8,128)S(1)}, f32[8,768]{1,0:T(8,128)S(1)}, f32[24,416]{1,0:T(8...) custom-call(f32[4,24,768]{2,1,0:T(8,128)S(1)} %get-tuple-element.51.refs_0_, ...), custom_call_target="tpu_custom_call" | custom-call | tf_op jit(solution)/shard_map/pallas_call | solution.py:623
  12.5 0.5 %collective-permute-start.5 = (f32[104,128]{1,0:T(8,128)S(1)}, f32[104,128]{1,0:T(8,128)S(1)}, u32[]{:S(2)}, u32[]{:S(2)}) collective-permute-start(f32[104,128]{1,0:T(8,128)S(1)} %get-tuple-element.67), channel_id=1, source_target_pairs={{0,9},{1,8},{2,11},{3,10},{4,13},{5,12},{6,15},{7,14},{8,1},{9,0},... | collective-permute-start | bytes 159752 | tf_op jit(solution)/shard_map/ppermute | solution.py:641
  13.0 0.2 collective-permute-start.6
  13.3 3.4 %collective-permute-start.7 = (f32[24,416]{1,0:T(8,128)S(1)}, f32[24,416]{1,0:T(8,128)S(1)}, u32[]{:S(2)}, u32[]{:S(2)}) collective-permute-start(f32[24,416]{1,0:T(8,128)S(1)} %get-tuple-element.70), channel_id=1, source_target_pairs={{1,2},{2,1},{3,4},{4,3},{5,6},{6,5},{9,10},{10,9},{11,12},{12,11},... | collective-permute-start | bytes 119816 | tf_op jit(solution)/shard_map/ppermute | solution.py:642
  16.7 0.1 collective-permute-start.9
  16.7 1.6 %collective-permute-start.8 = (f32[40,128]{1,0:T(8,128)S(1)}, f32[40,128]{1,0:T(8,128)S(1)}, u32[]{:S(2)}, u32[]{:S(2)}) collective-permute-start(f32[40,128]{1,0:T(8,128)S(1)} %get-tuple-element.76), channel_id=1, source_target_pairs={{0,1},{1,0},{2,3},{3,2},{4,5},{5,4},{6,7},{7,6},{8,9},{9,8},{10,11... | collective-permute-start | bytes 61448 | tf_op jit(solution)/shard_map/ppermute | solution.py:655
  18.4 0.4 %shard_map.119.refs_0_ = f32[4,24,768]{2,1,0:T(8,128)S(1)} custom-call(f32[4,24,768]{2,1,0:T(8,128)S(1)} %get-tuple-element.51.refs_0_, f32[8,768]{1,0:T(8,128)S(1)} %get-tuple-element.64.refs_1_, f32[96,128]{1,0:T(8,128)S(1)} %get-tuple-element.65.refs_2_, bf16[96,96]{1,0:T(8,128)(2,1)S(1)} %get-tuple-element.66.refs_3_, ...), custom_call_target="tpu_custom_call" | custom-call | tf_op jit(solution)/shard_map/pallas_call | solution.py:623
  18.8 0.6 %shard_map.120 = (f32[4,24,768]{2,1,0:T(8,128)S(1)}, f32[8,768]{1,0:T(8,128)S(1)}, f32[96,768]{1,0:T(8,128)S(1)}) custom-call(f32[4,24,768]{2,1,0:T(8,128)S(1)} %shard_map.119.refs_0_, f32[96,128]{1,0:T(8,128)S(1)} %get-tuple-element.49.refs_1_, f32[8,768]{1,0:T(8,128)S(1)} %copy-done.1, f32[24,544]{1,0:T(8,128)S(1)} %collective-permute-done.6.near.refs_3_.refs_15_, ...), custom_call_target="tpu_custom_call" | custom-call | tf_op jit(solution)/shard_map/pallas_call | solution.py:623
  19.4 0.7 %collective-permute-done.9.refs_18_ = f32[64,128]{1,0:T(8,128)S(1)} collective-permute-done((f32[64,128]{1,0:T(8,128)S(1)}, f32[64,128]{1,0:T(8,128)S(1)}, u32[]{:S(2)}, u32[]{:S(2)}) %collective-permute-start.9) | collective-permute-done | bytes 32800 | tf_op jit(solution)/shard_map/ppermute | solution.py:654
  20.1 0.6 %shard_map.121 = (f32[96,128]{1,0:T(8,128)S(1)}, f32[96,128]{1,0:T(8,128)S(1)}, f32[96,128]{1,0:T(8,128)S(1)}, f32[8,768]{1,0:T(8,128)S(1)}, f32[24,416]{1,0:T(8...) custom-call(f32[4,24,768]{2,1,0:T(8,128)S(1)} %get-tuple-element.71.refs_0_, ...), custom_call_target="tpu_custom_call" | custom-call | tf_op jit(solution)/shard_map/pallas_call | solution.py:623
  20.7 0.8 %collective-permute-start.10 = (f32[104,128]{1,0:T(8,128)S(1)}, f32[104,128]{1,0:T(8,128)S(1)}, u32[]{:S(2)}, u32[]{:S(2)}) collective-permute-start(f32[104,128]{1,0:T(8,128)S(1)} %get-tuple-element.79), channel_id=1, source_target_pairs={{0,9},{1,8},{2,11},{3,10},{4,13},{5,12},{6,15},{7,14},{8,1},{9,0},... | collective-permute-start | bytes 159752 | tf_op jit(solution)/shard_map/ppermute | solution.py:641
  21.4 0.6 %collective-permute-start.11 = (f32[24,544]{1,0:T(8,128)S(1)}, f32[24,544]{1,0:T(8,128)S(1)}, u32[]{:S(2)}, u32[]{:S(2)}) collective-permute-start(f32[24,544]{1,0:T(8,128)S(1)} %get-tuple-element.80), channel_id=1, source_target_pairs={{0,1},{1,0},{2,3},{3,2},{4,5},{5,4},{6,7},{7,6},{8,9},{9,8},{10,11... | collective-permute-start | bytes 156680 | tf_op jit(solution)/shard_map/ppermute | solution.py:643
  22.0 3.1 %collective-permute-start.12 = (f32[24,416]{1,0:T(8,128)S(1)}, f32[24,416]{1,0:T(8,128)S(1)}, u32[]{:S(2)}, u32[]{:S(2)}) collective-permute-start(f32[24,416]{1,0:T(8,128)S(1)} %get-tuple-element.82), channel_id=1, source_target_pairs={{1,2},{2,1},{3,4},{4,3},{5,6},{6,5},{9,10},{10,9},{11,12},{12,11},... | collective-permute-start | bytes 119816 | tf_op jit(solution)/shard_map/ppermute | solution.py:642
  25.2 0.1 collective-permute-start.14
  25.2 1.6 %collective-permute-start.13 = (f32[40,128]{1,0:T(8,128)S(1)}, f32[40,128]{1,0:T(8,128)S(1)}, u32[]{:S(2)}, u32[]{:S(2)}) collective-permute-start(f32[40,128]{1,0:T(8,128)S(1)} %get-tuple-element.85), channel_id=1, source_target_pairs={{0,1},{1,0},{2,3},{3,2},{4,5},{5,4},{6,7},{7,6},{8,9},{9,8},{10,11... | collective-permute-start | bytes 61448 | tf_op jit(solution)/shard_map/ppermute | solution.py:655
  26.9 0.4 %shard_map.123.refs_0_ = f32[4,24,768]{2,1,0:T(8,128)S(1)} custom-call(f32[4,24,768]{2,1,0:T(8,128)S(1)} %get-tuple-element.71.refs_0_, f32[8,768]{1,0:T(8,128)S(1)} %get-tuple-element.77.refs_1_, f32[96,128]{1,0:T(8,128)S(1)} %get-tuple-element.78.refs_2_, bf16[96,96]{1,0:T(8,128)(2,1)S(1)} %get-tuple-element.66.refs_3_, ...), custom_call_target="tpu_custom_call" | custom-call | tf_op jit(solution)/shard_map/pallas_call | solution.py:623
  27.3 0.5 %collective-permute-done.12.refs_4_.refs_10_ = f32[24,416]{1,0:T(8,128)S(1)} collective-permute-done((f32[24,416]{1,0:T(8,128)S(1)}, f32[24,416]{1,0:T(8,128)S(1)}, u32[]{:S(2)}, u32[]{:S(2)}) %collective-permute-start.12) | collective-permute-done | bytes 39968 | tf_op jit(solution)/shard_map/ppermute | solution.py:642
  27.7 0.6 %shard_map.124.refs_0_ = f32[4,24,768]{2,1,0:T(8,128)S(1)} custom-call(f32[4,24,768]{2,1,0:T(8,128)S(1)} %shard_map.123.refs_0_, f32[96,128]{1,0:T(8,128)S(1)} %get-tuple-element.49.refs_1_, f32[8,768]{1,0:T(8,128)S(1)} %copy-done.1, f32[24,544]{1,0:T(8,128)S(1)} %collective-permute-done.11.near.refs_3_.refs_9_, ...), custom_call_target="tpu_custom_call" | custom-call | tf_op jit(solution)/shard_map/pallas_call | solution.py:623
  28.3 0.2 collective-permute-done.14.refs_12_
  28.6 1.1 %shard_map.125 = (f32[4,24,768]{2,1,0:T(8,128)}, f32[4,24,64]{2,1,0:T(8,128)}) custom-call(f32[4,24,768]{2,1,0:T(8,128)S(1)} %shard_map.124.refs_0_, f32[96,128]{1,0:T(8,128)S(1)} %get-tuple-element.83.refs_1_, f32[96,128]{1,0:T(8,128)S(1)} %get-tuple-element.84.refs_2_, bf16[96,96]{1,0:T(8,128)(2,1)S(1)} %get-tuple-element.66.refs_3_, ...), custom_call_target="tpu_custom_call" | custom-call | tf_op jit(solution)/shard_map/pallas_call | solution.py:623
  (23 shorter events, 0.1 us)
Async XLA Ops:
  0.6 9.6 %copy-start.3 = (f32[4,24]{1,0:T(4,128)S(1)}, f32[4,24]{1,0:T(4,128)}, u32[]{:S(2)}) copy-start(f32[4,24]{1,0:T(4,128)} %refs_0_.3) | copy-start | bytes 1156
  0.6 9.6 %copy-start.4 = (s32[4,24]{1,0:T(4,128)S(1)}, s32[4,24]{1,0:T(4,128)}, u32[]{:S(2)}) copy-start(s32[4,24]{1,0:T(4,128)} %refs_2_.6) | copy-start | bytes 1156
  0.7 9.6 %copy-start.5 = (f32[32]{0:T(128)S(1)}, f32[32]{0:T(128)}, u32[]{:S(2)}) copy-start(f32[32]{0:T(128)} %refs_1_.3) | copy-start | bytes 388
  0.7 9.9 %copy-start.1 = (f32[8,768]{1,0:T(8,128)S(1)}, f32[8,768]{1,0:T(8,128)}, u32[]{:S(2)}) copy-start(f32[8,768]{1,0:T(8,128)} %constant.10.clone.refs_2_.refs_13_.refs_7_) | copy-start | bytes 73732
  2.2 9.7 %copy-start = (bf16[1536,128]{1,0:T(8,128)(2,1)S(1)}, bf16[1536,128]{1,0:T(8,128)(2,1)}, u32[]{:S(2)}) copy-start(bf16[1536,128]{1,0:T(8,128)(2,1)} %constant.11.clone.refs_14_.refs_5_.refs_8_) | copy-start | bytes 1179652
  2.2 6.3 %collective-permute-start = (f32[104,128]{1,0:T(8,128)S(1)}, f32[104,128]{1,0:T(8,128)S(1)}, u32[]{:S(2)}, u32[]{:S(2)}) collective-permute-start(f32[104,128]{1,0:T(8,128)S(1)} %get-tuple-element.46), channel_id=1, source_target_pairs={{0,9},{1,8},{2,11},{3,10},{4,13},{5,12},{6,15},{7,14},{8,1},{9,0},... | collective-permute-start | bytes 159752 | tf_op jit(solution)/shard_map/ppermute | solution.py:641
  4.9 3.6 %collective-permute-start.1 = (f32[24,544]{1,0:T(8,128)S(1)}, f32[24,544]{1,0:T(8,128)S(1)}, u32[]{:S(2)}, u32[]{:S(2)}) collective-permute-start(f32[24,544]{1,0:T(8,128)S(1)} %get-tuple-element.47), channel_id=1, source_target_pairs={{0,1},{1,0},{2,3},{3,2},{4,5},{5,4},{6,7},{7,6},{8,9},{9,8},{10,11... | collective-permute-start | bytes 156680 | tf_op jit(solution)/shard_map/ppermute | solution.py:643
  4.9 5.7 %collective-permute-start.2 = (f32[24,416]{1,0:T(8,128)S(1)}, f32[24,416]{1,0:T(8,128)S(1)}, u32[]{:S(2)}, u32[]{:S(2)}) collective-permute-start(f32[24,416]{1,0:T(8,128)S(1)} %get-tuple-element.50), channel_id=1, source_target_pairs={{1,2},{2,1},{3,4},{4,3},{5,6},{6,5},{9,10},{10,9},{11,12},{12,11},... | collective-permute-start | bytes 119816 | tf_op jit(solution)/shard_map/ppermute | solution.py:642
  8.5 3.4 %collective-permute-start.4 = (f32[64,128]{1,0:T(8,128)S(1)}, f32[64,128]{1,0:T(8,128)S(1)}, u32[]{:S(2)}, u32[]{:S(2)}) collective-permute-start(f32[64,128]{1,0:T(8,128)S(1)} %get-tuple-element.48.refs_4_), channel_id=1, source_target_pairs={{0,17},{1,16},{2,19},{3,18},{4,21},{5,20},{6,23},{7,22},{8,25},{9,... | collective-permute-start | bytes 98312 | tf_op jit(solution)/shard_map/ppermute | solution.py:654
  9.0 2.2 %collective-permute-start.3 = (f32[40,128]{1,0:T(8,128)S(1)}, f32[40,128]{1,0:T(8,128)S(1)}, u32[]{:S(2)}, u32[]{:S(2)}) collective-permute-start(f32[40,128]{1,0:T(8,128)S(1)} %get-tuple-element.63), channel_id=1, source_target_pairs={{0,1},{1,0},{2,3},{3,2},{4,5},{5,4},{6,7},{7,6},{8,9},{9,8},{10,11... | collective-permute-start | bytes 61448 | tf_op jit(solution)/shard_map/ppermute | solution.py:655
  10.6 1.4 %copy-start.2 = (bf16[384,256]{1,0:T(8,128)(2,1)S(1)}, bf16[384,256]{1,0:T(8,128)(2,1)}, u32[]{:S(2)}) copy-start(bf16[384,256]{1,0:T(8,128)(2,1)} %constant.9.clone.refs_12_) | copy-start | bytes 589828
  12.5 4.1 %collective-permute-start.5 = (f32[104,128]{1,0:T(8,128)S(1)}, f32[104,128]{1,0:T(8,128)S(1)}, u32[]{:S(2)}, u32[]{:S(2)}) collective-permute-start(f32[104,128]{1,0:T(8,128)S(1)} %get-tuple-element.67), channel_id=1, source_target_pairs={{0,9},{1,8},{2,11},{3,10},{4,13},{5,12},{6,15},{7,14},{8,1},{9,0},... | collective-permute-start | bytes 159752 | tf_op jit(solution)/shard_map/ppermute | solution.py:641
  13.0 3.6 %collective-permute-start.6 = (f32[24,544]{1,0:T(8,128)S(1)}, f32[24,544]{1,0:T(8,128)S(1)}, u32[]{:S(2)}, u32[]{:S(2)}) collective-permute-start(f32[24,544]{1,0:T(8,128)S(1)} %get-tuple-element.68), channel_id=1, source_target_pairs={{0,1},{1,0},{2,3},{3,2},{4,5},{5,4},{6,7},{7,6},{8,9},{9,8},{10,11... | collective-permute-start | bytes 156680 | tf_op jit(solution)/shard_map/ppermute | solution.py:643
  13.3 5.5 %collective-permute-start.7 = (f32[24,416]{1,0:T(8,128)S(1)}, f32[24,416]{1,0:T(8,128)S(1)}, u32[]{:S(2)}, u32[]{:S(2)}) collective-permute-start(f32[24,416]{1,0:T(8,128)S(1)} %get-tuple-element.70), channel_id=1, source_target_pairs={{1,2},{2,1},{3,4},{4,3},{5,6},{6,5},{9,10},{10,9},{11,12},{12,11},... | collective-permute-start | bytes 119816 | tf_op jit(solution)/shard_map/ppermute | solution.py:642
  16.7 3.4 %collective-permute-start.9 = (f32[64,128]{1,0:T(8,128)S(1)}, f32[64,128]{1,0:T(8,128)S(1)}, u32[]{:S(2)}, u32[]{:S(2)}) collective-permute-start(f32[64,128]{1,0:T(8,128)S(1)} %get-tuple-element.69.refs_6_), channel_id=1, source_target_pairs={{0,17},{1,16},{2,19},{3,18},{4,21},{5,20},{6,23},{7,22},{8,25},{9,... | collective-permute-start | bytes 98312 | tf_op jit(solution)/shard_map/ppermute | solution.py:654
  16.7 2.6 %collective-permute-start.8 = (f32[40,128]{1,0:T(8,128)S(1)}, f32[40,128]{1,0:T(8,128)S(1)}, u32[]{:S(2)}, u32[]{:S(2)}) collective-permute-start(f32[40,128]{1,0:T(8,128)S(1)} %get-tuple-element.76), channel_id=1, source_target_pairs={{0,1},{1,0},{2,3},{3,2},{4,5},{5,4},{6,7},{7,6},{8,9},{9,8},{10,11... | collective-permute-start | bytes 61448 | tf_op jit(solution)/shard_map/ppermute | solution.py:655
  20.7 4.5 %collective-permute-start.10 = (f32[104,128]{1,0:T(8,128)S(1)}, f32[104,128]{1,0:T(8,128)S(1)}, u32[]{:S(2)}, u32[]{:S(2)}) collective-permute-start(f32[104,128]{1,0:T(8,128)S(1)} %get-tuple-element.79), channel_id=1, source_target_pairs={{0,9},{1,8},{2,11},{3,10},{4,13},{5,12},{6,15},{7,14},{8,1},{9,0},... | collective-permute-start | bytes 159752 | tf_op jit(solution)/shard_map/ppermute | solution.py:641
  21.4 3.7 %collective-permute-start.11 = (f32[24,544]{1,0:T(8,128)S(1)}, f32[24,544]{1,0:T(8,128)S(1)}, u32[]{:S(2)}, u32[]{:S(2)}) collective-permute-start(f32[24,544]{1,0:T(8,128)S(1)} %get-tuple-element.80), channel_id=1, source_target_pairs={{0,1},{1,0},{2,3},{3,2},{4,5},{5,4},{6,7},{7,6},{8,9},{9,8},{10,11... | collective-permute-start | bytes 156680 | tf_op jit(solution)/shard_map/ppermute | solution.py:643
  22.0 5.7 %collective-permute-start.12 = (f32[24,416]{1,0:T(8,128)S(1)}, f32[24,416]{1,0:T(8,128)S(1)}, u32[]{:S(2)}, u32[]{:S(2)}) collective-permute-start(f32[24,416]{1,0:T(8,128)S(1)} %get-tuple-element.82), channel_id=1, source_target_pairs={{1,2},{2,1},{3,4},{4,3},{5,6},{6,5},{9,10},{10,9},{11,12},{12,11},... | collective-permute-start | bytes 119816 | tf_op jit(solution)/shard_map/ppermute | solution.py:642
  25.2 3.4 %collective-permute-start.14 = (f32[64,128]{1,0:T(8,128)S(1)}, f32[64,128]{1,0:T(8,128)S(1)}, u32[]{:S(2)}, u32[]{:S(2)}) collective-permute-start(f32[64,128]{1,0:T(8,128)S(1)} %get-tuple-element.81.refs_6_), channel_id=1, source_target_pairs={{0,17},{1,16},{2,19},{3,18},{4,21},{5,20},{6,23},{7,22},{8,25},{9,... | collective-permute-start | bytes 98312 | tf_op jit(solution)/shard_map/ppermute | solution.py:654
  25.2 3.1 %collective-permute-start.13 = (f32[40,128]{1,0:T(8,128)S(1)}, f32[40,128]{1,0:T(8,128)S(1)}, u32[]{:S(2)}, u32[]{:S(2)}) collective-permute-start(f32[40,128]{1,0:T(8,128)S(1)} %get-tuple-element.85), channel_id=1, source_target_pairs={{0,1},{1,0},{2,3},{3,2},{4,5},{5,4},{6,7},{7,6},{8,9},{9,8},{10,11... | collective-permute-start | bytes 61448 | tf_op jit(solution)/shard_map/ppermute | solution.py:655

commit v14 on v13

--- a/solution.py
+++ b/solution.py
@@ -385,11 +385,18 @@
 
 
 def map_kernel(plan, axes, *refs):
-    turning, drag, mask, order_twice, _, refs = *refs[:5], refs[5:]
+    inputs, (order_twice, _), refs = refs[:6], refs[6:8], refs[8:]
+    tables, (turning, drag, mask, done) = refs[9:12], refs[12:]
+    targets = (turning, drag, mask, *tables)
+    copies = [pltpu.make_async_copy(*pair, done.at[k]) for k, pair in enumerate(zip(inputs, targets))]
+    for copy in copies:
+        copy.start()
     permute_out, permute_some_out, slots_out, turn_out, turn_edge_out = refs[:5]
-    sea_out, sea_order_out, sea_some_out, keep_out = refs[5:]
+    sea_out, sea_order_out, sea_some_out, keep_out = refs[5:9]
     columns, rows, cols = plan.columns, plan.rows, plan.cols
     order = order_twice[:, :columns]
+    for copy in copies[:3]:
+        copy.wait()
     sea = jnp.broadcast_to(column_of(plan, row_of(plan, mask).astype(F32)), (columns, LANES))
     turn = jnp.broadcast_to(column_of(plan, row_of(plan, turning)), (columns, LANES))
     sea_out[...] = sea
@@ -423,6 +430,8 @@
     keep = 1.0 - drag[...].reshape(1, plan.depth)
     blank = jnp.zeros((1, LANES - 2 * plan.depth), F32)
     keep_out[...] = jnp.broadcast_to(jnp.concatenate([keep, keep, blank], axis=1), (8, LANES))
+    for copy in copies[3:]:
+        copy.wait()
 
 
 class Directions:
@@ -603,7 +612,7 @@
 
 
 def per_device(plan, axes, spectra, turning, currents, drag_rates, land_mask, ocean_target):
-    stokes_once, stokes, rates, grow = (
+    stokes_once, *tables = (
         jnp.asarray(table) for table in build_tables(NFREQ, NDIR, drag_rates.shape[0])
     )
     columns, rows, cols, spectral = plan.columns, plan.rows, plan.cols, plan.spectral
@@ -620,10 +629,11 @@
     spans = spectral // 256
 
     def call(kernel, outs, scratch, *args, space_in=pltpu.VMEM, space_out=pltpu.VMEM):
+        spaces = space_in if isinstance(space_in, list) else [space_in] * len(args)
         return pl.pallas_call(
             functools.partial(kernel, plan, axes),
             out_shape=outs,
-            in_specs=[pl.BlockSpec(memory_space=space_in)] * len(args),
+            in_specs=[pl.BlockSpec(memory_space=space) for space in spaces],
             out_specs=[pl.BlockSpec(memory_space=space_out)] * len(outs),
             scratch_shapes=scratch,
             compiler_params=params,
@@ -696,17 +706,25 @@
                 state,
                 shape((some, LANES), F32),
                 shape((8, LANES), F32),
+                *[shape(table.shape, table.dtype) for table in tables],
             ],
-            [],
-            turning,
-            drag_rates,
-            land_mask,
+            [
+                pltpu.VMEM(turning.shape, F32),
+                pltpu.VMEM(drag_rates.shape, F32),
+                pltpu.VMEM(land_mask.shape, jnp.int32),
+                pltpu.SemaphoreType.DMA((6,)),
+            ],
+            *[
+                pltpu.with_memory_space_constraint(array, pltpu.HBM)
+                for array in (turning, drag_rates, land_mask, *tables)
+            ],
             order,
             first,
+            space_in=[pltpu.HBM] * 6 + [pltpu.VMEM] * 2,
         )
 
     made, came = exchange(*sent[-2:], sent[:-2], maps)
-    permute, permute_some, slots, turn, turn_edge, sea, sea_order, sea_some, keep = made
+    permute, permute_some, slots, turn, turn_edge, sea, sea_order, sea_some, keep, stokes, rates, grow = made
     for step in range(STEPS - 1):
         turned, turned_edge, turned_order = call(
             move_kernel,

time: 29.9 us -> 29.9 us (level)
  Pallas kernels: 6.66 us -> 7.52 us
  waiting for transfers between devices: 2.2 us -> 1.75 us
  starting transfers between devices: 19.9 us -> 19.6 us
    pallas_call x13, Pallas kernels: 6.66 us -> 7.52 us  [call(): pl.pallas_call(functools.partial(kernel, plan, axes), out_shape=outs, in_...]
    ppermute x3, waiting for transfers between devices: 1.7 us -> 1.07 us  [exchange(): from_y = lax.ppermute(first, both_axes, plan.crossing(2))]
  transfers between devices with their start and end apart: 15 -> 15, of which waited for: 4 -> 3; matrix products, arithmetic and copies ran while one was open for 0% -> 0% of each run, Pallas kernels for 10% -> 13%
where the time goes in v14:
time: 29.9 us; the launch traced here: 29.7 us
  starting transfers between devices  19.6 us (66%)
  Pallas kernels  7.52 us (25%)
  waiting for transfers between devices  1.75 us (6%)
  between operations  0.84 us (3%)
    ppermute x3, starting transfers between devices, exchange(): far_in = lax.ppermute(to_far, axes[0], others)  10 us
    pallas_call x13, Pallas kernels, call(): pl.pallas_call(functools.partial(kernel, plan, axes), out_shape=outs, in_...  7.52 us
    ppermute x3, starting transfers between devices, exchange(): got = [lax.ppermute(to_mate, axes[0], pairs), from_y]  4.18 us
    ppermute x3, starting transfers between devices, exchange(): from_x = lax.ppermute(to_x, both_axes, plan.crossing(1))  3.8 us
    ppermute x3, waiting for transfers between devices, exchange(): from_y = lax.ppermute(first, both_axes, plan.crossing(2))  1.07 us
    ppermute x3, starting transfers between devices, exchange(): near_in = lax.ppermute(to_near, axes[0], pairs)  0.97 us
    ppermute x3, waiting for transfers between devices, exchange(): far_in = lax.ppermute(to_far, axes[0], others)  0.65 us
    ppermute x3, starting transfers between devices, exchange(): from_y = lax.ppermute(first, both_axes, plan.crossing(2))  0.63 us
  transfers between devices with their start and end apart: 15, of which 3 were waited for; matrix products, arithmetic and copies ran while one was open for 0% of the time, Pallas kernels for 13%

profile of v14, /device:TPU:1, one launch (start us, length us, event | category | flops | bytes accessed | tf_op | source)
XLA Modules:
  0.0 29.7 jit_solution(4045068196809388505)
XLA Ops:
  0.6 1.5 %shard_map.113 = (f32[4,24,768]{2,1,0:T(8,128)S(1)}, f32[96,128]{1,0:T(8,128)S(1)}, f32[96,128]{1,0:T(8,128)S(1)}, bf16[96,192]{1,0:T(8,128)(2,1)S(1)}, f32[104,...) custom-call(f32[4,24,768]{2,1,0:T(8,128)} %refs_0_.2, f32[4,24,64]{2,1,0:T(8,128)} %refs_1_.2, ...), custom_call_target="tpu_custom_call" | custom-call | tf_op jit(solution)/shard_map/pallas_call | solution.py:633
  2.2 2.7 %collective-permute-start = (f32[104,128]{1,0:T(8,128)S(1)}, f32[104,128]{1,0:T(8,128)S(1)}, u32[]{:S(2)}, u32[]{:S(2)}) collective-permute-start(f32[104,128]{1,0:T(8,128)S(1)} %get-tuple-element.49), channel_id=1, source_target_pairs={{0,9},{1,8},{2,11},{3,10},{4,13},{5,12},{6,15},{7,14},{8,1},{9,0},... | collective-permute-start | bytes 159752 | tf_op jit(solution)/shard_map/ppermute | solution.py:651
  4.8 0.0 collective-permute-start.1
  4.8 3.6 %collective-permute-start.2 = (f32[24,416]{1,0:T(8,128)S(1)}, f32[24,416]{1,0:T(8,128)S(1)}, u32[]{:S(2)}, u32[]{:S(2)}) collective-permute-start(f32[24,416]{1,0:T(8,128)S(1)} %get-tuple-element.54), channel_id=1, source_target_pairs={{1,2},{2,1},{3,4},{4,3},{5,6},{6,5},{9,10},{10,9},{11,12},{12,11},... | collective-permute-start | bytes 119816 | tf_op jit(solution)/shard_map/ppermute | solution.py:652
  8.5 0.0 collective-permute-done.from_x
  8.5 0.5 %collective-permute-start.4 = (f32[64,128]{1,0:T(8,128)S(1)}, f32[64,128]{1,0:T(8,128)S(1)}, u32[]{:S(2)}, u32[]{:S(2)}) collective-permute-start(f32[64,128]{1,0:T(8,128)S(1)} %get-tuple-element.51.refs_7_), channel_id=1, source_target_pairs={{0,17},{1,16},{2,19},{3,18},{4,21},{5,20},{6,23},{7,22},{8,25},{9,... | collective-permute-start | bytes 98312 | tf_op jit(solution)/shard_map/ppermute | solution.py:664
  9.0 1.2 %collective-permute-start.3 = (f32[40,128]{1,0:T(8,128)S(1)}, f32[40,128]{1,0:T(8,128)S(1)}, u32[]{:S(2)}, u32[]{:S(2)}) collective-permute-start(f32[40,128]{1,0:T(8,128)S(1)} %get-tuple-element.69), channel_id=1, source_target_pairs={{0,1},{1,0},{2,3},{3,2},{4,5},{5,4},{6,7},{7,6},{8,9},{9,8},{10,11... | collective-permute-start | bytes 61448 | tf_op jit(solution)/shard_map/ppermute | solution.py:665
  10.2 1.2 %shard_map.115 = (bf16[96,96]{1,0:T(8,128)(2,1)S(1)}, bf16[64,96]{1,0:T(8,128)(2,1)S(1)}, s32[8,128]{1,0:T(8,128)S(1)}, f32[96,128]{1,0:T(8,128)S(1)}, f32[8,128...) custom-call(f32[4,24]{1,0:T(4,128)} %refs_0_.3, ...), custom_call_target="tpu_custom_call" | custom-call | tf_op jit(solution)/shard_map/pallas_call | solution.py:633
  11.4 0.0 collective-permute-done.2.refs_4_.refs_16_
  11.4 0.6 %shard_map.116 = (f32[4,24,768]{2,1,0:T(8,128)S(1)}, f32[8,768]{1,0:T(8,128)S(1)}, f32[96,768]{1,0:T(8,128)S(1)}) custom-call(f32[4,24,768]{2,1,0:T(8,128)S(1)} %get-tuple-element.47.refs_0_, f32[96,128]{1,0:T(8,128)S(1)} %get-tuple-element.52.refs_1_, f32[8,768]{1,0:T(8,128)S(1)} %get-tuple-element.53.refs_2_.refs_13_.refs_7_, ...), custom_call_target="tpu_custom_call" | custom-call | tf_op jit(solution)/shard_map/pallas_call | solution.py:633
  12.0 0.0 collective-permute-done.4.refs_18_
  12.0 0.6 %shard_map.117 = (f32[96,128]{1,0:T(8,128)S(1)}, f32[96,128]{1,0:T(8,128)S(1)}, f32[96,128]{1,0:T(8,128)S(1)}, f32[8,768]{1,0:T(8,128)S(1)}, f32[24,416]{1,0:T(8...) custom-call(f32[4,24,768]{2,1,0:T(8,128)S(1)} %get-tuple-element.55.refs_0_, ...), custom_call_target="tpu_custom_call" | custom-call | tf_op jit(solution)/shard_map/pallas_call | solution.py:633
  12.6 0.5 %collective-permute-start.5 = (f32[104,128]{1,0:T(8,128)S(1)}, f32[104,128]{1,0:T(8,128)S(1)}, u32[]{:S(2)}, u32[]{:S(2)}) collective-permute-start(f32[104,128]{1,0:T(8,128)S(1)} %get-tuple-element.73), channel_id=1, source_target_pairs={{0,9},{1,8},{2,11},{3,10},{4,13},{5,12},{6,15},{7,14},{8,1},{9,0},... | collective-permute-start | bytes 159752 | tf_op jit(solution)/shard_map/ppermute | solution.py:651
  13.1 0.2 collective-permute-start.6
  13.3 3.4 %collective-permute-start.7 = (f32[24,416]{1,0:T(8,128)S(1)}, f32[24,416]{1,0:T(8,128)S(1)}, u32[]{:S(2)}, u32[]{:S(2)}) collective-permute-start(f32[24,416]{1,0:T(8,128)S(1)} %get-tuple-element.76), channel_id=1, source_target_pairs={{1,2},{2,1},{3,4},{4,3},{5,6},{6,5},{9,10},{10,9},{11,12},{12,11},... | collective-permute-start | bytes 119816 | tf_op jit(solution)/shard_map/ppermute | solution.py:652
  16.7 0.1 collective-permute-start.9
  16.8 1.5 %collective-permute-start.8 = (f32[40,128]{1,0:T(8,128)S(1)}, f32[40,128]{1,0:T(8,128)S(1)}, u32[]{:S(2)}, u32[]{:S(2)}) collective-permute-start(f32[40,128]{1,0:T(8,128)S(1)} %get-tuple-element.82), channel_id=1, source_target_pairs={{0,1},{1,0},{2,3},{3,2},{4,5},{5,4},{6,7},{7,6},{8,9},{9,8},{10,11... | collective-permute-start | bytes 61448 | tf_op jit(solution)/shard_map/ppermute | solution.py:665
  18.3 0.4 %shard_map.119.refs_0_ = f32[4,24,768]{2,1,0:T(8,128)S(1)} custom-call(f32[4,24,768]{2,1,0:T(8,128)S(1)} %get-tuple-element.55.refs_0_, f32[8,768]{1,0:T(8,128)S(1)} %get-tuple-element.70.refs_1_, f32[96,128]{1,0:T(8,128)S(1)} %get-tuple-element.71.refs_2_, bf16[96,96]{1,0:T(8,128)(2,1)S(1)} %get-tuple-element.72.refs_3_, ...), custom_call_target="tpu_custom_call" | custom-call | tf_op jit(solution)/shard_map/pallas_call | solution.py:633
  18.7 0.0 collective-permute-done.7.refs_4_.refs_16_
  18.7 0.6 %shard_map.120 = (f32[4,24,768]{2,1,0:T(8,128)S(1)}, f32[8,768]{1,0:T(8,128)S(1)}, f32[96,768]{1,0:T(8,128)S(1)}) custom-call(f32[4,24,768]{2,1,0:T(8,128)S(1)} %shard_map.119.refs_0_, f32[96,128]{1,0:T(8,128)S(1)} %get-tuple-element.52.refs_1_, f32[8,768]{1,0:T(8,128)S(1)} %get-tuple-element.53.refs_2_.refs_13_.refs_7_, ...), custom_call_target="tpu_custom_call" | custom-call | tf_op jit(solution)/shard_map/pallas_call | solution.py:633
  19.3 0.8 %collective-permute-done.9.refs_18_ = f32[64,128]{1,0:T(8,128)S(1)} collective-permute-done((f32[64,128]{1,0:T(8,128)S(1)}, f32[64,128]{1,0:T(8,128)S(1)}, u32[]{:S(2)}, u32[]{:S(2)}) %collective-permute-start.9) | collective-permute-done | bytes 32800 | tf_op jit(solution)/shard_map/ppermute | solution.py:664
  20.1 0.6 %shard_map.121 = (f32[96,128]{1,0:T(8,128)S(1)}, f32[96,128]{1,0:T(8,128)S(1)}, f32[96,128]{1,0:T(8,128)S(1)}, f32[8,768]{1,0:T(8,128)S(1)}, f32[24,416]{1,0:T(8...) custom-call(f32[4,24,768]{2,1,0:T(8,128)S(1)} %get-tuple-element.77.refs_0_, ...), custom_call_target="tpu_custom_call" | custom-call | tf_op jit(solution)/shard_map/pallas_call | solution.py:633
  20.7 0.6 %collective-permute-start.10 = (f32[104,128]{1,0:T(8,128)S(1)}, f32[104,128]{1,0:T(8,128)S(1)}, u32[]{:S(2)}, u32[]{:S(2)}) collective-permute-start(f32[104,128]{1,0:T(8,128)S(1)} %get-tuple-element.85), channel_id=1, source_target_pairs={{0,9},{1,8},{2,11},{3,10},{4,13},{5,12},{6,15},{7,14},{8,1},{9,0},... | collective-permute-start | bytes 159752 | tf_op jit(solution)/shard_map/ppermute | solution.py:651
  21.3 0.7 %collective-permute-start.11 = (f32[24,544]{1,0:T(8,128)S(1)}, f32[24,544]{1,0:T(8,128)S(1)}, u32[]{:S(2)}, u32[]{:S(2)}) collective-permute-start(f32[24,544]{1,0:T(8,128)S(1)} %get-tuple-element.86), channel_id=1, source_target_pairs={{0,1},{1,0},{2,3},{3,2},{4,5},{5,4},{6,7},{7,6},{8,9},{9,8},{10,11... | collective-permute-start | bytes 156680 | tf_op jit(solution)/shard_map/ppermute | solution.py:653
  22.1 3.1 %collective-permute-start.12 = (f32[24,416]{1,0:T(8,128)S(1)}, f32[24,416]{1,0:T(8,128)S(1)}, u32[]{:S(2)}, u32[]{:S(2)}) collective-permute-start(f32[24,416]{1,0:T(8,128)S(1)} %get-tuple-element.88), channel_id=1, source_target_pairs={{1,2},{2,1},{3,4},{4,3},{5,6},{6,5},{9,10},{10,9},{11,12},{12,11},... | collective-permute-start | bytes 119816 | tf_op jit(solution)/shard_map/ppermute | solution.py:652
  25.2 0.1 collective-permute-start.14
  25.3 1.5 %collective-permute-start.13 = (f32[40,128]{1,0:T(8,128)S(1)}, f32[40,128]{1,0:T(8,128)S(1)}, u32[]{:S(2)}, u32[]{:S(2)}) collective-permute-start(f32[40,128]{1,0:T(8,128)S(1)} %get-tuple-element.91), channel_id=1, source_target_pairs={{0,1},{1,0},{2,3},{3,2},{4,5},{5,4},{6,7},{7,6},{8,9},{9,8},{10,11... | collective-permute-start | bytes 61448 | tf_op jit(solution)/shard_map/ppermute | solution.py:665
  26.8 0.4 %shard_map.123.refs_0_ = f32[4,24,768]{2,1,0:T(8,128)S(1)} custom-call(f32[4,24,768]{2,1,0:T(8,128)S(1)} %get-tuple-element.77.refs_0_, f32[8,768]{1,0:T(8,128)S(1)} %get-tuple-element.83.refs_1_, f32[96,128]{1,0:T(8,128)S(1)} %get-tuple-element.84.refs_2_, bf16[96,96]{1,0:T(8,128)(2,1)S(1)} %get-tuple-element.72.refs_3_, ...), custom_call_target="tpu_custom_call" | custom-call | tf_op jit(solution)/shard_map/pallas_call | solution.py:633
  27.2 0.6 %collective-permute-done.12.refs_4_.refs_10_ = f32[24,416]{1,0:T(8,128)S(1)} collective-permute-done((f32[24,416]{1,0:T(8,128)S(1)}, f32[24,416]{1,0:T(8,128)S(1)}, u32[]{:S(2)}, u32[]{:S(2)}) %collective-permute-start.12) | collective-permute-done | bytes 39968 | tf_op jit(solution)/shard_map/ppermute | solution.py:652
  27.8 0.6 %shard_map.124.refs_0_ = f32[4,24,768]{2,1,0:T(8,128)S(1)} custom-call(f32[4,24,768]{2,1,0:T(8,128)S(1)} %shard_map.123.refs_0_, f32[96,128]{1,0:T(8,128)S(1)} %get-tuple-element.52.refs_1_, f32[8,768]{1,0:T(8,128)S(1)} %get-tuple-element.53.refs_2_.refs_13_.refs_7_, f32[24,544]{1,0:T(8,128)S(1)} %collective-permute-done.11.near.refs_3_.refs_9_, ...), custom_call_target="tpu_custom_call" | custom-call | tf_op jit(solution)/shard_map/pallas_call | solution.py:633
  28.4 0.2 collective-permute-done.14.refs_12_
  28.6 1.1 %shard_map.125 = (f32[4,24,768]{2,1,0:T(8,128)}, f32[4,24,64]{2,1,0:T(8,128)}) custom-call(f32[4,24,768]{2,1,0:T(8,128)S(1)} %shard_map.124.refs_0_, f32[96,128]{1,0:T(8,128)S(1)} %get-tuple-element.89.refs_1_, f32[96,128]{1,0:T(8,128)S(1)} %get-tuple-element.90.refs_2_, bf16[96,96]{1,0:T(8,128)(2,1)S(1)} %get-tuple-element.72.refs_3_, ...), custom_call_target="tpu_custom_call" | custom-call | tf_op jit(solution)/shard_map/pallas_call | solution.py:633
  (11 shorter events, 0.0 us)
Async XLA Ops:
  2.2 6.3 %collective-permute-start = (f32[104,128]{1,0:T(8,128)S(1)}, f32[104,128]{1,0:T(8,128)S(1)}, u32[]{:S(2)}, u32[]{:S(2)}) collective-permute-start(f32[104,128]{1,0:T(8,128)S(1)} %get-tuple-element.49), channel_id=1, source_target_pairs={{0,9},{1,8},{2,11},{3,10},{4,13},{5,12},{6,15},{7,14},{8,1},{9,0},... | collective-permute-start | bytes 159752 | tf_op jit(solution)/shard_map/ppermute | solution.py:651
  4.8 3.6 %collective-permute-start.1 = (f32[24,544]{1,0:T(8,128)S(1)}, f32[24,544]{1,0:T(8,128)S(1)}, u32[]{:S(2)}, u32[]{:S(2)}) collective-permute-start(f32[24,544]{1,0:T(8,128)S(1)} %get-tuple-element.50), channel_id=1, source_target_pairs={{0,1},{1,0},{2,3},{3,2},{4,5},{5,4},{6,7},{7,6},{8,9},{9,8},{10,11... | collective-permute-start | bytes 156680 | tf_op jit(solution)/shard_map/ppermute | solution.py:653
  4.8 6.5 %collective-permute-start.2 = (f32[24,416]{1,0:T(8,128)S(1)}, f32[24,416]{1,0:T(8,128)S(1)}, u32[]{:S(2)}, u32[]{:S(2)}) collective-permute-start(f32[24,416]{1,0:T(8,128)S(1)} %get-tuple-element.54), channel_id=1, source_target_pairs={{1,2},{2,1},{3,4},{4,3},{5,6},{6,5},{9,10},{10,9},{11,12},{12,11},... | collective-permute-start | bytes 119816 | tf_op jit(solution)/shard_map/ppermute | solution.py:652
  8.5 3.5 %collective-permute-start.4 = (f32[64,128]{1,0:T(8,128)S(1)}, f32[64,128]{1,0:T(8,128)S(1)}, u32[]{:S(2)}, u32[]{:S(2)}) collective-permute-start(f32[64,128]{1,0:T(8,128)S(1)} %get-tuple-element.51.refs_7_), channel_id=1, source_target_pairs={{0,17},{1,16},{2,19},{3,18},{4,21},{5,20},{6,23},{7,22},{8,25},{9,... | collective-permute-start | bytes 98312 | tf_op jit(solution)/shard_map/ppermute | solution.py:664
  9.0 3.0 %collective-permute-start.3 = (f32[40,128]{1,0:T(8,128)S(1)}, f32[40,128]{1,0:T(8,128)S(1)}, u32[]{:S(2)}, u32[]{:S(2)}) collective-permute-start(f32[40,128]{1,0:T(8,128)S(1)} %get-tuple-element.69), channel_id=1, source_target_pairs={{0,1},{1,0},{2,3},{3,2},{4,5},{5,4},{6,7},{7,6},{8,9},{9,8},{10,11... | collective-permute-start | bytes 61448 | tf_op jit(solution)/shard_map/ppermute | solution.py:665
  12.6 4.1 %collective-permute-start.5 = (f32[104,128]{1,0:T(8,128)S(1)}, f32[104,128]{1,0:T(8,128)S(1)}, u32[]{:S(2)}, u32[]{:S(2)}) collective-permute-start(f32[104,128]{1,0:T(8,128)S(1)} %get-tuple-element.73), channel_id=1, source_target_pairs={{0,9},{1,8},{2,11},{3,10},{4,13},{5,12},{6,15},{7,14},{8,1},{9,0},... | collective-permute-start | bytes 159752 | tf_op jit(solution)/shard_map/ppermute | solution.py:651
  13.1 3.6 %collective-permute-start.6 = (f32[24,544]{1,0:T(8,128)S(1)}, f32[24,544]{1,0:T(8,128)S(1)}, u32[]{:S(2)}, u32[]{:S(2)}) collective-permute-start(f32[24,544]{1,0:T(8,128)S(1)} %get-tuple-element.74), channel_id=1, source_target_pairs={{0,1},{1,0},{2,3},{3,2},{4,5},{5,4},{6,7},{7,6},{8,9},{9,8},{10,11... | collective-permute-start | bytes 156680 | tf_op jit(solution)/shard_map/ppermute | solution.py:653
  13.3 5.4 %collective-permute-start.7 = (f32[24,416]{1,0:T(8,128)S(1)}, f32[24,416]{1,0:T(8,128)S(1)}, u32[]{:S(2)}, u32[]{:S(2)}) collective-permute-start(f32[24,416]{1,0:T(8,128)S(1)} %get-tuple-element.76), channel_id=1, source_target_pairs={{1,2},{2,1},{3,4},{4,3},{5,6},{6,5},{9,10},{10,9},{11,12},{12,11},... | collective-permute-start | bytes 119816 | tf_op jit(solution)/shard_map/ppermute | solution.py:652
  16.7 3.4 %collective-permute-start.9 = (f32[64,128]{1,0:T(8,128)S(1)}, f32[64,128]{1,0:T(8,128)S(1)}, u32[]{:S(2)}, u32[]{:S(2)}) collective-permute-start(f32[64,128]{1,0:T(8,128)S(1)} %get-tuple-element.75.refs_6_), channel_id=1, source_target_pairs={{0,17},{1,16},{2,19},{3,18},{4,21},{5,20},{6,23},{7,22},{8,25},{9,... | collective-permute-start | bytes 98312 | tf_op jit(solution)/shard_map/ppermute | solution.py:664
  16.8 2.5 %collective-permute-start.8 = (f32[40,128]{1,0:T(8,128)S(1)}, f32[40,128]{1,0:T(8,128)S(1)}, u32[]{:S(2)}, u32[]{:S(2)}) collective-permute-start(f32[40,128]{1,0:T(8,128)S(1)} %get-tuple-element.82), channel_id=1, source_target_pairs={{0,1},{1,0},{2,3},{3,2},{4,5},{5,4},{6,7},{7,6},{8,9},{9,8},{10,11... | collective-permute-start | bytes 61448 | tf_op jit(solution)/shard_map/ppermute | solution.py:665
  20.7 4.5 %collective-permute-start.10 = (f32[104,128]{1,0:T(8,128)S(1)}, f32[104,128]{1,0:T(8,128)S(1)}, u32[]{:S(2)}, u32[]{:S(2)}) collective-permute-start(f32[104,128]{1,0:T(8,128)S(1)} %get-tuple-element.85), channel_id=1, source_target_pairs={{0,9},{1,8},{2,11},{3,10},{4,13},{5,12},{6,15},{7,14},{8,1},{9,0},... | collective-permute-start | bytes 159752 | tf_op jit(solution)/shard_map/ppermute | solution.py:651
  21.3 3.8 %collective-permute-start.11 = (f32[24,544]{1,0:T(8,128)S(1)}, f32[24,544]{1,0:T(8,128)S(1)}, u32[]{:S(2)}, u32[]{:S(2)}) collective-permute-start(f32[24,544]{1,0:T(8,128)S(1)} %get-tuple-element.86), channel_id=1, source_target_pairs={{0,1},{1,0},{2,3},{3,2},{4,5},{5,4},{6,7},{7,6},{8,9},{9,8},{10,11... | collective-permute-start | bytes 156680 | tf_op jit(solution)/shard_map/ppermute | solution.py:653
  22.1 5.7 %collective-permute-start.12 = (f32[24,416]{1,0:T(8,128)S(1)}, f32[24,416]{1,0:T(8,128)S(1)}, u32[]{:S(2)}, u32[]{:S(2)}) collective-permute-start(f32[24,416]{1,0:T(8,128)S(1)} %get-tuple-element.88), channel_id=1, source_target_pairs={{1,2},{2,1},{3,4},{4,3},{5,6},{6,5},{9,10},{10,9},{11,12},{12,11},... | collective-permute-start | bytes 119816 | tf_op jit(solution)/shard_map/ppermute | solution.py:652
  25.2 3.4 %collective-permute-start.14 = (f32[64,128]{1,0:T(8,128)S(1)}, f32[64,128]{1,0:T(8,128)S(1)}, u32[]{:S(2)}, u32[]{:S(2)}) collective-permute-start(f32[64,128]{1,0:T(8,128)S(1)} %get-tuple-element.87.refs_6_), channel_id=1, source_target_pairs={{0,17},{1,16},{2,19},{3,18},{4,21},{5,20},{6,23},{7,22},{8,25},{9,... | collective-permute-start | bytes 98312 | tf_op jit(solution)/shard_map/ppermute | solution.py:664
  25.3 3.1 %collective-permute-start.13 = (f32[40,128]{1,0:T(8,128)S(1)}, f32[40,128]{1,0:T(8,128)S(1)}, u32[]{:S(2)}, u32[]{:S(2)}) collective-permute-start(f32[40,128]{1,0:T(8,128)S(1)} %get-tuple-element.91), channel_id=1, source_target_pairs={{0,1},{1,0},{2,3},{3,2},{4,5},{5,4},{6,7},{7,6},{8,9},{9,8},{10,11... | collective-permute-start | bytes 61448 | tf_op jit(solution)/shard_map/ppermute | solution.py:665

commit v15 on v13

--- a/solution.py
+++ b/solution.py
@@ -454,6 +454,35 @@
     masks = Directions(block)
     place = lax.broadcasted_iota(jnp.int32, block, 0)
     outside = place == jnp.where(masks.eastward, 0, cols - 1)
+
+    def edge_tile(first, second, tile):
+        half = tile % (tiles // 2)
+        half = slice(half * LANES, (half + 1) * LANES)
+        came = jnp.where(even, first[:, half], second[:, half])
+        return came if tile < tiles // 2 else pltpu.roll(came, LANES - NDIR // 2, 1)
+
+    def fill(row, tile):
+        lanes = slice(tile * LANES, (tile + 1) * LANES)
+        rate = turn[row * cols : (row + 1) * cols, :]
+        stay, along_x, along_y, gain = (rates[k : k + 1, lanes] for k in range(4))
+        center = waves[row, :, lanes]
+        south = waves[row - 1, :, lanes] if row else edge_tile(far, near, tile)
+        north = waves[row + 1, :, lanes] if row < rows - 1 else edge_tile(near, far, tile)
+        moved = (
+            stay * center
+            + jnp.where(outside, 0.0, along_x)
+            * jnp.where(
+                masks.eastward, pltpu.roll(center, 1, 0), pltpu.roll(center, cols - 1, 0)
+            )
+            + along_y * jnp.where(masks.northward, south, north)
+        )
+        turned_out[row, :, lanes] = masks.turned(moved, rate, gain)
+
+    if len(refs) == 1:
+        for row in range(rows):
+            for tile in range(tiles):
+                fill(row, tile)
+        return
     for tile in range(tiles):
         lanes = slice(tile * LANES, (tile + 1) * LANES)
         stay, along_x, along_y, gain = (rates[k : k + 1, lanes] for k in range(4))

time: 29.9 us -> 29.9 us (level)
  transfers between devices with their start and end apart: 15 -> 15, of which waited for: 4 -> 4; matrix products, arithmetic and copies ran while one was open for 0% -> 0% of each run, Pallas kernels for 10% -> 9%
where the time goes in v15:
time: 29.9 us; the launch traced here: 29.7 us
  starting transfers between devices  19.9 us (67%)
  Pallas kernels  6.58 us (22%)
  waiting for transfers between devices  2.28 us (8%)
  between operations  0.89 us (3%)
    ppermute x3, starting transfers between devices, exchange(): far_in = lax.ppermute(to_far, axes[0], others)  10 us
    pallas_call x13, Pallas kernels, call(): pl.pallas_call(functools.partial(kernel, plan, axes), out_shape=outs, in_...  6.58 us
    ppermute x3, starting transfers between devices, exchange(): got = [lax.ppermute(to_mate, axes[0], pairs), from_y]  4.46 us
    ppermute x3, starting transfers between devices, exchange(): from_x = lax.ppermute(to_x, both_axes, plan.crossing(1))  3.93 us
    ppermute x3, waiting for transfers between devices, exchange(): from_y = lax.ppermute(first, both_axes, plan.crossing(2))  1.78 us
    ppermute x3, starting transfers between devices, exchange(): near_in = lax.ppermute(to_near, axes[0], pairs)  0.84 us
    ppermute x3, starting transfers between devices, exchange(): from_y = lax.ppermute(first, both_axes, plan.crossing(2))  0.63 us
  transfers between devices with their start and end apart: 15, of which 4 were waited for; matrix products, arithmetic and copies ran while one was open for 0% of the time, Pallas kernels for 9%

profile of v15, /device:TPU:1, one launch (start us, length us, event | category | flops | bytes accessed | tf_op | source)
XLA Modules:
  0.0 29.7 jit_solution(12367690756635058567)
XLA Ops:
  0.7 0.0 copy-start.1
  0.7 1.6 %shard_map.113 = (f32[4,24,768]{2,1,0:T(8,128)S(1)}, f32[96,128]{1,0:T(8,128)S(1)}, f32[96,128]{1,0:T(8,128)S(1)}, bf16[96,192]{1,0:T(8,128)(2,1)S(1)}, f32[104,...) custom-call(f32[4,24,768]{2,1,0:T(8,128)} %refs_0_.2, f32[4,24,64]{2,1,0:T(8,128)} %refs_1_.2, ...), custom_call_target="tpu_custom_call" | custom-call | tf_op jit(solution)/shard_map/pallas_call | solution.py:652
  2.2 0.0 copy-start
  2.2 2.7 %collective-permute-start = (f32[104,128]{1,0:T(8,128)S(1)}, f32[104,128]{1,0:T(8,128)S(1)}, u32[]{:S(2)}, u32[]{:S(2)}) collective-permute-start(f32[104,128]{1,0:T(8,128)S(1)} %get-tuple-element.46), channel_id=1, source_target_pairs={{0,9},{1,8},{2,11},{3,10},{4,13},{5,12},{6,15},{7,14},{8,1},{9,0},... | collective-permute-start | bytes 159752 | tf_op jit(solution)/shard_map/ppermute | solution.py:670
  4.9 0.0 collective-permute-start.1
  4.9 3.6 %collective-permute-start.2 = (f32[24,416]{1,0:T(8,128)S(1)}, f32[24,416]{1,0:T(8,128)S(1)}, u32[]{:S(2)}, u32[]{:S(2)}) collective-permute-start(f32[24,416]{1,0:T(8,128)S(1)} %get-tuple-element.50), channel_id=1, source_target_pairs={{1,2},{2,1},{3,4},{4,3},{5,6},{6,5},{9,10},{10,9},{11,12},{12,11},... | collective-permute-start | bytes 119816 | tf_op jit(solution)/shard_map/ppermute | solution.py:671
  8.5 0.5 %collective-permute-start.4 = (f32[64,128]{1,0:T(8,128)S(1)}, f32[64,128]{1,0:T(8,128)S(1)}, u32[]{:S(2)}, u32[]{:S(2)}) collective-permute-start(f32[64,128]{1,0:T(8,128)S(1)} %get-tuple-element.48.refs_4_), channel_id=1, source_target_pairs={{0,17},{1,16},{2,19},{3,18},{4,21},{5,20},{6,23},{7,22},{8,25},{9,... | collective-permute-start | bytes 98312 | tf_op jit(solution)/shard_map/ppermute | solution.py:683
  9.0 1.2 %collective-permute-start.3 = (f32[40,128]{1,0:T(8,128)S(1)}, f32[40,128]{1,0:T(8,128)S(1)}, u32[]{:S(2)}, u32[]{:S(2)}) collective-permute-start(f32[40,128]{1,0:T(8,128)S(1)} %get-tuple-element.63), channel_id=1, source_target_pairs={{0,1},{1,0},{2,3},{3,2},{4,5},{5,4},{6,7},{7,6},{8,9},{9,8},{10,11... | collective-permute-start | bytes 61448 | tf_op jit(solution)/shard_map/ppermute | solution.py:684
  10.3 0.3 %shard_map.115 = (bf16[96,96]{1,0:T(8,128)(2,1)S(1)}, bf16[64,96]{1,0:T(8,128)(2,1)S(1)}, s32[8,128]{1,0:T(8,128)S(1)}, f32[96,128]{1,0:T(8,128)S(1)}, f32[8,128...) custom-call(f32[4,24]{1,0:T(4,128)S(1)} %copy-done.3, ...), custom_call_target="tpu_custom_call" | custom-call | tf_op jit(solution)/shard_map/pallas_call | solution.py:652
  10.6 0.0 copy-start.2
  10.6 0.6 %shard_map.116 = (f32[4,24,768]{2,1,0:T(8,128)S(1)}, f32[8,768]{1,0:T(8,128)S(1)}, f32[96,768]{1,0:T(8,128)S(1)}) custom-call(f32[4,24,768]{2,1,0:T(8,128)S(1)} %get-tuple-element.44.refs_0_, f32[96,128]{1,0:T(8,128)S(1)} %get-tuple-element.49.refs_1_, f32[8,768]{1,0:T(8,128)S(1)} %copy-done.1, f32[24,544]{1,0:T(8,128)S(1)} %collective-permute-done.1.near.refs_3_.refs_15_, ...), custom_call_target="tpu_custom_call" | custom-call | tf_op jit(solution)/shard_map/pallas_call | solution.py:652
  11.2 0.7 %collective-permute-done.4.refs_18_ = f32[64,128]{1,0:T(8,128)S(1)} collective-permute-done((f32[64,128]{1,0:T(8,128)S(1)}, f32[64,128]{1,0:T(8,128)S(1)}, u32[]{:S(2)}, u32[]{:S(2)}) %collective-permute-start.4) | collective-permute-done | bytes 32800 | tf_op jit(solution)/shard_map/ppermute | solution.py:683
  12.0 0.6 %shard_map.117 = (f32[96,128]{1,0:T(8,128)S(1)}, f32[96,128]{1,0:T(8,128)S(1)}, f32[96,128]{1,0:T(8,128)S(1)}, f32[8,768]{1,0:T(8,128)S(1)}, f32[24,416]{1,0:T(8...) custom-call(f32[4,24,768]{2,1,0:T(8,128)S(1)} %get-tuple-element.51.refs_0_, ...), custom_call_target="tpu_custom_call" | custom-call | tf_op jit(solution)/shard_map/pallas_call | solution.py:652
  12.5 0.5 %collective-permute-start.5 = (f32[104,128]{1,0:T(8,128)S(1)}, f32[104,128]{1,0:T(8,128)S(1)}, u32[]{:S(2)}, u32[]{:S(2)}) collective-permute-start(f32[104,128]{1,0:T(8,128)S(1)} %get-tuple-element.67), channel_id=1, source_target_pairs={{0,9},{1,8},{2,11},{3,10},{4,13},{5,12},{6,15},{7,14},{8,1},{9,0},... | collective-permute-start | bytes 159752 | tf_op jit(solution)/shard_map/ppermute | solution.py:670
  13.0 0.2 collective-permute-start.6
  13.3 3.4 %collective-permute-start.7 = (f32[24,416]{1,0:T(8,128)S(1)}, f32[24,416]{1,0:T(8,128)S(1)}, u32[]{:S(2)}, u32[]{:S(2)}) collective-permute-start(f32[24,416]{1,0:T(8,128)S(1)} %get-tuple-element.70), channel_id=1, source_target_pairs={{1,2},{2,1},{3,4},{4,3},{5,6},{6,5},{9,10},{10,9},{11,12},{12,11},... | collective-permute-start | bytes 119816 | tf_op jit(solution)/shard_map/ppermute | solution.py:671
  16.7 0.1 collective-permute-start.9
  16.7 1.6 %collective-permute-start.8 = (f32[40,128]{1,0:T(8,128)S(1)}, f32[40,128]{1,0:T(8,128)S(1)}, u32[]{:S(2)}, u32[]{:S(2)}) collective-permute-start(f32[40,128]{1,0:T(8,128)S(1)} %get-tuple-element.76), channel_id=1, source_target_pairs={{0,1},{1,0},{2,3},{3,2},{4,5},{5,4},{6,7},{7,6},{8,9},{9,8},{10,11... | collective-permute-start | bytes 61448 | tf_op jit(solution)/shard_map/ppermute | solution.py:684
  18.4 0.4 %shard_map.119.refs_0_ = f32[4,24,768]{2,1,0:T(8,128)S(1)} custom-call(f32[4,24,768]{2,1,0:T(8,128)S(1)} %get-tuple-element.51.refs_0_, f32[8,768]{1,0:T(8,128)S(1)} %get-tuple-element.64.refs_1_, f32[96,128]{1,0:T(8,128)S(1)} %get-tuple-element.65.refs_2_, bf16[96,96]{1,0:T(8,128)(2,1)S(1)} %get-tuple-element.66.refs_3_, ...), custom_call_target="tpu_custom_call" | custom-call | tf_op jit(solution)/shard_map/pallas_call | solution.py:652
  18.8 0.6 %shard_map.120 = (f32[4,24,768]{2,1,0:T(8,128)S(1)}, f32[8,768]{1,0:T(8,128)S(1)}, f32[96,768]{1,0:T(8,128)S(1)}) custom-call(f32[4,24,768]{2,1,0:T(8,128)S(1)} %shard_map.119.refs_0_, f32[96,128]{1,0:T(8,128)S(1)} %get-tuple-element.49.refs_1_, f32[8,768]{1,0:T(8,128)S(1)} %copy-done.1, f32[24,544]{1,0:T(8,128)S(1)} %collective-permute-done.6.near.refs_3_.refs_15_, ...), custom_call_target="tpu_custom_call" | custom-call | tf_op jit(solution)/shard_map/pallas_call | solution.py:652
  19.4 0.7 %collective-permute-done.9.refs_18_ = f32[64,128]{1,0:T(8,128)S(1)} collective-permute-done((f32[64,128]{1,0:T(8,128)S(1)}, f32[64,128]{1,0:T(8,128)S(1)}, u32[]{:S(2)}, u32[]{:S(2)}) %collective-permute-start.9) | collective-permute-done | bytes 32800 | tf_op jit(solution)/shard_map/ppermute | solution.py:683
  20.1 0.6 %shard_map.121 = (f32[96,128]{1,0:T(8,128)S(1)}, f32[96,128]{1,0:T(8,128)S(1)}, f32[96,128]{1,0:T(8,128)S(1)}, f32[8,768]{1,0:T(8,128)S(1)}, f32[24,416]{1,0:T(8...) custom-call(f32[4,24,768]{2,1,0:T(8,128)S(1)} %get-tuple-element.71.refs_0_, ...), custom_call_target="tpu_custom_call" | custom-call | tf_op jit(solution)/shard_map/pallas_call | solution.py:652
  20.7 0.8 %collective-permute-start.10 = (f32[104,128]{1,0:T(8,128)S(1)}, f32[104,128]{1,0:T(8,128)S(1)}, u32[]{:S(2)}, u32[]{:S(2)}) collective-permute-start(f32[104,128]{1,0:T(8,128)S(1)} %get-tuple-element.79), channel_id=1, source_target_pairs={{0,9},{1,8},{2,11},{3,10},{4,13},{5,12},{6,15},{7,14},{8,1},{9,0},... | collective-permute-start | bytes 159752 | tf_op jit(solution)/shard_map/ppermute | solution.py:670
  21.4 0.6 %collective-permute-start.11 = (f32[24,544]{1,0:T(8,128)S(1)}, f32[24,544]{1,0:T(8,128)S(1)}, u32[]{:S(2)}, u32[]{:S(2)}) collective-permute-start(f32[24,544]{1,0:T(8,128)S(1)} %get-tuple-element.80), channel_id=1, source_target_pairs={{0,1},{1,0},{2,3},{3,2},{4,5},{5,4},{6,7},{7,6},{8,9},{9,8},{10,11... | collective-permute-start | bytes 156680 | tf_op jit(solution)/shard_map/ppermute | solution.py:672
  22.0 3.1 %collective-permute-start.12 = (f32[24,416]{1,0:T(8,128)S(1)}, f32[24,416]{1,0:T(8,128)S(1)}, u32[]{:S(2)}, u32[]{:S(2)}) collective-permute-start(f32[24,416]{1,0:T(8,128)S(1)} %get-tuple-element.82), channel_id=1, source_target_pairs={{1,2},{2,1},{3,4},{4,3},{5,6},{6,5},{9,10},{10,9},{11,12},{12,11},... | collective-permute-start | bytes 119816 | tf_op jit(solution)/shard_map/ppermute | solution.py:671
  25.2 0.1 collective-permute-start.14
  25.2 1.6 %collective-permute-start.13 = (f32[40,128]{1,0:T(8,128)S(1)}, f32[40,128]{1,0:T(8,128)S(1)}, u32[]{:S(2)}, u32[]{:S(2)}) collective-permute-start(f32[40,128]{1,0:T(8,128)S(1)} %get-tuple-element.85), channel_id=1, source_target_pairs={{0,1},{1,0},{2,3},{3,2},{4,5},{5,4},{6,7},{7,6},{8,9},{9,8},{10,11... | collective-permute-start | bytes 61448 | tf_op jit(solution)/shard_map/ppermute | solution.py:684
  26.9 0.4 %shard_map.123.refs_0_ = f32[4,24,768]{2,1,0:T(8,128)S(1)} custom-call(f32[4,24,768]{2,1,0:T(8,128)S(1)} %get-tuple-element.71.refs_0_, f32[8,768]{1,0:T(8,128)S(1)} %get-tuple-element.77.refs_1_, f32[96,128]{1,0:T(8,128)S(1)} %get-tuple-element.78.refs_2_, bf16[96,96]{1,0:T(8,128)(2,1)S(1)} %get-tuple-element.66.refs_3_, ...), custom_call_target="tpu_custom_call" | custom-call | tf_op jit(solution)/shard_map/pallas_call | solution.py:652
  27.3 0.5 %collective-permute-done.12.refs_4_.refs_10_ = f32[24,416]{1,0:T(8,128)S(1)} collective-permute-done((f32[24,416]{1,0:T(8,128)S(1)}, f32[24,416]{1,0:T(8,128)S(1)}, u32[]{:S(2)}, u32[]{:S(2)}) %collective-permute-start.12) | collective-permute-done | bytes 39968 | tf_op jit(solution)/shard_map/ppermute | solution.py:671
  27.7 0.5 %shard_map.124.refs_0_ = f32[4,24,768]{2,1,0:T(8,128)S(1)} custom-call(f32[4,24,768]{2,1,0:T(8,128)S(1)} %shard_map.123.refs_0_, f32[96,128]{1,0:T(8,128)S(1)} %get-tuple-element.49.refs_1_, f32[8,768]{1,0:T(8,128)S(1)} %copy-done.1, f32[24,544]{1,0:T(8,128)S(1)} %collective-permute-done.11.near.refs_3_.refs_9_, ...), custom_call_target="tpu_custom_call" | custom-call | tf_op jit(solution)/shard_map/pallas_call | solution.py:652
  28.2 0.3 %collective-permute-done.14.refs_12_ = f32[64,128]{1,0:T(8,128)S(1)} collective-permute-done((f32[64,128]{1,0:T(8,128)S(1)}, f32[64,128]{1,0:T(8,128)S(1)}, u32[]{:S(2)}, u32[]{:S(2)}) %collective-permute-start.14) | collective-permute-done | bytes 32800 | tf_op jit(solution)/shard_map/ppermute | solution.py:683
  28.6 1.1 %shard_map.125 = (f32[4,24,768]{2,1,0:T(8,128)}, f32[4,24,64]{2,1,0:T(8,128)}) custom-call(f32[4,24,768]{2,1,0:T(8,128)S(1)} %shard_map.124.refs_0_, f32[96,128]{1,0:T(8,128)S(1)} %get-tuple-element.83.refs_1_, f32[96,128]{1,0:T(8,128)S(1)} %get-tuple-element.84.refs_2_, bf16[96,96]{1,0:T(8,128)(2,1)S(1)} %get-tuple-element.66.refs_3_, ...), custom_call_target="tpu_custom_call" | custom-call | tf_op jit(solution)/shard_map/pallas_call | solution.py:652
  (23 shorter events, 0.1 us)
Async XLA Ops:
  0.6 9.6 %copy-start.3 = (f32[4,24]{1,0:T(4,128)S(1)}, f32[4,24]{1,0:T(4,128)}, u32[]{:S(2)}) copy-start(f32[4,24]{1,0:T(4,128)} %refs_0_.3) | copy-start | bytes 1156
  0.6 9.6 %copy-start.4 = (s32[4,24]{1,0:T(4,128)S(1)}, s32[4,24]{1,0:T(4,128)}, u32[]{:S(2)}) copy-start(s32[4,24]{1,0:T(4,128)} %refs_2_.6) | copy-start | bytes 1156
  0.7 9.6 %copy-start.5 = (f32[32]{0:T(128)S(1)}, f32[32]{0:T(128)}, u32[]{:S(2)}) copy-start(f32[32]{0:T(128)} %refs_1_.3) | copy-start | bytes 388
  0.7 9.9 %copy-start.1 = (f32[8,768]{1,0:T(8,128)S(1)}, f32[8,768]{1,0:T(8,128)}, u32[]{:S(2)}) copy-start(f32[8,768]{1,0:T(8,128)} %constant.10.clone.refs_2_.refs_13_.refs_7_) | copy-start | bytes 73732
  2.2 9.7 %copy-start = (bf16[1536,128]{1,0:T(8,128)(2,1)S(1)}, bf16[1536,128]{1,0:T(8,128)(2,1)}, u32[]{:S(2)}) copy-start(bf16[1536,128]{1,0:T(8,128)(2,1)} %constant.11.clone.refs_14_.refs_5_.refs_8_) | copy-start | bytes 1179652
  2.2 6.3 %collective-permute-start = (f32[104,128]{1,0:T(8,128)S(1)}, f32[104,128]{1,0:T(8,128)S(1)}, u32[]{:S(2)}, u32[]{:S(2)}) collective-permute-start(f32[104,128]{1,0:T(8,128)S(1)} %get-tuple-element.46), channel_id=1, source_target_pairs={{0,9},{1,8},{2,11},{3,10},{4,13},{5,12},{6,15},{7,14},{8,1},{9,0},... | collective-permute-start | bytes 159752 | tf_op jit(solution)/shard_map/ppermute | solution.py:670
  4.9 3.6 %collective-permute-start.1 = (f32[24,544]{1,0:T(8,128)S(1)}, f32[24,544]{1,0:T(8,128)S(1)}, u32[]{:S(2)}, u32[]{:S(2)}) collective-permute-start(f32[24,544]{1,0:T(8,128)S(1)} %get-tuple-element.47), channel_id=1, source_target_pairs={{0,1},{1,0},{2,3},{3,2},{4,5},{5,4},{6,7},{7,6},{8,9},{9,8},{10,11... | collective-permute-start | bytes 156680 | tf_op jit(solution)/shard_map/ppermute | solution.py:672
  4.9 5.7 %collective-permute-start.2 = (f32[24,416]{1,0:T(8,128)S(1)}, f32[24,416]{1,0:T(8,128)S(1)}, u32[]{:S(2)}, u32[]{:S(2)}) collective-permute-start(f32[24,416]{1,0:T(8,128)S(1)} %get-tuple-element.50), channel_id=1, source_target_pairs={{1,2},{2,1},{3,4},{4,3},{5,6},{6,5},{9,10},{10,9},{11,12},{12,11},... | collective-permute-start | bytes 119816 | tf_op jit(solution)/shard_map/ppermute | solution.py:671
  8.5 3.4 %collective-permute-start.4 = (f32[64,128]{1,0:T(8,128)S(1)}, f32[64,128]{1,0:T(8,128)S(1)}, u32[]{:S(2)}, u32[]{:S(2)}) collective-permute-start(f32[64,128]{1,0:T(8,128)S(1)} %get-tuple-element.48.refs_4_), channel_id=1, source_target_pairs={{0,17},{1,16},{2,19},{3,18},{4,21},{5,20},{6,23},{7,22},{8,25},{9,... | collective-permute-start | bytes 98312 | tf_op jit(solution)/shard_map/ppermute | solution.py:683
  9.0 2.2 %collective-permute-start.3 = (f32[40,128]{1,0:T(8,128)S(1)}, f32[40,128]{1,0:T(8,128)S(1)}, u32[]{:S(2)}, u32[]{:S(2)}) collective-permute-start(f32[40,128]{1,0:T(8,128)S(1)} %get-tuple-element.63), channel_id=1, source_target_pairs={{0,1},{1,0},{2,3},{3,2},{4,5},{5,4},{6,7},{7,6},{8,9},{9,8},{10,11... | collective-permute-start | bytes 61448 | tf_op jit(solution)/shard_map/ppermute | solution.py:684
  10.6 1.4 %copy-start.2 = (bf16[384,256]{1,0:T(8,128)(2,1)S(1)}, bf16[384,256]{1,0:T(8,128)(2,1)}, u32[]{:S(2)}) copy-start(bf16[384,256]{1,0:T(8,128)(2,1)} %constant.9.clone.refs_12_) | copy-start | bytes 589828
  12.5 4.1 %collective-permute-start.5 = (f32[104,128]{1,0:T(8,128)S(1)}, f32[104,128]{1,0:T(8,128)S(1)}, u32[]{:S(2)}, u32[]{:S(2)}) collective-permute-start(f32[104,128]{1,0:T(8,128)S(1)} %get-tuple-element.67), channel_id=1, source_target_pairs={{0,9},{1,8},{2,11},{3,10},{4,13},{5,12},{6,15},{7,14},{8,1},{9,0},... | collective-permute-start | bytes 159752 | tf_op jit(solution)/shard_map/ppermute | solution.py:670
  13.0 3.6 %collective-permute-start.6 = (f32[24,544]{1,0:T(8,128)S(1)}, f32[24,544]{1,0:T(8,128)S(1)}, u32[]{:S(2)}, u32[]{:S(2)}) collective-permute-start(f32[24,544]{1,0:T(8,128)S(1)} %get-tuple-element.68), channel_id=1, source_target_pairs={{0,1},{1,0},{2,3},{3,2},{4,5},{5,4},{6,7},{7,6},{8,9},{9,8},{10,11... | collective-permute-start | bytes 156680 | tf_op jit(solution)/shard_map/ppermute | solution.py:672
  13.3 5.5 %collective-permute-start.7 = (f32[24,416]{1,0:T(8,128)S(1)}, f32[24,416]{1,0:T(8,128)S(1)}, u32[]{:S(2)}, u32[]{:S(2)}) collective-permute-start(f32[24,416]{1,0:T(8,128)S(1)} %get-tuple-element.70), channel_id=1, source_target_pairs={{1,2},{2,1},{3,4},{4,3},{5,6},{6,5},{9,10},{10,9},{11,12},{12,11},... | collective-permute-start | bytes 119816 | tf_op jit(solution)/shard_map/ppermute | solution.py:671
  16.7 3.4 %collective-permute-start.9 = (f32[64,128]{1,0:T(8,128)S(1)}, f32[64,128]{1,0:T(8,128)S(1)}, u32[]{:S(2)}, u32[]{:S(2)}) collective-permute-start(f32[64,128]{1,0:T(8,128)S(1)} %get-tuple-element.69.refs_6_), channel_id=1, source_target_pairs={{0,17},{1,16},{2,19},{3,18},{4,21},{5,20},{6,23},{7,22},{8,25},{9,... | collective-permute-start | bytes 98312 | tf_op jit(solution)/shard_map/ppermute | solution.py:683
  16.7 2.6 %collective-permute-start.8 = (f32[40,128]{1,0:T(8,128)S(1)}, f32[40,128]{1,0:T(8,128)S(1)}, u32[]{:S(2)}, u32[]{:S(2)}) collective-permute-start(f32[40,128]{1,0:T(8,128)S(1)} %get-tuple-element.76), channel_id=1, source_target_pairs={{0,1},{1,0},{2,3},{3,2},{4,5},{5,4},{6,7},{7,6},{8,9},{9,8},{10,11... | collective-permute-start | bytes 61448 | tf_op jit(solution)/shard_map/ppermute | solution.py:684
  20.7 4.5 %collective-permute-start.10 = (f32[104,128]{1,0:T(8,128)S(1)}, f32[104,128]{1,0:T(8,128)S(1)}, u32[]{:S(2)}, u32[]{:S(2)}) collective-permute-start(f32[104,128]{1,0:T(8,128)S(1)} %get-tuple-element.79), channel_id=1, source_target_pairs={{0,9},{1,8},{2,11},{3,10},{4,13},{5,12},{6,15},{7,14},{8,1},{9,0},... | collective-permute-start | bytes 159752 | tf_op jit(solution)/shard_map/ppermute | solution.py:670
  21.4 3.7 %collective-permute-start.11 = (f32[24,544]{1,0:T(8,128)S(1)}, f32[24,544]{1,0:T(8,128)S(1)}, u32[]{:S(2)}, u32[]{:S(2)}) collective-permute-start(f32[24,544]{1,0:T(8,128)S(1)} %get-tuple-element.80), channel_id=1, source_target_pairs={{0,1},{1,0},{2,3},{3,2},{4,5},{5,4},{6,7},{7,6},{8,9},{9,8},{10,11... | collective-permute-start | bytes 156680 | tf_op jit(solution)/shard_map/ppermute | solution.py:672
  22.0 5.7 %collective-permute-start.12 = (f32[24,416]{1,0:T(8,128)S(1)}, f32[24,416]{1,0:T(8,128)S(1)}, u32[]{:S(2)}, u32[]{:S(2)}) collective-permute-start(f32[24,416]{1,0:T(8,128)S(1)} %get-tuple-element.82), channel_id=1, source_target_pairs={{1,2},{2,1},{3,4},{4,3},{5,6},{6,5},{9,10},{10,9},{11,12},{12,11},... | collective-permute-start | bytes 119816 | tf_op jit(solution)/shard_map/ppermute | solution.py:671
  25.2 3.4 %collective-permute-start.14 = (f32[64,128]{1,0:T(8,128)S(1)}, f32[64,128]{1,0:T(8,128)S(1)}, u32[]{:S(2)}, u32[]{:S(2)}) collective-permute-start(f32[64,128]{1,0:T(8,128)S(1)} %get-tuple-element.81.refs_6_), channel_id=1, source_target_pairs={{0,17},{1,16},{2,19},{3,18},{4,21},{5,20},{6,23},{7,22},{8,25},{9,... | collective-permute-start | bytes 98312 | tf_op jit(solution)/shard_map/ppermute | solution.py:683
  25.2 3.0 %collective-permute-start.13 = (f32[40,128]{1,0:T(8,128)S(1)}, f32[40,128]{1,0:T(8,128)S(1)}, u32[]{:S(2)}, u32[]{:S(2)}) collective-permute-start(f32[40,128]{1,0:T(8,128)S(1)} %get-tuple-element.85), channel_id=1, source_target_pairs={{0,1},{1,0},{2,3},{3,2},{4,5},{5,4},{6,7},{7,6},{8,9},{9,8},{10,11... | collective-permute-start | bytes 61448 | tf_op jit(solution)/shard_map/ppermute | solution.py:684

commit v16 on v14

--- a/solution.py
+++ b/solution.py
@@ -463,6 +463,35 @@
     masks = Directions(block)
     place = lax.broadcasted_iota(jnp.int32, block, 0)
     outside = place == jnp.where(masks.eastward, 0, cols - 1)
+
+    def edge_tile(first, second, tile):
+        half = tile % (tiles // 2)
+        half = slice(half * LANES, (half + 1) * LANES)
+        came = jnp.where(even, first[:, half], second[:, half])
+        return came if tile < tiles // 2 else pltpu.roll(came, LANES - NDIR // 2, 1)
+
+    def fill(row, tile):
+        lanes = slice(tile * LANES, (tile + 1) * LANES)
+        rate = turn[row * cols : (row + 1) * cols, :]
+        stay, along_x, along_y, gain = (rates[k : k + 1, lanes] for k in range(4))
+        center = waves[row, :, lanes]
+        south = waves[row - 1, :, lanes] if row else edge_tile(far, near, tile)
+        north = waves[row + 1, :, lanes] if row < rows - 1 else edge_tile(near, far, tile)
+        moved = (
+            stay * center
+            + jnp.where(outside, 0.0, along_x)
+            * jnp.where(
+                masks.eastward, pltpu.roll(center, 1, 0), pltpu.roll(center, cols - 1, 0)
+            )
+            + along_y * jnp.where(masks.northward, south, north)
+        )
+        turned_out[row, :, lanes] = masks.turned(moved, rate, gain)
+
+    if len(refs) == 1:
+        for row in range(rows):
+            for tile in range(tiles):
+                fill(row, tile)
+        return
     for tile in range(tiles):
         lanes = slice(tile * LANES, (tile + 1) * LANES)
         stay, along_x, along_y, gain = (rates[k : k + 1, lanes] for k in range(4))

time: 29.9 us -> 29.9 us (level)
  transfers between devices with their start and end apart: 15 -> 15, of which waited for: 3 -> 3; matrix products, arithmetic and copies ran while one was open for 0% -> 0% of each run, Pallas kernels for 13% -> 12%
where the time goes in v16:
time: 29.9 us; the launch traced here: 29.7 us
  starting transfers between devices  19.6 us (66%)
  Pallas kernels  7.45 us (25%)
  waiting for transfers between devices  1.82 us (6%)
  between operations  0.84 us (3%)
    ppermute x3, starting transfers between devices, exchange(): far_in = lax.ppermute(to_far, axes[0], others)  10 us
    pallas_call x13, Pallas kernels, call(): pl.pallas_call(functools.partial(kernel, plan, axes), out_shape=outs, in_...  7.45 us
    ppermute x3, starting transfers between devices, exchange(): got = [lax.ppermute(to_mate, axes[0], pairs), from_y]  4.18 us
    ppermute x3, starting transfers between devices, exchange(): from_x = lax.ppermute(to_x, both_axes, plan.crossing(1))  3.8 us
    ppermute x3, waiting for transfers between devices, exchange(): from_y = lax.ppermute(first, both_axes, plan.crossing(2))  1.14 us
    ppermute x3, starting transfers between devices, exchange(): near_in = lax.ppermute(to_near, axes[0], pairs)  0.97 us
    ppermute x3, waiting for transfers between devices, exchange(): far_in = lax.ppermute(to_far, axes[0], others)  0.65 us
    ppermute x3, starting transfers between devices, exchange(): from_y = lax.ppermute(first, both_axes, plan.crossing(2))  0.63 us
  transfers between devices with their start and end apart: 15, of which 3 were waited for; matrix products, arithmetic and copies ran while one was open for 0% of the time, Pallas kernels for 12%

profile of v16, /device:TPU:1, one launch (start us, length us, event | category | flops | bytes accessed | tf_op | source)
XLA Modules:
  0.0 29.7 jit_solution(6058547285798553092)
XLA Ops:
  0.6 1.5 %shard_map.113 = (f32[4,24,768]{2,1,0:T(8,128)S(1)}, f32[96,128]{1,0:T(8,128)S(1)}, f32[96,128]{1,0:T(8,128)S(1)}, bf16[96,192]{1,0:T(8,128)(2,1)S(1)}, f32[104,...) custom-call(f32[4,24,768]{2,1,0:T(8,128)} %refs_0_.2, f32[4,24,64]{2,1,0:T(8,128)} %refs_1_.2, ...), custom_call_target="tpu_custom_call" | custom-call | tf_op jit(solution)/shard_map/pallas_call | solution.py:662
  2.2 2.7 %collective-permute-start = (f32[104,128]{1,0:T(8,128)S(1)}, f32[104,128]{1,0:T(8,128)S(1)}, u32[]{:S(2)}, u32[]{:S(2)}) collective-permute-start(f32[104,128]{1,0:T(8,128)S(1)} %get-tuple-element.49), channel_id=1, source_target_pairs={{0,9},{1,8},{2,11},{3,10},{4,13},{5,12},{6,15},{7,14},{8,1},{9,0},... | collective-permute-start | bytes 159752 | tf_op jit(solution)/shard_map/ppermute | solution.py:680
  4.8 0.0 collective-permute-start.1
  4.8 3.6 %collective-permute-start.2 = (f32[24,416]{1,0:T(8,128)S(1)}, f32[24,416]{1,0:T(8,128)S(1)}, u32[]{:S(2)}, u32[]{:S(2)}) collective-permute-start(f32[24,416]{1,0:T(8,128)S(1)} %get-tuple-element.54), channel_id=1, source_target_pairs={{1,2},{2,1},{3,4},{4,3},{5,6},{6,5},{9,10},{10,9},{11,12},{12,11},... | collective-permute-start | bytes 119816 | tf_op jit(solution)/shard_map/ppermute | solution.py:681
  8.5 0.0 collective-permute-done.from_x
  8.5 0.5 %collective-permute-start.4 = (f32[64,128]{1,0:T(8,128)S(1)}, f32[64,128]{1,0:T(8,128)S(1)}, u32[]{:S(2)}, u32[]{:S(2)}) collective-permute-start(f32[64,128]{1,0:T(8,128)S(1)} %get-tuple-element.51.refs_7_), channel_id=1, source_target_pairs={{0,17},{1,16},{2,19},{3,18},{4,21},{5,20},{6,23},{7,22},{8,25},{9,... | collective-permute-start | bytes 98312 | tf_op jit(solution)/shard_map/ppermute | solution.py:693
  9.0 1.2 %collective-permute-start.3 = (f32[40,128]{1,0:T(8,128)S(1)}, f32[40,128]{1,0:T(8,128)S(1)}, u32[]{:S(2)}, u32[]{:S(2)}) collective-permute-start(f32[40,128]{1,0:T(8,128)S(1)} %get-tuple-element.69), channel_id=1, source_target_pairs={{0,1},{1,0},{2,3},{3,2},{4,5},{5,4},{6,7},{7,6},{8,9},{9,8},{10,11... | collective-permute-start | bytes 61448 | tf_op jit(solution)/shard_map/ppermute | solution.py:694
  10.2 1.2 %shard_map.115 = (bf16[96,96]{1,0:T(8,128)(2,1)S(1)}, bf16[64,96]{1,0:T(8,128)(2,1)S(1)}, s32[8,128]{1,0:T(8,128)S(1)}, f32[96,128]{1,0:T(8,128)S(1)}, f32[8,128...) custom-call(f32[4,24]{1,0:T(4,128)} %refs_0_.3, ...), custom_call_target="tpu_custom_call" | custom-call | tf_op jit(solution)/shard_map/pallas_call | solution.py:662
  11.4 0.0 collective-permute-done.2.refs_4_.refs_16_
  11.4 0.6 %shard_map.116 = (f32[4,24,768]{2,1,0:T(8,128)S(1)}, f32[8,768]{1,0:T(8,128)S(1)}, f32[96,768]{1,0:T(8,128)S(1)}) custom-call(f32[4,24,768]{2,1,0:T(8,128)S(1)} %get-tuple-element.47.refs_0_, f32[96,128]{1,0:T(8,128)S(1)} %get-tuple-element.52.refs_1_, f32[8,768]{1,0:T(8,128)S(1)} %get-tuple-element.53.refs_2_.refs_13_.refs_7_, ...), custom_call_target="tpu_custom_call" | custom-call | tf_op jit(solution)/shard_map/pallas_call | solution.py:662
  12.0 0.0 collective-permute-done.4.refs_18_
  12.0 0.6 %shard_map.117 = (f32[96,128]{1,0:T(8,128)S(1)}, f32[96,128]{1,0:T(8,128)S(1)}, f32[96,128]{1,0:T(8,128)S(1)}, f32[8,768]{1,0:T(8,128)S(1)}, f32[24,416]{1,0:T(8...) custom-call(f32[4,24,768]{2,1,0:T(8,128)S(1)} %get-tuple-element.55.refs_0_, ...), custom_call_target="tpu_custom_call" | custom-call | tf_op jit(solution)/shard_map/pallas_call | solution.py:662
  12.6 0.5 %collective-permute-start.5 = (f32[104,128]{1,0:T(8,128)S(1)}, f32[104,128]{1,0:T(8,128)S(1)}, u32[]{:S(2)}, u32[]{:S(2)}) collective-permute-start(f32[104,128]{1,0:T(8,128)S(1)} %get-tuple-element.73), channel_id=1, source_target_pairs={{0,9},{1,8},{2,11},{3,10},{4,13},{5,12},{6,15},{7,14},{8,1},{9,0},... | collective-permute-start | bytes 159752 | tf_op jit(solution)/shard_map/ppermute | solution.py:680
  13.1 0.2 collective-permute-start.6
  13.3 3.4 %collective-permute-start.7 = (f32[24,416]{1,0:T(8,128)S(1)}, f32[24,416]{1,0:T(8,128)S(1)}, u32[]{:S(2)}, u32[]{:S(2)}) collective-permute-start(f32[24,416]{1,0:T(8,128)S(1)} %get-tuple-element.76), channel_id=1, source_target_pairs={{1,2},{2,1},{3,4},{4,3},{5,6},{6,5},{9,10},{10,9},{11,12},{12,11},... | collective-permute-start | bytes 119816 | tf_op jit(solution)/shard_map/ppermute | solution.py:681
  16.7 0.1 collective-permute-start.9
  16.8 1.5 %collective-permute-start.8 = (f32[40,128]{1,0:T(8,128)S(1)}, f32[40,128]{1,0:T(8,128)S(1)}, u32[]{:S(2)}, u32[]{:S(2)}) collective-permute-start(f32[40,128]{1,0:T(8,128)S(1)} %get-tuple-element.82), channel_id=1, source_target_pairs={{0,1},{1,0},{2,3},{3,2},{4,5},{5,4},{6,7},{7,6},{8,9},{9,8},{10,11... | collective-permute-start | bytes 61448 | tf_op jit(solution)/shard_map/ppermute | solution.py:694
  18.3 0.4 %shard_map.119.refs_0_ = f32[4,24,768]{2,1,0:T(8,128)S(1)} custom-call(f32[4,24,768]{2,1,0:T(8,128)S(1)} %get-tuple-element.55.refs_0_, f32[8,768]{1,0:T(8,128)S(1)} %get-tuple-element.70.refs_1_, f32[96,128]{1,0:T(8,128)S(1)} %get-tuple-element.71.refs_2_, bf16[96,96]{1,0:T(8,128)(2,1)S(1)} %get-tuple-element.72.refs_3_, ...), custom_call_target="tpu_custom_call" | custom-call | tf_op jit(solution)/shard_map/pallas_call | solution.py:662
  18.7 0.0 collective-permute-done.7.refs_4_.refs_16_
  18.7 0.6 %shard_map.120 = (f32[4,24,768]{2,1,0:T(8,128)S(1)}, f32[8,768]{1,0:T(8,128)S(1)}, f32[96,768]{1,0:T(8,128)S(1)}) custom-call(f32[4,24,768]{2,1,0:T(8,128)S(1)} %shard_map.119.refs_0_, f32[96,128]{1,0:T(8,128)S(1)} %get-tuple-element.52.refs_1_, f32[8,768]{1,0:T(8,128)S(1)} %get-tuple-element.53.refs_2_.refs_13_.refs_7_, ...), custom_call_target="tpu_custom_call" | custom-call | tf_op jit(solution)/shard_map/pallas_call | solution.py:662
  19.3 0.8 %collective-permute-done.9.refs_18_ = f32[64,128]{1,0:T(8,128)S(1)} collective-permute-done((f32[64,128]{1,0:T(8,128)S(1)}, f32[64,128]{1,0:T(8,128)S(1)}, u32[]{:S(2)}, u32[]{:S(2)}) %collective-permute-start.9) | collective-permute-done | bytes 32800 | tf_op jit(solution)/shard_map/ppermute | solution.py:693
  20.1 0.6 %shard_map.121 = (f32[96,128]{1,0:T(8,128)S(1)}, f32[96,128]{1,0:T(8,128)S(1)}, f32[96,128]{1,0:T(8,128)S(1)}, f32[8,768]{1,0:T(8,128)S(1)}, f32[24,416]{1,0:T(8...) custom-call(f32[4,24,768]{2,1,0:T(8,128)S(1)} %get-tuple-element.77.refs_0_, ...), custom_call_target="tpu_custom_call" | custom-call | tf_op jit(solution)/shard_map/pallas_call | solution.py:662
  20.7 0.6 %collective-permute-start.10 = (f32[104,128]{1,0:T(8,128)S(1)}, f32[104,128]{1,0:T(8,128)S(1)}, u32[]{:S(2)}, u32[]{:S(2)}) collective-permute-start(f32[104,128]{1,0:T(8,128)S(1)} %get-tuple-element.85), channel_id=1, source_target_pairs={{0,9},{1,8},{2,11},{3,10},{4,13},{5,12},{6,15},{7,14},{8,1},{9,0},... | collective-permute-start | bytes 159752 | tf_op jit(solution)/shard_map/ppermute | solution.py:680
  21.3 0.7 %collective-permute-start.11 = (f32[24,544]{1,0:T(8,128)S(1)}, f32[24,544]{1,0:T(8,128)S(1)}, u32[]{:S(2)}, u32[]{:S(2)}) collective-permute-start(f32[24,544]{1,0:T(8,128)S(1)} %get-tuple-element.86), channel_id=1, source_target_pairs={{0,1},{1,0},{2,3},{3,2},{4,5},{5,4},{6,7},{7,6},{8,9},{9,8},{10,11... | collective-permute-start | bytes 156680 | tf_op jit(solution)/shard_map/ppermute | solution.py:682
  22.1 3.1 %collective-permute-start.12 = (f32[24,416]{1,0:T(8,128)S(1)}, f32[24,416]{1,0:T(8,128)S(1)}, u32[]{:S(2)}, u32[]{:S(2)}) collective-permute-start(f32[24,416]{1,0:T(8,128)S(1)} %get-tuple-element.88), channel_id=1, source_target_pairs={{1,2},{2,1},{3,4},{4,3},{5,6},{6,5},{9,10},{10,9},{11,12},{12,11},... | collective-permute-start | bytes 119816 | tf_op jit(solution)/shard_map/ppermute | solution.py:681
  25.2 0.1 collective-permute-start.14
  25.3 1.5 %collective-permute-start.13 = (f32[40,128]{1,0:T(8,128)S(1)}, f32[40,128]{1,0:T(8,128)S(1)}, u32[]{:S(2)}, u32[]{:S(2)}) collective-permute-start(f32[40,128]{1,0:T(8,128)S(1)} %get-tuple-element.91), channel_id=1, source_target_pairs={{0,1},{1,0},{2,3},{3,2},{4,5},{5,4},{6,7},{7,6},{8,9},{9,8},{10,11... | collective-permute-start | bytes 61448 | tf_op jit(solution)/shard_map/ppermute | solution.py:694
  26.8 0.4 %shard_map.123.refs_0_ = f32[4,24,768]{2,1,0:T(8,128)S(1)} custom-call(f32[4,24,768]{2,1,0:T(8,128)S(1)} %get-tuple-element.77.refs_0_, f32[8,768]{1,0:T(8,128)S(1)} %get-tuple-element.83.refs_1_, f32[96,128]{1,0:T(8,128)S(1)} %get-tuple-element.84.refs_2_, bf16[96,96]{1,0:T(8,128)(2,1)S(1)} %get-tuple-element.72.refs_3_, ...), custom_call_target="tpu_custom_call" | custom-call | tf_op jit(solution)/shard_map/pallas_call | solution.py:662
  27.2 0.6 %collective-permute-done.12.refs_4_.refs_10_ = f32[24,416]{1,0:T(8,128)S(1)} collective-permute-done((f32[24,416]{1,0:T(8,128)S(1)}, f32[24,416]{1,0:T(8,128)S(1)}, u32[]{:S(2)}, u32[]{:S(2)}) %collective-permute-start.12) | collective-permute-done | bytes 39968 | tf_op jit(solution)/shard_map/ppermute | solution.py:681
  27.8 0.5 %shard_map.124.refs_0_ = f32[4,24,768]{2,1,0:T(8,128)S(1)} custom-call(f32[4,24,768]{2,1,0:T(8,128)S(1)} %shard_map.123.refs_0_, f32[96,128]{1,0:T(8,128)S(1)} %get-tuple-element.52.refs_1_, f32[8,768]{1,0:T(8,128)S(1)} %get-tuple-element.53.refs_2_.refs_13_.refs_7_, f32[24,544]{1,0:T(8,128)S(1)} %collective-permute-done.11.near.refs_3_.refs_9_, ...), custom_call_target="tpu_custom_call" | custom-call | tf_op jit(solution)/shard_map/pallas_call | solution.py:662
  28.3 0.3 %collective-permute-done.14.refs_12_ = f32[64,128]{1,0:T(8,128)S(1)} collective-permute-done((f32[64,128]{1,0:T(8,128)S(1)}, f32[64,128]{1,0:T(8,128)S(1)}, u32[]{:S(2)}, u32[]{:S(2)}) %collective-permute-start.14) | collective-permute-done | bytes 32800 | tf_op jit(solution)/shard_map/ppermute | solution.py:693
  28.6 1.1 %shard_map.125 = (f32[4,24,768]{2,1,0:T(8,128)}, f32[4,24,64]{2,1,0:T(8,128)}) custom-call(f32[4,24,768]{2,1,0:T(8,128)S(1)} %shard_map.124.refs_0_, f32[96,128]{1,0:T(8,128)S(1)} %get-tuple-element.89.refs_1_, f32[96,128]{1,0:T(8,128)S(1)} %get-tuple-element.90.refs_2_, bf16[96,96]{1,0:T(8,128)(2,1)S(1)} %get-tuple-element.72.refs_3_, ...), custom_call_target="tpu_custom_call" | custom-call | tf_op jit(solution)/shard_map/pallas_call | solution.py:662
  (11 shorter events, 0.0 us)
Async XLA Ops:
  2.2 6.3 %collective-permute-start = (f32[104,128]{1,0:T(8,128)S(1)}, f32[104,128]{1,0:T(8,128)S(1)}, u32[]{:S(2)}, u32[]{:S(2)}) collective-permute-start(f32[104,128]{1,0:T(8,128)S(1)} %get-tuple-element.49), channel_id=1, source_target_pairs={{0,9},{1,8},{2,11},{3,10},{4,13},{5,12},{6,15},{7,14},{8,1},{9,0},... | collective-permute-start | bytes 159752 | tf_op jit(solution)/shard_map/ppermute | solution.py:680
  4.8 3.6 %collective-permute-start.1 = (f32[24,544]{1,0:T(8,128)S(1)}, f32[24,544]{1,0:T(8,128)S(1)}, u32[]{:S(2)}, u32[]{:S(2)}) collective-permute-start(f32[24,544]{1,0:T(8,128)S(1)} %get-tuple-element.50), channel_id=1, source_target_pairs={{0,1},{1,0},{2,3},{3,2},{4,5},{5,4},{6,7},{7,6},{8,9},{9,8},{10,11... | collective-permute-start | bytes 156680 | tf_op jit(solution)/shard_map/ppermute | solution.py:682
  4.8 6.5 %collective-permute-start.2 = (f32[24,416]{1,0:T(8,128)S(1)}, f32[24,416]{1,0:T(8,128)S(1)}, u32[]{:S(2)}, u32[]{:S(2)}) collective-permute-start(f32[24,416]{1,0:T(8,128)S(1)} %get-tuple-element.54), channel_id=1, source_target_pairs={{1,2},{2,1},{3,4},{4,3},{5,6},{6,5},{9,10},{10,9},{11,12},{12,11},... | collective-permute-start | bytes 119816 | tf_op jit(solution)/shard_map/ppermute | solution.py:681
  8.5 3.5 %collective-permute-start.4 = (f32[64,128]{1,0:T(8,128)S(1)}, f32[64,128]{1,0:T(8,128)S(1)}, u32[]{:S(2)}, u32[]{:S(2)}) collective-permute-start(f32[64,128]{1,0:T(8,128)S(1)} %get-tuple-element.51.refs_7_), channel_id=1, source_target_pairs={{0,17},{1,16},{2,19},{3,18},{4,21},{5,20},{6,23},{7,22},{8,25},{9,... | collective-permute-start | bytes 98312 | tf_op jit(solution)/shard_map/ppermute | solution.py:693
  9.0 3.0 %collective-permute-start.3 = (f32[40,128]{1,0:T(8,128)S(1)}, f32[40,128]{1,0:T(8,128)S(1)}, u32[]{:S(2)}, u32[]{:S(2)}) collective-permute-start(f32[40,128]{1,0:T(8,128)S(1)} %get-tuple-element.69), channel_id=1, source_target_pairs={{0,1},{1,0},{2,3},{3,2},{4,5},{5,4},{6,7},{7,6},{8,9},{9,8},{10,11... | collective-permute-start | bytes 61448 | tf_op jit(solution)/shard_map/ppermute | solution.py:694
  12.6 4.1 %collective-permute-start.5 = (f32[104,128]{1,0:T(8,128)S(1)}, f32[104,128]{1,0:T(8,128)S(1)}, u32[]{:S(2)}, u32[]{:S(2)}) collective-permute-start(f32[104,128]{1,0:T(8,128)S(1)} %get-tuple-element.73), channel_id=1, source_target_pairs={{0,9},{1,8},{2,11},{3,10},{4,13},{5,12},{6,15},{7,14},{8,1},{9,0},... | collective-permute-start | bytes 159752 | tf_op jit(solution)/shard_map/ppermute | solution.py:680
  13.1 3.6 %collective-permute-start.6 = (f32[24,544]{1,0:T(8,128)S(1)}, f32[24,544]{1,0:T(8,128)S(1)}, u32[]{:S(2)}, u32[]{:S(2)}) collective-permute-start(f32[24,544]{1,0:T(8,128)S(1)} %get-tuple-element.74), channel_id=1, source_target_pairs={{0,1},{1,0},{2,3},{3,2},{4,5},{5,4},{6,7},{7,6},{8,9},{9,8},{10,11... | collective-permute-start | bytes 156680 | tf_op jit(solution)/shard_map/ppermute | solution.py:682
  13.3 5.4 %collective-permute-start.7 = (f32[24,416]{1,0:T(8,128)S(1)}, f32[24,416]{1,0:T(8,128)S(1)}, u32[]{:S(2)}, u32[]{:S(2)}) collective-permute-start(f32[24,416]{1,0:T(8,128)S(1)} %get-tuple-element.76), channel_id=1, source_target_pairs={{1,2},{2,1},{3,4},{4,3},{5,6},{6,5},{9,10},{10,9},{11,12},{12,11},... | collective-permute-start | bytes 119816 | tf_op jit(solution)/shard_map/ppermute | solution.py:681
  16.7 3.4 %collective-permute-start.9 = (f32[64,128]{1,0:T(8,128)S(1)}, f32[64,128]{1,0:T(8,128)S(1)}, u32[]{:S(2)}, u32[]{:S(2)}) collective-permute-start(f32[64,128]{1,0:T(8,128)S(1)} %get-tuple-element.75.refs_6_), channel_id=1, source_target_pairs={{0,17},{1,16},{2,19},{3,18},{4,21},{5,20},{6,23},{7,22},{8,25},{9,... | collective-permute-start | bytes 98312 | tf_op jit(solution)/shard_map/ppermute | solution.py:693
  16.8 2.5 %collective-permute-start.8 = (f32[40,128]{1,0:T(8,128)S(1)}, f32[40,128]{1,0:T(8,128)S(1)}, u32[]{:S(2)}, u32[]{:S(2)}) collective-permute-start(f32[40,128]{1,0:T(8,128)S(1)} %get-tuple-element.82), channel_id=1, source_target_pairs={{0,1},{1,0},{2,3},{3,2},{4,5},{5,4},{6,7},{7,6},{8,9},{9,8},{10,11... | collective-permute-start | bytes 61448 | tf_op jit(solution)/shard_map/ppermute | solution.py:694
  20.7 4.5 %collective-permute-start.10 = (f32[104,128]{1,0:T(8,128)S(1)}, f32[104,128]{1,0:T(8,128)S(1)}, u32[]{:S(2)}, u32[]{:S(2)}) collective-permute-start(f32[104,128]{1,0:T(8,128)S(1)} %get-tuple-element.85), channel_id=1, source_target_pairs={{0,9},{1,8},{2,11},{3,10},{4,13},{5,12},{6,15},{7,14},{8,1},{9,0},... | collective-permute-start | bytes 159752 | tf_op jit(solution)/shard_map/ppermute | solution.py:680
  21.3 3.8 %collective-permute-start.11 = (f32[24,544]{1,0:T(8,128)S(1)}, f32[24,544]{1,0:T(8,128)S(1)}, u32[]{:S(2)}, u32[]{:S(2)}) collective-permute-start(f32[24,544]{1,0:T(8,128)S(1)} %get-tuple-element.86), channel_id=1, source_target_pairs={{0,1},{1,0},{2,3},{3,2},{4,5},{5,4},{6,7},{7,6},{8,9},{9,8},{10,11... | collective-permute-start | bytes 156680 | tf_op jit(solution)/shard_map/ppermute | solution.py:682
  22.1 5.7 %collective-permute-start.12 = (f32[24,416]{1,0:T(8,128)S(1)}, f32[24,416]{1,0:T(8,128)S(1)}, u32[]{:S(2)}, u32[]{:S(2)}) collective-permute-start(f32[24,416]{1,0:T(8,128)S(1)} %get-tuple-element.88), channel_id=1, source_target_pairs={{1,2},{2,1},{3,4},{4,3},{5,6},{6,5},{9,10},{10,9},{11,12},{12,11},... | collective-permute-start | bytes 119816 | tf_op jit(solution)/shard_map/ppermute | solution.py:681
  25.2 3.4 %collective-permute-start.14 = (f32[64,128]{1,0:T(8,128)S(1)}, f32[64,128]{1,0:T(8,128)S(1)}, u32[]{:S(2)}, u32[]{:S(2)}) collective-permute-start(f32[64,128]{1,0:T(8,128)S(1)} %get-tuple-element.87.refs_6_), channel_id=1, source_target_pairs={{0,17},{1,16},{2,19},{3,18},{4,21},{5,20},{6,23},{7,22},{8,25},{9,... | collective-permute-start | bytes 98312 | tf_op jit(solution)/shard_map/ppermute | solution.py:693
  25.3 3.0 %collective-permute-start.13 = (f32[40,128]{1,0:T(8,128)S(1)}, f32[40,128]{1,0:T(8,128)S(1)}, u32[]{:S(2)}, u32[]{:S(2)}) collective-permute-start(f32[40,128]{1,0:T(8,128)S(1)} %get-tuple-element.91), channel_id=1, source_target_pairs={{0,1},{1,0},{2,3},{3,2},{4,5},{5,4},{6,7},{7,6},{8,9},{9,8},{10,11... | collective-permute-start | bytes 61448 | tf_op jit(solution)/shard_map/ppermute | solution.py:694
